TPU v7x, 32 devices: a whole 2x2x4 slice. The times are simulated.
32 devices in a mesh: groups: 2 (over y), seq: 4 (over z), fsdp: 4 (over x, core).
Axes of the slice: x: 2, y: 2, z: 4, core: 2. Of those that a mesh axis runs over, the one named last changes fastest.
Arguments:
- normed_layer_input: bfloat16 [1024, 8192], P(('groups', 'seq'), 'fsdp'), parts along dimension 0, may hold values from -6 to 6
- frozen_query_rows: bfloat16 [1024, 4096], P(('groups', 'seq'), 'fsdp'), parts along dimension 0, may hold values from -16 to 16
- frozen_key_rows: bfloat16 [1024, 512], P(('groups', 'seq'), 'fsdp'), parts along dimension 0, may hold values from -16 to 16
- frozen_value_rows: bfloat16 [1024, 512], P(('groups', 'seq'), 'fsdp'), parts along dimension 0, may hold values from -6 to 6
- output_gradient: bfloat16 [1024, 4096], P(('groups', 'seq'), 'fsdp'), parts along dimension 0, may hold values from -0.059814453 to 0.059814453
- segment: int32 [1024], P(('groups', 'seq')), parts along dimension 0, may hold values from 0 to 15, never falling along the last dimension, each value on 1 to 64 neighbouring positions
- adapter_down_weight: bfloat16 [8192, 32], P('fsdp'), may hold values from -0.0625 to 0.0625
- query_up_weight: bfloat16 [16, 4096], P(None, 'fsdp'), may hold values from -0.375 to 0.375
- value_up_weight: bfloat16 [16, 512], P(None, 'fsdp'), may hold values from -0.75 to 0.75
Outputs:
- grad_down: float32 [16384, 32], P(('groups', 'fsdp')), parts along dimension 0
- query_up_gradient: float32 [32, 4096], P('groups', 'fsdp'), parts along dimension 0
- value_up_gradient: float32 [32, 512], P('groups', 'fsdp'), parts along dimension 0
There are 2 independent parts, one for each index of `groups`. A program takes and returns all parts, laid end to end along the dimension named above; an argument that names none is the same for every part. Nothing has to cross between parts.
Inputs may be any that keep to these rules, and one draw needn't show every extreme that they name: `segment`: document numbers never fall along the window; each document spans 1 to 64 consecutive tokens, and one spans exactly 64.
All inputs are finite; a program needn't handle non-finite values.
Results may differ from a plain program's by a relative error of at most 0.012.
The roundings to bfloat16 on the way count: a program that leaves them out, or rounds other values in their place, can miss the bound.
Values may be sent and summed in bfloat16 or wider, within the bound.
No kernel may reach another device: no remote copies, remote signals or barrier semaphores. Data moves between devices by JAX's collectives and lax.ppermute only.
A program may use at most 64 MiB of HBM per device.

v0:
```python
import math

import jax
import jax.numpy as jnp
from jax import lax
from jax.sharding import PartitionSpec as P

HEAD_SIZE = 128
ADAPTER_RANK = 16


ADAPTER_SCALE = 2.0
ROPE_BASE = 500000.0
NEG_FILL = -1e30
HIGH_PRECISION = lax.Precision.HIGHEST


def apply_rotation(vectors, token_positions, sign):
    half = vectors.shape[-1] // 2
    freqs = ROPE_BASE ** (-(2.0 * jnp.arange(half, dtype=jnp.float32)) / vectors.shape[-1])
    angles = token_positions.astype(jnp.float32)[:, None] * freqs[None, :]
    cosine = jnp.cos(angles)[:, None, :]
    sine = sign * jnp.sin(angles)[:, None, :]
    first = vectors[..., :half]
    second = vectors[..., half:]
    return jnp.concatenate(
        [first * cosine - second * sine, second * cosine + first * sine], axis=-1
    )


def contract_rows(left, right):
    return lax.dot_general(
        left, right, (((0,), (0,)), ((), ())), precision=None, preferred_element_type=jnp.float32
    )


def body(
    normed_layer_input,
    frozen_query_rows,
    frozen_key_rows,
    frozen_value_rows,
    output_gradient,
    segment,
    adapter_down_weight,
    query_up_weight,
    value_up_weight,
):
    tok_here = normed_layer_input.shape[0]
    seq_count = lax.axis_size("seq")
    seq_index = lax.axis_index("seq")
    heads_here = frozen_query_rows.shape[1] // HEAD_SIZE
    total = tok_here * seq_count
    longest_doc = total // 8
    inv_root = 1.0 / math.sqrt(HEAD_SIZE)
    value_partial_sum = jnp.dot(
        normed_layer_input, adapter_down_weight, preferred_element_type=jnp.float32
    )
    adapter_product = lax.psum(value_partial_sum, "fsdp").astype(jnp.bfloat16)
    query_adapter_codes = adapter_product[:, :ADAPTER_RANK]
    value_adapter_codes = adapter_product[:, ADAPTER_RANK:]
    own_pos = seq_index * tok_here + jnp.arange(tok_here, dtype=jnp.int32)
    rotated_query = frozen_query_rows.astype(jnp.float32) + ADAPTER_SCALE * jnp.dot(
        query_adapter_codes, query_up_weight, preferred_element_type=jnp.float32
    )
    rotated_query = apply_rotation(
        rotated_query.reshape(tok_here, heads_here, HEAD_SIZE), own_pos, 1.0
    ).astype(jnp.bfloat16)
    query_rows = rotated_query.reshape(tok_here * heads_here, HEAD_SIZE)
    grad_rows = output_gradient.reshape(tok_here * heads_here, HEAD_SIZE)
    keys_here = (
        apply_rotation(
            frozen_key_rows.astype(jnp.float32).reshape(tok_here, 1, HEAD_SIZE), own_pos, 1.0
        )
        .reshape(tok_here, HEAD_SIZE)
        .astype(jnp.bfloat16)
    )
    values_here = (
        frozen_value_rows.astype(jnp.float32)
        + ADAPTER_SCALE
        * jnp.dot(value_adapter_codes, value_up_weight, preferred_element_type=jnp.float32)
    ).astype(jnp.bfloat16)
    q_recv, o_recv = (
        lax.all_to_all(query_rows, "seq", split_axis=0, concat_axis=0, tiled=True),
        lax.all_to_all(grad_rows, "seq", split_axis=0, concat_axis=0, tiled=True),
    )
    keys_all, values_all, seg_all = (
        lax.all_gather(keys_here, "seq", axis=0, tiled=True),
        lax.all_gather(values_here, "seq", axis=0, tiled=True),
        lax.all_gather(segment, "seq", axis=0, tiled=True),
    )
    rows_all = tok_here * heads_here
    piece = rows_all // seq_count
    row_ids = jnp.arange(rows_all, dtype=jnp.int32)
    source = row_ids // piece
    flat = seq_index * piece + row_ids % piece
    query_pos = source * tok_here + flat // heads_here
    query_seg = jnp.take(seg_all, query_pos)
    key_pos = jnp.arange(total, dtype=jnp.int32)
    block_count = min(seq_count, 16)
    per_block = seq_count // block_count
    block_rows = per_block * piece
    dq_parts = []
    value_acc = jnp.zeros((total, HEAD_SIZE), jnp.float32)
    for block in range(block_count):
        row_lo = block * block_rows
        row_hi = row_lo + block_rows
        first_token = block * per_block * tok_here
        key_lo = max(0, first_token - longest_doc)
        key_hi = first_token + per_block * tok_here
        q_blk = q_recv[row_lo:row_hi]
        o_blk = o_recv[row_lo:row_hi]
        k_pre = keys_all[key_lo:key_hi]
        v_pre = values_all[key_lo:key_hi]
        scores = jnp.dot(q_blk, k_pre.T, preferred_element_type=jnp.float32) * inv_root
        allowed = (key_pos[key_lo:key_hi][None, :] <= query_pos[row_lo:row_hi][:, None]) & (
            seg_all[key_lo:key_hi][None, :] == query_seg[row_lo:row_hi][:, None]
        )
        scores = jnp.where(allowed, scores, NEG_FILL)
        top = jnp.max(scores, axis=-1, keepdims=True)
        expo = jnp.exp(scores - top)
        weights = expo / jnp.sum(expo, axis=-1, keepdims=True)
        weights_b = weights.astype(jnp.bfloat16)
        dprob = jnp.dot(o_blk, v_pre.T, preferred_element_type=jnp.float32)
        delta = jnp.sum(weights * dprob, axis=-1, keepdims=True)
        dscore = (weights * (dprob - delta) * inv_root).astype(jnp.bfloat16)
        dq_parts.append(jnp.dot(dscore, k_pre, preferred_element_type=jnp.float32))
        value_acc = value_acc.at[key_lo:key_hi].add(contract_rows(weights_b, o_blk))
    dq_rows = jnp.concatenate(dq_parts, axis=0)
    qgrad_rows = (
        apply_rotation(dq_rows.reshape(rows_all, 1, HEAD_SIZE), query_pos, -1.0)
        .reshape(rows_all, HEAD_SIZE)
        .astype(jnp.bfloat16)
    )
    query_gradient_local = lax.all_to_all(
        qgrad_rows, "seq", split_axis=0, concat_axis=0, tiled=True
    ).reshape(tok_here, heads_here * HEAD_SIZE)
    query_codes = ADAPTER_SCALE * jnp.dot(
        query_gradient_local, query_up_weight.T, preferred_element_type=jnp.float32
    )
    query_up_partial = ADAPTER_SCALE * jnp.dot(
        query_adapter_codes.T, query_gradient_local, preferred_element_type=jnp.float32
    )
    value_gradient_local = lax.psum_scatter(value_acc, "seq", scatter_dimension=0, tiled=True)
    value_codes = ADAPTER_SCALE * jnp.dot(
        value_gradient_local, value_up_weight.astype(jnp.float32).T, precision=HIGH_PRECISION
    )
    value_up_partial = ADAPTER_SCALE * jnp.dot(
        value_adapter_codes.astype(jnp.float32).T, value_gradient_local, precision=HIGH_PRECISION
    )
    code_q_all, code_v_all = lax.psum((query_codes, value_codes), "fsdp")
    dlow = jnp.concatenate([code_q_all, code_v_all], axis=1).astype(jnp.bfloat16)
    down_part = contract_rows(normed_layer_input, dlow)
    grad_down, query_up_gradient, value_up_gradient = lax.psum(
        (down_part, query_up_partial, value_up_partial), "seq"
    )
    return (grad_down, query_up_gradient, value_up_gradient)


def solution(mesh):
    in_specs = (
        P(("groups", "seq"), "fsdp"),
        P(("groups", "seq"), "fsdp"),
        P(("groups", "seq"), "fsdp"),
        P(("groups", "seq"), "fsdp"),
        P(("groups", "seq"), "fsdp"),
        P(("groups", "seq")),
        P("fsdp", None),
        P(None, "fsdp"),
        P(None, "fsdp"),
    )
    out_specs = (P(("groups", "fsdp"), None), P("groups", "fsdp"), P("groups", "fsdp"))
    return jax.shard_map(body, mesh=mesh, in_specs=in_specs, out_specs=out_specs, check_vma=False)
```

profile of v0, /device:TPU:0, one launch (start us, length us, event | category | flops | bytes accessed | tf_op | source)
XLA Modules:
  0.0 172.4 jit_solution(4933399203785064795)
XLA Ops:
  7.2 1.0 copy-done
  8.2 1.2 fusion.103
  9.4 12.7 %psum.42 = bf16[128,32]{0,1:T(8,128)(2,1)S(1)} all-reduce(f32[128,32]{0,1:T(8,128)S(1)} %fusion.103), channel_id=1, replica_groups=mesh['groups'=2,'seq'=4,'fsdp'=4] {'fsdp'}, use_global_device_ids=true, to_apply=%region_0.0 | all-reduce | flops 4096 | bytes 24576 | tf_op jit(solution)/shard_map/psum | solution.py:58
  23.1 0.8 pad_maximum_fusion
  23.9 5.0 %all-to-all-start = ((bf16[4,256,128]{2,1,0:T(8,128)(2,1)}), bf16[4,256,128]{2,1,0:T(8,128)(2,1)S(1)}, u32[]{:S(2)}, u32[]{:S(2)}) async-start(bf16[4,256,128]{2,1,0:T(8,128)(2,1)} %pad_maximum_fusion), calls=%async_computation | async-start | bytes 524288 | tf_op jit(solution)/shard_map/all_to_all | solution.py:83
  29.0 0.8 all_to_all.15
  30.2 12.9 %all-gather = bf16[512,1,128]{0,2,1:T(8,128)(2,1)S(1)} all-gather(bf16[128,1,128]{0,2,1:T(8,128)(2,1)S(1)} %pad_maximum_fusion.2), channel_id=2, replica_groups=mesh['groups'=2,'seq'=4,'fsdp'=4] {'seq'}, dimensions={0}, use_global_device_ids=true | all-gather | bytes 163840 | tf_op jit(solution)/shard_map/all_gather | solution.py:87
  43.1 0.7 copy-done.10
  43.8 9.4 %all-gather.1 = s32[4,1,128]{2,1,0:T(1,128)S(1)} all-gather(s32[1,1,128]{2,1,0:T(1,128)S(1)} %bitcast.111), channel_id=1, replica_groups=mesh['groups'=2,'seq'=4,'fsdp'=4] {'seq'}, dimensions={0}, use_global_device_ids=true | all-gather | bytes 2560 | tf_op jit(solution)/shard_map/all_gather | solution.py:89
  53.3 6.9 %gather_fusion = s32[1024]{0:T(1024)S(1)} fusion(s32[512]{0:T(512)S(1)} %bitcast.106, s32[1024]{0:T(1024)S(1)} %broadcast_clamp_fusion), kind=kCustom, calls=%fused_computation | custom fusion | bytes 12288 | tf_op jit(solution)/shard_map/jit(_take)/gather | solution.py:97
  60.4 0.5 copy-done.8
  61.2 13.6 %all_gather.11 = bf16[512,128]{1,0:T(8,128)(2,1)S(1)} all-gather(bf16[128,128]{1,0:T(8,128)(2,1)S(1)} %fusion.10), channel_id=1, replica_groups=mesh['groups'=2,'seq'=4,'fsdp'=4] {'seq'}, dimensions={0}, use_global_device_ids=true | all-gather | bytes 163840 | tf_op jit(solution)/shard_map/all_gather | solution.py:88
  74.8 3.4 %all-to-all-start.1 = ((bf16[4,256,128]{2,1,0:T(8,128)(2,1)}), bf16[4,256,128]{2,1,0:T(8,128)(2,1)S(1)}, u32[]{:S(2)}, u32[]{:S(2)}) async-start(bf16[4,256,128]{2,1,0:T(8,128)(2,1)} %all_to_all.15), calls=%async_computation.1 | async-start | bytes 524288 | tf_op jit(solution)/shard_map/all_to_all | solution.py:84
  78.2 0.3 fusion.100
  78.6 0.3 fusion.101
  79.3 0.3 fusion.102
  79.6 5.3 %all-to-all-done.1 = bf16[4,256,128]{2,1,0:T(8,128)(2,1)S(1)} async-done(((bf16[4,256,128]{2,1,0:T(8,128)(2,1)}), bf16[4,256,128]{2,1,0:T(8,128)(2,1)S(1)}, u32[]{:S(2)}, u32[]{:S(2)}) %all-to-all-start.1) | async-done | bytes 262176 | tf_op jit(solution)/shard_map/all_to_all | solution.py:84
  86.7 1.2 fusion.14
  87.9 0.8 copy.27
  88.7 3.4 %all-to-all-start.2 = ((bf16[4,256,128]{2,1,0:T(8,128)(2,1)}), bf16[4,256,128]{2,1,0:T(8,128)(2,1)S(1)}, u32[]{:S(2)}, u32[]{:S(2)}) async-start(bf16[4,256,128]{2,1,0:T(8,128)(2,1)} %bitcast.25), calls=%async_computation.2 | async-start | bytes 524288 | tf_op jit(solution)/shard_map/all_to_all | solution.py:134
  92.9 0.7 copy-done.1
  93.7 5.2 %all-to-all-done.2 = bf16[4,256,128]{2,1,0:T(8,128)(2,1)S(1)} async-done(((bf16[4,256,128]{2,1,0:T(8,128)(2,1)}), bf16[4,256,128]{2,1,0:T(8,128)(2,1)S(1)}, u32[]{:S(2)}, u32[]{:S(2)}) %all-to-all-start.2) | async-done | bytes 262176 | tf_op jit(solution)/shard_map/all_to_all | solution.py:134
  99.2 0.8 convolution_multiply_fusion.5
  100.0 16.3 %reduce-scatter.2.cloned.1.call-done = f32[128,128]{1,0:T(8,128)} async-done(((f32[512,128]{1,0:T(8,128)}), f32[128,128]{1,0:T(8,128)}) %reduce-scatter.2.cloned.1.call-update) | async-done | bytes 65552 | tf_op jit(solution)/shard_map/reduce_scatter | solution.py:143
  116.3 1.0 convolution_multiply_fusion.8
  117.3 10.2 %all-reduce.1 = (bf16[128,16]{0,1:T(8,128)(2,1)S(1)}, bf16[128,16]{0,1:T(8,128)(2,1)S(1)}) all-reduce(f32[128,16]{0,1:T(8,128)S(1)} %convolution_multiply_fusion.8, f32[128,16]{0,1:T(8,128)S(1)} %convolution_multiply_fusion.9), channel_id=1, replica_groups=mesh['groups'=2,'seq'=4,'fsdp'=4] {'fsdp'}, use_global_device_ids=true, to_apply=%region_15.16 | all-reduce | flops 4096 | bytes 24576 | tf_op jit(solution)/shard_map/psum | solution.py:150
  127.5 0.9 convolution_bitcast_fusion
  128.4 0.8 copy-done.3
  129.4 9.9 %psum.47 = f32[16,128]{1,0:T(8,128)} all-reduce(f32[16,128]{1,0:T(8,128)S(1)} %convolution_multiply_fusion.7), channel_id=1, replica_groups=mesh['groups'=2,'seq'=4,'fsdp'=4] {'seq'}, use_global_device_ids=true, to_apply=%region_18.19 | all-reduce | flops 2048 | bytes 16384 | tf_op jit(solution)/shard_map/psum | solution.py:153
  139.3 24.0 %all-reduce.5.cloned.1.call-done = (f32[2048,32]{0,1:T(8,128)}, f32[16,1024]{1,0:T(8,128)}) async-done(((f32[2048,32]{0,1:T(8,128)}, f32[16,1024]{1,0:T(8,128)}), (f32[2048,32]{0,1:T(8,128)}, f32[16,1024]{1,0:T(8,128)})) %all-reduce.5.cloned.1.call-update) | async-done | bytes 327696 | tf_op jit(solution)/shard_map/psum | solution.py:153
  163.2 1.7 copy.34
  164.9 0.6 copy.35
  (72 shorter events, 5.3 us)
Async XLA Ops:
  7.2 1.0 copy-start
  8.2 13.9 %copy-start.2 = (bf16[128,1024]{1,0:T(8,128)(2,1)S(1)}, bf16[128,1024]{1,0:T(8,128)(2,1)}, u32[]{:S(2)}) copy-start(bf16[128,1024]{1,0:T(8,128)(2,1)} %param.18) | copy-start | bytes 786436
  8.2 13.9 %copy-start.5 = (bf16[16,1024]{1,0:T(8,128)(2,1)S(1)}, bf16[16,1024]{1,0:T(8,128)(2,1)}, u32[]{:S(2)}) copy-start(bf16[16,1024]{1,0:T(8,128)(2,1)} %param.24) | copy-start | bytes 98308
  23.9 5.1 %copy-start.4 = (bf16[128,1024]{1,0:T(8,128)(2,1)S(1)}, bf16[128,1024]{1,0:T(8,128)(2,1)}, u32[]{:S(2)}) copy-start(bf16[128,1024]{1,0:T(8,128)(2,1)} %param.21) | copy-start | bytes 786436
  23.9 50.9 %all-to-all-start = ((bf16[4,256,128]{2,1,0:T(8,128)(2,1)}), bf16[4,256,128]{2,1,0:T(8,128)(2,1)S(1)}, u32[]{:S(2)}, u32[]{:S(2)}) async-start(bf16[4,256,128]{2,1,0:T(8,128)(2,1)} %pad_maximum_fusion), calls=%async_computation | async-start | bytes 524288 | tf_op jit(solution)/shard_map/all_to_all | solution.py:83
  29.0 0.8 copy-start.7
  43.1 0.7 copy-start.10
  60.1 0.8 copy-start.8
  60.3 0.7 copy-start.9
  74.8 10.2 %all-to-all-start.1 = ((bf16[4,256,128]{2,1,0:T(8,128)(2,1)}), bf16[4,256,128]{2,1,0:T(8,128)(2,1)S(1)}, u32[]{:S(2)}, u32[]{:S(2)}) async-start(bf16[4,256,128]{2,1,0:T(8,128)(2,1)} %all_to_all.15), calls=%async_computation.1 | async-start | bytes 524288 | tf_op jit(solution)/shard_map/all_to_all | solution.py:84
  88.7 10.2 %all-to-all-start.2 = ((bf16[4,256,128]{2,1,0:T(8,128)(2,1)}), bf16[4,256,128]{2,1,0:T(8,128)(2,1)S(1)}, u32[]{:S(2)}, u32[]{:S(2)}) async-start(bf16[4,256,128]{2,1,0:T(8,128)(2,1)} %bitcast.25), calls=%async_computation.2 | async-start | bytes 524288 | tf_op jit(solution)/shard_map/all_to_all | solution.py:134
  92.1 24.2 %reduce-scatter.2.cloned.1.call-start = ((), (), s32[]{:S(2)}) async-start(), calls=%async_computation.4 | async-start | bytes 327680 | tf_op jit(solution)/shard_map/reduce_scatter | solution.py:143
  92.9 0.7 copy-start.1
  93.6 69.6 %all-reduce.5.cloned.1.call-start = ((), (), s32[]{:S(2)}) async-start(), calls=%async_computation.5 | async-start | bytes 655360 | tf_op jit(solution)/shard_map/psum | solution.py:153
  128.4 0.8 copy-start.3
  163.2 1.7 copy-start.6
Sparse Core Ops, SparseCore 0:
  95.8 20.4 reduce-scatter.1
  128.6 34.6 all-reduce.4
where the time goes:
time: 173 us; the launch traced here: 172 us
  blocking collectives  68.7 us (40%)
  waiting for transfers between devices  50.9 us (29%)
  local copies, waits for them, and re-layouts  15.2 us (9%)
  between operations  14.3 us (8%)
  starting transfers between devices  11.9 us (7%)
  matrix products  8.16 us (5%)
  other arithmetic  3.18 us (2%)
    psum x1, waiting for transfers between devices, body(): lax.psum((down_part, query_up_partial, value_up_partial), 'seq')  24 us
    reduce_scatter x1, waiting for transfers between devices, body(): lax.psum_scatter(value_acc, 'seq', scatter_dimension=0, tiled=True)  16.3 us
    all_gather x1, blocking collectives, body(): lax.all_gather(values_here, 'seq', axis=0, tiled=True)  13.6 us
    all_gather x1, blocking collectives, body(): lax.all_gather(keys_here, 'seq', axis=0, tiled=True)  12.9 us
    psum x1, blocking collectives, body(): adapter_product = lax.psum(value_partial_sum, 'fsdp').astype(jnp.bfloat16)  12.7 us
    psum x1, blocking collectives, body(): code_q_all, code_v_all = lax.psum((query_codes, value_codes), 'fsdp')  10.2 us
    psum x1, blocking collectives, body(): lax.psum((down_part, query_up_partial, value_up_partial), 'seq')  9.86 us
    all_gather x1, blocking collectives, body(): lax.all_gather(segment, 'seq', axis=0, tiled=True)  9.42 us
  transfers between devices with their start and end apart: 5, of which 4 were waited for; matrix products, arithmetic and copies ran while one was open for 6% of the time, Pallas kernels for 0%

commit v1 on v0

v1 whole, which is shorter than its diff:
```python
import functools
import math

import jax
import jax.numpy as jnp
from jax import lax
from jax.experimental import pallas as pl
from jax.experimental.pallas import tpu as pltpu
from jax.sharding import PartitionSpec as P

HEAD = 128
HALF = HEAD // 2
RANK = 16
SCALE = 2.0
ROPE_BASE = 500000.0
NEG_FILL = -1e30
INV_ROOT = 1.0 / math.sqrt(HEAD)
F32 = jnp.float32
BF16 = jnp.bfloat16
EXACT = lax.Precision.HIGHEST
LIMIT = 50 * 1024 * 1024


def dot(left, right, left_dim, right_dim, precision=None):
    return lax.dot_general(
        left,
        right,
        (((left_dim,), (right_dim,)), ((), ())),
        precision=precision,
        preferred_element_type=F32,
    )


def call(kernel, out_shapes, scratch=(), flops=1 << 20):
    return pl.pallas_call(
        kernel,
        out_shape=[jax.ShapeDtypeStruct(s, d) for s, d in out_shapes],
        scratch_shapes=list(scratch),
        compiler_params=pltpu.CompilerParams(vmem_limit_bytes=LIMIT),
        cost_estimate=pl.CostEstimate(flops=flops, bytes_accessed=1 << 20, transcendentals=0),
    )


def lowrank_kernel(send, x_ref, a_ref, k_ref, v_ref, seg_ref, part_ref, pack_ref):
    part_ref[...] = dot(a_ref[...], x_ref[...], 1, 1)
    tok = k_ref.shape[0]
    pack_ref[0:send] = k_ref[tok - send : tok]
    pack_ref[send : 2 * send] = v_ref[tok - send : tok]
    pack_ref[2 * send :] = jnp.broadcast_to(seg_ref[...].astype(F32), (16, tok)).astype(BF16)


def rotate_rows(u, cos, sin):
    return u * cos + pltpu.roll(u, HALF, 1) * sin


def scores_kernel(
    halo, send, blocks, heads,
    low_ref, q_ref, k_ref, o_ref, seg_ref, pack_ref, base_ref, cos_ref, sin_ref, wq_ref, wv_ref,
    w_ref, kt_ref, dv_ref, code_ref, back_ref, bias_ref, keys_ref,
):
    tok = q_ref.shape[0]
    keys = halo + tok
    low = low_ref[...].astype(BF16)
    cos, sin = cos_ref[...], sin_ref[...]
    cos2 = jnp.concatenate([cos, cos], axis=1)
    sin2 = jnp.concatenate([-sin, sin], axis=1)
    raw = [pack_ref[b, 0:send] for b in range(blocks)] + [k_ref[...]]
    keys_ref[...] = rotate_rows(jnp.concatenate(raw, axis=0).astype(F32), cos2, sin2).astype(BF16)
    key_rows = keys_ref[...]
    kt_ref[...] = key_rows.astype(F32).T.astype(BF16)
    seg_here = seg_ref[...].astype(F32)
    cols = []
    for b in range(blocks):
        row = pack_ref[b, 2 * send : 2 * send + 16].astype(F32)[0:1]
        cols.append(jnp.broadcast_to(row, (tok, tok)).T[tok - send :])
    cols.append(jnp.broadcast_to(seg_here, (tok, tok)).T)
    seg_col = jnp.concatenate(cols, axis=0)
    offset = lax.broadcasted_iota(jnp.int32, (keys, tok), 0) - halo
    query = lax.broadcasted_iota(jnp.int32, (keys, tok), 1)
    allowed = (offset <= query) & (offset + base_ref[0] >= 0) & (seg_col == seg_here)
    bias_ref[...] = jnp.where(allowed, 0.0, NEG_FILL)
    q0 = q_ref[...].astype(F32) + SCALE * dot(low[:RANK], wq_ref[...], 0, 0)
    cos_here, sin_here = cos2[halo:], sin2[halo:]
    dv = jnp.zeros((keys, HEAD), F32)
    for h in range(heads):
        cut = slice(h * HEAD, (h + 1) * HEAD)
        qr = rotate_rows(q0[:, cut], cos_here, sin_here).astype(BF16)
        s = dot(key_rows, qr, 1, 1) * INV_ROOT + bias_ref[...]
        e = jnp.exp(s - jnp.max(s, axis=0, keepdims=True))
        w = e * (1.0 / jnp.sum(e, axis=0, keepdims=True))
        w_ref[h] = w
        dv = dv + dot(w.astype(BF16), o_ref[:, cut], 1, 0)
    dv_ref[...] = dv
    wv = wv_ref[...].astype(F32)
    code_ref[...] = SCALE * dot(wv, dv[halo:], 1, 1, EXACT)
    for b in range(blocks):
        part = dv[b * send : (b + 1) * send]
        if send < tok:
            part = jnp.concatenate([jnp.zeros((tok - send, HEAD), F32), part], axis=0)
        back_ref[b] = SCALE * dot(wv, part, 1, 1, EXACT)


def grads_kernel(
    halo, send, blocks, heads,
    low_ref, lowv_ref, v_ref, pack_ref, o_ref, w_ref, kt_ref, dv_ref, cost_ref, sint_ref, wq_ref, wv_ref,
    code_ref, up_ref, vals_ref, qg_ref,
):
    tok = o_ref.shape[0]
    low = low_ref[...].astype(BF16)
    wv = wv_ref[...]

    def values(rows, codes):
        return (rows.astype(F32) + SCALE * dot(codes, wv, 0, 0)[tok - rows.shape[0] :]).astype(BF16)

    for b in range(blocks):
        vals_ref[b * send : (b + 1) * send] = values(pack_ref[b, send : 2 * send], lowv_ref[b])
    vals_ref[halo:] = values(v_ref[...], low[RANK:])
    vals = vals_ref[...]
    kt = kt_ref[...]
    cos, sin = cost_ref[...], sint_ref[...]
    for h in range(heads):
        cut = slice(h * HEAD, (h + 1) * HEAD)
        dp = dot(vals, o_ref[:, cut], 1, 1)
        w = w_ref[h]
        delta = jnp.sum(w * dp, axis=0, keepdims=True)
        ds = (w * (dp - delta) * INV_ROOT).astype(BF16)
        dq = dot(kt, ds, 1, 0)
        first, second = dq[:HALF], dq[HALF:]
        qg_ref[h * HEAD : h * HEAD + HALF] = (first * cos + second * sin).astype(BF16)
        qg_ref[h * HEAD + HALF : (h + 1) * HEAD] = (second * cos - first * sin).astype(BF16)
    qg = qg_ref[...]
    code_ref[...] = SCALE * dot(wq_ref[...], qg, 1, 0)
    up_q = SCALE * dot(low[:RANK], qg, 1, 1)
    dv = dv_ref[...]
    up_v = dot(low[RANK:].astype(F32), dv[halo:], 1, 0, EXACT)
    for b in range(blocks):
        codes = lowv_ref[b].astype(F32)
        part = dv[b * send : (b + 1) * send]
        if send < tok:
            part = jnp.concatenate([jnp.zeros((tok - send, HEAD), F32), part], axis=0)
        up_v = up_v + dot(codes, part, 1, 0, EXACT)
    up_ref[:, : heads * HEAD] = up_q.astype(up_ref.dtype)
    up_ref[:, heads * HEAD :] = (SCALE * up_v).astype(up_ref.dtype)


def down_kernel(dl_ref, x_ref, part_ref):
    part_ref[...] = dot(dl_ref[...], x_ref[...], 1, 0)


def pair_kernel(split, dl_ref, dlp_ref, x_ref, xp_ref, up_ref, upp_ref, send_ref):
    rows, wide = dl_ref.shape[0], x_ref.shape[1]
    part = dot(dl_ref[...], x_ref[...], 1, 0) + dot(dlp_ref[...], xp_ref[...], 1, 0)
    send_ref[:, :wide] = part.astype(BF16)
    up = (up_ref[...].astype(F32) + upp_ref[...].astype(F32)).astype(BF16)
    size = up.shape[1]
    send_ref[0:RANK, wide:] = up[:, :split]
    send_ref[RANK:rows, wide : wide + size - split] = up[:, split:]
    if 2 * split > size:
        send_ref[RANK:rows, wide + size - split :] = jnp.zeros((rows - RANK, 2 * split - size), BF16)


def final_kernel(split, mine_ref, other_ref, down_ref, upq_ref, upv_ref):
    wide = down_ref.shape[1]
    total = mine_ref[...].astype(F32) + other_ref[...].astype(F32)
    down_ref[...] = total[:, :wide]
    size = upq_ref.shape[1]
    upq_ref[:, :split] = total[:RANK, wide:]
    upq_ref[:, split:] = total[RANK:, wide : wide + size - split]
    upv_ref[...] = total[RANK:, wide + size - split : wide + size - split + HEAD]


def body(x, q, k, v, o, segment, a, wq, wv):
    tok, wide = x.shape
    seq_count = lax.axis_size("seq")
    fsdp_count = lax.axis_size("fsdp")
    seq_index = lax.axis_index("seq")
    heads = q.shape[1] // HEAD
    longest = tok * seq_count // 8
    blocks = -(-longest // tok)
    send = longest if blocks == 1 else tok
    halo = blocks * send
    keys = halo + tok
    paired = seq_count == 4 and fsdp_count == 4

    def swap(array, axis, bit):
        size = lax.axis_size(axis)
        return lax.ppermute(array, axis, [(i, i ^ bit) for i in range(size)])

    def shift(array, by):
        moves = [(i, i + by) for i in range(seq_count) if 0 <= i + by < seq_count]
        return lax.ppermute(array, "seq", moves)

    def cross(array):
        moves = [
            (s * fsdp_count + f, (s ^ 1) * fsdp_count + (f ^ 2))
            for s in range(seq_count)
            for f in range(fsdp_count)
        ]
        return lax.ppermute(array, ("seq", "fsdp"), moves)

    def sum_fsdp(array):
        if fsdp_count & (fsdp_count - 1):
            return lax.psum(array, "fsdp")
        bit = 1
        while bit < fsdp_count:
            array = array + swap(array, "fsdp", bit)
            bit *= 2
        return array

    seg_row = segment.reshape(1, tok)
    part, pack = call(
        functools.partial(lowrank_kernel, send),
        [((2 * RANK, tok), F32), ((2 * send + 16, tok), BF16)],
    )(x, a.T, k, v, seg_row)
    part, pack, x = lax.optimization_barrier((part, pack, x))
    if paired:
        x_pair = swap(x, "seq", 1)
    packs = jnp.stack([shift(pack, d) for d in range(blocks, 0, -1)])
    start = seq_index * tok
    base = start.reshape(1).astype(jnp.int32)
    freqs = ROPE_BASE ** (-(2.0 * jnp.arange(HALF, dtype=F32)) / HEAD)
    positions = (start - halo + jnp.arange(keys, dtype=jnp.int32)).astype(F32)
    angles = positions[:, None] * freqs[None, :]
    cos, sin = jnp.cos(angles), jnp.sin(angles)
    here = (start + jnp.arange(tok, dtype=jnp.int32)).astype(F32)
    angles_t = freqs[:, None] * here[None, :]
    cos_t, sin_t = jnp.cos(angles_t), jnp.sin(angles_t)

    low = sum_fsdp(part)
    low_v = low[RANK:].astype(BF16)
    lows = jnp.stack([shift(low_v, d) for d in range(blocks, 0, -1)])

    specs = [pl.BlockSpec(memory_space=pltpu.VMEM)] * 11
    specs[6] = pl.BlockSpec(memory_space=pltpu.SMEM)
    w, kt, dv, code_v, back = pl.pallas_call(
        functools.partial(scores_kernel, halo, send, blocks, heads),
        out_shape=[
            jax.ShapeDtypeStruct((heads, keys, tok), F32),
            jax.ShapeDtypeStruct((HEAD, keys), BF16),
            jax.ShapeDtypeStruct((keys, HEAD), F32),
            jax.ShapeDtypeStruct((RANK, tok), F32),
            jax.ShapeDtypeStruct((blocks, RANK, tok), F32),
        ],
        in_specs=specs,
        scratch_shapes=[pltpu.VMEM((keys, tok), F32), pltpu.VMEM((keys, HEAD), BF16)],
        compiler_params=pltpu.CompilerParams(vmem_limit_bytes=LIMIT),
    )(low, q, k, o, seg_row, packs, base, cos, sin, wq, wv)

    for b, d in enumerate(range(blocks, 0, -1)):
        code_v = code_v + shift(back[b], -d)
    code_q, up = call(
        functools.partial(grads_kernel, halo, send, blocks, heads),
        [((RANK, tok), F32), ((RANK, (heads + 1) * HEAD), BF16 if paired else F32)],
        [pltpu.VMEM((keys, HEAD), BF16), pltpu.VMEM((heads * HEAD, tok), BF16)],
    )(low, lows, v, packs, o, w, kt, dv, cos_t, sin_t, wq, wv)
    codes = jnp.concatenate([code_q, code_v], axis=0)

    if not paired:
        dlow = sum_fsdp(codes).astype(BF16)
        (down,) = call(down_kernel, [((2 * RANK, wide), F32)])(dlow, x)
        down, up = lax.psum((down, up), "seq")
        return down.T, up[:, : heads * HEAD], up[:, heads * HEAD :]

    up_pair = swap(up, "seq", 1)
    codes = codes + swap(codes, "fsdp", 1)
    dlow = (codes + swap(codes, "fsdp", 2)).astype(BF16)
    dlow_pair = (swap(codes, "seq", 1) + cross(codes)).astype(BF16)
    split = -(-(heads + 1) // 2) * HEAD
    (mine,) = call(functools.partial(pair_kernel, split), [((2 * RANK, wide + split), BF16)])(
        dlow, dlow_pair, x, x_pair, up, up_pair
    )
    other = swap(mine, "seq", 2)
    down, up_q, up_v = call(
        functools.partial(final_kernel, split),
        [((2 * RANK, wide), F32), ((RANK, heads * HEAD), F32), ((RANK, HEAD), F32)],
    )(mine, other)
    return down.T, up_q, up_v


def solution(mesh):
    rows = ("groups", "seq")
    in_specs = (
        P(rows, "fsdp"),
        P(rows, "fsdp"),
        P(rows, "fsdp"),
        P(rows, "fsdp"),
        P(rows, "fsdp"),
        P(rows),
        P("fsdp", None),
        P(None, "fsdp"),
        P(None, "fsdp"),
    )
    out_specs = (P(("groups", "fsdp"), None), P("groups", "fsdp"), P("groups", "fsdp"))
    return jax.shard_map(body, mesh=mesh, in_specs=in_specs, out_specs=out_specs, check_vma=False)
```

time: 173 us -> 53.4 us (0.31)
  blocking collectives: 68.7 us -> 0 us
  waiting for transfers between devices: 50.9 us -> 23 us
  between operations: 14.3 us -> 0.85 us
  local copies, waits for them, and re-layouts: 15.2 us -> 4.15 us
  matrix products: 8.16 us -> 0 us
  starting transfers between devices: 11.9 us -> 19.6 us
  Pallas kernels: 0 us -> 4.65 us
  other arithmetic: 3.18 us -> 0.67 us
    all_gather x3 -> x0, blocking collectives: 36 us -> none  [the longest x1 13.6 us: body(): lax.all_gather(values_here, 'seq', axis=0, tiled=True)]
    psum x3 -> x0, blocking collectives: 32.8 us -> none  [the longest x1 12.7 us: body(): adapter_product = lax.psum(value_partial_sum, 'fsdp').astype(jnp.bfloat16)]
    psum x1 -> x0, waiting for transfers between devices: 24 us -> none  [body(): lax.psum((down_part, query_up_partial, value_up_partial), 'seq')]
    ppermute x0 -> x12, waiting for transfers between devices: none -> 23 us  [the longest x8 20 us: swap(): return lax.ppermute(array, axis, [(i, i ^ bit) for i in range(size)])]
    ppermute x0 -> x12, starting transfers between devices: none -> 19.6 us  [the longest x3 9.38 us: shift(): return lax.ppermute(array, 'seq', moves)]
    reduce_scatter x1 -> x0, waiting for transfers between devices: 16.3 us -> none  [body(): lax.psum_scatter(value_acc, 'seq', scatter_dimension=0, tiled=True)]
    all_to_all x3 -> x0, starting transfers between devices: 11.8 us -> none  [the longest x1 5 us: body(): lax.all_to_all(query_rows, 'seq', split_axis=0, concat_axis=0, tiled=True)]
    all_to_all x3 -> x0, waiting for transfers between devices: 10.5 us -> none  [the longest x1 5.3 us: body(): lax.all_to_all(grad_rows, 'seq', split_axis=0, concat_axis=0, tiled=True)]
  transfers between devices with their start and end apart: 5 -> 12, of which waited for: 4 -> 5; matrix products, arithmetic and copies ran while one was open for 6% -> 1% of each run, Pallas kernels for 0% -> 6%
where the time goes in v1:
time: 53.4 us; the launch traced here: 52.9 us
  waiting for transfers between devices  23 us (43%)
  starting transfers between devices  19.6 us (37%)
  Pallas kernels  4.65 us (9%)
  local copies, waits for them, and re-layouts  4.15 us (8%)
  between operations  0.85 us (2%)
  other arithmetic  0.67 us (1%)
    ppermute x8, waiting for transfers between devices, swap(): return lax.ppermute(array, axis, [(i, i ^ bit) for i in range(size)])  20 us
    ppermute x3, starting transfers between devices, shift(): return lax.ppermute(array, 'seq', moves)  9.38 us
    ppermute x8, starting transfers between devices, swap(): return lax.ppermute(array, axis, [(i, i ^ bit) for i in range(size)])  9.19 us
    unnamed x24, local copies, waits for them, and re-layouts  4.14 us
    pallas_call x1, Pallas kernels, body(): call(functools.partial(grads_kernel, halo, send, blocks, heads), [((RANK,...  2.13 us
    ppermute x3, waiting for transfers between devices, shift(): return lax.ppermute(array, 'seq', moves)  1.89 us
    pallas_call x1, Pallas kernels, body(): pl.pallas_call(functools.partial(scores_kernel, halo, send, blocks, heads...  1.24 us
    ppermute x1, waiting for transfers between devices, cross(): return lax.ppermute(array, ('seq', 'fsdp'), moves)  1.11 us
  transfers between devices with their start and end apart: 12, of which 5 were waited for; matrix products, arithmetic and copies ran while one was open for 1% of the time, Pallas kernels for 6%

profile of v1, /device:TPU:0, one launch (start us, length us, event | category | flops | bytes accessed | tf_op | source)
XLA Modules:
  0.0 52.9 jit_solution(12184426224825607492)
XLA Ops:
  0.6 0.6 %copy-done.11 = s32[128]{0:T(128)S(1)} copy-done((s32[128]{0:T(128)S(1)}, s32[128]{0:T(128)}, u32[]{:S(2)}) %copy-start.11) | copy-done | bytes 536
  1.3 1.0 %copy-done = bf16[128,2048]{1,0:T(8,128)(2,1)S(1)} copy-done((bf16[128,2048]{1,0:T(8,128)(2,1)S(1)}, bf16[128,2048]{1,0:T(8,128)(2,1)}, u32[]{:S(2)}) %copy-start) | copy-done | bytes 524312
  2.3 0.9 %copy-done.4 = bf16[2048,32]{0,1:T(8,128)(2,1)S(1)} copy-done((bf16[2048,32]{0,1:T(8,128)(2,1)S(1)}, bf16[2048,32]{0,1:T(8,128)(2,1)}, u32[]{:S(2)}) %copy-start.4) | copy-done | bytes 131096
  3.2 0.8 %copy-done.5 = bf16[128,128]{1,0:T(8,128)(2,1)S(1)} copy-done((bf16[128,128]{1,0:T(8,128)(2,1)S(1)}, bf16[128,128]{1,0:T(8,128)(2,1)}, u32[]{:S(2)}) %copy-start.5) | copy-done | bytes 32792
  4.0 0.8 %copy-done.7 = bf16[128,128]{1,0:T(8,128)(2,1)S(1)} copy-done((bf16[128,128]{1,0:T(8,128)(2,1)S(1)}, bf16[128,128]{1,0:T(8,128)(2,1)}, u32[]{:S(2)}) %copy-start.7) | copy-done | bytes 32792
  4.8 0.3 shard_map.112
  5.0 0.5 collective-permute-start
  5.6 4.5 %collective-permute-start.3 = (bf16[144,128]{1,0:T(8,128)(2,1)S(1)}, bf16[144,128]{1,0:T(8,128)(2,1)S(1)}, u32[]{:S(2)}, u32[]{:S(2)}) collective-permute-start(bf16[144,128]{1,0:T(8,128)(2,1)S(1)} %get-tuple-element.21), channel_id=1, source_target_pairs={{0,4},{4,8},{8,12},{1,5},{5,9},{9,13},{2,6},{6,10},{10,14},{3,7},{... | collective-permute-start | bytes 110600 | tf_op jit(solution)/shard_map/ppermute | solution.py:191
  10.1 0.4 multiply_sine_fusion
  10.5 0.0 copy-start.10
  10.5 1.6 %collective-permute-start.1 = (f32[32,128]{1,0:T(8,128)S(1)}, f32[32,128]{1,0:T(8,128)S(1)}, u32[]{:S(2)}, u32[]{:S(2)}) collective-permute-start(f32[32,128]{1,0:T(8,128)S(1)} %add.39), channel_id=1, source_target_pairs={{0,2},{1,3},{2,0},{3,1},{4,6},{5,7},{6,4},{7,5},{8,10},{9,11},{10,... | collective-permute-start | bytes 49160 | tf_op jit(solution)/shard_map/ppermute | solution.py:187
  12.1 2.2 %collective-permute-done.1 = f32[32,128]{1,0:T(8,128)S(1)} collective-permute-done((f32[32,128]{1,0:T(8,128)S(1)}, f32[32,128]{1,0:T(8,128)S(1)}, u32[]{:S(2)}, u32[]{:S(2)}) %collective-permute-start.1) | collective-permute-done | bytes 16416 | tf_op jit(solution)/shard_map/ppermute | solution.py:187
  14.4 3.5 %collective-permute-start.2 = (bf16[16,128]{1,0:T(8,128)(2,1)S(1)}, bf16[16,128]{1,0:T(8,128)(2,1)S(1)}, u32[]{:S(2)}, u32[]{:S(2)}) collective-permute-start(bf16[16,128]{1,0:T(8,128)(2,1)S(1)} %slice.7), channel_id=1, source_target_pairs={{0,4},{4,8},{8,12},{1,5},{5,9},{9,13},{2,6},{6,10},{10,14},{3,7},{... | collective-permute-start | bytes 12296 | tf_op jit(solution)/shard_map/ppermute | solution.py:191
  17.9 1.2 %shard_map.113 = (f32[8,192,128]{2,1,0:T(8,128)S(1)}, bf16[128,192]{1,0:T(8,128)(2,1)S(1)}, f32[192,128]{1,0:T(8,128)S(1)}, f32[16,128]{1,0:T(8,128)S(1)}, f32[1,16,128]{2,1,0:T(8,128)S(1)}) custom-call(f32[32,128]{1,0:T(8,128)S(1)} %add.40.low_ref, bf16[128,1024]{1,0:T(8,128)(2,1)S(1)} %copy-done.3, bf16[128,128]{1,0:T(8,128)(2,1)S(1)} %copy-done.6, ...), custom_call_target="tpu_custom_call" | custom-call | tf_op jit(solution)/shard_map/pallas_call | solution.py:235
  19.2 1.4 %collective-permute-start.4 = (f32[16,128]{1,0:T(8,128)S(1)}, f32[16,128]{1,0:T(8,128)S(1)}, u32[]{:S(2)}, u32[]{:S(2)}) collective-permute-start(f32[16,128]{1,0:T(8,128)S(1)} %bitcast.13), channel_id=1, source_target_pairs={{4,0},{8,4},{12,8},{5,1},{9,5},{13,9},{6,2},{10,6},{14,10},{7,3},{... | collective-permute-start | bytes 24584 | tf_op jit(solution)/shard_map/ppermute | solution.py:191
  20.6 0.2 multiply_sine_fusion.1
  20.8 0.0 collective-permute-done.2
  20.8 0.0 copy-start.1
  20.8 2.1 %shard_map.114 = (f32[16,128]{1,0:T(8,128)S(1)}, bf16[16,1152]{1,0:T(8,128)(2,1)S(1)}) custom-call(f32[32,128]{1,0:T(8,128)S(1)} %add.40.low_ref, bf16[1,16,128]{2,1,0:T(8,128)(2,1)S(1)} %bitcast.10, bf16[128,128]{1,0:T(8,128)(2,1)S(1)} %copy-done.8, bf16[1,144,128]{2,1,0:T(8,128)(2,1)S(1)} %bitcast.8, bf16[128,1024]{1,0:T(8,128)(2,1)S(1)} %copy-done.2, ...), custom_call_target="tpu_custom_call" | custom-call | flops 1048576 | bytes 1048576 | tf_op jit(solution)/shard_map/pallas_call | solution.py:251
  22.9 1.9 %collective-permute-done.4 = f32[16,128]{1,0:T(8,128)S(1)} collective-permute-done((f32[16,128]{1,0:T(8,128)S(1)}, f32[16,128]{1,0:T(8,128)S(1)}, u32[]{:S(2)}, u32[]{:S(2)}) %collective-permute-start.4) | collective-permute-done | bytes 8224 | tf_op jit(solution)/shard_map/ppermute | solution.py:191
  24.8 0.0 collective-permute-start.5
  24.9 1.6 %collective-permute-start.9 = (bf16[128,2048]{1,0:T(8,128)(2,1)S(1)}, bf16[128,2048]{1,0:T(8,128)(2,1)S(1)}, u32[]{:S(2)}, u32[]{:S(2)}) collective-permute-start(bf16[128,2048]{1,0:T(8,128)(2,1)S(1)} %copy-done.1), channel_id=1, source_target_pairs={{0,4},{4,0},{8,12},{12,8},{1,5},{5,1},{9,13},{13,9},{2,6},{6,2},{1... | collective-permute-start | bytes 1572872 | tf_op jit(solution)/shard_map/ppermute | solution.py:187
  26.5 1.5 %collective-permute-start.6 = (f32[32,128]{1,0:T(8,128)S(1)}, f32[32,128]{1,0:T(8,128)S(1)}, u32[]{:S(2)}, u32[]{:S(2)}) collective-permute-start(f32[32,128]{1,0:T(8,128)S(1)} %fusion), channel_id=1, source_target_pairs={{0,2},{1,3},{2,0},{3,1},{4,6},{5,7},{6,4},{7,5},{8,10},{9,11},{10,... | collective-permute-start | bytes 49160 | tf_op jit(solution)/shard_map/ppermute | solution.py:187
  28.0 1.1 %collective-permute-start.10 = (bf16[16,1152]{1,0:T(8,128)(2,1)S(1)}, bf16[16,1152]{1,0:T(8,128)(2,1)S(1)}, u32[]{:S(2)}, u32[]{:S(2)}) collective-permute-start(bf16[16,1152]{1,0:T(8,128)(2,1)S(1)} %get-tuple-element.29.up_ref), channel_id=1, source_target_pairs={{0,4},{4,0},{8,12},{12,8},{1,5},{5,1},{9,13},{13,9},{2,6},{6,2},{1... | collective-permute-start | bytes 110600 | tf_op jit(solution)/shard_map/ppermute | solution.py:187
  29.1 0.9 %collective-permute-start.7 = (f32[32,128]{1,0:T(8,128)S(1)}, f32[32,128]{1,0:T(8,128)S(1)}, u32[]{:S(2)}, u32[]{:S(2)}) collective-permute-start(f32[32,128]{1,0:T(8,128)S(1)} %fusion), channel_id=1, source_target_pairs={{0,4},{4,0},{8,12},{12,8},{1,5},{5,1},{9,13},{13,9},{2,6},{6,2},{1... | collective-permute-start | bytes 49160 | tf_op jit(solution)/shard_map/ppermute | solution.py:187
  30.0 1.1 %collective-permute-start.8 = (f32[32,128]{1,0:T(8,128)S(1)}, f32[32,128]{1,0:T(8,128)S(1)}, u32[]{:S(2)}, u32[]{:S(2)}) collective-permute-start(f32[32,128]{1,0:T(8,128)S(1)} %fusion), channel_id=1, source_target_pairs={{0,6},{1,7},{2,4},{3,5},{4,2},{5,3},{6,0},{7,1},{8,14},{9,15},{10,... | collective-permute-start | bytes 49160 | tf_op jit(solution)/shard_map/ppermute | solution.py:199
  31.1 9.4 %collective-permute-done.7 = f32[32,128]{1,0:T(8,128)S(1)} collective-permute-done((f32[32,128]{1,0:T(8,128)S(1)}, f32[32,128]{1,0:T(8,128)S(1)}, u32[]{:S(2)}, u32[]{:S(2)}) %collective-permute-start.7) | collective-permute-done | bytes 16416 | tf_op jit(solution)/shard_map/ppermute | solution.py:187
  40.5 1.1 %collective-permute-done.8 = f32[32,128]{1,0:T(8,128)S(1)} collective-permute-done((f32[32,128]{1,0:T(8,128)S(1)}, f32[32,128]{1,0:T(8,128)S(1)}, u32[]{:S(2)}, u32[]{:S(2)}) %collective-permute-start.8) | collective-permute-done | bytes 16416 | tf_op jit(solution)/shard_map/ppermute | solution.py:199
  41.6 0.3 shard_map.115.mine_ref
  41.9 1.9 %collective-permute-start.11 = (bf16[32,2688]{1,0:T(8,128)(2,1)S(1)}, bf16[32,2688]{1,0:T(8,128)(2,1)S(1)}, u32[]{:S(2)}, u32[]{:S(2)}) collective-permute-start(bf16[32,2688]{1,0:T(8,128)(2,1)S(1)} %shard_map.115.mine_ref), channel_id=1, source_target_pairs={{0,8},{4,12},{8,0},{12,4},{1,9},{5,13},{9,1},{13,5},{2,10},{6,14},... | collective-permute-start | bytes 516104 | tf_op jit(solution)/shard_map/ppermute | solution.py:187
  43.9 8.4 %collective-permute-done.11.other_ref = bf16[32,2688]{1,0:T(8,128)(2,1)S(1)} collective-permute-done((bf16[32,2688]{1,0:T(8,128)(2,1)S(1)}, bf16[32,2688]{1,0:T(8,128)(2,1)S(1)}, u32[]{:S(2)}, u32[]{:S(2)}) %collective-permute-start.11) | collective-permute-done | bytes 172064 | tf_op jit(solution)/shard_map/ppermute | solution.py:187
  52.2 0.7 %shard_map.116 = (f32[32,2048]{1,0:T(8,128)}, f32[16,1024]{1,0:T(8,128)}, f32[16,128]{1,0:T(8,128)}) custom-call(bf16[32,2688]{1,0:T(8,128)(2,1)S(1)} %shard_map.115.mine_ref, bf16[32,2688]{1,0:T(8,128)(2,1)S(1)} %collective-permute-done.11.other_ref), custom_call_target="tpu_custom_call" | custom-call | flops 1048576 | bytes 1048576 | tf_op jit(solution)/shard_map/pallas_call | solution.py:273
  (34 shorter events, 0.1 us)
Async XLA Ops:
  0.6 0.7 %copy-start.11 = (s32[128]{0:T(128)S(1)}, s32[128]{0:T(128)}, u32[]{:S(2)}) copy-start(s32[128]{0:T(128)} %param.14) | copy-start | bytes 1540
  1.3 1.0 %copy-start = (bf16[128,2048]{1,0:T(8,128)(2,1)S(1)}, bf16[128,2048]{1,0:T(8,128)(2,1)}, u32[]{:S(2)}) copy-start(bf16[128,2048]{1,0:T(8,128)(2,1)} %x_ref.2) | copy-start | bytes 1572868
  2.3 0.9 %copy-start.4 = (bf16[2048,32]{0,1:T(8,128)(2,1)S(1)}, bf16[2048,32]{0,1:T(8,128)(2,1)}, u32[]{:S(2)}) copy-start(bf16[2048,32]{0,1:T(8,128)(2,1)} %param.15) | copy-start | bytes 393220
  3.2 0.8 %copy-start.5 = (bf16[128,128]{1,0:T(8,128)(2,1)S(1)}, bf16[128,128]{1,0:T(8,128)(2,1)}, u32[]{:S(2)}) copy-start(bf16[128,128]{1,0:T(8,128)(2,1)} %k_ref.3) | copy-start | bytes 98308
  4.0 0.8 %copy-start.7 = (bf16[128,128]{1,0:T(8,128)(2,1)S(1)}, bf16[128,128]{1,0:T(8,128)(2,1)}, u32[]{:S(2)}) copy-start(bf16[128,128]{1,0:T(8,128)(2,1)} %v_ref.3) | copy-start | bytes 98308
  4.8 13.1 %copy-start.3 = (bf16[128,1024]{1,0:T(8,128)(2,1)S(1)}, bf16[128,1024]{1,0:T(8,128)(2,1)}, u32[]{:S(2)}) copy-start(bf16[128,1024]{1,0:T(8,128)(2,1)} %q_ref.1) | copy-start | bytes 786436
  5.0 12.8 %copy-start.2 = (bf16[128,1024]{1,0:T(8,128)(2,1)S(1)}, bf16[128,1024]{1,0:T(8,128)(2,1)}, u32[]{:S(2)}) copy-start(bf16[128,1024]{1,0:T(8,128)(2,1)} %o_ref.3) | copy-start | bytes 786436
  5.0 5.5 %collective-permute-start = (f32[32,128]{1,0:T(8,128)S(1)}, f32[32,128]{1,0:T(8,128)S(1)}, u32[]{:S(2)}, u32[]{:S(2)}) collective-permute-start(f32[32,128]{1,0:T(8,128)S(1)} %get-tuple-element.20), channel_id=1, source_target_pairs={{0,1},{1,0},{2,3},{3,2},{4,5},{5,4},{6,7},{7,6},{8,9},{9,8},{10,11... | collective-permute-start | bytes 49160 | tf_op jit(solution)/shard_map/ppermute | solution.py:187
  5.6 12.3 %collective-permute-start.3 = (bf16[144,128]{1,0:T(8,128)(2,1)S(1)}, bf16[144,128]{1,0:T(8,128)(2,1)S(1)}, u32[]{:S(2)}, u32[]{:S(2)}) collective-permute-start(bf16[144,128]{1,0:T(8,128)(2,1)S(1)} %get-tuple-element.21), channel_id=1, source_target_pairs={{0,4},{4,8},{8,12},{1,5},{5,9},{9,13},{2,6},{6,10},{10,14},{3,7},{... | collective-permute-start | bytes 110600 | tf_op jit(solution)/shard_map/ppermute | solution.py:191
  10.5 7.4 %copy-start.10 = (bf16[16,128]{1,0:T(8,128)(2,1)S(1)}, bf16[16,128]{1,0:T(8,128)(2,1)}, u32[]{:S(2)}) copy-start(bf16[16,128]{1,0:T(8,128)(2,1)} %wv_ref.3) | copy-start | bytes 12292
  10.5 3.8 %collective-permute-start.1 = (f32[32,128]{1,0:T(8,128)S(1)}, f32[32,128]{1,0:T(8,128)S(1)}, u32[]{:S(2)}, u32[]{:S(2)}) collective-permute-start(f32[32,128]{1,0:T(8,128)S(1)} %add.39), channel_id=1, source_target_pairs={{0,2},{1,3},{2,0},{3,1},{4,6},{5,7},{6,4},{7,5},{8,10},{9,11},{10,... | collective-permute-start | bytes 49160 | tf_op jit(solution)/shard_map/ppermute | solution.py:187
  12.1 5.8 %copy-start.9 = (bf16[16,1024]{1,0:T(8,128)(2,1)S(1)}, bf16[16,1024]{1,0:T(8,128)(2,1)}, u32[]{:S(2)}) copy-start(bf16[16,1024]{1,0:T(8,128)(2,1)} %wq_ref.3) | copy-start | bytes 98308
  12.1 5.8 %copy-start.6 = (bf16[128,128]{1,0:T(8,128)(2,1)S(1)}, bf16[128,128]{1,0:T(8,128)(2,1)}, u32[]{:S(2)}) copy-start(bf16[128,128]{1,0:T(8,128)(2,1)} %k_ref.3) | copy-start | bytes 98308
  14.4 6.4 %collective-permute-start.2 = (bf16[16,128]{1,0:T(8,128)(2,1)S(1)}, bf16[16,128]{1,0:T(8,128)(2,1)S(1)}, u32[]{:S(2)}, u32[]{:S(2)}) collective-permute-start(bf16[16,128]{1,0:T(8,128)(2,1)S(1)} %slice.7), channel_id=1, source_target_pairs={{0,4},{4,8},{8,12},{1,5},{5,9},{9,13},{2,6},{6,10},{10,14},{3,7},{... | collective-permute-start | bytes 12296 | tf_op jit(solution)/shard_map/ppermute | solution.py:191
  19.2 1.6 %copy-start.8 = (bf16[128,128]{1,0:T(8,128)(2,1)S(1)}, bf16[128,128]{1,0:T(8,128)(2,1)}, u32[]{:S(2)}) copy-start(bf16[128,128]{1,0:T(8,128)(2,1)} %v_ref.3) | copy-start | bytes 98308
  19.2 5.7 %collective-permute-start.4 = (f32[16,128]{1,0:T(8,128)S(1)}, f32[16,128]{1,0:T(8,128)S(1)}, u32[]{:S(2)}, u32[]{:S(2)}) collective-permute-start(f32[16,128]{1,0:T(8,128)S(1)} %bitcast.13), channel_id=1, source_target_pairs={{4,0},{8,4},{12,8},{5,1},{9,5},{13,9},{6,2},{10,6},{14,10},{7,3},{... | collective-permute-start | bytes 24584 | tf_op jit(solution)/shard_map/ppermute | solution.py:191
  20.8 4.0 %copy-start.1 = (bf16[128,2048]{1,0:T(8,128)(2,1)S(1)}, bf16[128,2048]{1,0:T(8,128)(2,1)}, u32[]{:S(2)}) copy-start(bf16[128,2048]{1,0:T(8,128)(2,1)} %x_ref.2) | copy-start | bytes 1572868
  24.8 1.7 %collective-permute-start.5 = (f32[32,128]{1,0:T(8,128)S(1)}, f32[32,128]{1,0:T(8,128)S(1)}, u32[]{:S(2)}, u32[]{:S(2)}) collective-permute-start(f32[32,128]{1,0:T(8,128)S(1)} %pad_maximum_fusion), channel_id=1, source_target_pairs={{0,1},{1,0},{2,3},{3,2},{4,5},{5,4},{6,7},{7,6},{8,9},{9,8},{10,11... | collective-permute-start | bytes 49160 | tf_op jit(solution)/shard_map/ppermute | solution.py:187
  24.9 16.8 %collective-permute-start.9 = (bf16[128,2048]{1,0:T(8,128)(2,1)S(1)}, bf16[128,2048]{1,0:T(8,128)(2,1)S(1)}, u32[]{:S(2)}, u32[]{:S(2)}) collective-permute-start(bf16[128,2048]{1,0:T(8,128)(2,1)S(1)} %copy-done.1), channel_id=1, source_target_pairs={{0,4},{4,0},{8,12},{12,8},{1,5},{5,1},{9,13},{13,9},{2,6},{6,2},{1... | collective-permute-start | bytes 1572872 | tf_op jit(solution)/shard_map/ppermute | solution.py:187
  26.5 4.6 %collective-permute-start.6 = (f32[32,128]{1,0:T(8,128)S(1)}, f32[32,128]{1,0:T(8,128)S(1)}, u32[]{:S(2)}, u32[]{:S(2)}) collective-permute-start(f32[32,128]{1,0:T(8,128)S(1)} %fusion), channel_id=1, source_target_pairs={{0,2},{1,3},{2,0},{3,1},{4,6},{5,7},{6,4},{7,5},{8,10},{9,11},{10,... | collective-permute-start | bytes 49160 | tf_op jit(solution)/shard_map/ppermute | solution.py:187
  28.0 13.6 %collective-permute-start.10 = (bf16[16,1152]{1,0:T(8,128)(2,1)S(1)}, bf16[16,1152]{1,0:T(8,128)(2,1)S(1)}, u32[]{:S(2)}, u32[]{:S(2)}) collective-permute-start(bf16[16,1152]{1,0:T(8,128)(2,1)S(1)} %get-tuple-element.29.up_ref), channel_id=1, source_target_pairs={{0,4},{4,0},{8,12},{12,8},{1,5},{5,1},{9,13},{13,9},{2,6},{6,2},{1... | collective-permute-start | bytes 110600 | tf_op jit(solution)/shard_map/ppermute | solution.py:187
  29.1 11.4 %collective-permute-start.7 = (f32[32,128]{1,0:T(8,128)S(1)}, f32[32,128]{1,0:T(8,128)S(1)}, u32[]{:S(2)}, u32[]{:S(2)}) collective-permute-start(f32[32,128]{1,0:T(8,128)S(1)} %fusion), channel_id=1, source_target_pairs={{0,4},{4,0},{8,12},{12,8},{1,5},{5,1},{9,13},{13,9},{2,6},{6,2},{1... | collective-permute-start | bytes 49160 | tf_op jit(solution)/shard_map/ppermute | solution.py:187
  30.0 11.6 %collective-permute-start.8 = (f32[32,128]{1,0:T(8,128)S(1)}, f32[32,128]{1,0:T(8,128)S(1)}, u32[]{:S(2)}, u32[]{:S(2)}) collective-permute-start(f32[32,128]{1,0:T(8,128)S(1)} %fusion), channel_id=1, source_target_pairs={{0,6},{1,7},{2,4},{3,5},{4,2},{5,3},{6,0},{7,1},{8,14},{9,15},{10,... | collective-permute-start | bytes 49160 | tf_op jit(solution)/shard_map/ppermute | solution.py:199
  41.9 10.3 %collective-permute-start.11 = (bf16[32,2688]{1,0:T(8,128)(2,1)S(1)}, bf16[32,2688]{1,0:T(8,128)(2,1)S(1)}, u32[]{:S(2)}, u32[]{:S(2)}) collective-permute-start(bf16[32,2688]{1,0:T(8,128)(2,1)S(1)} %shard_map.115.mine_ref), channel_id=1, source_target_pairs={{0,8},{4,12},{8,0},{12,4},{1,9},{5,13},{9,1},{13,5},{2,10},{6,14},... | collective-permute-start | bytes 516104 | tf_op jit(solution)/shard_map/ppermute | solution.py:187

commit v2 on v1

v2 whole, which is shorter than its diff:
```python
import functools
import math

import jax
import jax.numpy as jnp
from jax import lax
from jax.experimental import pallas as pl
from jax.experimental.pallas import tpu as pltpu
from jax.sharding import PartitionSpec as P

HEAD = 128
HALF = HEAD // 2
RANK = 16
SCALE = 2.0
ROPE_BASE = 500000.0
NEG_FILL = -1e30
INV_ROOT = 1.0 / math.sqrt(HEAD)
F32 = jnp.float32
BF16 = jnp.bfloat16
EXACT = lax.Precision.HIGHEST
LIMIT = 40 * 1024 * 1024
FULL = 63 * 1024 * 1024


def dot(left, right, left_dim, right_dim, precision=None):
    return lax.dot_general(
        left,
        right,
        (((left_dim,), (right_dim,)), ((), ())),
        precision=precision,
        preferred_element_type=F32,
    )


def call(kernel, out_shapes, scratch=(), limit=LIMIT, cost=1, **specs):
    return pl.pallas_call(
        kernel,
        out_shape=[jax.ShapeDtypeStruct(s, d) for s, d in out_shapes],
        **specs,
        scratch_shapes=list(scratch),
        compiler_params=pltpu.CompilerParams(vmem_limit_bytes=limit),
        cost_estimate=pl.CostEstimate(flops=cost, bytes_accessed=cost, transcendentals=0),
    )


def lowrank_kernel(x_hbm, a_hbm, part_ref, x_ref, a_ref, sems):
    copies = [
        pltpu.make_async_copy(x_hbm, x_ref, sems.at[0]),
        pltpu.make_async_copy(a_hbm, a_ref, sems.at[1]),
    ]
    for copy in copies:
        copy.start()
    for copy in copies:
        copy.wait()
    part_ref[...] = dot(a_ref[...], x_ref[...], 1, 1)


def rotate_rows(u, cos, sin):
    return u * cos + pltpu.roll(u, HALF, 1) * sin


def wide_tables(cos, sin):
    return jnp.concatenate([cos, cos], axis=1), jnp.concatenate([-sin, sin], axis=1)


def column(row, tok):
    return jnp.broadcast_to(row, (tok, tok)).T


def project_kernel(
    heads,
    low_ref, q_ref, k_ref, v_ref, o_ref, seg_ref, cos_ref, sin_ref, wq_ref, wv_ref,
    qr_ref, kt_ref, s_ref, dp_ref, bias_ref,
):
    tok = q_ref.shape[0]
    low = low_ref[...].astype(BF16)
    cos, sin = wide_tables(cos_ref[...], sin_ref[...])
    keys = rotate_rows(k_ref[...].astype(F32), cos, sin)
    kt_ref[...] = keys.T.astype(BF16)
    keys = keys.astype(BF16)
    vals = (v_ref[...].astype(F32) + SCALE * dot(low[RANK:], wv_ref[...], 0, 0)).astype(BF16)
    seg_here = seg_ref[...].astype(F32)
    key = lax.broadcasted_iota(jnp.int32, (tok, tok), 0)
    query = lax.broadcasted_iota(jnp.int32, (tok, tok), 1)
    allowed = (key <= query) & (column(seg_here, tok) == seg_here)
    bias_ref[...] = jnp.where(allowed, 0.0, NEG_FILL)
    q0 = q_ref[...].astype(F32) + SCALE * dot(low[:RANK], wq_ref[...], 0, 0)
    for h in range(heads):
        cut = slice(h * HEAD, (h + 1) * HEAD)
        qr = rotate_rows(q0[:, cut], cos, sin).astype(BF16)
        qr_ref[h] = qr
        s_ref[h] = dot(keys, qr, 1, 1) * INV_ROOT + bias_ref[...]
        dp_ref[h] = dot(vals, o_ref[:, cut], 1, 1)


def softmax_kernel(
    send, blocks, heads,
    qr_ref, s_ref, o_ref, seg_ref, pack_ref, base_ref, cos_ref, sin_ref, wv_ref,
    w_ref, kt_ref, dv_ref, code_ref, back_ref, bias_ref, keys_ref,
):
    tok = qr_ref.shape[1]
    halo = send * blocks
    cos, sin = wide_tables(cos_ref[...], sin_ref[...])
    keys = jnp.concatenate([pack_ref[b, 0:send] for b in range(blocks)], axis=0)
    keys = rotate_rows(keys.astype(F32), cos, sin)
    kt_ref[...] = keys.T.astype(BF16)
    keys_ref[...] = keys.astype(BF16)
    seg_here = seg_ref[...].astype(F32)
    cols = []
    for b in range(blocks):
        row = pack_ref[b, 2 * send + RANK :].astype(F32)[0:1]
        cols.append(column(row, tok)[tok - send :])
    seg_col = jnp.concatenate(cols, axis=0)
    offset = lax.broadcasted_iota(jnp.int32, (halo, tok), 0)
    allowed = (offset + base_ref[0] >= halo) & (seg_col == seg_here)
    bias_ref[...] = jnp.where(allowed, 0.0, NEG_FILL)
    dv = jnp.zeros((halo + tok, HEAD), F32)
    for h in range(heads):
        far = dot(keys_ref[...], qr_ref[h], 1, 1) * INV_ROOT + bias_ref[...]
        s = jnp.concatenate([far, s_ref[h]], axis=0)
        e = jnp.exp(s - jnp.max(s, axis=0, keepdims=True))
        w = e * (1.0 / jnp.sum(e, axis=0, keepdims=True))
        w_ref[h] = w
        dv = dv + dot(w.astype(BF16), o_ref[:, h * HEAD : (h + 1) * HEAD], 1, 0)
    dv_ref[...] = dv
    wv = wv_ref[...].astype(F32)
    code_ref[...] = SCALE * dot(wv, dv[halo:], 1, 1, EXACT)
    for b in range(blocks):
        part = dv[b * send : (b + 1) * send]
        if send < tok:
            part = jnp.concatenate([jnp.zeros((tok - send, HEAD), F32), part], axis=0)
        back_ref[b] = SCALE * dot(wv, part, 1, 1, EXACT)


def grads_kernel(
    send, blocks, heads,
    low_ref, pack_ref, o_ref, w_ref, dp_ref, kt_ref, kth_ref, dv_ref, cost_ref, sint_ref, wq_ref, wv_ref,
    code_ref, up_ref, vals_ref, qg_ref,
):
    tok = o_ref.shape[0]
    halo = send * blocks
    low = low_ref[...].astype(BF16)
    wv = wv_ref[...]
    codes = [pack_ref[b, 2 * send : 2 * send + RANK] for b in range(blocks)]
    for b in range(blocks):
        rows = pack_ref[b, send : 2 * send].astype(F32)
        add = SCALE * dot(codes[b], wv, 0, 0)[tok - send :]
        vals_ref[b * send : (b + 1) * send] = (rows + add).astype(BF16)
    kt = jnp.concatenate([kth_ref[...], kt_ref[...]], axis=1)
    cos, sin = cost_ref[...], sint_ref[...]
    for h in range(heads):
        far = dot(vals_ref[...], o_ref[:, h * HEAD : (h + 1) * HEAD], 1, 1)
        dp = jnp.concatenate([far, dp_ref[h]], axis=0)
        w = w_ref[h]
        delta = jnp.sum(w * dp, axis=0, keepdims=True)
        ds = (w * (dp - delta) * INV_ROOT).astype(BF16)
        dq = dot(kt, ds, 1, 0)
        first, second = dq[:HALF], dq[HALF:]
        qg_ref[h * HEAD : h * HEAD + HALF] = (first * cos + second * sin).astype(BF16)
        qg_ref[h * HEAD + HALF : (h + 1) * HEAD] = (second * cos - first * sin).astype(BF16)
    qg = qg_ref[...]
    code_ref[...] = SCALE * dot(wq_ref[...], qg, 1, 0)
    up_q = SCALE * dot(low[:RANK], qg, 1, 1)
    dv = dv_ref[...]
    up_v = dot(low[RANK:].astype(F32), dv[halo:], 1, 0, EXACT)
    for b in range(blocks):
        part = dv[b * send : (b + 1) * send]
        if send < tok:
            part = jnp.concatenate([jnp.zeros((tok - send, HEAD), F32), part], axis=0)
        up_v = up_v + dot(codes[b].astype(F32), part, 1, 0, EXACT)
    up_ref[:, : heads * HEAD] = up_q.astype(up_ref.dtype)
    up_ref[:, heads * HEAD :] = (SCALE * up_v).astype(up_ref.dtype)


def down_kernel(dl_ref, x_ref, part_ref):
    part_ref[...] = dot(dl_ref[...], x_ref[...], 1, 0)


def pair_kernel(split, dl_ref, dlp_ref, x_ref, xp_ref, up_ref, upp_ref, send_ref):
    rows, wide = dl_ref.shape[0], x_ref.shape[1]
    part = dot(dl_ref[...], x_ref[...], 1, 0) + dot(dlp_ref[...], xp_ref[...], 1, 0)
    send_ref[:, :wide] = part.astype(BF16)
    up = (up_ref[...].astype(F32) + upp_ref[...].astype(F32)).astype(BF16)
    size = up.shape[1]
    send_ref[0:RANK, wide:] = up[:, :split]
    send_ref[RANK:rows, wide : wide + size - split] = up[:, split:]
    if 2 * split > size:
        send_ref[RANK:rows, wide + size - split :] = jnp.zeros((rows - RANK, 2 * split - size), BF16)


def final_kernel(split, mine_ref, other_ref, down_ref, upq_ref, upv_ref):
    wide = down_ref.shape[1]
    total = mine_ref[...].astype(F32) + other_ref[...].astype(F32)
    down_ref[...] = total[:, :wide]
    size = upq_ref.shape[1]
    upq_ref[:, :split] = total[:RANK, wide:]
    upq_ref[:, split:] = total[RANK:, wide : wide + size - split]
    upv_ref[...] = total[RANK:, wide + size - split : wide + size - split + HEAD]


def body(x, q, k, v, o, segment, a, wq, wv):
    tok, wide = x.shape
    seq_count = lax.axis_size("seq")
    fsdp_count = lax.axis_size("fsdp")
    seq_index = lax.axis_index("seq")
    heads = q.shape[1] // HEAD
    longest = tok * seq_count // 8
    blocks = -(-longest // tok)
    send = longest if blocks == 1 else tok
    halo = blocks * send
    keys = halo + tok
    paired = seq_count == 4 and fsdp_count == 4

    def swap(array, axis, bit):
        size = lax.axis_size(axis)
        return lax.ppermute(array, axis, [(i, i ^ bit) for i in range(size)])

    def shift(array, by):
        moves = [(i, (i + by) % seq_count) for i in range(seq_count)]
        return lax.ppermute(array, "seq", moves)

    def cross(array):
        moves = [
            (s * fsdp_count + f, (s ^ 1) * fsdp_count + (f ^ 2))
            for s in range(seq_count)
            for f in range(fsdp_count)
        ]
        return lax.ppermute(array, ("seq", "fsdp"), moves)

    def sum_fsdp(array):
        if fsdp_count & (fsdp_count - 1):
            return lax.psum(array, "fsdp")
        bit = 1
        while bit < fsdp_count:
            array = array + swap(array, "fsdp", bit)
            bit *= 2
        return array

    seg_row = segment.reshape(1, tok)
    hbm = pl.BlockSpec(memory_space=pltpu.HBM)
    (part,) = call(
        lowrank_kernel,
        [((2 * RANK, tok), F32)],
        [
            pltpu.VMEM((tok, wide), BF16),
            pltpu.VMEM((2 * RANK, wide), BF16),
            pltpu.SemaphoreType.DMA((2,)),
        ],
        limit=FULL,
        in_specs=[hbm, hbm],
    )(x, a.T)
    if paired:
        part, x = lax.optimization_barrier((part, x))
        x_pair = swap(x, "seq", 1)
    start = seq_index * tok
    base = start.reshape(1).astype(jnp.int32)
    freqs = ROPE_BASE ** (-(2.0 * jnp.arange(HALF, dtype=F32)) / HEAD)
    positions = (start - halo + jnp.arange(keys, dtype=jnp.int32)).astype(F32)
    angles = positions[:, None] * freqs[None, :]
    cos, sin = jnp.cos(angles), jnp.sin(angles)
    here = (start + jnp.arange(tok, dtype=jnp.int32)).astype(F32)
    angles_t = freqs[:, None] * here[None, :]
    cos_t, sin_t = jnp.cos(angles_t), jnp.sin(angles_t)

    low = sum_fsdp(part)
    seg_rows = jnp.broadcast_to(seg_row, (16, tok)).astype(BF16)
    pack = jnp.concatenate(
        [k[tok - send :], v[tok - send :], low[RANK:].astype(BF16), seg_rows], axis=0
    )
    packs = jnp.stack([shift(pack, d) for d in range(blocks, 0, -1)])
    qr, kt, s, dp = call(
        functools.partial(project_kernel, heads),
        [
            ((heads, tok, HEAD), BF16),
            ((HEAD, tok), BF16),
            ((heads, tok, tok), F32),
            ((heads, tok, tok), F32),
        ],
        [pltpu.VMEM((tok, tok), F32)],
    )(low, q, k, v, o, seg_row, cos[halo:], sin[halo:], wq, wv)
    specs = [pl.BlockSpec(memory_space=pltpu.VMEM)] * 9
    specs[5] = pl.BlockSpec(memory_space=pltpu.SMEM)
    w, kt_far, dv, code_v, back = call(
        functools.partial(softmax_kernel, send, blocks, heads),
        [
            ((heads, keys, tok), F32),
            ((HEAD, halo), BF16),
            ((keys, HEAD), F32),
            ((RANK, tok), F32),
            ((blocks, RANK, tok), F32),
        ],
        [pltpu.VMEM((halo, tok), F32), pltpu.VMEM((halo, HEAD), BF16)],
        in_specs=specs,
    )(qr, s, o, seg_row, packs, base, cos[:halo], sin[:halo], wv)
    for b, d in enumerate(range(blocks, 0, -1)):
        code_v = code_v + shift(back[b], -d)
    code_q, up = call(
        functools.partial(grads_kernel, send, blocks, heads),
        [((RANK, tok), F32), ((RANK, (heads + 1) * HEAD), BF16 if paired else F32)],
        [pltpu.VMEM((halo, HEAD), BF16), pltpu.VMEM((heads * HEAD, tok), BF16)],
        cost=6 << 20,
    )(low, packs, o, w, dp, kt, kt_far, dv, cos_t, sin_t, wq, wv)
    codes = jnp.concatenate([code_q, code_v], axis=0)

    if not paired:
        dlow = sum_fsdp(codes).astype(BF16)
        (down,) = call(down_kernel, [((2 * RANK, wide), F32)])(dlow, x)
        down, up = lax.psum((down, up), "seq")
        return down.T, up[:, : heads * HEAD], up[:, heads * HEAD :]

    up_pair = swap(up, "seq", 1)
    codes, x_pair = lax.optimization_barrier((codes, x_pair))
    codes = codes + swap(codes, "fsdp", 1)
    dlow = (codes + swap(codes, "fsdp", 2)).astype(BF16)
    dlow_pair = (swap(codes, "seq", 1) + cross(codes)).astype(BF16)
    split = -(-(heads + 1) // 2) * HEAD
    (mine,) = call(functools.partial(pair_kernel, split), [((2 * RANK, wide + split), BF16)])(
        dlow, dlow_pair, x, x_pair, up, up_pair
    )
    other = swap(mine, "seq", 2)
    down, up_q, up_v = call(
        functools.partial(final_kernel, split),
        [((2 * RANK, wide), F32), ((RANK, heads * HEAD), F32), ((RANK, HEAD), F32)],
    )(mine, other)
    return down.T, up_q, up_v


def solution(mesh):
    rows = ("groups", "seq")
    in_specs = (
        P(rows, "fsdp"),
        P(rows, "fsdp"),
        P(rows, "fsdp"),
        P(rows, "fsdp"),
        P(rows, "fsdp"),
        P(rows),
        P("fsdp", None),
        P(None, "fsdp"),
        P(None, "fsdp"),
    )
    out_specs = (P(("groups", "fsdp"), None), P("groups", "fsdp"), P("groups", "fsdp"))
    return jax.shard_map(body, mesh=mesh, in_specs=in_specs, out_specs=out_specs, check_vma=False)
```

time: 53.4 us -> 46.5 us (0.87)
  starting transfers between devices: 19.6 us -> 13.3 us
  local copies, waits for them, and re-layouts: 4.15 us -> 1.3 us
  Pallas kernels: 4.65 us -> 7.17 us
  waiting for transfers between devices: 23 us -> 22.2 us
  other arithmetic: 0.67 us -> 1.41 us
    ppermute x8, waiting for transfers between devices: 20 us -> 11.6 us  [swap(): return lax.ppermute(array, axis, [(i, i ^ bit) for i in range(size)])]
    ppermute x3 -> x2, starting transfers between devices: 9.38 us -> 2.91 us  [shift(): return lax.ppermute(array, 'seq', moves)]
    ppermute x3 -> x2, waiting for transfers between devices: 1.89 us -> 8.28 us  [shift(): return lax.ppermute(array, 'seq', moves)]
    unnamed x24 -> x16, local copies, waits for them, and re-layouts: 4.14 us -> 1.26 us
    pallas_call x3 -> x4, Pallas kernels: 3.63 us -> 6.17 us  [the longest x1 2.12 us: body(): call(functools.partial(grads_kernel, send, blocks, heads), [((RANK, tok),...]
    ppermute x1, waiting for transfers between devices: 1.11 us -> 2.35 us  [cross(): return lax.ppermute(array, ('seq', 'fsdp'), moves)]
    ppermute x8, starting transfers between devices: 9.19 us -> 9.99 us  [swap(): return lax.ppermute(array, axis, [(i, i ^ bit) for i in range(size)])]
    add x2, other arithmetic: 0.01 us -> 0.73 us  [sum_fsdp(): array = array + swap(array, 'fsdp', bit)]
  transfers between devices with their start and end apart: 12 -> 11, of which waited for: 5 -> 6; matrix products, arithmetic and copies ran while one was open for 1% -> 3% of each run, Pallas kernels for 6% -> 9%
where the time goes in v2:
time: 46.5 us; the launch traced here: 46.3 us
  waiting for transfers between devices  22.2 us (48%)
  starting transfers between devices  13.3 us (29%)
  Pallas kernels  7.17 us (15%)
  other arithmetic  1.41 us (3%)
  local copies, waits for them, and re-layouts  1.3 us (3%)
  between operations  0.86 us (2%)
    ppermute x8, waiting for transfers between devices, swap(): return lax.ppermute(array, axis, [(i, i ^ bit) for i in range(size)])  11.6 us
    ppermute x8, starting transfers between devices, swap(): return lax.ppermute(array, axis, [(i, i ^ bit) for i in range(size)])  9.99 us
    ppermute x2, waiting for transfers between devices, shift(): return lax.ppermute(array, 'seq', moves)  8.28 us
    ppermute x2, starting transfers between devices, shift(): return lax.ppermute(array, 'seq', moves)  2.91 us
    ppermute x1, waiting for transfers between devices, cross(): return lax.ppermute(array, ('seq', 'fsdp'), moves)  2.35 us
    pallas_call x1, Pallas kernels, body(): call(functools.partial(grads_kernel, send, blocks, heads), [((RANK, tok),...  2.12 us
    pallas_call x1, Pallas kernels, body(): call(lowrank_kernel, [((2 * RANK, tok), F32)], [pltpu.VMEM((tok, wide), B...  2.03 us
    pallas_call x1, Pallas kernels, body(): call(functools.partial(softmax_kernel, send, blocks, heads), [((heads, ke...  1.31 us
  transfers between devices with their start and end apart: 11, of which 6 were waited for; matrix products, arithmetic and copies ran while one was open for 3% of the time, Pallas kernels for 9%

profile of v2, /device:TPU:0, one launch (start us, length us, event | category | flops | bytes accessed | tf_op | source)
XLA Modules:
  0.0 46.3 jit_solution(14155323087123356782)
XLA Ops:
  0.6 2.0 %shard_map.112 = f32[32,128]{1,0:T(8,128)} custom-call(bf16[128,2048]{1,0:T(8,128)(2,1)} %x_ref, bf16[32,2048]{1,0:T(8,128)(2,1)} %bitcast.11), custom_call_target="tpu_custom_call" | custom-call | flops 1 | bytes 1 | tf_op jit(solution)/shard_map/pallas_call | solution.py:241
  2.7 0.5 %collective-permute-start = (f32[32,128]{1,0:T(8,128)}, f32[32,128]{1,0:T(8,128)S(1)}, u32[]{:S(2)}, u32[]{:S(2)}) collective-permute-start(f32[32,128]{1,0:T(8,128)} %shard_map.112), channel_id=1, source_target_pairs={{0,1},{1,0},{2,3},{3,2},{4,5},{5,4},{6,7},{7,6},{8,9},{9,8},{10,11... | collective-permute-start | bytes 49160 | tf_op jit(solution)/shard_map/ppermute | solution.py:216
  3.2 2.7 %collective-permute-start.4 = (bf16[128,2048]{1,0:T(8,128)(2,1)S(1)}, bf16[128,2048]{1,0:T(8,128)(2,1)S(1)}, u32[]{:S(2)}, u32[]{:S(2)}) collective-permute-start(bf16[128,2048]{1,0:T(8,128)(2,1)S(1)} %copy-done.1), channel_id=1, source_target_pairs={{0,4},{4,0},{8,12},{12,8},{1,5},{5,1},{9,13},{13,9},{2,6},{6,2},{1... | collective-permute-start | bytes 1572872 | tf_op jit(solution)/shard_map/ppermute | solution.py:216
  5.9 0.7 %add.39 = f32[32,128]{1,0:T(8,128)S(1)} add(f32[32,128]{1,0:T(8,128)} %shard_map.112, f32[32,128]{1,0:T(8,128)S(1)} %collective-permute-done) | non-fusion elementwise | flops 4096 | bytes 49152 | tf_op jit(solution)/shard_map/add | solution.py:235
  6.6 1.5 %collective-permute-start.1 = (f32[32,128]{1,0:T(8,128)S(1)}, f32[32,128]{1,0:T(8,128)S(1)}, u32[]{:S(2)}, u32[]{:S(2)}) collective-permute-start(f32[32,128]{1,0:T(8,128)S(1)} %add.39), channel_id=1, source_target_pairs={{0,2},{1,3},{2,0},{3,1},{4,6},{5,7},{6,4},{7,5},{8,10},{9,11},{10,... | collective-permute-start | bytes 49160 | tf_op jit(solution)/shard_map/ppermute | solution.py:216
  8.1 0.4 multiply_sine_fusion
  8.5 0.0 copy-start.7
  8.5 0.0 copy-start.4
  8.6 0.0 copy-start.3
  8.6 0.6 %copy-done.7 = s32[128]{0:T(128)S(1)} copy-done((s32[128]{0:T(128)S(1)}, s32[128]{0:T(128)}, u32[]{:S(2)}) %copy-start.7) | copy-done | bytes 536
  9.2 1.2 %collective-permute-done.1 = f32[32,128]{1,0:T(8,128)S(1)} collective-permute-done((f32[32,128]{1,0:T(8,128)S(1)}, f32[32,128]{1,0:T(8,128)S(1)}, u32[]{:S(2)}, u32[]{:S(2)}) %collective-permute-start.1) | collective-permute-done | bytes 16416 | tf_op jit(solution)/shard_map/ppermute | solution.py:216
  10.4 1.3 %collective-permute-start.2 = (bf16[160,128]{1,0:T(8,128)(2,1)S(1)}, bf16[160,128]{1,0:T(8,128)(2,1)S(1)}, u32[]{:S(2)}, u32[]{:S(2)}) collective-permute-start(bf16[160,128]{1,0:T(8,128)(2,1)S(1)} %pad_maximum_fusion), channel_id=1, source_target_pairs={{0,4},{4,8},{8,12},{12,0},{1,5},{5,9},{9,13},{13,1},{2,6},{6,10},{... | collective-permute-start | bytes 122888 | tf_op jit(solution)/shard_map/ppermute | solution.py:220
  11.8 0.0 copy-start.6
  11.8 0.6 %copy-done.6 = bf16[16,128]{1,0:T(8,128)(2,1)S(1)} copy-done((bf16[16,128]{1,0:T(8,128)(2,1)S(1)}, bf16[16,128]{1,0:T(8,128)(2,1)}, u32[]{:S(2)}) %copy-start.6) | copy-done | bytes 4120
  12.4 0.7 %shard_map.113 = (bf16[8,128,128]{2,1,0:T(8,128)(2,1)S(1)}, bf16[128,128]{1,0:T(8,128)(2,1)S(1)}, f32[8,128,128]{2,1,0:T(8,128)S(1)}, f32[8,128,128]{2,1,0:T(8,128)S(1)}) custom-call(f32[32,128]{1,0:T(8,128)S(1)} %add.40.low_ref, bf16[128,1024]{1,0:T(8,128)(2,1)S(1)} %copy-done.2, bf16[128,128]{1,0:T(8,128)(2,1)S(1)} %copy-done.4, ...), custom_call_target="tpu_custom_call" | custom-call | flops 1 | bytes 1 | tf_op jit(solution)/shard_map/pallas_call | solution.py:271
  13.2 8.3 %collective-permute-done.2 = bf16[160,128]{1,0:T(8,128)(2,1)S(1)} collective-permute-done((bf16[160,128]{1,0:T(8,128)(2,1)S(1)}, bf16[160,128]{1,0:T(8,128)(2,1)S(1)}, u32[]{:S(2)}, u32[]{:S(2)}) %collective-permute-start.2) | collective-permute-done | bytes 40992 | tf_op jit(solution)/shard_map/ppermute | solution.py:220
  21.4 1.3 %shard_map.114 = (f32[8,192,128]{2,1,0:T(8,128)S(1)}, bf16[128,64]{1,0:T(8,128)(2,1)S(1)}, f32[192,128]{1,0:T(8,128)S(1)}, f32[16,128]{1,0:T(8,128)S(1)}, f32[1,16,128]{2,1,0:T(8,128)S(1)}) custom-call(bf16[8,128,128]{2,1,0:T(8,128)(2,1)S(1)} %get-tuple-element.22.qr_ref, f32[8,128,128]{2,1,0:T(8,128)S(1)} %get-tuple-element.23.s_ref, ...), custom_call_target="tpu_custom_call" | custom-call | flops 1 | bytes 1 | tf_op jit(solution)/shard_map/pallas_call | solution.py:283
  22.8 1.6 %collective-permute-start.3 = (f32[16,128]{1,0:T(8,128)S(1)}, f32[16,128]{1,0:T(8,128)S(1)}, u32[]{:S(2)}, u32[]{:S(2)}) collective-permute-start(f32[16,128]{1,0:T(8,128)S(1)} %bitcast.10), channel_id=1, source_target_pairs={{0,12},{4,0},{8,4},{12,8},{1,13},{5,1},{9,5},{13,9},{2,14},{6,2},{... | collective-permute-start | bytes 24584 | tf_op jit(solution)/shard_map/ppermute | solution.py:220
  24.3 0.2 multiply_sine_fusion.1
  24.5 2.1 %shard_map.115 = (f32[16,128]{1,0:T(8,128)S(1)}, bf16[16,1152]{1,0:T(8,128)(2,1)S(1)}) custom-call(f32[32,128]{1,0:T(8,128)S(1)} %add.40.low_ref, bf16[1,160,128]{2,1,0:T(8,128)(2,1)S(1)} %bitcast.7, bf16[128,1024]{1,0:T(8,128)(2,1)S(1)} %copy-done, f32[8,192,128]{2,1,0:T(8,128)S(1)} %get-tuple-element.24.w_ref, ...), custom_call_target="tpu_custom_call" | custom-call | flops 6291456 | bytes 6291456 | tf_op jit(solution)/shard_map/pallas_call | solution.py:297
  26.7 0.1 collective-permute-start.5
  26.8 1.2 %collective-permute-done.5 = f32[32,128]{1,0:T(8,128)S(1)} collective-permute-done((f32[32,128]{1,0:T(8,128)S(1)}, f32[32,128]{1,0:T(8,128)S(1)}, u32[]{:S(2)}, u32[]{:S(2)}) %collective-permute-start.5) | collective-permute-done | bytes 16416 | tf_op jit(solution)/shard_map/ppermute | solution.py:216
  28.0 1.5 %collective-permute-start.6 = (f32[32,128]{1,0:T(8,128)S(1)}, f32[32,128]{1,0:T(8,128)S(1)}, u32[]{:S(2)}, u32[]{:S(2)}) collective-permute-start(f32[32,128]{1,0:T(8,128)S(1)} %add.46), channel_id=1, source_target_pairs={{0,2},{1,3},{2,0},{3,1},{4,6},{5,7},{6,4},{7,5},{8,10},{9,11},{10,... | collective-permute-start | bytes 49160 | tf_op jit(solution)/shard_map/ppermute | solution.py:216
  29.5 0.4 collective-permute-start.9
  29.9 1.6 %collective-permute-start.7 = (f32[32,128]{1,0:T(8,128)S(1)}, f32[32,128]{1,0:T(8,128)S(1)}, u32[]{:S(2)}, u32[]{:S(2)}) collective-permute-start(f32[32,128]{1,0:T(8,128)S(1)} %add.46), channel_id=1, source_target_pairs={{0,4},{4,0},{8,12},{12,8},{1,5},{5,1},{9,13},{13,9},{2,6},{6,2},{1... | collective-permute-start | bytes 49160 | tf_op jit(solution)/shard_map/ppermute | solution.py:216
  31.5 0.4 collective-permute-start.8
  31.9 1.9 %collective-permute-done.7 = f32[32,128]{1,0:T(8,128)S(1)} collective-permute-done((f32[32,128]{1,0:T(8,128)S(1)}, f32[32,128]{1,0:T(8,128)S(1)}, u32[]{:S(2)}, u32[]{:S(2)}) %collective-permute-start.7) | collective-permute-done | bytes 16416 | tf_op jit(solution)/shard_map/ppermute | solution.py:216
  33.8 2.4 %collective-permute-done.8 = f32[32,128]{1,0:T(8,128)S(1)} collective-permute-done((f32[32,128]{1,0:T(8,128)S(1)}, f32[32,128]{1,0:T(8,128)S(1)}, u32[]{:S(2)}, u32[]{:S(2)}) %collective-permute-start.8) | collective-permute-done | bytes 16416 | tf_op jit(solution)/shard_map/ppermute | solution.py:228
  36.1 0.3 shard_map.116.mine_ref
  36.4 1.7 %collective-permute-start.10 = (bf16[32,2688]{1,0:T(8,128)(2,1)S(1)}, bf16[32,2688]{1,0:T(8,128)(2,1)S(1)}, u32[]{:S(2)}, u32[]{:S(2)}) collective-permute-start(bf16[32,2688]{1,0:T(8,128)(2,1)S(1)} %shard_map.116.mine_ref), channel_id=1, source_target_pairs={{0,8},{4,12},{8,0},{12,4},{1,9},{5,13},{9,1},{13,5},{2,10},{6,14},... | collective-permute-start | bytes 516104 | tf_op jit(solution)/shard_map/ppermute | solution.py:216
  38.1 7.4 %collective-permute-done.10.other_ref = bf16[32,2688]{1,0:T(8,128)(2,1)S(1)} collective-permute-done((bf16[32,2688]{1,0:T(8,128)(2,1)S(1)}, bf16[32,2688]{1,0:T(8,128)(2,1)S(1)}, u32[]{:S(2)}, u32[]{:S(2)}) %collective-permute-start.10) | collective-permute-done | bytes 172064 | tf_op jit(solution)/shard_map/ppermute | solution.py:216
  45.5 0.7 %shard_map.117 = (f32[32,2048]{1,0:T(8,128)}, f32[16,1024]{1,0:T(8,128)}, f32[16,128]{1,0:T(8,128)}) custom-call(bf16[32,2688]{1,0:T(8,128)(2,1)S(1)} %shard_map.116.mine_ref, bf16[32,2688]{1,0:T(8,128)(2,1)S(1)} %collective-permute-done.10.other_ref), custom_call_target="tpu_custom_call" | custom-call | flops 1 | bytes 1 | tf_op jit(solution)/shard_map/pallas_call | solution.py:321
  (36 shorter events, 0.1 us)
Async XLA Ops:
  0.6 2.6 %copy-start.1 = (bf16[128,2048]{1,0:T(8,128)(2,1)S(1)}, bf16[128,2048]{1,0:T(8,128)(2,1)}, u32[]{:S(2)}) copy-start(bf16[128,2048]{1,0:T(8,128)(2,1)} %x_ref) | copy-start | bytes 1572868
  2.7 3.2 %collective-permute-start = (f32[32,128]{1,0:T(8,128)}, f32[32,128]{1,0:T(8,128)S(1)}, u32[]{:S(2)}, u32[]{:S(2)}) collective-permute-start(f32[32,128]{1,0:T(8,128)} %shard_map.112), channel_id=1, source_target_pairs={{0,1},{1,0},{2,3},{3,2},{4,5},{5,4},{6,7},{7,6},{8,9},{9,8},{10,11... | collective-permute-start | bytes 49160 | tf_op jit(solution)/shard_map/ppermute | solution.py:216
  3.2 23.5 %collective-permute-start.4 = (bf16[128,2048]{1,0:T(8,128)(2,1)S(1)}, bf16[128,2048]{1,0:T(8,128)(2,1)S(1)}, u32[]{:S(2)}, u32[]{:S(2)}) collective-permute-start(bf16[128,2048]{1,0:T(8,128)(2,1)S(1)} %copy-done.1), channel_id=1, source_target_pairs={{0,4},{4,0},{8,12},{12,8},{1,5},{5,1},{9,13},{13,9},{2,6},{6,2},{1... | collective-permute-start | bytes 1572872 | tf_op jit(solution)/shard_map/ppermute | solution.py:216
  6.6 3.7 %collective-permute-start.1 = (f32[32,128]{1,0:T(8,128)S(1)}, f32[32,128]{1,0:T(8,128)S(1)}, u32[]{:S(2)}, u32[]{:S(2)}) collective-permute-start(f32[32,128]{1,0:T(8,128)S(1)} %add.39), channel_id=1, source_target_pairs={{0,2},{1,3},{2,0},{3,1},{4,6},{5,7},{6,4},{7,5},{8,10},{9,11},{10,... | collective-permute-start | bytes 49160 | tf_op jit(solution)/shard_map/ppermute | solution.py:216
  8.1 2.3 %slice-start.1 = ((bf16[128,128]{1,0:T(8,128)(2,1)}), bf16[64,128]{1,0:T(8,128)(2,1)S(1)}, s32[]{:S(2)}) async-start(bf16[128,128]{1,0:T(8,128)(2,1)} %v_ref.1), calls=%async_computation.1 | async-start | bytes 32768 | tf_op jit(solution)/shard_map/slice | solution.py:268
  8.1 3.7 %copy-start.5 = (bf16[128,128]{1,0:T(8,128)(2,1)S(1)}, bf16[128,128]{1,0:T(8,128)(2,1)}, u32[]{:S(2)}) copy-start(bf16[128,128]{1,0:T(8,128)(2,1)} %v_ref.1) | copy-start | bytes 98308
  8.5 0.7 %copy-start.7 = (s32[128]{0:T(128)S(1)}, s32[128]{0:T(128)}, u32[]{:S(2)}) copy-start(s32[128]{0:T(128)} %param.14) | copy-start | bytes 1540
  8.5 3.3 %copy-start.4 = (bf16[128,128]{1,0:T(8,128)(2,1)S(1)}, bf16[128,128]{1,0:T(8,128)(2,1)}, u32[]{:S(2)}) copy-start(bf16[128,128]{1,0:T(8,128)(2,1)} %k_ref.1) | copy-start | bytes 98308
  8.5 1.8 %slice-start = ((bf16[128,128]{1,0:T(8,128)(2,1)}), bf16[64,128]{1,0:T(8,128)(2,1)S(1)}, s32[]{:S(2)}) async-start(bf16[128,128]{1,0:T(8,128)(2,1)} %k_ref.1), calls=%async_computation | async-start | bytes 32768 | tf_op jit(solution)/shard_map/slice | solution.py:268
  8.6 3.2 %copy-start.3 = (bf16[16,1024]{1,0:T(8,128)(2,1)S(1)}, bf16[16,1024]{1,0:T(8,128)(2,1)}, u32[]{:S(2)}) copy-start(bf16[16,1024]{1,0:T(8,128)(2,1)} %wq_ref.3) | copy-start | bytes 98308
  9.2 2.6 %copy-start = (bf16[128,1024]{1,0:T(8,128)(2,1)S(1)}, bf16[128,1024]{1,0:T(8,128)(2,1)}, u32[]{:S(2)}) copy-start(bf16[128,1024]{1,0:T(8,128)(2,1)} %o_ref.5) | copy-start | bytes 786436
  9.2 2.6 %copy-start.2 = (bf16[128,1024]{1,0:T(8,128)(2,1)S(1)}, bf16[128,1024]{1,0:T(8,128)(2,1)}, u32[]{:S(2)}) copy-start(bf16[128,1024]{1,0:T(8,128)(2,1)} %q_ref.1) | copy-start | bytes 786436
  10.4 11.1 %collective-permute-start.2 = (bf16[160,128]{1,0:T(8,128)(2,1)S(1)}, bf16[160,128]{1,0:T(8,128)(2,1)S(1)}, u32[]{:S(2)}, u32[]{:S(2)}) collective-permute-start(bf16[160,128]{1,0:T(8,128)(2,1)S(1)} %pad_maximum_fusion), channel_id=1, source_target_pairs={{0,4},{4,8},{8,12},{12,0},{1,5},{5,9},{9,13},{13,1},{2,6},{6,10},{... | collective-permute-start | bytes 122888 | tf_op jit(solution)/shard_map/ppermute | solution.py:220
  11.8 0.7 %copy-start.6 = (bf16[16,128]{1,0:T(8,128)(2,1)S(1)}, bf16[16,128]{1,0:T(8,128)(2,1)}, u32[]{:S(2)}) copy-start(bf16[16,128]{1,0:T(8,128)(2,1)} %wv_ref.5) | copy-start | bytes 12292
  22.8 3.9 %collective-permute-start.3 = (f32[16,128]{1,0:T(8,128)S(1)}, f32[16,128]{1,0:T(8,128)S(1)}, u32[]{:S(2)}, u32[]{:S(2)}) collective-permute-start(f32[16,128]{1,0:T(8,128)S(1)} %bitcast.10), channel_id=1, source_target_pairs={{0,12},{4,0},{8,4},{12,8},{1,13},{5,1},{9,5},{13,9},{2,14},{6,2},{... | collective-permute-start | bytes 24584 | tf_op jit(solution)/shard_map/ppermute | solution.py:220
  26.7 1.2 %collective-permute-start.5 = (f32[32,128]{1,0:T(8,128)S(1)}, f32[32,128]{1,0:T(8,128)S(1)}, u32[]{:S(2)}, u32[]{:S(2)}) collective-permute-start(f32[32,128]{1,0:T(8,128)S(1)} %pad_maximum_fusion.1), channel_id=1, source_target_pairs={{0,1},{1,0},{2,3},{3,2},{4,5},{5,4},{6,7},{7,6},{8,9},{9,8},{10,11... | collective-permute-start | bytes 49160 | tf_op jit(solution)/shard_map/ppermute | solution.py:216
  28.0 3.9 %collective-permute-start.6 = (f32[32,128]{1,0:T(8,128)S(1)}, f32[32,128]{1,0:T(8,128)S(1)}, u32[]{:S(2)}, u32[]{:S(2)}) collective-permute-start(f32[32,128]{1,0:T(8,128)S(1)} %add.46), channel_id=1, source_target_pairs={{0,2},{1,3},{2,0},{3,1},{4,6},{5,7},{6,4},{7,5},{8,10},{9,11},{10,... | collective-permute-start | bytes 49160 | tf_op jit(solution)/shard_map/ppermute | solution.py:216
  29.5 6.7 %collective-permute-start.9 = (bf16[16,1152]{1,0:T(8,128)(2,1)S(1)}, bf16[16,1152]{1,0:T(8,128)(2,1)S(1)}, u32[]{:S(2)}, u32[]{:S(2)}) collective-permute-start(bf16[16,1152]{1,0:T(8,128)(2,1)S(1)} %get-tuple-element.35.up_ref), channel_id=1, source_target_pairs={{0,4},{4,0},{8,12},{12,8},{1,5},{5,1},{9,13},{13,9},{2,6},{6,2},{1... | collective-permute-start | bytes 110600 | tf_op jit(solution)/shard_map/ppermute | solution.py:216
  29.9 3.9 %collective-permute-start.7 = (f32[32,128]{1,0:T(8,128)S(1)}, f32[32,128]{1,0:T(8,128)S(1)}, u32[]{:S(2)}, u32[]{:S(2)}) collective-permute-start(f32[32,128]{1,0:T(8,128)S(1)} %add.46), channel_id=1, source_target_pairs={{0,4},{4,0},{8,12},{12,8},{1,5},{5,1},{9,13},{13,9},{2,6},{6,2},{1... | collective-permute-start | bytes 49160 | tf_op jit(solution)/shard_map/ppermute | solution.py:216
  31.5 4.6 %collective-permute-start.8 = (f32[32,128]{1,0:T(8,128)S(1)}, f32[32,128]{1,0:T(8,128)S(1)}, u32[]{:S(2)}, u32[]{:S(2)}) collective-permute-start(f32[32,128]{1,0:T(8,128)S(1)} %add.46), channel_id=1, source_target_pairs={{0,6},{1,7},{2,4},{3,5},{4,2},{5,3},{6,0},{7,1},{8,14},{9,15},{10,... | collective-permute-start | bytes 49160 | tf_op jit(solution)/shard_map/ppermute | solution.py:228
  36.4 9.1 %collective-permute-start.10 = (bf16[32,2688]{1,0:T(8,128)(2,1)S(1)}, bf16[32,2688]{1,0:T(8,128)(2,1)S(1)}, u32[]{:S(2)}, u32[]{:S(2)}) collective-permute-start(bf16[32,2688]{1,0:T(8,128)(2,1)S(1)} %shard_map.116.mine_ref), channel_id=1, source_target_pairs={{0,8},{4,12},{8,0},{12,4},{1,9},{5,13},{9,1},{13,5},{2,10},{6,14},... | collective-permute-start | bytes 516104 | tf_op jit(solution)/shard_map/ppermute | solution.py:216

commit v3 on v2

--- a/solution.py
+++ b/solution.py
@@ -19,7 +19,7 @@
 BF16 = jnp.bfloat16
 EXACT = lax.Precision.HIGHEST
 LIMIT = 40 * 1024 * 1024
-FULL = 63 * 1024 * 1024
+FULL = 55168 * 1024
 
 
 def dot(left, right, left_dim, right_dim, precision=None):
@@ -44,10 +44,8 @@
 
 
 def lowrank_kernel(x_hbm, a_hbm, part_ref, x_ref, a_ref, sems):
-    copies = [
-        pltpu.make_async_copy(x_hbm, x_ref, sems.at[0]),
-        pltpu.make_async_copy(a_hbm, a_ref, sems.at[1]),
-    ]
+    pairs = [(x_hbm, x_ref), (a_hbm, a_ref)]
+    copies = [pltpu.make_async_copy(src, dst, sems.at[i]) for i, (src, dst) in enumerate(pairs)]
     for copy in copies:
         copy.start()
     for copy in copies:
@@ -70,16 +68,18 @@
 def project_kernel(
     heads,
     low_ref, q_ref, k_ref, v_ref, o_ref, seg_ref, cos_ref, sin_ref, wq_ref, wv_ref,
-    qr_ref, kt_ref, s_ref, dp_ref, bias_ref,
+    qr_ref, kt_ref, s_ref, dp_ref, cost_ref, sint_ref, bias_ref,
 ):
     tok = q_ref.shape[0]
     low = low_ref[...].astype(BF16)
+    cost_ref[...] = cos_ref[...].T
+    sint_ref[...] = sin_ref[...].T
     cos, sin = wide_tables(cos_ref[...], sin_ref[...])
     keys = rotate_rows(k_ref[...].astype(F32), cos, sin)
     kt_ref[...] = keys.T.astype(BF16)
     keys = keys.astype(BF16)
     vals = (v_ref[...].astype(F32) + SCALE * dot(low[RANK:], wv_ref[...], 0, 0)).astype(BF16)
-    seg_here = seg_ref[...].astype(F32)
+    seg_here = seg_ref[...].astype(F32)[0:1]
     key = lax.broadcasted_iota(jnp.int32, (tok, tok), 0)
     query = lax.broadcasted_iota(jnp.int32, (tok, tok), 1)
     allowed = (key <= query) & (column(seg_here, tok) == seg_here)
@@ -105,7 +105,7 @@
     keys = rotate_rows(keys.astype(F32), cos, sin)
     kt_ref[...] = keys.T.astype(BF16)
     keys_ref[...] = keys.astype(BF16)
-    seg_here = seg_ref[...].astype(F32)
+    seg_here = seg_ref[...].astype(F32)[0:1]
     cols = []
     for b in range(blocks):
         row = pack_ref[b, 2 * send + RANK :].astype(F32)[0:1]
@@ -176,11 +176,10 @@
     part_ref[...] = dot(dl_ref[...], x_ref[...], 1, 0)
 
 
-def pair_kernel(split, dl_ref, dlp_ref, x_ref, xp_ref, up_ref, upp_ref, send_ref):
+def partial_kernel(split, dl_ref, x_ref, up_ref, send_ref):
     rows, wide = dl_ref.shape[0], x_ref.shape[1]
-    part = dot(dl_ref[...], x_ref[...], 1, 0) + dot(dlp_ref[...], xp_ref[...], 1, 0)
-    send_ref[:, :wide] = part.astype(BF16)
-    up = (up_ref[...].astype(F32) + upp_ref[...].astype(F32)).astype(BF16)
+    send_ref[:, :wide] = dot(dl_ref[...], x_ref[...], 1, 0).astype(BF16)
+    up = up_ref[...]
     size = up.shape[1]
     send_ref[0:RANK, wide:] = up[:, :split]
     send_ref[RANK:rows, wide : wide + size - split] = up[:, split:]
@@ -188,9 +187,11 @@
         send_ref[RANK:rows, wide + size - split :] = jnp.zeros((rows - RANK, 2 * split - size), BF16)
 
 
-def final_kernel(split, mine_ref, other_ref, down_ref, upq_ref, upv_ref):
+def final_kernel(split, mine_ref, one_ref, two_ref, three_ref, down_ref, upq_ref, upv_ref):
     wide = down_ref.shape[1]
-    total = mine_ref[...].astype(F32) + other_ref[...].astype(F32)
+    near = mine_ref[...].astype(F32) + one_ref[...].astype(F32)
+    far = two_ref[...].astype(F32) + three_ref[...].astype(F32)
+    total = near + far
     down_ref[...] = total[:, :wide]
     size = upq_ref.shape[1]
     upq_ref[:, :split] = total[:RANK, wide:]
@@ -209,7 +210,7 @@
     send = longest if blocks == 1 else tok
     halo = blocks * send
     keys = halo + tok
-    paired = seq_count == 4 and fsdp_count == 4
+    direct = seq_count == 4
 
     def swap(array, axis, bit):
         size = lax.axis_size(axis)
@@ -218,14 +219,6 @@
     def shift(array, by):
         moves = [(i, (i + by) % seq_count) for i in range(seq_count)]
         return lax.ppermute(array, "seq", moves)
-
-    def cross(array):
-        moves = [
-            (s * fsdp_count + f, (s ^ 1) * fsdp_count + (f ^ 2))
-            for s in range(seq_count)
-            for f in range(fsdp_count)
-        ]
-        return lax.ppermute(array, ("seq", "fsdp"), moves)
 
     def sum_fsdp(array):
         if fsdp_count & (fsdp_count - 1):
@@ -237,7 +230,6 @@
         return array
 
     seg_row = segment.reshape(1, tok)
-    hbm = pl.BlockSpec(memory_space=pltpu.HBM)
     (part,) = call(
         lowrank_kernel,
         [((2 * RANK, tok), F32)],
@@ -247,37 +239,32 @@
             pltpu.SemaphoreType.DMA((2,)),
         ],
         limit=FULL,
-        in_specs=[hbm, hbm],
+        in_specs=[pl.BlockSpec(memory_space=pltpu.HBM)] * 2,
     )(x, a.T)
-    if paired:
-        part, x = lax.optimization_barrier((part, x))
-        x_pair = swap(x, "seq", 1)
+    seg_rows = jnp.broadcast_to(seg_row, (16, tok)).astype(BF16)
     start = seq_index * tok
     base = start.reshape(1).astype(jnp.int32)
     freqs = ROPE_BASE ** (-(2.0 * jnp.arange(HALF, dtype=F32)) / HEAD)
     positions = (start - halo + jnp.arange(keys, dtype=jnp.int32)).astype(F32)
     angles = positions[:, None] * freqs[None, :]
     cos, sin = jnp.cos(angles), jnp.sin(angles)
-    here = (start + jnp.arange(tok, dtype=jnp.int32)).astype(F32)
-    angles_t = freqs[:, None] * here[None, :]
-    cos_t, sin_t = jnp.cos(angles_t), jnp.sin(angles_t)
-
     low = sum_fsdp(part)
-    seg_rows = jnp.broadcast_to(seg_row, (16, tok)).astype(BF16)
     pack = jnp.concatenate(
         [k[tok - send :], v[tok - send :], low[RANK:].astype(BF16), seg_rows], axis=0
     )
     packs = jnp.stack([shift(pack, d) for d in range(blocks, 0, -1)])
-    qr, kt, s, dp = call(
+    qr, kt, s, dp, cos_t, sin_t = call(
         functools.partial(project_kernel, heads),
         [
             ((heads, tok, HEAD), BF16),
             ((HEAD, tok), BF16),
             ((heads, tok, tok), F32),
             ((heads, tok, tok), F32),
+            ((HALF, tok), F32),
+            ((HALF, tok), F32),
         ],
         [pltpu.VMEM((tok, tok), F32)],
-    )(low, q, k, v, o, seg_row, cos[halo:], sin[halo:], wq, wv)
+    )(low, q, k, v, o, seg_rows, cos[halo:], sin[halo:], wq, wv)
     specs = [pl.BlockSpec(memory_space=pltpu.VMEM)] * 9
     specs[5] = pl.BlockSpec(memory_space=pltpu.SMEM)
     w, kt_far, dv, code_v, back = call(
@@ -291,37 +278,31 @@
         ],
         [pltpu.VMEM((halo, tok), F32), pltpu.VMEM((halo, HEAD), BF16)],
         in_specs=specs,
-    )(qr, s, o, seg_row, packs, base, cos[:halo], sin[:halo], wv)
+    )(qr, s, o, seg_rows, packs, base, cos[:halo], sin[:halo], wv)
     for b, d in enumerate(range(blocks, 0, -1)):
         code_v = code_v + shift(back[b], -d)
     code_q, up = call(
         functools.partial(grads_kernel, send, blocks, heads),
-        [((RANK, tok), F32), ((RANK, (heads + 1) * HEAD), BF16 if paired else F32)],
+        [((RANK, tok), F32), ((RANK, (heads + 1) * HEAD), BF16 if direct else F32)],
         [pltpu.VMEM((halo, HEAD), BF16), pltpu.VMEM((heads * HEAD, tok), BF16)],
         cost=6 << 20,
     )(low, packs, o, w, dp, kt, kt_far, dv, cos_t, sin_t, wq, wv)
     codes = jnp.concatenate([code_q, code_v], axis=0)
 
-    if not paired:
-        dlow = sum_fsdp(codes).astype(BF16)
+    dlow = sum_fsdp(codes).astype(BF16)
+    if not direct:
         (down,) = call(down_kernel, [((2 * RANK, wide), F32)])(dlow, x)
         down, up = lax.psum((down, up), "seq")
         return down.T, up[:, : heads * HEAD], up[:, heads * HEAD :]
 
-    up_pair = swap(up, "seq", 1)
-    codes, x_pair = lax.optimization_barrier((codes, x_pair))
-    codes = codes + swap(codes, "fsdp", 1)
-    dlow = (codes + swap(codes, "fsdp", 2)).astype(BF16)
-    dlow_pair = (swap(codes, "seq", 1) + cross(codes)).astype(BF16)
     split = -(-(heads + 1) // 2) * HEAD
-    (mine,) = call(functools.partial(pair_kernel, split), [((2 * RANK, wide + split), BF16)])(
-        dlow, dlow_pair, x, x_pair, up, up_pair
-    )
-    other = swap(mine, "seq", 2)
+    (mine,) = call(functools.partial(partial_kernel, split), [((2 * RANK, wide + split), BF16)])(
+        dlow, x, up
+    )
     down, up_q, up_v = call(
         functools.partial(final_kernel, split),
         [((2 * RANK, wide), F32), ((RANK, heads * HEAD), F32), ((RANK, HEAD), F32)],
-    )(mine, other)
+    )(mine, *[swap(mine, "seq", bit) for bit in (1, 2, 3)])
     return down.T, up_q, up_v
 
 

time: 46.5 us -> 42.6 us (0.916)
  waiting for transfers between devices: 22.2 us -> 19.5 us
  other arithmetic: 1.41 us -> 0.48 us
  Pallas kernels: 7.17 us -> 6.48 us
    ppermute x2, waiting for transfers between devices: 8.28 us -> 2.04 us  [shift(): return lax.ppermute(array, 'seq', moves)]
    ppermute x8 -> x7, waiting for transfers between devices: 11.6 us -> 17.5 us  [swap(): return lax.ppermute(array, axis, [(i, i ^ bit) for i in range(size)])]
    ppermute x1 -> x0, waiting for transfers between devices: 2.35 us -> none  [cross(): return lax.ppermute(array, ('seq', 'fsdp'), moves)]
    ppermute x2, starting transfers between devices: 2.91 us -> 4.19 us  [shift(): return lax.ppermute(array, 'seq', moves)]
    add x2 -> x3, other arithmetic: 0.73 us -> 0.01 us  [sum_fsdp(): array = array + swap(array, 'fsdp', bit)]
    slice x2, local copies, waits for them, and re-layouts: 0.01 us -> 0.69 us  [body(): k[tok - send:]]
    pallas_call x1, Pallas kernels: 2.03 us -> 1.37 us  [body(): call(lowrank_kernel, [((2 * RANK, tok), F32)], [pltpu.VMEM((tok, wide), B...]
    ppermute x8 -> x7, starting transfers between devices: 9.99 us -> 9.37 us  [swap(): return lax.ppermute(array, axis, [(i, i ^ bit) for i in range(size)])]
  transfers between devices with their start and end apart: 11 -> 9, of which waited for: 6 -> 7; matrix products, arithmetic and copies ran while one was open for 3% -> 1% of each run, Pallas kernels for 9% -> 7%
where the time goes in v3:
time: 42.6 us; the launch traced here: 42.3 us
  waiting for transfers between devices  19.5 us (46%)
  starting transfers between devices  13.6 us (32%)
  Pallas kernels  6.48 us (15%)
  local copies, waits for them, and re-layouts  1.47 us (3%)
  between operations  0.82 us (2%)
  other arithmetic  0.48 us (1%)
    ppermute x7, waiting for transfers between devices, swap(): return lax.ppermute(array, axis, [(i, i ^ bit) for i in range(size)])  17.5 us
    ppermute x7, starting transfers between devices, swap(): return lax.ppermute(array, axis, [(i, i ^ bit) for i in range(size)])  9.37 us
    ppermute x2, starting transfers between devices, shift(): return lax.ppermute(array, 'seq', moves)  4.19 us
    pallas_call x1, Pallas kernels, body(): call(functools.partial(grads_kernel, send, blocks, heads), [((RANK, tok),...  2.11 us
    ppermute x2, waiting for transfers between devices, shift(): return lax.ppermute(array, 'seq', moves)  2.04 us
    pallas_call x1, Pallas kernels, body(): call(lowrank_kernel, [((2 * RANK, tok), F32)], [pltpu.VMEM((tok, wide), B...  1.37 us
    pallas_call x1, Pallas kernels, body(): call(functools.partial(softmax_kernel, send, blocks, heads), [((heads, ke...  1.31 us
  transfers between devices with their start and end apart: 9, of which 7 were waited for; matrix products, arithmetic and copies ran while one was open for 1% of the time, Pallas kernels for 7%

profile of v3, /device:TPU:0, one launch (start us, length us, event | category | flops | bytes accessed | tf_op | source)
XLA Modules:
  0.0 42.3 jit_solution(17688206068574522635)
XLA Ops:
  0.6 1.4 %shard_map.112 = f32[32,128]{1,0:T(8,128)S(1)} custom-call(bf16[128,2048]{1,0:T(8,128)(2,1)} %x_ref.1, bf16[32,2048]{1,0:T(8,128)(2,1)} %bitcast.8), custom_call_target="tpu_custom_call" | custom-call | flops 1 | bytes 1 | tf_op jit(solution)/shard_map/pallas_call | solution.py:233
  2.0 0.5 %collective-permute-start = (f32[32,128]{1,0:T(8,128)S(1)}, f32[32,128]{1,0:T(8,128)S(1)}, u32[]{:S(2)}, u32[]{:S(2)}) collective-permute-start(f32[32,128]{1,0:T(8,128)S(1)} %shard_map.112), channel_id=1, source_target_pairs={{0,1},{1,0},{2,3},{3,2},{4,5},{5,4},{6,7},{7,6},{8,9},{9,8},{10,11... | collective-permute-start | bytes 49160 | tf_op jit(solution)/shard_map/ppermute | solution.py:217
  2.5 0.8 %collective-permute-done = f32[32,128]{1,0:T(8,128)S(1)} collective-permute-done((f32[32,128]{1,0:T(8,128)S(1)}, f32[32,128]{1,0:T(8,128)S(1)}, u32[]{:S(2)}, u32[]{:S(2)}) %collective-permute-start) | collective-permute-done | bytes 16416 | tf_op jit(solution)/shard_map/ppermute | solution.py:217
  3.4 2.8 %collective-permute-start.1 = (f32[32,128]{1,0:T(8,128)S(1)}, f32[32,128]{1,0:T(8,128)S(1)}, u32[]{:S(2)}, u32[]{:S(2)}) collective-permute-start(f32[32,128]{1,0:T(8,128)S(1)} %add.26), channel_id=1, source_target_pairs={{0,2},{1,3},{2,0},{3,1},{4,6},{5,7},{6,4},{7,5},{8,10},{9,11},{10,... | collective-permute-start | bytes 49160 | tf_op jit(solution)/shard_map/ppermute | solution.py:217
  6.2 1.7 %collective-permute-done.1 = f32[32,128]{1,0:T(8,128)S(1)} collective-permute-done((f32[32,128]{1,0:T(8,128)S(1)}, f32[32,128]{1,0:T(8,128)S(1)}, u32[]{:S(2)}, u32[]{:S(2)}) %collective-permute-start.1) | collective-permute-done | bytes 16416 | tf_op jit(solution)/shard_map/ppermute | solution.py:217
  8.0 0.7 %slice-done = bf16[64,128]{1,0:T(8,128)(2,1)S(1)} async-done(((bf16[128,128]{1,0:T(8,128)(2,1)}), bf16[64,128]{1,0:T(8,128)(2,1)S(1)}, s32[]{:S(2)}) %slice-start) | async-done | bytes 16408 | tf_op jit(solution)/shard_map/slice | solution.py:253
  8.6 0.0 slice-done.1
  8.7 0.0 copy-start.2
  8.7 2.2 %collective-permute-start.2 = (bf16[160,128]{1,0:T(8,128)(2,1)S(1)}, bf16[160,128]{1,0:T(8,128)(2,1)S(1)}, u32[]{:S(2)}, u32[]{:S(2)}) collective-permute-start(bf16[160,128]{1,0:T(8,128)(2,1)S(1)} %pad_maximum_fusion), channel_id=1, source_target_pairs={{0,4},{4,8},{8,12},{12,0},{1,5},{5,9},{9,13},{13,1},{2,6},{6,10},{... | collective-permute-start | bytes 122888 | tf_op jit(solution)/shard_map/ppermute | solution.py:221
  10.8 0.4 multiply_sine_fusion
  11.3 0.0 copy-start.3
  11.3 0.0 copy-start.4
  11.3 0.0 copy-start.6
  11.4 0.7 %copy-done.3 = bf16[16,1024]{1,0:T(8,128)(2,1)S(1)} copy-done((bf16[16,1024]{1,0:T(8,128)(2,1)S(1)}, bf16[16,1024]{1,0:T(8,128)(2,1)}, u32[]{:S(2)}) %copy-start.3) | copy-done | bytes 32792
  12.1 0.0 copy-done.4
  12.1 0.7 %shard_map.113 = (bf16[8,128,128]{2,1,0:T(8,128)(2,1)S(1)}, bf16[128,128]{1,0:T(8,128)(2,1)S(1)}, f32[8,128,128]{2,1,0:T(8,128)S(1)}, f32[8,128,128]{2,1,0:T(8,1...) custom-call(f32[32,128]{1,0:T(8,128)S(1)} %add.27.low_ref, bf16[128,1024]{1,0:T(8,128)(2,1)S(1)} %copy-done.2, ...), custom_call_target="tpu_custom_call" | custom-call | flops 1 | bytes 1 | tf_op jit(solution)/shard_map/pallas_call | solution.py:256
  12.8 2.0 %collective-permute-done.2 = bf16[160,128]{1,0:T(8,128)(2,1)S(1)} collective-permute-done((bf16[160,128]{1,0:T(8,128)(2,1)S(1)}, bf16[160,128]{1,0:T(8,128)(2,1)S(1)}, u32[]{:S(2)}, u32[]{:S(2)}) %collective-permute-start.2) | collective-permute-done | bytes 40992 | tf_op jit(solution)/shard_map/ppermute | solution.py:221
  14.8 1.3 %shard_map.114 = (f32[8,192,128]{2,1,0:T(8,128)S(1)}, bf16[128,64]{1,0:T(8,128)(2,1)S(1)}, f32[192,128]{1,0:T(8,128)S(1)}, f32[16,128]{1,0:T(8,128)S(1)}, f32[1,16,128]{2,1,0:T(8,128)S(1)}) custom-call(bf16[8,128,128]{2,1,0:T(8,128)(2,1)S(1)} %get-tuple-element.19.qr_ref, f32[8,128,128]{2,1,0:T(8,128)S(1)} %get-tuple-element.20.s_ref, ...), custom_call_target="tpu_custom_call" | custom-call | flops 1 | bytes 1 | tf_op jit(solution)/shard_map/pallas_call | solution.py:270
  16.2 2.0 %collective-permute-start.3 = (f32[16,128]{1,0:T(8,128)S(1)}, f32[16,128]{1,0:T(8,128)S(1)}, u32[]{:S(2)}, u32[]{:S(2)}) collective-permute-start(f32[16,128]{1,0:T(8,128)S(1)} %bitcast.7), channel_id=1, source_target_pairs={{0,12},{4,0},{8,4},{12,8},{1,13},{5,1},{9,5},{13,9},{2,14},{6,2},{... | collective-permute-start | bytes 24584 | tf_op jit(solution)/shard_map/ppermute | solution.py:221
  18.2 2.1 %shard_map.115 = (f32[16,128]{1,0:T(8,128)S(1)}, bf16[16,1152]{1,0:T(8,128)(2,1)S(1)}) custom-call(f32[32,128]{1,0:T(8,128)S(1)} %add.27.low_ref, bf16[1,160,128]{2,1,0:T(8,128)(2,1)S(1)} %bitcast.6, bf16[128,1024]{1,0:T(8,128)(2,1)S(1)} %copy-done, f32[8,192,128]{2,1,0:T(8,128)S(1)} %get-tuple-element.21.w_ref, ...), custom_call_target="tpu_custom_call" | custom-call | flops 6291456 | bytes 6291456 | tf_op jit(solution)/shard_map/pallas_call | solution.py:284
  20.3 0.0 collective-permute-done.3
  20.3 0.1 collective-permute-start.4
  20.4 1.2 %collective-permute-done.4 = f32[32,128]{1,0:T(8,128)S(1)} collective-permute-done((f32[32,128]{1,0:T(8,128)S(1)}, f32[32,128]{1,0:T(8,128)S(1)}, u32[]{:S(2)}, u32[]{:S(2)}) %collective-permute-start.4) | collective-permute-done | bytes 16416 | tf_op jit(solution)/shard_map/ppermute | solution.py:217
  21.6 1.5 %collective-permute-start.5 = (f32[32,128]{1,0:T(8,128)S(1)}, f32[32,128]{1,0:T(8,128)S(1)}, u32[]{:S(2)}, u32[]{:S(2)}) collective-permute-start(f32[32,128]{1,0:T(8,128)S(1)} %fusion), channel_id=1, source_target_pairs={{0,2},{1,3},{2,0},{3,1},{4,6},{5,7},{6,4},{7,5},{8,10},{9,11},{10,... | collective-permute-start | bytes 49160 | tf_op jit(solution)/shard_map/ppermute | solution.py:217
  23.1 2.2 %collective-permute-done.5 = f32[32,128]{1,0:T(8,128)S(1)} collective-permute-done((f32[32,128]{1,0:T(8,128)S(1)}, f32[32,128]{1,0:T(8,128)S(1)}, u32[]{:S(2)}, u32[]{:S(2)}) %collective-permute-start.5) | collective-permute-done | bytes 16416 | tf_op jit(solution)/shard_map/ppermute | solution.py:217
  25.3 0.2 shard_map.116.mine_ref
  25.5 3.3 %collective-permute-start.8 = (bf16[32,2688]{1,0:T(8,128)(2,1)S(1)}, bf16[32,2688]{1,0:T(8,128)(2,1)S(1)}, u32[]{:S(2)}, u32[]{:S(2)}) collective-permute-start(bf16[32,2688]{1,0:T(8,128)(2,1)S(1)} %shard_map.116.mine_ref), channel_id=1, source_target_pairs={{0,12},{4,8},{8,4},{12,0},{1,13},{5,9},{9,5},{13,1},{2,14},{6,10},... | collective-permute-start | bytes 516104 | tf_op jit(solution)/shard_map/ppermute | solution.py:217
  28.8 0.0 collective-permute-start.7
  28.8 1.2 %collective-permute-start.6 = (bf16[32,2688]{1,0:T(8,128)(2,1)S(1)}, bf16[32,2688]{1,0:T(8,128)(2,1)S(1)}, u32[]{:S(2)}, u32[]{:S(2)}) collective-permute-start(bf16[32,2688]{1,0:T(8,128)(2,1)S(1)} %shard_map.116.mine_ref), channel_id=1, source_target_pairs={{0,4},{4,0},{8,12},{12,8},{1,5},{5,1},{9,13},{13,9},{2,6},{6,2},{1... | collective-permute-start | bytes 516104 | tf_op jit(solution)/shard_map/ppermute | solution.py:217
  30.0 4.7 %collective-permute-done.8.three_ref = bf16[32,2688]{1,0:T(8,128)(2,1)S(1)} collective-permute-done((bf16[32,2688]{1,0:T(8,128)(2,1)S(1)}, bf16[32,2688]{1,0:T(8,128)(2,1)S(1)}, u32[]{:S(2)}, u32[]{:S(2)}) %collective-permute-start.8) | collective-permute-done | bytes 172064 | tf_op jit(solution)/shard_map/ppermute | solution.py:217
  34.7 6.8 %collective-permute-done.7.two_ref = bf16[32,2688]{1,0:T(8,128)(2,1)S(1)} collective-permute-done((bf16[32,2688]{1,0:T(8,128)(2,1)S(1)}, bf16[32,2688]{1,0:T(8,128)(2,1)S(1)}, u32[]{:S(2)}, u32[]{:S(2)}) %collective-permute-start.7) | collective-permute-done | bytes 172064 | tf_op jit(solution)/shard_map/ppermute | solution.py:217
  41.5 0.8 %shard_map.117 = (f32[32,2048]{1,0:T(8,128)}, f32[16,1024]{1,0:T(8,128)}, f32[16,128]{1,0:T(8,128)}) custom-call(bf16[32,2688]{1,0:T(8,128)(2,1)S(1)} %shard_map.116.mine_ref, bf16[32,2688]{1,0:T(8,128)(2,1)S(1)} %collective-permute-done.6.one_ref, bf16[32,2688]{1,0:T(8,128)(2,1)S(1)} %collective-permute-done.7.two_ref, ...), custom_call_target="tpu_custom_call" | custom-call | flops 1 | bytes 1 | tf_op jit(solution)/shard_map/pallas_call | solution.py:302
  (29 shorter events, 0.1 us)
Async XLA Ops:
  2.0 1.4 %collective-permute-start = (f32[32,128]{1,0:T(8,128)S(1)}, f32[32,128]{1,0:T(8,128)S(1)}, u32[]{:S(2)}, u32[]{:S(2)}) collective-permute-start(f32[32,128]{1,0:T(8,128)S(1)} %shard_map.112), channel_id=1, source_target_pairs={{0,1},{1,0},{2,3},{3,2},{4,5},{5,4},{6,7},{7,6},{8,9},{9,8},{10,11... | collective-permute-start | bytes 49160 | tf_op jit(solution)/shard_map/ppermute | solution.py:217
  3.4 2.8 %copy-start.7 = (s32[128]{0:T(128)S(1)}, s32[128]{0:T(128)}, u32[]{:S(2)}) copy-start(s32[128]{0:T(128)} %param.14) | copy-start | bytes 1540
  3.4 4.5 %collective-permute-start.1 = (f32[32,128]{1,0:T(8,128)S(1)}, f32[32,128]{1,0:T(8,128)S(1)}, u32[]{:S(2)}, u32[]{:S(2)}) collective-permute-start(f32[32,128]{1,0:T(8,128)S(1)} %add.26), channel_id=1, source_target_pairs={{0,2},{1,3},{2,0},{3,1},{4,6},{5,7},{6,4},{7,5},{8,10},{9,11},{10,... | collective-permute-start | bytes 49160 | tf_op jit(solution)/shard_map/ppermute | solution.py:217
  7.9 0.7 %slice-start = ((bf16[128,128]{1,0:T(8,128)(2,1)}), bf16[64,128]{1,0:T(8,128)(2,1)S(1)}, s32[]{:S(2)}) async-start(bf16[128,128]{1,0:T(8,128)(2,1)} %k_ref.1), calls=%async_computation | async-start | bytes 32768 | tf_op jit(solution)/shard_map/slice | solution.py:253
  7.9 0.7 %slice-start.1 = ((bf16[128,128]{1,0:T(8,128)(2,1)}), bf16[64,128]{1,0:T(8,128)(2,1)S(1)}, s32[]{:S(2)}) async-start(bf16[128,128]{1,0:T(8,128)(2,1)} %v_ref.1), calls=%async_computation.1 | async-start | bytes 32768 | tf_op jit(solution)/shard_map/slice | solution.py:253
  8.7 2.7 %copy-start.5 = (bf16[128,128]{1,0:T(8,128)(2,1)S(1)}, bf16[128,128]{1,0:T(8,128)(2,1)}, u32[]{:S(2)}) copy-start(bf16[128,128]{1,0:T(8,128)(2,1)} %v_ref.1) | copy-start | bytes 98308
  8.7 2.7 %copy-start = (bf16[128,1024]{1,0:T(8,128)(2,1)S(1)}, bf16[128,1024]{1,0:T(8,128)(2,1)}, u32[]{:S(2)}) copy-start(bf16[128,1024]{1,0:T(8,128)(2,1)} %o_ref.5) | copy-start | bytes 786436
  8.7 2.7 %copy-start.2 = (bf16[128,1024]{1,0:T(8,128)(2,1)S(1)}, bf16[128,1024]{1,0:T(8,128)(2,1)}, u32[]{:S(2)}) copy-start(bf16[128,1024]{1,0:T(8,128)(2,1)} %q_ref.1) | copy-start | bytes 786436
  8.7 6.2 %collective-permute-start.2 = (bf16[160,128]{1,0:T(8,128)(2,1)S(1)}, bf16[160,128]{1,0:T(8,128)(2,1)S(1)}, u32[]{:S(2)}, u32[]{:S(2)}) collective-permute-start(bf16[160,128]{1,0:T(8,128)(2,1)S(1)} %pad_maximum_fusion), channel_id=1, source_target_pairs={{0,4},{4,8},{8,12},{12,0},{1,5},{5,9},{9,13},{13,1},{2,6},{6,10},{... | collective-permute-start | bytes 122888 | tf_op jit(solution)/shard_map/ppermute | solution.py:221
  11.3 0.8 %copy-start.3 = (bf16[16,1024]{1,0:T(8,128)(2,1)S(1)}, bf16[16,1024]{1,0:T(8,128)(2,1)}, u32[]{:S(2)}) copy-start(bf16[16,1024]{1,0:T(8,128)(2,1)} %wq_ref.3) | copy-start | bytes 98308
  11.3 0.8 %copy-start.4 = (bf16[128,128]{1,0:T(8,128)(2,1)S(1)}, bf16[128,128]{1,0:T(8,128)(2,1)}, u32[]{:S(2)}) copy-start(bf16[128,128]{1,0:T(8,128)(2,1)} %k_ref.1) | copy-start | bytes 98308
  11.3 0.8 %copy-start.6 = (bf16[16,128]{1,0:T(8,128)(2,1)S(1)}, bf16[16,128]{1,0:T(8,128)(2,1)}, u32[]{:S(2)}) copy-start(bf16[16,128]{1,0:T(8,128)(2,1)} %wv_ref.5) | copy-start | bytes 12292
  16.2 4.1 %collective-permute-start.3 = (f32[16,128]{1,0:T(8,128)S(1)}, f32[16,128]{1,0:T(8,128)S(1)}, u32[]{:S(2)}, u32[]{:S(2)}) collective-permute-start(f32[16,128]{1,0:T(8,128)S(1)} %bitcast.7), channel_id=1, source_target_pairs={{0,12},{4,0},{8,4},{12,8},{1,13},{5,1},{9,5},{13,9},{2,14},{6,2},{... | collective-permute-start | bytes 24584 | tf_op jit(solution)/shard_map/ppermute | solution.py:221
  18.2 7.2 %copy-start.1 = (bf16[128,2048]{1,0:T(8,128)(2,1)S(1)}, bf16[128,2048]{1,0:T(8,128)(2,1)}, u32[]{:S(2)}) copy-start(bf16[128,2048]{1,0:T(8,128)(2,1)} %x_ref.1) | copy-start | bytes 1572868
  20.3 1.2 %collective-permute-start.4 = (f32[32,128]{1,0:T(8,128)S(1)}, f32[32,128]{1,0:T(8,128)S(1)}, u32[]{:S(2)}, u32[]{:S(2)}) collective-permute-start(f32[32,128]{1,0:T(8,128)S(1)} %pad_maximum_fusion.1), channel_id=1, source_target_pairs={{0,1},{1,0},{2,3},{3,2},{4,5},{5,4},{6,7},{7,6},{8,9},{9,8},{10,11... | collective-permute-start | bytes 49160 | tf_op jit(solution)/shard_map/ppermute | solution.py:217
  21.6 3.7 %collective-permute-start.5 = (f32[32,128]{1,0:T(8,128)S(1)}, f32[32,128]{1,0:T(8,128)S(1)}, u32[]{:S(2)}, u32[]{:S(2)}) collective-permute-start(f32[32,128]{1,0:T(8,128)S(1)} %fusion), channel_id=1, source_target_pairs={{0,2},{1,3},{2,0},{3,1},{4,6},{5,7},{6,4},{7,5},{8,10},{9,11},{10,... | collective-permute-start | bytes 49160 | tf_op jit(solution)/shard_map/ppermute | solution.py:217
  25.5 9.2 %collective-permute-start.8 = (bf16[32,2688]{1,0:T(8,128)(2,1)S(1)}, bf16[32,2688]{1,0:T(8,128)(2,1)S(1)}, u32[]{:S(2)}, u32[]{:S(2)}) collective-permute-start(bf16[32,2688]{1,0:T(8,128)(2,1)S(1)} %shard_map.116.mine_ref), channel_id=1, source_target_pairs={{0,12},{4,8},{8,4},{12,0},{1,13},{5,9},{9,5},{13,1},{2,14},{6,10},... | collective-permute-start | bytes 516104 | tf_op jit(solution)/shard_map/ppermute | solution.py:217
  28.8 12.7 %collective-permute-start.7 = (bf16[32,2688]{1,0:T(8,128)(2,1)S(1)}, bf16[32,2688]{1,0:T(8,128)(2,1)S(1)}, u32[]{:S(2)}, u32[]{:S(2)}) collective-permute-start(bf16[32,2688]{1,0:T(8,128)(2,1)S(1)} %shard_map.116.mine_ref), channel_id=1, source_target_pairs={{0,8},{4,12},{8,0},{12,4},{1,9},{5,13},{9,1},{13,5},{2,10},{6,14},... | collective-permute-start | bytes 516104 | tf_op jit(solution)/shard_map/ppermute | solution.py:217
  28.8 12.7 %collective-permute-start.6 = (bf16[32,2688]{1,0:T(8,128)(2,1)S(1)}, bf16[32,2688]{1,0:T(8,128)(2,1)S(1)}, u32[]{:S(2)}, u32[]{:S(2)}) collective-permute-start(bf16[32,2688]{1,0:T(8,128)(2,1)S(1)} %shard_map.116.mine_ref), channel_id=1, source_target_pairs={{0,4},{4,0},{8,12},{12,8},{1,5},{5,1},{9,13},{13,9},{2,6},{6,2},{1... | collective-permute-start | bytes 516104 | tf_op jit(solution)/shard_map/ppermute | solution.py:217

commit v4 on v3

--- a/solution.py
+++ b/solution.py
@@ -96,7 +96,7 @@
 def softmax_kernel(
     send, blocks, heads,
     qr_ref, s_ref, o_ref, seg_ref, pack_ref, base_ref, cos_ref, sin_ref, wv_ref,
-    w_ref, kt_ref, dv_ref, code_ref, back_ref, bias_ref, keys_ref,
+    w_ref, kt_ref, dv_ref, code_ref, bias_ref, keys_ref,
 ):
     tok = qr_ref.shape[1]
     halo = send * blocks
@@ -108,7 +108,7 @@
     seg_here = seg_ref[...].astype(F32)[0:1]
     cols = []
     for b in range(blocks):
-        row = pack_ref[b, 2 * send + RANK :].astype(F32)[0:1]
+        row = pack_ref[b, 2 * send :].astype(F32)[0:1]
         cols.append(column(row, tok)[tok - send :])
     seg_col = jnp.concatenate(cols, axis=0)
     offset = lax.broadcasted_iota(jnp.int32, (halo, tok), 0)
@@ -124,24 +124,24 @@
         dv = dv + dot(w.astype(BF16), o_ref[:, h * HEAD : (h + 1) * HEAD], 1, 0)
     dv_ref[...] = dv
     wv = wv_ref[...].astype(F32)
-    code_ref[...] = SCALE * dot(wv, dv[halo:], 1, 1, EXACT)
+    code_ref[0:RANK] = SCALE * dot(wv, dv[halo:], 1, 1, EXACT)
     for b in range(blocks):
         part = dv[b * send : (b + 1) * send]
         if send < tok:
             part = jnp.concatenate([jnp.zeros((tok - send, HEAD), F32), part], axis=0)
-        back_ref[b] = SCALE * dot(wv, part, 1, 1, EXACT)
+        code_ref[(b + 1) * RANK : (b + 2) * RANK] = SCALE * dot(wv, part, 1, 1, EXACT)
 
 
 def grads_kernel(
     send, blocks, heads,
-    low_ref, pack_ref, o_ref, w_ref, dp_ref, kt_ref, kth_ref, dv_ref, cost_ref, sint_ref, wq_ref, wv_ref,
+    low_ref, far_ref, pack_ref, o_ref, w_ref, dp_ref, kt_ref, kth_ref, dv_ref, cost_ref, sint_ref, wq_ref, wv_ref,
     code_ref, up_ref, vals_ref, qg_ref,
 ):
     tok = o_ref.shape[0]
     halo = send * blocks
     low = low_ref[...].astype(BF16)
     wv = wv_ref[...]
-    codes = [pack_ref[b, 2 * send : 2 * send + RANK] for b in range(blocks)]
+    codes = [far_ref[b] for b in range(blocks)]
     for b in range(blocks):
         rows = pack_ref[b, send : 2 * send].astype(F32)
         add = SCALE * dot(codes[b], wv, 0, 0)[tok - send :]
@@ -176,27 +176,29 @@
     part_ref[...] = dot(dl_ref[...], x_ref[...], 1, 0)
 
 
-def partial_kernel(split, dl_ref, x_ref, up_ref, send_ref):
-    rows, wide = dl_ref.shape[0], x_ref.shape[1]
-    send_ref[:, :wide] = dot(dl_ref[...], x_ref[...], 1, 0).astype(BF16)
-    up = up_ref[...]
-    size = up.shape[1]
-    send_ref[0:RANK, wide:] = up[:, :split]
-    send_ref[RANK:rows, wide : wide + size - split] = up[:, split:]
-    if 2 * split > size:
-        send_ref[RANK:rows, wide + size - split :] = jnp.zeros((rows - RANK, 2 * split - size), BF16)
-
-
-def final_kernel(split, mine_ref, one_ref, two_ref, three_ref, down_ref, upq_ref, upv_ref):
-    wide = down_ref.shape[1]
-    near = mine_ref[...].astype(F32) + one_ref[...].astype(F32)
-    far = two_ref[...].astype(F32) + three_ref[...].astype(F32)
-    total = near + far
-    down_ref[...] = total[:, :wide]
-    size = upq_ref.shape[1]
-    upq_ref[:, :split] = total[:RANK, wide:]
-    upq_ref[:, split:] = total[RANK:, wide : wide + size - split]
-    upv_ref[...] = total[RANK:, wide + size - split : wide + size - split + HEAD]
+def partial_kernel(own_ref, x_ref, up_ref, near_ref, part_ref, both_ref):
+    part = dot(own_ref[...], x_ref[...], 1, 0).astype(BF16)
+    wide, size = part.shape[1], up_ref.shape[1]
+    half = both_ref.shape[1] - wide
+    part_ref[...] = part
+    both_ref[:, :wide] = part
+    up = (up_ref[...].astype(F32) + near_ref[...].astype(F32)).astype(BF16)
+    both_ref[:RANK, wide:] = up[:, :half]
+    both_ref[RANK:, wide : wide + size - half] = up[:, half:]
+    if 2 * half > size:
+        both_ref[RANK:, wide + size - half :] = jnp.zeros((RANK, 2 * half - size), BF16)
+
+
+def final_kernel(mine_ref, one_ref, two_ref, three_ref, down_ref, upq_ref, upv_ref):
+    wide = one_ref.shape[1]
+    near = mine_ref[:, :wide].astype(F32) + one_ref[...].astype(F32)
+    far = two_ref[:, :wide].astype(F32) + three_ref[...].astype(F32)
+    down_ref[...] = near + far
+    up = mine_ref[:, wide:].astype(F32) + two_ref[:, wide:].astype(F32)
+    half, size = up.shape[1], upq_ref.shape[1]
+    upq_ref[:, :half] = up[:RANK]
+    upq_ref[:, half:] = up[RANK:, : size - half]
+    upv_ref[...] = up[RANK:, size - half : size - half + HEAD]
 
 
 def body(x, q, k, v, o, segment, a, wq, wv):
@@ -219,6 +221,12 @@
     def shift(array, by):
         moves = [(i, (i + by) % seq_count) for i in range(seq_count)]
         return lax.ppermute(array, "seq", moves)
+
+    def sum_four(array):
+        if fsdp_count != 4:
+            return sum_fsdp(array)
+        one, two, three = [swap(array, "fsdp", bit) for bit in (1, 2, 3)]
+        return (array + one) + (two + three)
 
     def sum_fsdp(array):
         if fsdp_count & (fsdp_count - 1):
@@ -248,11 +256,10 @@
     positions = (start - halo + jnp.arange(keys, dtype=jnp.int32)).astype(F32)
     angles = positions[:, None] * freqs[None, :]
     cos, sin = jnp.cos(angles), jnp.sin(angles)
+    pack = jnp.concatenate([k[tok - send :], v[tok - send :], seg_rows], axis=0)
+    packs = jnp.stack([shift(pack, d) for d in range(blocks, 0, -1)])
     low = sum_fsdp(part)
-    pack = jnp.concatenate(
-        [k[tok - send :], v[tok - send :], low[RANK:].astype(BF16), seg_rows], axis=0
-    )
-    packs = jnp.stack([shift(pack, d) for d in range(blocks, 0, -1)])
+    lows = jnp.stack([shift(low[RANK:].astype(BF16), d) for d in range(blocks, 0, -1)])
     qr, kt, s, dp, cos_t, sin_t = call(
         functools.partial(project_kernel, heads),
         [
@@ -264,45 +271,50 @@
             ((HALF, tok), F32),
         ],
         [pltpu.VMEM((tok, tok), F32)],
+        cost=3 << 20,
     )(low, q, k, v, o, seg_rows, cos[halo:], sin[halo:], wq, wv)
     specs = [pl.BlockSpec(memory_space=pltpu.VMEM)] * 9
     specs[5] = pl.BlockSpec(memory_space=pltpu.SMEM)
-    w, kt_far, dv, code_v, back = call(
+    w, kt_far, dv, codes_v = call(
         functools.partial(softmax_kernel, send, blocks, heads),
         [
             ((heads, keys, tok), F32),
             ((HEAD, halo), BF16),
             ((keys, HEAD), F32),
-            ((RANK, tok), F32),
-            ((blocks, RANK, tok), F32),
+            (((blocks + 1) * RANK, tok), F32),
         ],
         [pltpu.VMEM((halo, tok), F32), pltpu.VMEM((halo, HEAD), BF16)],
         in_specs=specs,
+        cost=5 << 20,
     )(qr, s, o, seg_rows, packs, base, cos[:halo], sin[:halo], wv)
+    codes_v, lows = lax.optimization_barrier((codes_v, lows))
+    code_v = codes_v[:RANK]
     for b, d in enumerate(range(blocks, 0, -1)):
-        code_v = code_v + shift(back[b], -d)
+        code_v = code_v + shift(codes_v[(b + 1) * RANK : (b + 2) * RANK], -d)
     code_q, up = call(
         functools.partial(grads_kernel, send, blocks, heads),
         [((RANK, tok), F32), ((RANK, (heads + 1) * HEAD), BF16 if direct else F32)],
         [pltpu.VMEM((halo, HEAD), BF16), pltpu.VMEM((heads * HEAD, tok), BF16)],
         cost=6 << 20,
-    )(low, packs, o, w, dp, kt, kt_far, dv, cos_t, sin_t, wq, wv)
+    )(low, lows, packs, o, w, dp, kt, kt_far, dv, cos_t, sin_t, wq, wv)
+
     codes = jnp.concatenate([code_q, code_v], axis=0)
-
-    dlow = sum_fsdp(codes).astype(BF16)
     if not direct:
+        dlow = sum_fsdp(codes).astype(BF16)
         (down,) = call(down_kernel, [((2 * RANK, wide), F32)])(dlow, x)
         down, up = lax.psum((down, up), "seq")
         return down.T, up[:, : heads * HEAD], up[:, heads * HEAD :]
 
-    split = -(-(heads + 1) // 2) * HEAD
-    (mine,) = call(functools.partial(partial_kernel, split), [((2 * RANK, wide + split), BF16)])(
-        dlow, x, up
-    )
+    near_up = swap(up, "seq", 1)
+    dlow = sum_fsdp(codes).astype(BF16)
+    half = -(-(heads + 1) // 2) * HEAD
+    part, both = call(
+        partial_kernel, [((2 * RANK, wide), BF16), ((2 * RANK, wide + half), BF16)]
+    )(dlow, x, up, near_up)
     down, up_q, up_v = call(
-        functools.partial(final_kernel, split),
+        final_kernel,
         [((2 * RANK, wide), F32), ((RANK, heads * HEAD), F32), ((RANK, HEAD), F32)],
-    )(mine, *[swap(mine, "seq", bit) for bit in (1, 2, 3)])
+    )(both, swap(part, "seq", 1), swap(both, "seq", 2), swap(part, "seq", 3))
     return down.T, up_q, up_v
 
 

time: 42.6 us -> 40.7 us (0.955)
  waiting for transfers between devices: 19.5 us -> 16.5 us
  starting transfers between devices: 13.6 us -> 14.3 us
    ppermute x2 -> x3, starting transfers between devices: 4.19 us -> 6 us  [shift(): return lax.ppermute(array, 'seq', moves)]
    ppermute x2 -> x3, waiting for transfers between devices: 2.04 us -> 0.53 us  [shift(): return lax.ppermute(array, 'seq', moves)]
    ppermute x7 -> x8, waiting for transfers between devices: 17.5 us -> 16 us  [swap(): return lax.ppermute(array, axis, [(i, i ^ bit) for i in range(size)])]
    ppermute x7 -> x8, starting transfers between devices: 9.37 us -> 8.28 us  [swap(): return lax.ppermute(array, axis, [(i, i ^ bit) for i in range(size)])]
  transfers between devices with their start and end apart: 9 -> 11, of which waited for: 7 -> 8; matrix products, arithmetic and copies ran while one was open for 1% -> 1% of each run, Pallas kernels for 7% -> 10%
where the time goes in v4:
time: 40.7 us; the launch traced here: 40.1 us
  waiting for transfers between devices  16.5 us (41%)
  starting transfers between devices  14.3 us (35%)
  Pallas kernels  6.49 us (16%)
  local copies, waits for them, and re-layouts  1.49 us (4%)
  between operations  0.83 us (2%)
  other arithmetic  0.48 us (1%)
    ppermute x8, waiting for transfers between devices, swap(): return lax.ppermute(array, axis, [(i, i ^ bit) for i in range(size)])  16 us
    ppermute x8, starting transfers between devices, swap(): return lax.ppermute(array, axis, [(i, i ^ bit) for i in range(size)])  8.28 us
    ppermute x3, starting transfers between devices, shift(): return lax.ppermute(array, 'seq', moves)  6 us
    pallas_call x1, Pallas kernels, body(): call(functools.partial(grads_kernel, send, blocks, heads), [((RANK, tok),...  2.11 us
    pallas_call x1, Pallas kernels, body(): call(lowrank_kernel, [((2 * RANK, tok), F32)], [pltpu.VMEM((tok, wide), B...  1.37 us
    pallas_call x1, Pallas kernels, body(): call(functools.partial(softmax_kernel, send, blocks, heads), [((heads, ke...  1.32 us
  transfers between devices with their start and end apart: 11, of which 8 were waited for; matrix products, arithmetic and copies ran while one was open for 1% of the time, Pallas kernels for 10%

profile of v4, /device:TPU:0, one launch (start us, length us, event | category | flops | bytes accessed | tf_op | source)
XLA Modules:
  0.0 40.1 jit_solution(11759406479626894905)
XLA Ops:
  0.6 1.4 %shard_map.112 = f32[32,128]{1,0:T(8,128)S(1)} custom-call(bf16[128,2048]{1,0:T(8,128)(2,1)} %x_ref.1, bf16[32,2048]{1,0:T(8,128)(2,1)} %bitcast.8), custom_call_target="tpu_custom_call" | custom-call | flops 1 | bytes 1 | tf_op jit(solution)/shard_map/pallas_call | solution.py:241
  2.0 0.5 %collective-permute-start = (f32[32,128]{1,0:T(8,128)S(1)}, f32[32,128]{1,0:T(8,128)S(1)}, u32[]{:S(2)}, u32[]{:S(2)}) collective-permute-start(f32[32,128]{1,0:T(8,128)S(1)} %shard_map.112), channel_id=1, source_target_pairs={{0,1},{1,0},{2,3},{3,2},{4,5},{5,4},{6,7},{7,6},{8,9},{9,8},{10,11... | collective-permute-start | bytes 49160 | tf_op jit(solution)/shard_map/ppermute | solution.py:219
  2.5 0.0 slice-start.1
  2.6 0.7 %slice-done = bf16[64,128]{1,0:T(8,128)(2,1)S(1)} async-done(((bf16[128,128]{1,0:T(8,128)(2,1)}), bf16[64,128]{1,0:T(8,128)(2,1)S(1)}, s32[]{:S(2)}) %slice-start) | async-done | bytes 16408 | tf_op jit(solution)/shard_map/slice | solution.py:259
  3.3 0.0 slice-done.1
  3.3 2.6 %collective-permute-start.2 = (bf16[144,128]{1,0:T(8,128)(2,1)S(1)}, bf16[144,128]{1,0:T(8,128)(2,1)S(1)}, u32[]{:S(2)}, u32[]{:S(2)}) collective-permute-start(bf16[144,128]{1,0:T(8,128)(2,1)S(1)} %pad_maximum_fusion), channel_id=1, source_target_pairs={{0,4},{4,8},{8,12},{12,0},{1,5},{5,9},{9,13},{13,1},{2,6},{6,10},{... | collective-permute-start | bytes 110600 | tf_op jit(solution)/shard_map/ppermute | solution.py:223
  5.9 1.6 %collective-permute-start.1 = (f32[32,128]{1,0:T(8,128)S(1)}, f32[32,128]{1,0:T(8,128)S(1)}, u32[]{:S(2)}, u32[]{:S(2)}) collective-permute-start(f32[32,128]{1,0:T(8,128)S(1)} %add.26), channel_id=1, source_target_pairs={{0,2},{1,3},{2,0},{3,1},{4,6},{5,7},{6,4},{7,5},{8,10},{9,11},{10,... | collective-permute-start | bytes 49160 | tf_op jit(solution)/shard_map/ppermute | solution.py:219
  7.5 2.2 %collective-permute-done.1 = f32[32,128]{1,0:T(8,128)S(1)} collective-permute-done((f32[32,128]{1,0:T(8,128)S(1)}, f32[32,128]{1,0:T(8,128)S(1)}, u32[]{:S(2)}, u32[]{:S(2)}) %collective-permute-start.1) | collective-permute-done | bytes 16416 | tf_op jit(solution)/shard_map/ppermute | solution.py:219
  9.7 1.6 %collective-permute-start.3 = (bf16[16,128]{1,0:T(8,128)(2,1)S(1)}, bf16[16,128]{1,0:T(8,128)(2,1)S(1)}, u32[]{:S(2)}, u32[]{:S(2)}) collective-permute-start(bf16[16,128]{1,0:T(8,128)(2,1)S(1)} %slice.44), channel_id=1, source_target_pairs={{0,4},{4,8},{8,12},{12,0},{1,5},{5,9},{9,13},{13,1},{2,6},{6,10},{... | collective-permute-start | bytes 12296 | tf_op jit(solution)/shard_map/ppermute | solution.py:223
  11.4 0.4 %multiply_sine_fusion = (f32[192,64]{1,0:T(8,128)S(1)}, f32[192,64]{1,0:T(8,128)S(1)}) fusion(f32[64]{0:T(128)S(1)} %multiply_power_fusion, f32[192]{0:T(256)S(1)} %add_convert_fusion.1), kind=kLoop, calls=%fused_computation | loop fusion | flops 12288 | bytes 99328 | tf_op jit(solution)/shard_map/sin | solution.py:258
  11.9 0.6 %copy-done.6 = bf16[16,128]{1,0:T(8,128)(2,1)S(1)} copy-done((bf16[16,128]{1,0:T(8,128)(2,1)S(1)}, bf16[16,128]{1,0:T(8,128)(2,1)}, u32[]{:S(2)}) %copy-start.6) | copy-done | bytes 4120
  12.5 0.1 copy-done.3
  12.6 0.0 copy-done.4
  12.6 0.7 %shard_map.113 = (bf16[8,128,128]{2,1,0:T(8,128)(2,1)S(1)}, bf16[128,128]{1,0:T(8,128)(2,1)S(1)}, f32[8,128,128]{2,1,0:T(8,128)S(1)}, f32[8,128,128]{2,1,0:T(8,1...) custom-call(f32[32,128]{1,0:T(8,128)S(1)} %add.27.low_ref, bf16[128,1024]{1,0:T(8,128)(2,1)S(1)} %copy-done.2, ...), custom_call_target="tpu_custom_call" | custom-call | flops 3145728 | bytes 3145728 | tf_op jit(solution)/shard_map/pallas_call | solution.py:263
  13.4 1.3 %shard_map.114 = (f32[8,192,128]{2,1,0:T(8,128)S(1)}, bf16[128,64]{1,0:T(8,128)(2,1)S(1)}, f32[192,128]{1,0:T(8,128)S(1)}, f32[32,128]{1,0:T(8,128)S(1)}) custom-call(bf16[8,128,128]{2,1,0:T(8,128)(2,1)S(1)} %get-tuple-element.22.qr_ref, f32[8,128,128]{2,1,0:T(8,128)S(1)} %get-tuple-element.23.s_ref, bf16[128,1024]{1,0:T(8,128)(2,1)S(1)} %copy-done, ...), custom_call_target="tpu_custom_call" | custom-call | flops 5242880 | bytes 5242880 | tf_op jit(solution)/shard_map/pallas_call | solution.py:278
  14.7 0.5 %collective-permute-done.3 = bf16[16,128]{1,0:T(8,128)(2,1)S(1)} collective-permute-done((bf16[16,128]{1,0:T(8,128)(2,1)S(1)}, bf16[16,128]{1,0:T(8,128)(2,1)S(1)}, u32[]{:S(2)}, u32[]{:S(2)}) %collective-permute-start.3) | collective-permute-done | bytes 4128 | tf_op jit(solution)/shard_map/ppermute | solution.py:223
  15.2 1.8 %collective-permute-start.4 = (f32[16,128]{1,0:T(8,128)S(1)}, f32[16,128]{1,0:T(8,128)S(1)}, u32[]{:S(2)}, u32[]{:S(2)}) collective-permute-start(f32[16,128]{1,0:T(8,128)S(1)} %slice.36), channel_id=1, source_target_pairs={{0,12},{4,0},{8,4},{12,8},{1,13},{5,1},{9,5},{13,9},{2,14},{6,2},{... | collective-permute-start | bytes 24584 | tf_op jit(solution)/shard_map/ppermute | solution.py:223
  17.0 2.1 %shard_map.115 = (f32[16,128]{1,0:T(8,128)S(1)}, bf16[16,1152]{1,0:T(8,128)(2,1)S(1)}) custom-call(f32[32,128]{1,0:T(8,128)S(1)} %add.27.low_ref, bf16[1,16,128]{2,1,0:T(8,128)(2,1)S(1)} %bitcast.7, bf16[1,144,128]{2,1,0:T(8,128)(2,1)S(1)} %bitcast.6, bf16[128,1024]{1,0:T(8,128)(2,1)S(1)} %copy-done, f32[8,192,128]{2,1,0:T(8,128)S(1)} %get-tuple-element.26.w_ref, ...), custom_call_target="tpu_custom_call" | custom-call | flops 6291456 | bytes 6291456 | tf_op jit(solution)/shard_map/pallas_call | solution.py:294
  19.1 0.1 collective-permute-start.5
  19.2 1.2 %collective-permute-done.5 = f32[32,128]{1,0:T(8,128)S(1)} collective-permute-done((f32[32,128]{1,0:T(8,128)S(1)}, f32[32,128]{1,0:T(8,128)S(1)}, u32[]{:S(2)}, u32[]{:S(2)}) %collective-permute-start.5) | collective-permute-done | bytes 16416 | tf_op jit(solution)/shard_map/ppermute | solution.py:219
  20.4 1.5 %collective-permute-start.6 = (f32[32,128]{1,0:T(8,128)S(1)}, f32[32,128]{1,0:T(8,128)S(1)}, u32[]{:S(2)}, u32[]{:S(2)}) collective-permute-start(f32[32,128]{1,0:T(8,128)S(1)} %fusion), channel_id=1, source_target_pairs={{0,2},{1,3},{2,0},{3,1},{4,6},{5,7},{6,4},{7,5},{8,10},{9,11},{10,... | collective-permute-start | bytes 49160 | tf_op jit(solution)/shard_map/ppermute | solution.py:219
  21.9 0.8 %collective-permute-start.7 = (bf16[16,1152]{1,0:T(8,128)(2,1)S(1)}, bf16[16,1152]{1,0:T(8,128)(2,1)S(1)}, u32[]{:S(2)}, u32[]{:S(2)}) collective-permute-start(bf16[16,1152]{1,0:T(8,128)(2,1)S(1)} %get-tuple-element.35.up_ref), channel_id=1, source_target_pairs={{0,4},{4,0},{8,12},{12,8},{1,5},{5,1},{9,13},{13,9},{2,6},{6,2},{1... | collective-permute-start | bytes 110600 | tf_op jit(solution)/shard_map/ppermute | solution.py:219
  22.6 1.5 %collective-permute-done.6 = f32[32,128]{1,0:T(8,128)S(1)} collective-permute-done((f32[32,128]{1,0:T(8,128)S(1)}, f32[32,128]{1,0:T(8,128)S(1)}, u32[]{:S(2)}, u32[]{:S(2)}) %collective-permute-start.6) | collective-permute-done | bytes 16416 | tf_op jit(solution)/shard_map/ppermute | solution.py:219
  24.1 1.7 %collective-permute-done.7.near_ref = bf16[16,1152]{1,0:T(8,128)(2,1)S(1)} collective-permute-done((bf16[16,1152]{1,0:T(8,128)(2,1)S(1)}, bf16[16,1152]{1,0:T(8,128)(2,1)S(1)}, u32[]{:S(2)}, u32[]{:S(2)}) %collective-permute-start.7) | collective-permute-done | bytes 36896 | tf_op jit(solution)/shard_map/ppermute | solution.py:219
  25.8 0.2 shard_map.116
  26.0 1.8 %collective-permute-start.9 = (bf16[32,2688]{1,0:T(8,128)(2,1)S(1)}, bf16[32,2688]{1,0:T(8,128)(2,1)S(1)}, u32[]{:S(2)}, u32[]{:S(2)}) collective-permute-start(bf16[32,2688]{1,0:T(8,128)(2,1)S(1)} %get-tuple-element.36.mine_ref), channel_id=1, source_target_pairs={{0,8},{4,12},{8,0},{12,4},{1,9},{5,13},{9,1},{13,5},{2,10},{6,14},... | collective-permute-start | bytes 516104 | tf_op jit(solution)/shard_map/ppermute | solution.py:219
  27.9 1.5 %collective-permute-start.10 = (bf16[32,2048]{1,0:T(8,128)(2,1)S(1)}, bf16[32,2048]{1,0:T(8,128)(2,1)S(1)}, u32[]{:S(2)}, u32[]{:S(2)}) collective-permute-start(bf16[32,2048]{1,0:T(8,128)(2,1)S(1)} %get-tuple-element.37), channel_id=1, source_target_pairs={{0,12},{4,8},{8,4},{12,0},{1,13},{5,9},{9,5},{13,1},{2,14},{6,10},... | collective-permute-start | bytes 393224 | tf_op jit(solution)/shard_map/ppermute | solution.py:219
  29.4 0.5 %collective-permute-start.8 = (bf16[32,2048]{1,0:T(8,128)(2,1)S(1)}, bf16[32,2048]{1,0:T(8,128)(2,1)S(1)}, u32[]{:S(2)}, u32[]{:S(2)}) collective-permute-start(bf16[32,2048]{1,0:T(8,128)(2,1)S(1)} %get-tuple-element.37), channel_id=1, source_target_pairs={{0,4},{4,0},{8,12},{12,8},{1,5},{5,1},{9,13},{13,9},{2,6},{6,2},{1... | collective-permute-start | bytes 393224 | tf_op jit(solution)/shard_map/ppermute | solution.py:219
  29.9 7.1 %collective-permute-done.10.three_ref = bf16[32,2048]{1,0:T(8,128)(2,1)S(1)} collective-permute-done((bf16[32,2048]{1,0:T(8,128)(2,1)S(1)}, bf16[32,2048]{1,0:T(8,128)(2,1)S(1)}, u32[]{:S(2)}, u32[]{:S(2)}) %collective-permute-start.10) | collective-permute-done | bytes 131104 | tf_op jit(solution)/shard_map/ppermute | solution.py:219
  37.0 2.1 %collective-permute-done.8.one_ref = bf16[32,2048]{1,0:T(8,128)(2,1)S(1)} collective-permute-done((bf16[32,2048]{1,0:T(8,128)(2,1)S(1)}, bf16[32,2048]{1,0:T(8,128)(2,1)S(1)}, u32[]{:S(2)}, u32[]{:S(2)}) %collective-permute-start.8) | collective-permute-done | bytes 131104 | tf_op jit(solution)/shard_map/ppermute | solution.py:219
  39.1 0.2 collective-permute-done.9.two_ref
  39.3 0.8 %shard_map.117 = (f32[32,2048]{1,0:T(8,128)}, f32[16,1024]{1,0:T(8,128)}, f32[16,128]{1,0:T(8,128)}) custom-call(bf16[32,2688]{1,0:T(8,128)(2,1)S(1)} %get-tuple-element.36.mine_ref, bf16[32,2048]{1,0:T(8,128)(2,1)S(1)} %collective-permute-done.8.one_ref, bf16[32,2688]{1,0:T(8,128)(2,1)S(1)} %collective-permute-done.9.two_ref, ...), custom_call_target="tpu_custom_call" | custom-call | flops 1 | bytes 1 | tf_op jit(solution)/shard_map/pallas_call | solution.py:314
  (34 shorter events, 0.1 us)
Async XLA Ops:
  0.6 1.9 %copy-start.7 = (s32[128]{0:T(128)S(1)}, s32[128]{0:T(128)}, u32[]{:S(2)}) copy-start(s32[128]{0:T(128)} %param.14) | copy-start | bytes 1540
  2.0 3.9 %collective-permute-start = (f32[32,128]{1,0:T(8,128)S(1)}, f32[32,128]{1,0:T(8,128)S(1)}, u32[]{:S(2)}, u32[]{:S(2)}) collective-permute-start(f32[32,128]{1,0:T(8,128)S(1)} %shard_map.112), channel_id=1, source_target_pairs={{0,1},{1,0},{2,3},{3,2},{4,5},{5,4},{6,7},{7,6},{8,9},{9,8},{10,11... | collective-permute-start | bytes 49160 | tf_op jit(solution)/shard_map/ppermute | solution.py:219
  2.5 0.7 %slice-start = ((bf16[128,128]{1,0:T(8,128)(2,1)}), bf16[64,128]{1,0:T(8,128)(2,1)S(1)}, s32[]{:S(2)}) async-start(bf16[128,128]{1,0:T(8,128)(2,1)} %k_ref.1), calls=%async_computation | async-start | bytes 32768 | tf_op jit(solution)/shard_map/slice | solution.py:259
  2.5 0.7 %slice-start.1 = ((bf16[128,128]{1,0:T(8,128)(2,1)}), bf16[64,128]{1,0:T(8,128)(2,1)S(1)}, s32[]{:S(2)}) async-start(bf16[128,128]{1,0:T(8,128)(2,1)} %v_ref.1), calls=%async_computation.1 | async-start | bytes 32768 | tf_op jit(solution)/shard_map/slice | solution.py:259
  3.3 10.1 %collective-permute-start.2 = (bf16[144,128]{1,0:T(8,128)(2,1)S(1)}, bf16[144,128]{1,0:T(8,128)(2,1)S(1)}, u32[]{:S(2)}, u32[]{:S(2)}) collective-permute-start(bf16[144,128]{1,0:T(8,128)(2,1)S(1)} %pad_maximum_fusion), channel_id=1, source_target_pairs={{0,4},{4,8},{8,12},{12,0},{1,5},{5,9},{9,13},{13,1},{2,6},{6,10},{... | collective-permute-start | bytes 110600 | tf_op jit(solution)/shard_map/ppermute | solution.py:223
  5.9 3.8 %collective-permute-start.1 = (f32[32,128]{1,0:T(8,128)S(1)}, f32[32,128]{1,0:T(8,128)S(1)}, u32[]{:S(2)}, u32[]{:S(2)}) collective-permute-start(f32[32,128]{1,0:T(8,128)S(1)} %add.26), channel_id=1, source_target_pairs={{0,2},{1,3},{2,0},{3,1},{4,6},{5,7},{6,4},{7,5},{8,10},{9,11},{10,... | collective-permute-start | bytes 49160 | tf_op jit(solution)/shard_map/ppermute | solution.py:219
  9.7 2.2 %copy-start.5 = (bf16[128,128]{1,0:T(8,128)(2,1)S(1)}, bf16[128,128]{1,0:T(8,128)(2,1)}, u32[]{:S(2)}) copy-start(bf16[128,128]{1,0:T(8,128)(2,1)} %v_ref.1) | copy-start | bytes 98308
  9.7 2.2 %copy-start = (bf16[128,1024]{1,0:T(8,128)(2,1)S(1)}, bf16[128,1024]{1,0:T(8,128)(2,1)}, u32[]{:S(2)}) copy-start(bf16[128,1024]{1,0:T(8,128)(2,1)} %o_ref.5) | copy-start | bytes 786436
  9.7 2.2 %copy-start.2 = (bf16[128,1024]{1,0:T(8,128)(2,1)S(1)}, bf16[128,1024]{1,0:T(8,128)(2,1)}, u32[]{:S(2)}) copy-start(bf16[128,1024]{1,0:T(8,128)(2,1)} %q_ref.1) | copy-start | bytes 786436
  9.7 5.5 %collective-permute-start.3 = (bf16[16,128]{1,0:T(8,128)(2,1)S(1)}, bf16[16,128]{1,0:T(8,128)(2,1)S(1)}, u32[]{:S(2)}, u32[]{:S(2)}) collective-permute-start(bf16[16,128]{1,0:T(8,128)(2,1)S(1)} %slice.44), channel_id=1, source_target_pairs={{0,4},{4,8},{8,12},{12,0},{1,5},{5,9},{9,13},{13,1},{2,6},{6,10},{... | collective-permute-start | bytes 12296 | tf_op jit(solution)/shard_map/ppermute | solution.py:223
  11.8 0.7 %copy-start.6 = (bf16[16,128]{1,0:T(8,128)(2,1)S(1)}, bf16[16,128]{1,0:T(8,128)(2,1)}, u32[]{:S(2)}) copy-start(bf16[16,128]{1,0:T(8,128)(2,1)} %wv_ref.5) | copy-start | bytes 12292
  11.8 0.8 %copy-start.3 = (bf16[16,1024]{1,0:T(8,128)(2,1)S(1)}, bf16[16,1024]{1,0:T(8,128)(2,1)}, u32[]{:S(2)}) copy-start(bf16[16,1024]{1,0:T(8,128)(2,1)} %wq_ref.3) | copy-start | bytes 98308
  11.9 0.8 %copy-start.4 = (bf16[128,128]{1,0:T(8,128)(2,1)S(1)}, bf16[128,128]{1,0:T(8,128)(2,1)}, u32[]{:S(2)}) copy-start(bf16[128,128]{1,0:T(8,128)(2,1)} %k_ref.1) | copy-start | bytes 98308
  15.2 3.9 %collective-permute-start.4 = (f32[16,128]{1,0:T(8,128)S(1)}, f32[16,128]{1,0:T(8,128)S(1)}, u32[]{:S(2)}, u32[]{:S(2)}) collective-permute-start(f32[16,128]{1,0:T(8,128)S(1)} %slice.36), channel_id=1, source_target_pairs={{0,12},{4,0},{8,4},{12,8},{1,13},{5,1},{9,5},{13,9},{2,14},{6,2},{... | collective-permute-start | bytes 24584 | tf_op jit(solution)/shard_map/ppermute | solution.py:223
  17.0 8.9 %copy-start.1 = (bf16[128,2048]{1,0:T(8,128)(2,1)S(1)}, bf16[128,2048]{1,0:T(8,128)(2,1)}, u32[]{:S(2)}) copy-start(bf16[128,2048]{1,0:T(8,128)(2,1)} %x_ref.1) | copy-start | bytes 1572868
  19.1 1.2 %collective-permute-start.5 = (f32[32,128]{1,0:T(8,128)S(1)}, f32[32,128]{1,0:T(8,128)S(1)}, u32[]{:S(2)}, u32[]{:S(2)}) collective-permute-start(f32[32,128]{1,0:T(8,128)S(1)} %pad_maximum_fusion.1), channel_id=1, source_target_pairs={{0,1},{1,0},{2,3},{3,2},{4,5},{5,4},{6,7},{7,6},{8,9},{9,8},{10,11... | collective-permute-start | bytes 49160 | tf_op jit(solution)/shard_map/ppermute | solution.py:219
  20.4 3.7 %collective-permute-start.6 = (f32[32,128]{1,0:T(8,128)S(1)}, f32[32,128]{1,0:T(8,128)S(1)}, u32[]{:S(2)}, u32[]{:S(2)}) collective-permute-start(f32[32,128]{1,0:T(8,128)S(1)} %fusion), channel_id=1, source_target_pairs={{0,2},{1,3},{2,0},{3,1},{4,6},{5,7},{6,4},{7,5},{8,10},{9,11},{10,... | collective-permute-start | bytes 49160 | tf_op jit(solution)/shard_map/ppermute | solution.py:219
  21.9 4.0 %collective-permute-start.7 = (bf16[16,1152]{1,0:T(8,128)(2,1)S(1)}, bf16[16,1152]{1,0:T(8,128)(2,1)S(1)}, u32[]{:S(2)}, u32[]{:S(2)}) collective-permute-start(bf16[16,1152]{1,0:T(8,128)(2,1)S(1)} %get-tuple-element.35.up_ref), channel_id=1, source_target_pairs={{0,4},{4,0},{8,12},{12,8},{1,5},{5,1},{9,13},{13,9},{2,6},{6,2},{1... | collective-permute-start | bytes 110600 | tf_op jit(solution)/shard_map/ppermute | solution.py:219
  26.0 13.2 %collective-permute-start.9 = (bf16[32,2688]{1,0:T(8,128)(2,1)S(1)}, bf16[32,2688]{1,0:T(8,128)(2,1)S(1)}, u32[]{:S(2)}, u32[]{:S(2)}) collective-permute-start(bf16[32,2688]{1,0:T(8,128)(2,1)S(1)} %get-tuple-element.36.mine_ref), channel_id=1, source_target_pairs={{0,8},{4,12},{8,0},{12,4},{1,9},{5,13},{9,1},{13,5},{2,10},{6,14},... | collective-permute-start | bytes 516104 | tf_op jit(solution)/shard_map/ppermute | solution.py:219
  27.9 9.1 %collective-permute-start.10 = (bf16[32,2048]{1,0:T(8,128)(2,1)S(1)}, bf16[32,2048]{1,0:T(8,128)(2,1)S(1)}, u32[]{:S(2)}, u32[]{:S(2)}) collective-permute-start(bf16[32,2048]{1,0:T(8,128)(2,1)S(1)} %get-tuple-element.37), channel_id=1, source_target_pairs={{0,12},{4,8},{8,4},{12,0},{1,13},{5,9},{9,5},{13,1},{2,14},{6,10},... | collective-permute-start | bytes 393224 | tf_op jit(solution)/shard_map/ppermute | solution.py:219
  29.4 9.7 %collective-permute-start.8 = (bf16[32,2048]{1,0:T(8,128)(2,1)S(1)}, bf16[32,2048]{1,0:T(8,128)(2,1)S(1)}, u32[]{:S(2)}, u32[]{:S(2)}) collective-permute-start(bf16[32,2048]{1,0:T(8,128)(2,1)S(1)} %get-tuple-element.37), channel_id=1, source_target_pairs={{0,4},{4,0},{8,12},{12,8},{1,5},{5,1},{9,13},{13,9},{2,6},{6,2},{1... | collective-permute-start | bytes 393224 | tf_op jit(solution)/shard_map/ppermute | solution.py:219

commit v5 on v4

v5 whole, which is shorter than its diff:
```python
import functools
import math

import jax
import jax.numpy as jnp
from jax import lax
from jax.experimental import pallas as pl
from jax.experimental.pallas import tpu as pltpu
from jax.sharding import PartitionSpec as P

HEAD = 128
HALF = HEAD // 2
RANK = 16
SCALE = 2.0
ROPE_BASE = 500000.0
NEG_FILL = -1e30
INV_ROOT = 1.0 / math.sqrt(HEAD)
F32 = jnp.float32
BF16 = jnp.bfloat16
LIMIT = 40 * 1024 * 1024
FULL = 55168 * 1024


def dot(left, right, left_dim, right_dim):
    return lax.dot_general(
        left,
        right,
        (((left_dim,), (right_dim,)), ((), ())),
        preferred_element_type=F32,
    )


def call(kernel, out_shapes, scratch=(), limit=LIMIT, cost=1, **specs):
    return pl.pallas_call(
        kernel,
        out_shape=[jax.ShapeDtypeStruct(s, d) for s, d in out_shapes],
        **specs,
        scratch_shapes=list(scratch),
        compiler_params=pltpu.CompilerParams(vmem_limit_bytes=limit),
        cost_estimate=pl.CostEstimate(flops=cost, bytes_accessed=cost, transcendentals=0),
    )


def lowrank_kernel(x_hbm, a_hbm, part_ref, x_ref, a_ref, sems):
    pairs = [(x_hbm, x_ref), (a_hbm, a_ref)]
    copies = [pltpu.make_async_copy(src, dst, sems.at[i]) for i, (src, dst) in enumerate(pairs)]
    for copy in copies:
        copy.start()
    for copy in copies:
        copy.wait()
    part_ref[...] = dot(a_ref[...], x_ref[...], 1, 1)


def rotate_rows(u, cos, sin):
    return u * cos + pltpu.roll(u, HALF, 1) * sin


def wide_tables(cos, sin):
    return jnp.concatenate([cos, cos], axis=1), jnp.concatenate([-sin, sin], axis=1)


def column(row, tok):
    return jnp.broadcast_to(row, (tok, tok)).T


def lanes(array, count):
    return jnp.concatenate([array] * count, axis=1)


def head_rows(ref, first, count):
    parts = [ref[:, h * HEAD : (h + 1) * HEAD] for h in range(first, first + count)]
    return jnp.concatenate(parts, axis=0)


def split_dot(left, right, left_dim, right_dim):
    high = right.astype(BF16)
    rest = (right - high.astype(F32)).astype(BF16)
    return dot(left, high, left_dim, right_dim) + dot(left, rest, left_dim, right_dim)


def by_token(array, send, tok):
    if send == tok:
        return array
    gap = jnp.zeros((tok - send, array.shape[1]), array.dtype)
    return jnp.concatenate([array[:tok], gap, array[tok:]], axis=0)


def project_kernel(
    count, heads,
    low_ref, q_ref, k_ref, v_ref, o_ref, seg_ref, cos_ref, sin_ref, wq_ref, wv_ref,
    qr_ref, kt_ref, s_ref, dp_ref, cost_ref, sint_ref,
):
    tok = q_ref.shape[0]
    low = low_ref[...].astype(BF16)
    cost_ref[...] = cos_ref[...].T
    sint_ref[...] = sin_ref[...].T
    cos, sin = wide_tables(cos_ref[...], sin_ref[...])
    keys = rotate_rows(k_ref[...].astype(F32), cos, sin)
    kt_ref[...] = keys.T.astype(BF16)
    keys = keys.astype(BF16)
    vals = (v_ref[...].astype(F32) + SCALE * dot(low[RANK:], wv_ref[...], 0, 0)).astype(BF16)
    seg_here = seg_ref[...].astype(F32)[0:1]
    key = lax.broadcasted_iota(jnp.int32, (tok, tok), 0)
    query = lax.broadcasted_iota(jnp.int32, (tok, tok), 1)
    allowed = (key <= query) & (column(seg_here, tok) == seg_here)
    bias = lanes(jnp.where(allowed, 0.0, NEG_FILL), count)
    q0 = q_ref[...].astype(F32) + SCALE * dot(low[:RANK], wq_ref[...], 0, 0)
    for g in range(0, heads, count):
        cut = slice(g * tok, (g + count) * tok)
        parts = [q0[:, h * HEAD : (h + 1) * HEAD] for h in range(g, g + count)]
        qr = jnp.concatenate([rotate_rows(u, cos, sin).astype(BF16) for u in parts], axis=0)
        qr_ref[cut] = qr
        s_ref[:, cut] = dot(keys, qr, 1, 1) * INV_ROOT + bias
        dp_ref[:, cut] = dot(vals, head_rows(o_ref, g, count), 1, 1)


def softmax_kernel(
    count, send, blocks, heads,
    qr_ref, s_ref, o_ref, seg_ref, pack_ref, base_ref, cos_ref, sin_ref, wv_ref,
    w_ref, kt_ref, dv_ref, code_ref,
):
    tok = o_ref.shape[0]
    halo = send * blocks
    cos, sin = wide_tables(cos_ref[...], sin_ref[...])
    keys = jnp.concatenate([pack_ref[b, 0:send] for b in range(blocks)], axis=0)
    keys = rotate_rows(keys.astype(F32), cos, sin)
    kt_ref[...] = keys.T.astype(BF16)
    keys = keys.astype(BF16)
    seg_here = seg_ref[...].astype(F32)[0:1]
    cols = []
    for b in range(blocks):
        row = pack_ref[b, 2 * send :].astype(F32)[0:1]
        cols.append(column(row, tok)[tok - send :])
    seg_col = jnp.concatenate(cols, axis=0)
    offset = lax.broadcasted_iota(jnp.int32, (halo, tok), 0)
    allowed = (offset + base_ref[0] >= halo) & (seg_col == seg_here)
    bias = lanes(jnp.where(allowed, 0.0, NEG_FILL), count)
    dv = jnp.zeros((tok + halo, HEAD), F32)
    for g in range(0, heads, count):
        cut = slice(g * tok, (g + count) * tok)
        far = dot(keys, qr_ref[cut], 1, 1) * INV_ROOT + bias
        s = jnp.concatenate([s_ref[:, cut], far], axis=0)
        e = jnp.exp(s - jnp.max(s, axis=0, keepdims=True))
        w = e * (1.0 / jnp.sum(e, axis=0, keepdims=True))
        w_ref[:, cut] = w
        dv = dv + dot(w.astype(BF16), head_rows(o_ref, g, count), 1, 0)
    dv_ref[...] = dv
    codes = SCALE * split_dot(wv_ref[...], by_token(dv, send, tok), 1, 1)
    for b in range(blocks + 1):
        code_ref[b * RANK : (b + 1) * RANK] = codes[:, b * tok : (b + 1) * tok]


def grads_kernel(
    count, send, blocks, heads,
    low_ref, far_ref, pack_ref, o_ref, w_ref, dp_ref, kt_ref, kth_ref, dv_ref, cost_ref, sint_ref, wq_ref, wv_ref,
    code_ref, up_ref, qg_ref,
):
    tok = o_ref.shape[0]
    low = low_ref[...].astype(BF16)
    wv = wv_ref[...]
    vals = []
    for b in range(blocks):
        rows = pack_ref[b, send : 2 * send].astype(F32)
        add = SCALE * dot(far_ref[b], wv, 0, 0)[tok - send :]
        vals.append((rows + add).astype(BF16))
    vals = jnp.concatenate(vals, axis=0)
    kt = jnp.concatenate([kt_ref[...], kth_ref[...]], axis=1)
    cos, sin = lanes(cost_ref[...], count), lanes(sint_ref[...], count)
    for g in range(0, heads, count):
        cut = slice(g * tok, (g + count) * tok)
        far = dot(vals, head_rows(o_ref, g, count), 1, 1)
        dp = jnp.concatenate([dp_ref[:, cut], far], axis=0)
        w = w_ref[:, cut]
        delta = jnp.sum(w * dp, axis=0, keepdims=True)
        ds = (w * (dp - delta) * INV_ROOT).astype(BF16)
        dq = dot(kt, ds, 1, 0)
        first, second = dq[:HALF], dq[HALF:]
        first, second = first * cos + second * sin, second * cos - first * sin
        turned = jnp.concatenate([first.astype(BF16), second.astype(BF16)], axis=0)
        for h in range(count):
            qg_ref[(g + h) * HEAD : (g + h + 1) * HEAD] = turned[:, h * tok : (h + 1) * tok]
    qg = qg_ref[...]
    code_ref[...] = SCALE * dot(wq_ref[...], qg, 1, 0)
    up_ref[:, : heads * HEAD] = (SCALE * dot(low[:RANK], qg, 1, 1)).astype(up_ref.dtype)
    codes = jnp.concatenate([low[RANK:]] + [far_ref[b] for b in range(blocks)], axis=1)
    up_v = SCALE * split_dot(codes, by_token(dv_ref[...], send, tok), 1, 0)
    up_ref[:, heads * HEAD :] = up_v.astype(up_ref.dtype)


def down_kernel(dl_ref, x_ref, part_ref):
    part_ref[...] = dot(dl_ref[...], x_ref[...], 1, 0)


def partial_kernel(own_ref, x_ref, up_ref, send_ref):
    part = dot(own_ref[...], x_ref[...], 1, 0).astype(BF16)
    wide, size = part.shape[1], up_ref.shape[1]
    half = send_ref.shape[1] - wide
    send_ref[:, :wide] = part
    send_ref[:RANK, wide:] = up_ref[:, :half]
    send_ref[RANK:, wide : wide + size - half] = up_ref[:, half:]
    if 2 * half > size:
        send_ref[RANK:, wide + size - half :] = jnp.zeros((RANK, 2 * half - size), BF16)


def final_kernel(mine_ref, one_ref, two_ref, three_ref, down_ref, upq_ref, upv_ref):
    near = mine_ref[...].astype(F32) + one_ref[...].astype(F32)
    far = two_ref[...].astype(F32) + three_ref[...].astype(F32)
    total = near + far
    wide, size = down_ref.shape[1], upq_ref.shape[1]
    half = total.shape[1] - wide
    down_ref[...] = total[:, :wide]
    upq_ref[:, :half] = total[:RANK, wide:]
    upq_ref[:, half:] = total[RANK:, wide : wide + size - half]
    upv_ref[...] = total[RANK:, wide + size - half : wide + size - half + HEAD]


def body(x, q, k, v, o, segment, a, wq, wv):
    tok, wide = x.shape
    seq_count = lax.axis_size("seq")
    fsdp_count = lax.axis_size("fsdp")
    seq_index = lax.axis_index("seq")
    heads = q.shape[1] // HEAD
    longest = tok * seq_count // 8
    blocks = -(-longest // tok)
    send = longest if blocks == 1 else tok
    halo = blocks * send
    keys = halo + tok
    direct = seq_count == 4

    def swap(array, axis, bit):
        size = lax.axis_size(axis)
        return lax.ppermute(array, axis, [(i, i ^ bit) for i in range(size)])

    def shift(array, by):
        moves = [(i, (i + by) % seq_count) for i in range(seq_count)]
        return lax.ppermute(array, "seq", moves)

    def sum_fsdp(array):
        if fsdp_count & (fsdp_count - 1):
            return lax.psum(array, "fsdp")
        bit = 1
        while bit < fsdp_count:
            array = array + swap(array, "fsdp", bit)
            bit *= 2
        return array

    seg_row = segment.reshape(1, tok)
    (part,) = call(
        lowrank_kernel,
        [((2 * RANK, tok), F32)],
        [
            pltpu.VMEM((tok, wide), BF16),
            pltpu.VMEM((2 * RANK, wide), BF16),
            pltpu.SemaphoreType.DMA((2,)),
        ],
        limit=FULL,
        in_specs=[pl.BlockSpec(memory_space=pltpu.HBM)] * 2,
    )(x, a.T)
    seg_rows = jnp.broadcast_to(seg_row, (16, tok)).astype(BF16)
    start = seq_index * tok
    base = start.reshape(1).astype(jnp.int32)
    freqs = ROPE_BASE ** (-(2.0 * jnp.arange(HALF, dtype=F32)) / HEAD)
    positions = (start - halo + jnp.arange(keys, dtype=jnp.int32)).astype(F32)
    angles = positions[:, None] * freqs[None, :]
    cos, sin = jnp.cos(angles), jnp.sin(angles)
    pack = jnp.concatenate([k[tok - send :], v[tok - send :], seg_rows], axis=0)
    packs = jnp.stack([shift(pack, d) for d in range(blocks, 0, -1)])
    low = sum_fsdp(part)
    low, cos, sin = lax.optimization_barrier((low, cos, sin))
    lows = jnp.stack([shift(low[RANK:].astype(BF16), d) for d in range(blocks, 0, -1)])
    count = heads if blocks == 1 else 1
    qr, kt, s, dp, cos_t, sin_t = call(
        functools.partial(project_kernel, count, heads),
        [
            ((heads * tok, HEAD), BF16),
            ((HEAD, tok), BF16),
            ((tok, heads * tok), F32),
            ((tok, heads * tok), F32),
            ((HALF, tok), F32),
            ((HALF, tok), F32),
        ],
        cost=3 << 20,
    )(low, q, k, v, o, seg_rows, cos[halo:], sin[halo:], wq, wv)
    specs = [pl.BlockSpec(memory_space=pltpu.VMEM)] * 9
    specs[5] = pl.BlockSpec(memory_space=pltpu.SMEM)
    w, kt_far, dv, codes_v = call(
        functools.partial(softmax_kernel, count, send, blocks, heads),
        [
            ((keys, heads * tok), F32),
            ((HEAD, halo), BF16),
            ((keys, HEAD), F32),
            (((blocks + 1) * RANK, tok), F32),
        ],
        in_specs=specs,
        cost=5 << 20,
    )(qr, s, o, seg_rows, packs, base, cos[:halo], sin[:halo], wv)
    codes_v, lows = lax.optimization_barrier((codes_v, lows))
    code_v = codes_v[:RANK]
    for b, d in enumerate(range(blocks, 0, -1)):
        code_v = code_v + shift(codes_v[(b + 1) * RANK : (b + 2) * RANK], -d)
    code_q, up = call(
        functools.partial(grads_kernel, count, send, blocks, heads),
        [((RANK, tok), F32), ((RANK, (heads + 1) * HEAD), BF16 if direct else F32)],
        [pltpu.VMEM((heads * HEAD, tok), BF16)],
        cost=6 << 20,
    )(low, lows, packs, o, w, dp, kt, kt_far, dv, cos_t, sin_t, wq, wv)
    codes = jnp.concatenate([code_q, code_v], axis=0)
    if not direct:
        dlow = sum_fsdp(codes).astype(BF16)
        (down,) = call(down_kernel, [((2 * RANK, wide), F32)])(dlow, x)
        down, up = lax.psum((down, up), "seq")
        return down.T, up[:, : heads * HEAD], up[:, heads * HEAD :]

    dlow = sum_fsdp(codes).astype(BF16)
    half = -(-(heads + 1) // 2) * HEAD
    (mine,) = call(partial_kernel, [((2 * RANK, wide + half), BF16)])(dlow, x, up)
    down, up_q, up_v = call(
        final_kernel,
        [((2 * RANK, wide), F32), ((RANK, heads * HEAD), F32), ((RANK, HEAD), F32)],
    )(mine, *[swap(mine, "seq", bit) for bit in (1, 2, 3)])
    return down.T, up_q, up_v


def solution(mesh):
    rows = ("groups", "seq")
    in_specs = (
        P(rows, "fsdp"),
        P(rows, "fsdp"),
        P(rows, "fsdp"),
        P(rows, "fsdp"),
        P(rows, "fsdp"),
        P(rows),
        P("fsdp", None),
        P(None, "fsdp"),
        P(None, "fsdp"),
    )
    out_specs = (P(("groups", "fsdp"), None), P("groups", "fsdp"), P("groups", "fsdp"))
    return jax.shard_map(body, mesh=mesh, in_specs=in_specs, out_specs=out_specs, check_vma=False)
```

time: 40.7 us -> 40.8 us (level)
  waiting for transfers between devices: 16.5 us -> 20.1 us
  Pallas kernels: 6.49 us -> 4.63 us
  starting transfers between devices: 14.3 us -> 13 us
    ppermute x3, waiting for transfers between devices: 0.53 us -> 3.59 us  [shift(): return lax.ppermute(array, 'seq', moves)]
    pallas_call x4, Pallas kernels: 4.34 us -> 2.47 us  [the longest x1 0.86 us: body(): call(functools.partial(grads_kernel, count, send, blocks, heads), [((RANK...]
    ppermute x3, starting transfers between devices: 6 us -> 4.98 us  [shift(): return lax.ppermute(array, 'seq', moves)]
    ppermute x8 -> x7, waiting for transfers between devices: 16 us -> 16.5 us  [swap(): return lax.ppermute(array, axis, [(i, i ^ bit) for i in range(size)])]
    ppermute x8 -> x7, starting transfers between devices: 8.28 us -> 8.02 us  [swap(): return lax.ppermute(array, axis, [(i, i ^ bit) for i in range(size)])]
  transfers between devices with their start and end apart: 11 -> 10, of which waited for: 8 -> 7; matrix products, arithmetic and copies ran while one was open for 1% -> 1% of each run, Pallas kernels for 10% -> 6%
where the time goes in v5:
time: 40.8 us; the launch traced here: 40.5 us
  waiting for transfers between devices  20.1 us (49%)
  starting transfers between devices  13 us (32%)
  Pallas kernels  4.63 us (11%)
  local copies, waits for them, and re-layouts  1.5 us (4%)
  between operations  0.81 us (2%)
  other arithmetic  0.47 us (1%)
    ppermute x7, waiting for transfers between devices, swap(): return lax.ppermute(array, axis, [(i, i ^ bit) for i in range(size)])  16.5 us
    ppermute x7, starting transfers between devices, swap(): return lax.ppermute(array, axis, [(i, i ^ bit) for i in range(size)])  8.02 us
    ppermute x3, starting transfers between devices, shift(): return lax.ppermute(array, 'seq', moves)  4.98 us
    ppermute x3, waiting for transfers between devices, shift(): return lax.ppermute(array, 'seq', moves)  3.59 us
    pallas_call x1, Pallas kernels, body(): call(lowrank_kernel, [((2 * RANK, tok), F32)], [pltpu.VMEM((tok, wide), B...  1.37 us
    pallas_call x1, Pallas kernels, body(): call(functools.partial(grads_kernel, count, send, blocks, heads), [((RANK...  0.86 us
  transfers between devices with their start and end apart: 10, of which 7 were waited for; matrix products, arithmetic and copies ran while one was open for 1% of the time, Pallas kernels for 6%

profile of v5, /device:TPU:0, one launch (start us, length us, event | category | flops | bytes accessed | tf_op | source)
XLA Modules:
  0.0 40.5 jit_solution(2266272223874284080)
XLA Ops:
  0.6 1.4 %shard_map.112 = f32[32,128]{1,0:T(8,128)S(1)} custom-call(bf16[128,2048]{1,0:T(8,128)(2,1)} %x_ref.1, bf16[32,2048]{1,0:T(8,128)(2,1)} %bitcast.8), custom_call_target="tpu_custom_call" | custom-call | flops 1 | bytes 1 | tf_op jit(solution)/shard_map/pallas_call | solution.py:248
  2.0 0.5 %collective-permute-start = (f32[32,128]{1,0:T(8,128)S(1)}, f32[32,128]{1,0:T(8,128)S(1)}, u32[]{:S(2)}, u32[]{:S(2)}) collective-permute-start(f32[32,128]{1,0:T(8,128)S(1)} %shard_map.112), channel_id=1, source_target_pairs={{0,1},{1,0},{2,3},{3,2},{4,5},{5,4},{6,7},{7,6},{8,9},{9,8},{10,11... | collective-permute-start | bytes 49160 | tf_op jit(solution)/shard_map/ppermute | solution.py:232
  2.5 0.0 slice-start.1
  2.6 0.7 %slice-done = bf16[64,128]{1,0:T(8,128)(2,1)S(1)} async-done(((bf16[128,128]{1,0:T(8,128)(2,1)}), bf16[64,128]{1,0:T(8,128)(2,1)S(1)}, s32[]{:S(2)}) %slice-start) | async-done | bytes 16408 | tf_op jit(solution)/shard_map/slice | solution.py:266
  3.3 0.0 slice-done.1
  3.3 2.6 %collective-permute-start.2 = (bf16[144,128]{1,0:T(8,128)(2,1)S(1)}, bf16[144,128]{1,0:T(8,128)(2,1)S(1)}, u32[]{:S(2)}, u32[]{:S(2)}) collective-permute-start(bf16[144,128]{1,0:T(8,128)(2,1)S(1)} %pad_maximum_fusion), channel_id=1, source_target_pairs={{0,4},{4,8},{8,12},{12,0},{1,5},{5,9},{9,13},{13,1},{2,6},{6,10},{... | collective-permute-start | bytes 110600 | tf_op jit(solution)/shard_map/ppermute | solution.py:236
  5.9 1.6 %collective-permute-start.1 = (f32[32,128]{1,0:T(8,128)S(1)}, f32[32,128]{1,0:T(8,128)S(1)}, u32[]{:S(2)}, u32[]{:S(2)}) collective-permute-start(f32[32,128]{1,0:T(8,128)S(1)} %add.26), channel_id=1, source_target_pairs={{0,2},{1,3},{2,0},{3,1},{4,6},{5,7},{6,4},{7,5},{8,10},{9,11},{10,... | collective-permute-start | bytes 49160 | tf_op jit(solution)/shard_map/ppermute | solution.py:232
  7.5 0.4 %multiply_sine_fusion = (f32[192,64]{1,0:T(8,128)S(1)}, f32[192,64]{1,0:T(8,128)S(1)}) fusion(f32[64]{0:T(128)S(1)} %multiply_power_fusion, f32[192]{0:T(256)S(1)} %add_convert_fusion.1), kind=kLoop, calls=%fused_computation | loop fusion | flops 12288 | bytes 99328 | tf_op jit(solution)/shard_map/sin | solution.py:265
  7.9 0.0 copy-start
  7.9 1.8 %collective-permute-done.1 = f32[32,128]{1,0:T(8,128)S(1)} collective-permute-done((f32[32,128]{1,0:T(8,128)S(1)}, f32[32,128]{1,0:T(8,128)S(1)}, u32[]{:S(2)}, u32[]{:S(2)}) %collective-permute-start.1) | collective-permute-done | bytes 16416 | tf_op jit(solution)/shard_map/ppermute | solution.py:232
  9.7 1.6 %collective-permute-start.3 = (bf16[16,128]{1,0:T(8,128)(2,1)S(1)}, bf16[16,128]{1,0:T(8,128)(2,1)S(1)}, u32[]{:S(2)}, u32[]{:S(2)}) collective-permute-start(bf16[16,128]{1,0:T(8,128)(2,1)S(1)} %slice.40), channel_id=1, source_target_pairs={{0,4},{4,8},{8,12},{12,0},{1,5},{5,9},{9,13},{13,1},{2,6},{6,10},{... | collective-permute-start | bytes 12296 | tf_op jit(solution)/shard_map/ppermute | solution.py:236
  11.4 0.0 copy-start.5
  11.4 0.0 copy-start.6
  11.5 0.7 %copy-done.5 = bf16[128,128]{1,0:T(8,128)(2,1)S(1)} copy-done((bf16[128,128]{1,0:T(8,128)(2,1)S(1)}, bf16[128,128]{1,0:T(8,128)(2,1)}, u32[]{:S(2)}) %copy-start.5) | copy-done | bytes 32792
  12.1 0.0 copy-done.3
  12.2 0.0 copy-done.4
  12.2 0.7 %shard_map.113 = (bf16[1024,128]{1,0:T(8,128)(2,1)S(1)}, bf16[128,128]{1,0:T(8,128)(2,1)S(1)}, f32[128,1024]{1,0:T(8,128)S(1)}, f32[128,1024]{1,0:T(8,128)S(1)},...) custom-call(f32[32,128]{1,0:T(8,128)S(1)} %add.27.low_ref, bf16[128,1024]{1,0:T(8,128)(2,1)S(1)} %copy-done.2, ...), custom_call_target="tpu_custom_call" | custom-call | flops 3145728 | bytes 3145728 | tf_op jit(solution)/shard_map/pallas_call | solution.py:272
  12.9 0.8 %shard_map.114 = (f32[192,1024]{1,0:T(8,128)S(1)}, bf16[128,64]{1,0:T(8,128)(2,1)S(1)}, f32[192,128]{1,0:T(8,128)S(1)}, f32[32,128]{1,0:T(8,128)S(1)}) custom-call(bf16[1024,128]{1,0:T(8,128)(2,1)S(1)} %get-tuple-element.26.qr_ref, f32[128,1024]{1,0:T(8,128)S(1)} %get-tuple-element.27.s_ref, bf16[128,1024]{1,0:T(8,128)(2,1)S(1)} %copy-done, ...), custom_call_target="tpu_custom_call" | custom-call | flops 5242880 | bytes 5242880 | tf_op jit(solution)/shard_map/pallas_call | solution.py:286
  13.6 1.6 %collective-permute-done.3 = bf16[16,128]{1,0:T(8,128)(2,1)S(1)} collective-permute-done((bf16[16,128]{1,0:T(8,128)(2,1)S(1)}, bf16[16,128]{1,0:T(8,128)(2,1)S(1)}, u32[]{:S(2)}, u32[]{:S(2)}) %collective-permute-start.3) | collective-permute-done | bytes 4128 | tf_op jit(solution)/shard_map/ppermute | solution.py:236
  15.2 0.8 %collective-permute-start.4 = (f32[16,128]{1,0:T(8,128)S(1)}, f32[16,128]{1,0:T(8,128)S(1)}, u32[]{:S(2)}, u32[]{:S(2)}) collective-permute-start(f32[16,128]{1,0:T(8,128)S(1)} %slice.36), channel_id=1, source_target_pairs={{0,12},{4,0},{8,4},{12,8},{1,13},{5,1},{9,5},{13,9},{2,14},{6,2},{... | collective-permute-start | bytes 24584 | tf_op jit(solution)/shard_map/ppermute | solution.py:236
  16.0 0.9 %shard_map.115 = (f32[16,128]{1,0:T(8,128)S(1)}, bf16[16,1152]{1,0:T(8,128)(2,1)S(1)}) custom-call(f32[32,128]{1,0:T(8,128)S(1)} %add.27.low_ref, bf16[1,16,128]{2,1,0:T(8,128)(2,1)S(1)} %bitcast.7, bf16[1,144,128]{2,1,0:T(8,128)(2,1)S(1)} %bitcast.6, bf16[128,1024]{1,0:T(8,128)(2,1)S(1)} %copy-done, f32[192,1024]{1,0:T(8,128)S(1)} %get-tuple-element.30.w_ref, ...), custom_call_target="tpu_custom_call" | custom-call | flops 6291456 | bytes 6291456 | tf_op jit(solution)/shard_map/pallas_call | solution.py:301
  16.8 2.0 %collective-permute-done.4 = f32[16,128]{1,0:T(8,128)S(1)} collective-permute-done((f32[16,128]{1,0:T(8,128)S(1)}, f32[16,128]{1,0:T(8,128)S(1)}, u32[]{:S(2)}, u32[]{:S(2)}) %collective-permute-start.4) | collective-permute-done | bytes 8224 | tf_op jit(solution)/shard_map/ppermute | solution.py:236
  18.9 1.2 %collective-permute-done.5 = f32[32,128]{1,0:T(8,128)S(1)} collective-permute-done((f32[32,128]{1,0:T(8,128)S(1)}, f32[32,128]{1,0:T(8,128)S(1)}, u32[]{:S(2)}, u32[]{:S(2)}) %collective-permute-start.5) | collective-permute-done | bytes 16416 | tf_op jit(solution)/shard_map/ppermute | solution.py:232
  20.0 1.5 %collective-permute-start.6 = (f32[32,128]{1,0:T(8,128)S(1)}, f32[32,128]{1,0:T(8,128)S(1)}, u32[]{:S(2)}, u32[]{:S(2)}) collective-permute-start(f32[32,128]{1,0:T(8,128)S(1)} %fusion), channel_id=1, source_target_pairs={{0,2},{1,3},{2,0},{3,1},{4,6},{5,7},{6,4},{7,5},{8,10},{9,11},{10,... | collective-permute-start | bytes 49160 | tf_op jit(solution)/shard_map/ppermute | solution.py:232
  21.5 2.2 %collective-permute-done.6 = f32[32,128]{1,0:T(8,128)S(1)} collective-permute-done((f32[32,128]{1,0:T(8,128)S(1)}, f32[32,128]{1,0:T(8,128)S(1)}, u32[]{:S(2)}, u32[]{:S(2)}) %collective-permute-start.6) | collective-permute-done | bytes 16416 | tf_op jit(solution)/shard_map/ppermute | solution.py:232
  23.8 0.2 shard_map.116.mine_ref
  24.0 0.2 collective-permute-start.7
  24.2 3.0 %collective-permute-start.8 = (bf16[32,2688]{1,0:T(8,128)(2,1)S(1)}, bf16[32,2688]{1,0:T(8,128)(2,1)S(1)}, u32[]{:S(2)}, u32[]{:S(2)}) collective-permute-start(bf16[32,2688]{1,0:T(8,128)(2,1)S(1)} %shard_map.116.mine_ref), channel_id=1, source_target_pairs={{0,8},{4,12},{8,0},{12,4},{1,9},{5,13},{9,1},{13,5},{2,10},{6,14},... | collective-permute-start | bytes 516104 | tf_op jit(solution)/shard_map/ppermute | solution.py:232
  27.2 1.3 %collective-permute-start.9 = (bf16[32,2688]{1,0:T(8,128)(2,1)S(1)}, bf16[32,2688]{1,0:T(8,128)(2,1)S(1)}, u32[]{:S(2)}, u32[]{:S(2)}) collective-permute-start(bf16[32,2688]{1,0:T(8,128)(2,1)S(1)} %shard_map.116.mine_ref), channel_id=1, source_target_pairs={{0,12},{4,8},{8,4},{12,0},{1,13},{5,9},{9,5},{13,1},{2,14},{6,10},... | collective-permute-start | bytes 516104 | tf_op jit(solution)/shard_map/ppermute | solution.py:232
  28.5 3.6 %collective-permute-done.7.one_ref = bf16[32,2688]{1,0:T(8,128)(2,1)S(1)} collective-permute-done((bf16[32,2688]{1,0:T(8,128)(2,1)S(1)}, bf16[32,2688]{1,0:T(8,128)(2,1)S(1)}, u32[]{:S(2)}, u32[]{:S(2)}) %collective-permute-start.7) | collective-permute-done | bytes 172064 | tf_op jit(solution)/shard_map/ppermute | solution.py:232
  32.0 7.7 %collective-permute-done.8.two_ref = bf16[32,2688]{1,0:T(8,128)(2,1)S(1)} collective-permute-done((bf16[32,2688]{1,0:T(8,128)(2,1)S(1)}, bf16[32,2688]{1,0:T(8,128)(2,1)S(1)}, u32[]{:S(2)}, u32[]{:S(2)}) %collective-permute-start.8) | collective-permute-done | bytes 172064 | tf_op jit(solution)/shard_map/ppermute | solution.py:232
  39.7 0.8 %shard_map.117 = (f32[32,2048]{1,0:T(8,128)}, f32[16,1024]{1,0:T(8,128)}, f32[16,128]{1,0:T(8,128)}) custom-call(bf16[32,2688]{1,0:T(8,128)(2,1)S(1)} %shard_map.116.mine_ref, bf16[32,2688]{1,0:T(8,128)(2,1)S(1)} %collective-permute-done.7.one_ref, bf16[32,2688]{1,0:T(8,128)(2,1)S(1)} %collective-permute-done.8.two_ref, ...), custom_call_target="tpu_custom_call" | custom-call | flops 1 | bytes 1 | tf_op jit(solution)/shard_map/pallas_call | solution.py:317
  (32 shorter events, 0.1 us)
Async XLA Ops:
  0.6 1.9 %copy-start.7 = (s32[128]{0:T(128)S(1)}, s32[128]{0:T(128)}, u32[]{:S(2)}) copy-start(s32[128]{0:T(128)} %param.14) | copy-start | bytes 1540
  2.0 3.9 %collective-permute-start = (f32[32,128]{1,0:T(8,128)S(1)}, f32[32,128]{1,0:T(8,128)S(1)}, u32[]{:S(2)}, u32[]{:S(2)}) collective-permute-start(f32[32,128]{1,0:T(8,128)S(1)} %shard_map.112), channel_id=1, source_target_pairs={{0,1},{1,0},{2,3},{3,2},{4,5},{5,4},{6,7},{7,6},{8,9},{9,8},{10,11... | collective-permute-start | bytes 49160 | tf_op jit(solution)/shard_map/ppermute | solution.py:232
  2.5 0.7 %slice-start = ((bf16[128,128]{1,0:T(8,128)(2,1)}), bf16[64,128]{1,0:T(8,128)(2,1)S(1)}, s32[]{:S(2)}) async-start(bf16[128,128]{1,0:T(8,128)(2,1)} %k_ref.1), calls=%async_computation | async-start | bytes 32768 | tf_op jit(solution)/shard_map/slice | solution.py:266
  2.5 0.7 %slice-start.1 = ((bf16[128,128]{1,0:T(8,128)(2,1)}), bf16[64,128]{1,0:T(8,128)(2,1)S(1)}, s32[]{:S(2)}) async-start(bf16[128,128]{1,0:T(8,128)(2,1)} %v_ref.1), calls=%async_computation.1 | async-start | bytes 32768 | tf_op jit(solution)/shard_map/slice | solution.py:266
  3.3 9.6 %collective-permute-start.2 = (bf16[144,128]{1,0:T(8,128)(2,1)S(1)}, bf16[144,128]{1,0:T(8,128)(2,1)S(1)}, u32[]{:S(2)}, u32[]{:S(2)}) collective-permute-start(bf16[144,128]{1,0:T(8,128)(2,1)S(1)} %pad_maximum_fusion), channel_id=1, source_target_pairs={{0,4},{4,8},{8,12},{12,0},{1,5},{5,9},{9,13},{13,1},{2,6},{6,10},{... | collective-permute-start | bytes 110600 | tf_op jit(solution)/shard_map/ppermute | solution.py:236
  5.9 3.8 %collective-permute-start.1 = (f32[32,128]{1,0:T(8,128)S(1)}, f32[32,128]{1,0:T(8,128)S(1)}, u32[]{:S(2)}, u32[]{:S(2)}) collective-permute-start(f32[32,128]{1,0:T(8,128)S(1)} %add.26), channel_id=1, source_target_pairs={{0,2},{1,3},{2,0},{3,1},{4,6},{5,7},{6,4},{7,5},{8,10},{9,11},{10,... | collective-permute-start | bytes 49160 | tf_op jit(solution)/shard_map/ppermute | solution.py:232
  7.5 4.0 %copy-start.2 = (bf16[128,1024]{1,0:T(8,128)(2,1)S(1)}, bf16[128,1024]{1,0:T(8,128)(2,1)}, u32[]{:S(2)}) copy-start(bf16[128,1024]{1,0:T(8,128)(2,1)} %q_ref.1) | copy-start | bytes 786436
  7.9 3.6 %copy-start = (bf16[128,1024]{1,0:T(8,128)(2,1)S(1)}, bf16[128,1024]{1,0:T(8,128)(2,1)}, u32[]{:S(2)}) copy-start(bf16[128,1024]{1,0:T(8,128)(2,1)} %o_ref.5) | copy-start | bytes 786436
  9.7 5.4 %collective-permute-start.3 = (bf16[16,128]{1,0:T(8,128)(2,1)S(1)}, bf16[16,128]{1,0:T(8,128)(2,1)S(1)}, u32[]{:S(2)}, u32[]{:S(2)}) collective-permute-start(bf16[16,128]{1,0:T(8,128)(2,1)S(1)} %slice.40), channel_id=1, source_target_pairs={{0,4},{4,8},{8,12},{12,0},{1,5},{5,9},{9,13},{13,1},{2,6},{6,10},{... | collective-permute-start | bytes 12296 | tf_op jit(solution)/shard_map/ppermute | solution.py:236
  11.4 0.8 %copy-start.5 = (bf16[128,128]{1,0:T(8,128)(2,1)S(1)}, bf16[128,128]{1,0:T(8,128)(2,1)}, u32[]{:S(2)}) copy-start(bf16[128,128]{1,0:T(8,128)(2,1)} %v_ref.1) | copy-start | bytes 98308
  11.4 0.8 %copy-start.6 = (bf16[16,128]{1,0:T(8,128)(2,1)S(1)}, bf16[16,128]{1,0:T(8,128)(2,1)}, u32[]{:S(2)}) copy-start(bf16[16,128]{1,0:T(8,128)(2,1)} %wv_ref.5) | copy-start | bytes 12292
  11.4 0.8 %copy-start.3 = (bf16[16,1024]{1,0:T(8,128)(2,1)S(1)}, bf16[16,1024]{1,0:T(8,128)(2,1)}, u32[]{:S(2)}) copy-start(bf16[16,1024]{1,0:T(8,128)(2,1)} %wq_ref.3) | copy-start | bytes 98308
  11.4 0.8 %copy-start.4 = (bf16[128,128]{1,0:T(8,128)(2,1)S(1)}, bf16[128,128]{1,0:T(8,128)(2,1)}, u32[]{:S(2)}) copy-start(bf16[128,128]{1,0:T(8,128)(2,1)} %k_ref.1) | copy-start | bytes 98308
  15.2 3.7 %collective-permute-start.4 = (f32[16,128]{1,0:T(8,128)S(1)}, f32[16,128]{1,0:T(8,128)S(1)}, u32[]{:S(2)}, u32[]{:S(2)}) collective-permute-start(f32[16,128]{1,0:T(8,128)S(1)} %slice.36), channel_id=1, source_target_pairs={{0,12},{4,0},{8,4},{12,8},{1,13},{5,1},{9,5},{13,9},{2,14},{6,2},{... | collective-permute-start | bytes 24584 | tf_op jit(solution)/shard_map/ppermute | solution.py:236
  16.0 7.8 %copy-start.1 = (bf16[128,2048]{1,0:T(8,128)(2,1)S(1)}, bf16[128,2048]{1,0:T(8,128)(2,1)}, u32[]{:S(2)}) copy-start(bf16[128,2048]{1,0:T(8,128)(2,1)} %x_ref.1) | copy-start | bytes 1572868
  18.9 1.2 %collective-permute-start.5 = (f32[32,128]{1,0:T(8,128)S(1)}, f32[32,128]{1,0:T(8,128)S(1)}, u32[]{:S(2)}, u32[]{:S(2)}) collective-permute-start(f32[32,128]{1,0:T(8,128)S(1)} %pad_maximum_fusion.1), channel_id=1, source_target_pairs={{0,1},{1,0},{2,3},{3,2},{4,5},{5,4},{6,7},{7,6},{8,9},{9,8},{10,11... | collective-permute-start | bytes 49160 | tf_op jit(solution)/shard_map/ppermute | solution.py:232
  20.0 3.7 %collective-permute-start.6 = (f32[32,128]{1,0:T(8,128)S(1)}, f32[32,128]{1,0:T(8,128)S(1)}, u32[]{:S(2)}, u32[]{:S(2)}) collective-permute-start(f32[32,128]{1,0:T(8,128)S(1)} %fusion), channel_id=1, source_target_pairs={{0,2},{1,3},{2,0},{3,1},{4,6},{5,7},{6,4},{7,5},{8,10},{9,11},{10,... | collective-permute-start | bytes 49160 | tf_op jit(solution)/shard_map/ppermute | solution.py:232
  24.0 8.0 %collective-permute-start.7 = (bf16[32,2688]{1,0:T(8,128)(2,1)S(1)}, bf16[32,2688]{1,0:T(8,128)(2,1)S(1)}, u32[]{:S(2)}, u32[]{:S(2)}) collective-permute-start(bf16[32,2688]{1,0:T(8,128)(2,1)S(1)} %shard_map.116.mine_ref), channel_id=1, source_target_pairs={{0,4},{4,0},{8,12},{12,8},{1,5},{5,1},{9,13},{13,9},{2,6},{6,2},{1... | collective-permute-start | bytes 516104 | tf_op jit(solution)/shard_map/ppermute | solution.py:232
  24.2 15.6 %collective-permute-start.8 = (bf16[32,2688]{1,0:T(8,128)(2,1)S(1)}, bf16[32,2688]{1,0:T(8,128)(2,1)S(1)}, u32[]{:S(2)}, u32[]{:S(2)}) collective-permute-start(bf16[32,2688]{1,0:T(8,128)(2,1)S(1)} %shard_map.116.mine_ref), channel_id=1, source_target_pairs={{0,8},{4,12},{8,0},{12,4},{1,9},{5,13},{9,1},{13,5},{2,10},{6,14},... | collective-permute-start | bytes 516104 | tf_op jit(solution)/shard_map/ppermute | solution.py:232
  27.2 12.5 %collective-permute-start.9 = (bf16[32,2688]{1,0:T(8,128)(2,1)S(1)}, bf16[32,2688]{1,0:T(8,128)(2,1)S(1)}, u32[]{:S(2)}, u32[]{:S(2)}) collective-permute-start(bf16[32,2688]{1,0:T(8,128)(2,1)S(1)} %shard_map.116.mine_ref), channel_id=1, source_target_pairs={{0,12},{4,8},{8,4},{12,0},{1,13},{5,9},{9,5},{13,1},{2,14},{6,10},... | collective-permute-start | bytes 516104 | tf_op jit(solution)/shard_map/ppermute | solution.py:232

commit v6 on v5

--- a/solution.py
+++ b/solution.py
@@ -18,7 +18,7 @@
 F32 = jnp.float32
 BF16 = jnp.bfloat16
 LIMIT = 40 * 1024 * 1024
-FULL = 55168 * 1024
+FULL = 55136 * 1024
 
 
 def dot(left, right, left_dim, right_dim):
@@ -41,14 +41,20 @@
     )
 
 
-def lowrank_kernel(x_hbm, a_hbm, part_ref, x_ref, a_ref, sems):
-    pairs = [(x_hbm, x_ref), (a_hbm, a_ref)]
-    copies = [pltpu.make_async_copy(src, dst, sems.at[i]) for i, (src, dst) in enumerate(pairs)]
-    for copy in copies:
-        copy.start()
+def lowrank_kernel(send, *refs):
+    sources, (part_ref, tails_ref, k_ref, v_ref, wq_ref) = refs[:5], refs[5:10]
+    x_ref, a_ref, sems = refs[10:]
+    targets = (x_ref, a_ref, k_ref, v_ref, wq_ref)
+    copies = []
+    for i, (source, target) in enumerate(zip(sources, targets)):
+        copies.append(pltpu.make_async_copy(source, target, sems.at[i]))
+        copies[-1].start()
     for copy in copies:
         copy.wait()
     part_ref[...] = dot(a_ref[...], x_ref[...], 1, 1)
+    tok = k_ref.shape[0]
+    tails_ref[0:send] = k_ref[tok - send :]
+    tails_ref[send:] = v_ref[tok - send :]
 
 
 def rotate_rows(u, cos, sin):
@@ -98,7 +104,7 @@
     keys = rotate_rows(k_ref[...].astype(F32), cos, sin)
     kt_ref[...] = keys.T.astype(BF16)
     keys = keys.astype(BF16)
-    vals = (v_ref[...].astype(F32) + SCALE * dot(low[RANK:], wv_ref[...], 0, 0)).astype(BF16)
+    vals = (v_ref[...].astype(F32) + dot(low[RANK:], wv_ref[...], 0, 0)).astype(BF16)
     seg_here = seg_ref[...].astype(F32)[0:1]
     key = lax.broadcasted_iota(jnp.int32, (tok, tok), 0)
     query = lax.broadcasted_iota(jnp.int32, (tok, tok), 1)
@@ -145,7 +151,7 @@
         w_ref[:, cut] = w
         dv = dv + dot(w.astype(BF16), head_rows(o_ref, g, count), 1, 0)
     dv_ref[...] = dv
-    codes = SCALE * split_dot(wv_ref[...], by_token(dv, send, tok), 1, 1)
+    codes = split_dot(wv_ref[...], by_token(dv, send, tok), 1, 1)
     for b in range(blocks + 1):
         code_ref[b * RANK : (b + 1) * RANK] = codes[:, b * tok : (b + 1) * tok]
 
@@ -161,7 +167,7 @@
     vals = []
     for b in range(blocks):
         rows = pack_ref[b, send : 2 * send].astype(F32)
-        add = SCALE * dot(far_ref[b], wv, 0, 0)[tok - send :]
+        add = dot(far_ref[b], wv, 0, 0)[tok - send :]
         vals.append((rows + add).astype(BF16))
     vals = jnp.concatenate(vals, axis=0)
     kt = jnp.concatenate([kt_ref[...], kth_ref[...]], axis=1)
@@ -225,7 +231,7 @@
     send = longest if blocks == 1 else tok
     halo = blocks * send
     keys = halo + tok
-    direct = seq_count == 4
+    direct = seq_count == 4 and fsdp_count == 4
 
     def swap(array, axis, bit):
         size = lax.axis_size(axis)
@@ -234,6 +240,19 @@
     def shift(array, by):
         moves = [(i, (i + by) % seq_count) for i in range(seq_count)]
         return lax.ppermute(array, "seq", moves)
+
+    def near(array, bit):
+        moves = []
+        for i in range(seq_count):
+            for f in range(fsdp_count):
+                if f % 2 == 0:
+                    to, flip = i ^ 1, bit
+                elif i in (1, 2):
+                    to, flip = 3 - i, bit
+                else:
+                    to, flip = i, 2
+                moves.append((i * fsdp_count + f, to * fsdp_count + (f ^ flip)))
+        return lax.ppermute(array, ("seq", "fsdp"), moves)
 
     def sum_fsdp(array):
         if fsdp_count & (fsdp_count - 1):
@@ -245,29 +264,44 @@
         return array
 
     seg_row = segment.reshape(1, tok)
-    (part,) = call(
-        lowrank_kernel,
-        [((2 * RANK, tok), F32)],
+    part, tails, k, v, wq = call(
+        functools.partial(lowrank_kernel, send),
+        [
+            ((2 * RANK, tok), F32),
+            ((2 * send, HEAD), BF16),
+            ((tok, HEAD), BF16),
+            ((tok, HEAD), BF16),
+            (wq.shape, BF16),
+        ],
         [
             pltpu.VMEM((tok, wide), BF16),
             pltpu.VMEM((2 * RANK, wide), BF16),
-            pltpu.SemaphoreType.DMA((2,)),
+            pltpu.SemaphoreType.DMA((5,)),
         ],
         limit=FULL,
-        in_specs=[pl.BlockSpec(memory_space=pltpu.HBM)] * 2,
-    )(x, a.T)
+        in_specs=[pl.BlockSpec(memory_space=pltpu.HBM)] * 5,
+    )(x, a.T, k, v, wq)
     seg_rows = jnp.broadcast_to(seg_row, (16, tok)).astype(BF16)
+    pack = jnp.concatenate([tails, seg_rows], axis=0)
+    wv = wv * SCALE
     start = seq_index * tok
     base = start.reshape(1).astype(jnp.int32)
     freqs = ROPE_BASE ** (-(2.0 * jnp.arange(HALF, dtype=F32)) / HEAD)
     positions = (start - halo + jnp.arange(keys, dtype=jnp.int32)).astype(F32)
     angles = positions[:, None] * freqs[None, :]
     cos, sin = jnp.cos(angles), jnp.sin(angles)
-    pack = jnp.concatenate([k[tok - send :], v[tok - send :], seg_rows], axis=0)
     packs = jnp.stack([shift(pack, d) for d in range(blocks, 0, -1)])
-    low = sum_fsdp(part)
-    low, cos, sin = lax.optimization_barrier((low, cos, sin))
-    lows = jnp.stack([shift(low[RANK:].astype(BF16), d) for d in range(blocks, 0, -1)])
+    if direct:
+        part = part + swap(part, "fsdp", 1)
+        low = part + swap(part, "fsdp", 2)
+        far = (near(part[RANK:], 0) + near(part[RANK:], 2)).astype(BF16)
+        early = (low, cos, sin, far, packs, wv)
+        low, cos, sin, far, packs, wv = lax.optimization_barrier(early)
+        mine = (seq_index == 2) == (lax.axis_index("fsdp") % 2 == 1)
+        lows = jnp.where(mine, far, swap(far, "fsdp", 1))[None]
+    else:
+        low = sum_fsdp(part)
+        lows = jnp.stack([shift(low[RANK:].astype(BF16), d) for d in range(blocks, 0, -1)])
     count = heads if blocks == 1 else 1
     qr, kt, s, dp, cos_t, sin_t = call(
         functools.partial(project_kernel, count, heads),

time: 40.8 us -> 42.3 us (1.037)
  starting transfers between devices: 13 us -> 14.8 us
  local copies, waits for them, and re-layouts: 1.5 us -> 0.2 us
  waiting for transfers between devices: 20.1 us -> 20.8 us
    ppermute x3 -> x2, waiting for transfers between devices: 3.59 us -> 0.54 us  [shift(): return lax.ppermute(array, 'seq', moves)]
    ppermute x0 -> x2, starting transfers between devices: none -> 3.02 us  [near(): return lax.ppermute(array, ('seq', 'fsdp'), moves)]
    ppermute x0 -> x2, waiting for transfers between devices: none -> 2.66 us  [near(): return lax.ppermute(array, ('seq', 'fsdp'), moves)]
    ppermute x7 -> x8, starting transfers between devices: 8.02 us -> 6.42 us  [swap(): return lax.ppermute(array, axis, [(i, i ^ bit) for i in range(size)])]
    ppermute x7 -> x8, waiting for transfers between devices: 16.5 us -> 17.6 us  [swap(): return lax.ppermute(array, axis, [(i, i ^ bit) for i in range(size)])]
    slice x5 -> x1, local copies, waits for them, and re-layouts: 0.72 us -> 0.01 us  [body(): far = (near(part[RANK:], 0) + near(part[RANK:], 2)).astype(BF16)]
    unnamed x16 -> x14, local copies, waits for them, and re-layouts: 0.76 us -> 0.16 us
    ppermute x3 -> x2, starting transfers between devices: 4.98 us -> 5.38 us  [shift(): return lax.ppermute(array, 'seq', moves)]
  transfers between devices with their start and end apart: 10 -> 12, of which waited for: 7 -> 8; matrix products, arithmetic and copies ran while one was open for 1% -> 1% of each run, Pallas kernels for 6% -> 5%
where the time goes in v6:
time: 42.3 us; the launch traced here: 42.2 us
  waiting for transfers between devices  20.8 us (49%)
  starting transfers between devices  14.8 us (35%)
  Pallas kernels  5 us (12%)
  between operations  0.87 us (2%)
  other arithmetic  0.49 us (1%)
    ppermute x8, waiting for transfers between devices, swap(): return lax.ppermute(array, axis, [(i, i ^ bit) for i in range(size)])  17.6 us
    ppermute x8, starting transfers between devices, swap(): return lax.ppermute(array, axis, [(i, i ^ bit) for i in range(size)])  6.42 us
    ppermute x2, starting transfers between devices, shift(): return lax.ppermute(array, 'seq', moves)  5.38 us
    ppermute x2, starting transfers between devices, near(): return lax.ppermute(array, ('seq', 'fsdp'), moves)  3.02 us
    ppermute x2, waiting for transfers between devices, near(): return lax.ppermute(array, ('seq', 'fsdp'), moves)  2.66 us
    pallas_call x1, Pallas kernels, body(): call(functools.partial(lowrank_kernel, send), [((2 * RANK, tok), F32), ((...  1.74 us
    pallas_call x1, Pallas kernels, body(): call(functools.partial(grads_kernel, count, send, blocks, heads), [((RANK...  0.86 us
  transfers between devices with their start and end apart: 12, of which 8 were waited for; matrix products, arithmetic and copies ran while one was open for 1% of the time, Pallas kernels for 5%

profile of v6, /device:TPU:0, one launch (start us, length us, event | category | flops | bytes accessed | tf_op | source)
XLA Modules:
  0.0 42.2 jit_solution(13627938261623988215)
XLA Ops:
  0.6 1.7 %shard_map.112 = (f32[32,128]{1,0:T(8,128)S(1)}, bf16[128,128]{1,0:T(8,128)(2,1)S(1)}, bf16[128,128]{1,0:T(8,128)(2,1)S(1)}, bf16[128,128]{1,0:T(8,128)(2,1)}, bf16[16,1024]{1,0:T(8,128)(2,1)}) custom-call(bf16[128,2048]{1,0:T(8,128)(2,1)} %x_ref.1, bf16[32,2048]{1,0:T(8,128)(2,1)} %bitcast.8, bf16[128,128]{1,0:T(8,128)(2,1)} %refs_2_.1, ...), custom_call_target="tpu_custom_call" | custom-call | flops 1 | bytes 1 | tf_op jit(solution)/shard_map/pallas_call | solution.py:267
  2.4 0.0 copy-start.6
  2.4 0.5 %collective-permute-start = (f32[32,128]{1,0:T(8,128)S(1)}, f32[32,128]{1,0:T(8,128)S(1)}, u32[]{:S(2)}, u32[]{:S(2)}) collective-permute-start(f32[32,128]{1,0:T(8,128)S(1)} %get-tuple-element.31), channel_id=1, source_target_pairs={{0,1},{1,0},{2,3},{3,2},{4,5},{5,4},{6,7},{7,6},{8,9},{9,8},{10,11... | collective-permute-start | bytes 49160 | tf_op jit(solution)/shard_map/ppermute | solution.py:238
  2.9 0.1 copy-done.6
  3.1 3.1 %collective-permute-start.4 = (bf16[144,128]{1,0:T(8,128)(2,1)S(1)}, bf16[144,128]{1,0:T(8,128)(2,1)S(1)}, u32[]{:S(2)}, u32[]{:S(2)}) collective-permute-start(bf16[144,128]{1,0:T(8,128)(2,1)S(1)} %pad_maximum_fusion), channel_id=1, source_target_pairs={{0,4},{4,8},{8,12},{12,0},{1,5},{5,9},{9,13},{13,1},{2,6},{6,10},{... | collective-permute-start | bytes 110600 | tf_op jit(solution)/shard_map/ppermute | solution.py:242
  6.2 0.4 multiply_sine_fusion
  6.6 0.0 copy-start.5
  6.6 0.0 copy-start.3
  6.6 0.0 copy-start
  6.6 0.0 copy-start.2
  6.7 2.6 %collective-permute-start.3 = (f32[16,128]{1,0:T(8,128)S(1)}, f32[16,128]{1,0:T(8,128)S(1)}, u32[]{:S(2)}, u32[]{:S(2)}) collective-permute-start(f32[16,128]{1,0:T(8,128)S(1)} %slice.29), channel_id=1, source_target_pairs={{0,6},{1,3},{2,4},{3,1},{4,2},{5,11},{6,0},{7,9},{8,14},{9,7},{10,... | collective-permute-start | bytes 24584 | tf_op jit(solution)/shard_map/ppermute | solution.py:255
  9.2 0.4 %collective-permute-start.2 = (f32[16,128]{1,0:T(8,128)S(1)}, f32[16,128]{1,0:T(8,128)S(1)}, u32[]{:S(2)}, u32[]{:S(2)}) collective-permute-start(f32[16,128]{1,0:T(8,128)S(1)} %slice.29), channel_id=1, source_target_pairs={{0,4},{1,3},{2,6},{3,1},{4,0},{5,9},{6,2},{7,11},{8,12},{9,5},{10,... | collective-permute-start | bytes 24584 | tf_op jit(solution)/shard_map/ppermute | solution.py:255
  9.7 0.5 %collective-permute-start.1 = (f32[32,128]{1,0:T(8,128)S(1)}, f32[32,128]{1,0:T(8,128)S(1)}, u32[]{:S(2)}, u32[]{:S(2)}) collective-permute-start(f32[32,128]{1,0:T(8,128)S(1)} %add.33), channel_id=1, source_target_pairs={{0,2},{1,3},{2,0},{3,1},{4,6},{5,7},{6,4},{7,5},{8,10},{9,11},{10,... | collective-permute-start | bytes 49160 | tf_op jit(solution)/shard_map/ppermute | solution.py:238
  10.2 1.1 %collective-permute-done.3 = f32[16,128]{1,0:T(8,128)S(1)} collective-permute-done((f32[16,128]{1,0:T(8,128)S(1)}, f32[16,128]{1,0:T(8,128)S(1)}, u32[]{:S(2)}, u32[]{:S(2)}) %collective-permute-start.3) | collective-permute-done | bytes 8224 | tf_op jit(solution)/shard_map/ppermute | solution.py:255
  11.4 1.5 %collective-permute-done.2 = f32[16,128]{1,0:T(8,128)S(1)} collective-permute-done((f32[16,128]{1,0:T(8,128)S(1)}, f32[16,128]{1,0:T(8,128)S(1)}, u32[]{:S(2)}, u32[]{:S(2)}) %collective-permute-start.2) | collective-permute-done | bytes 8224 | tf_op jit(solution)/shard_map/ppermute | solution.py:255
  12.9 0.5 %collective-permute-done.1 = f32[32,128]{1,0:T(8,128)S(1)} collective-permute-done((f32[32,128]{1,0:T(8,128)S(1)}, f32[32,128]{1,0:T(8,128)S(1)}, u32[]{:S(2)}, u32[]{:S(2)}) %collective-permute-start.1) | collective-permute-done | bytes 16416 | tf_op jit(solution)/shard_map/ppermute | solution.py:238
  13.4 0.0 collective-permute-done.4
  13.4 0.1 collective-permute-start.5
  13.6 0.7 %shard_map.113 = (bf16[1024,128]{1,0:T(8,128)(2,1)S(1)}, bf16[128,128]{1,0:T(8,128)(2,1)S(1)}, f32[128,1024]{1,0:T(8,128)S(1)}, f32[128,1024]{1,0:T(8,128)S(1)},...) custom-call(f32[32,128]{1,0:T(8,128)S(1)} %add.34.low_ref, bf16[128,1024]{1,0:T(8,128)(2,1)S(1)} %copy-done.2, ...), custom_call_target="tpu_custom_call" | custom-call | flops 3145728 | bytes 3145728 | tf_op jit(solution)/shard_map/pallas_call | solution.py:306
  14.3 0.8 %shard_map.114 = (f32[192,1024]{1,0:T(8,128)S(1)}, bf16[128,64]{1,0:T(8,128)(2,1)S(1)}, f32[192,128]{1,0:T(8,128)S(1)}, f32[32,128]{1,0:T(8,128)S(1)}) custom-call(bf16[1024,128]{1,0:T(8,128)(2,1)S(1)} %get-tuple-element.40.qr_ref, f32[128,1024]{1,0:T(8,128)S(1)} %get-tuple-element.41.s_ref, bf16[128,1024]{1,0:T(8,128)(2,1)S(1)} %copy-done, ...), custom_call_target="tpu_custom_call" | custom-call | flops 5242880 | bytes 5242880 | tf_op jit(solution)/shard_map/pallas_call | solution.py:320
  15.1 2.3 %collective-permute-start.6 = (f32[16,128]{1,0:T(8,128)S(1)}, f32[16,128]{1,0:T(8,128)S(1)}, u32[]{:S(2)}, u32[]{:S(2)}) collective-permute-start(f32[16,128]{1,0:T(8,128)S(1)} %slice.28), channel_id=1, source_target_pairs={{0,12},{4,0},{8,4},{12,8},{1,13},{5,1},{9,5},{13,9},{2,14},{6,2},{... | collective-permute-start | bytes 24584 | tf_op jit(solution)/shard_map/ppermute | solution.py:242
  17.4 0.9 %shard_map.115 = (f32[16,128]{1,0:T(8,128)S(1)}, bf16[16,1152]{1,0:T(8,128)(2,1)S(1)}) custom-call(f32[32,128]{1,0:T(8,128)S(1)} %add.34.low_ref, bf16[1,16,128]{2,1,0:T(8,128)(2,1)S(1)} %select_bitcast_fusion.far_ref, bf16[1,144,128]{2,1,0:T(8,128)(2,1)S(1)} %bitcast.7, bf16[128,1024]{1,0:T(8,128)(2,1)S(1)} %copy-done, ...), custom_call_target="tpu_custom_call" | custom-call | flops 6291456 | bytes 6291456 | tf_op jit(solution)/shard_map/pallas_call | solution.py:335
  18.3 0.5 %collective-permute-done.6 = f32[16,128]{1,0:T(8,128)S(1)} collective-permute-done((f32[16,128]{1,0:T(8,128)S(1)}, f32[16,128]{1,0:T(8,128)S(1)}, u32[]{:S(2)}, u32[]{:S(2)}) %collective-permute-start.6) | collective-permute-done | bytes 8224 | tf_op jit(solution)/shard_map/ppermute | solution.py:242
  18.8 1.2 %collective-permute-done.7 = f32[32,128]{1,0:T(8,128)S(1)} collective-permute-done((f32[32,128]{1,0:T(8,128)S(1)}, f32[32,128]{1,0:T(8,128)S(1)}, u32[]{:S(2)}, u32[]{:S(2)}) %collective-permute-start.7) | collective-permute-done | bytes 16416 | tf_op jit(solution)/shard_map/ppermute | solution.py:238
  20.0 0.5 %collective-permute-start.8 = (f32[32,128]{1,0:T(8,128)S(1)}, f32[32,128]{1,0:T(8,128)S(1)}, u32[]{:S(2)}, u32[]{:S(2)}) collective-permute-start(f32[32,128]{1,0:T(8,128)S(1)} %fusion), channel_id=1, source_target_pairs={{0,2},{1,3},{2,0},{3,1},{4,6},{5,7},{6,4},{7,5},{8,10},{9,11},{10,... | collective-permute-start | bytes 49160 | tf_op jit(solution)/shard_map/ppermute | solution.py:238
  20.5 3.2 %collective-permute-done.8 = f32[32,128]{1,0:T(8,128)S(1)} collective-permute-done((f32[32,128]{1,0:T(8,128)S(1)}, f32[32,128]{1,0:T(8,128)S(1)}, u32[]{:S(2)}, u32[]{:S(2)}) %collective-permute-start.8) | collective-permute-done | bytes 16416 | tf_op jit(solution)/shard_map/ppermute | solution.py:238
  23.7 0.2 shard_map.116.mine_ref
  23.9 4.1 %collective-permute-start.11 = (bf16[32,2688]{1,0:T(8,128)(2,1)S(1)}, bf16[32,2688]{1,0:T(8,128)(2,1)S(1)}, u32[]{:S(2)}, u32[]{:S(2)}) collective-permute-start(bf16[32,2688]{1,0:T(8,128)(2,1)S(1)} %shard_map.116.mine_ref), channel_id=1, source_target_pairs={{0,12},{4,8},{8,4},{12,0},{1,13},{5,9},{9,5},{13,1},{2,14},{6,10},... | collective-permute-start | bytes 516104 | tf_op jit(solution)/shard_map/ppermute | solution.py:238
  28.0 0.6 %collective-permute-start.9 = (bf16[32,2688]{1,0:T(8,128)(2,1)S(1)}, bf16[32,2688]{1,0:T(8,128)(2,1)S(1)}, u32[]{:S(2)}, u32[]{:S(2)}) collective-permute-start(bf16[32,2688]{1,0:T(8,128)(2,1)S(1)} %shard_map.116.mine_ref), channel_id=1, source_target_pairs={{0,4},{4,0},{8,12},{12,8},{1,5},{5,1},{9,13},{13,9},{2,6},{6,2},{1... | collective-permute-start | bytes 516104 | tf_op jit(solution)/shard_map/ppermute | solution.py:238
  28.7 4.7 %collective-permute-done.11.three_ref = bf16[32,2688]{1,0:T(8,128)(2,1)S(1)} collective-permute-done((bf16[32,2688]{1,0:T(8,128)(2,1)S(1)}, bf16[32,2688]{1,0:T(8,128)(2,1)S(1)}, u32[]{:S(2)}, u32[]{:S(2)}) %collective-permute-start.11) | collective-permute-done | bytes 172064 | tf_op jit(solution)/shard_map/ppermute | solution.py:238
  33.4 8.0 %collective-permute-done.10.two_ref = bf16[32,2688]{1,0:T(8,128)(2,1)S(1)} collective-permute-done((bf16[32,2688]{1,0:T(8,128)(2,1)S(1)}, bf16[32,2688]{1,0:T(8,128)(2,1)S(1)}, u32[]{:S(2)}, u32[]{:S(2)}) %collective-permute-start.10) | collective-permute-done | bytes 172064 | tf_op jit(solution)/shard_map/ppermute | solution.py:238
  41.4 0.8 %shard_map.117 = (f32[32,2048]{1,0:T(8,128)}, f32[16,1024]{1,0:T(8,128)}, f32[16,128]{1,0:T(8,128)}) custom-call(bf16[32,2688]{1,0:T(8,128)(2,1)S(1)} %shard_map.116.mine_ref, bf16[32,2688]{1,0:T(8,128)(2,1)S(1)} %collective-permute-done.9.one_ref, bf16[32,2688]{1,0:T(8,128)(2,1)S(1)} %collective-permute-done.10.two_ref, ...), custom_call_target="tpu_custom_call" | custom-call | flops 1 | bytes 1 | tf_op jit(solution)/shard_map/pallas_call | solution.py:351
  (33 shorter events, 0.1 us)
Async XLA Ops:
  2.4 0.7 %copy-start.6 = (s32[128]{0:T(128)S(1)}, s32[128]{0:T(128)}, u32[]{:S(2)}) copy-start(s32[128]{0:T(128)} %param.14) | copy-start | bytes 1540
  2.4 4.2 %collective-permute-start = (f32[32,128]{1,0:T(8,128)S(1)}, f32[32,128]{1,0:T(8,128)S(1)}, u32[]{:S(2)}, u32[]{:S(2)}) collective-permute-start(f32[32,128]{1,0:T(8,128)S(1)} %get-tuple-element.31), channel_id=1, source_target_pairs={{0,1},{1,0},{2,3},{3,2},{4,5},{5,4},{6,7},{7,6},{8,9},{9,8},{10,11... | collective-permute-start | bytes 49160 | tf_op jit(solution)/shard_map/ppermute | solution.py:238
  3.1 10.4 %collective-permute-start.4 = (bf16[144,128]{1,0:T(8,128)(2,1)S(1)}, bf16[144,128]{1,0:T(8,128)(2,1)S(1)}, u32[]{:S(2)}, u32[]{:S(2)}) collective-permute-start(bf16[144,128]{1,0:T(8,128)(2,1)S(1)} %pad_maximum_fusion), channel_id=1, source_target_pairs={{0,4},{4,8},{8,12},{12,0},{1,5},{5,9},{9,13},{13,1},{2,6},{6,10},{... | collective-permute-start | bytes 110600 | tf_op jit(solution)/shard_map/ppermute | solution.py:242
  6.1 7.4 %copy-start.4 = (bf16[128,128]{1,0:T(8,128)(2,1)S(1)}, bf16[128,128]{1,0:T(8,128)(2,1)}, u32[]{:S(2)}) copy-start(bf16[128,128]{1,0:T(8,128)(2,1)} %get-tuple-element.35.v_ref) | copy-start | bytes 98308
  6.6 3.1 %copy-start.5 = (bf16[16,128]{1,0:T(8,128)(2,1)S(1)}, bf16[16,128]{1,0:T(8,128)(2,1)}, u32[]{:S(2)}) copy-start(bf16[16,128]{1,0:T(8,128)(2,1)} %param.17) | copy-start | bytes 12292
  6.6 7.0 %copy-start.3 = (bf16[16,1024]{1,0:T(8,128)(2,1)S(1)}, bf16[16,1024]{1,0:T(8,128)(2,1)}, u32[]{:S(2)}) copy-start(bf16[16,1024]{1,0:T(8,128)(2,1)} %get-tuple-element.38.wq_ref) | copy-start | bytes 98308
  6.6 7.0 %copy-start = (bf16[128,1024]{1,0:T(8,128)(2,1)S(1)}, bf16[128,1024]{1,0:T(8,128)(2,1)}, u32[]{:S(2)}) copy-start(bf16[128,1024]{1,0:T(8,128)(2,1)} %o_ref.5) | copy-start | bytes 786436
  6.6 7.0 %copy-start.2 = (bf16[128,1024]{1,0:T(8,128)(2,1)S(1)}, bf16[128,1024]{1,0:T(8,128)(2,1)}, u32[]{:S(2)}) copy-start(bf16[128,1024]{1,0:T(8,128)(2,1)} %q_ref.1) | copy-start | bytes 786436
  6.7 4.7 %collective-permute-start.3 = (f32[16,128]{1,0:T(8,128)S(1)}, f32[16,128]{1,0:T(8,128)S(1)}, u32[]{:S(2)}, u32[]{:S(2)}) collective-permute-start(f32[16,128]{1,0:T(8,128)S(1)} %slice.29), channel_id=1, source_target_pairs={{0,6},{1,3},{2,4},{3,1},{4,2},{5,11},{6,0},{7,9},{8,14},{9,7},{10,... | collective-permute-start | bytes 24584 | tf_op jit(solution)/shard_map/ppermute | solution.py:255
  9.2 3.7 %collective-permute-start.2 = (f32[16,128]{1,0:T(8,128)S(1)}, f32[16,128]{1,0:T(8,128)S(1)}, u32[]{:S(2)}, u32[]{:S(2)}) collective-permute-start(f32[16,128]{1,0:T(8,128)S(1)} %slice.29), channel_id=1, source_target_pairs={{0,4},{1,3},{2,6},{3,1},{4,0},{5,9},{6,2},{7,11},{8,12},{9,5},{10,... | collective-permute-start | bytes 24584 | tf_op jit(solution)/shard_map/ppermute | solution.py:255
  9.7 3.7 %collective-permute-start.1 = (f32[32,128]{1,0:T(8,128)S(1)}, f32[32,128]{1,0:T(8,128)S(1)}, u32[]{:S(2)}, u32[]{:S(2)}) collective-permute-start(f32[32,128]{1,0:T(8,128)S(1)} %add.33), channel_id=1, source_target_pairs={{0,2},{1,3},{2,0},{3,1},{4,6},{5,7},{6,4},{7,5},{8,10},{9,11},{10,... | collective-permute-start | bytes 49160 | tf_op jit(solution)/shard_map/ppermute | solution.py:238
  13.4 1.6 %collective-permute-start.5 = (bf16[16,128]{1,0:T(8,128)(2,1)S(1)}, bf16[16,128]{1,0:T(8,128)(2,1)S(1)}, u32[]{:S(2)}, u32[]{:S(2)}) collective-permute-start(bf16[16,128]{1,0:T(8,128)(2,1)S(1)} %add_convert_fusion.1), channel_id=1, source_target_pairs={{0,1},{1,0},{2,3},{3,2},{4,5},{5,4},{6,7},{7,6},{8,9},{9,8},{10,11... | collective-permute-start | bytes 12296 | tf_op jit(solution)/shard_map/ppermute | solution.py:238
  15.1 3.7 %collective-permute-start.6 = (f32[16,128]{1,0:T(8,128)S(1)}, f32[16,128]{1,0:T(8,128)S(1)}, u32[]{:S(2)}, u32[]{:S(2)}) collective-permute-start(f32[16,128]{1,0:T(8,128)S(1)} %slice.28), channel_id=1, source_target_pairs={{0,12},{4,0},{8,4},{12,8},{1,13},{5,1},{9,5},{13,9},{2,14},{6,2},{... | collective-permute-start | bytes 24584 | tf_op jit(solution)/shard_map/ppermute | solution.py:242
  17.4 6.3 %copy-start.1 = (bf16[128,2048]{1,0:T(8,128)(2,1)S(1)}, bf16[128,2048]{1,0:T(8,128)(2,1)}, u32[]{:S(2)}) copy-start(bf16[128,2048]{1,0:T(8,128)(2,1)} %x_ref.1) | copy-start | bytes 1572868
  18.8 1.2 %collective-permute-start.7 = (f32[32,128]{1,0:T(8,128)S(1)}, f32[32,128]{1,0:T(8,128)S(1)}, u32[]{:S(2)}, u32[]{:S(2)}) collective-permute-start(f32[32,128]{1,0:T(8,128)S(1)} %pad_maximum_fusion.1), channel_id=1, source_target_pairs={{0,1},{1,0},{2,3},{3,2},{4,5},{5,4},{6,7},{7,6},{8,9},{9,8},{10,11... | collective-permute-start | bytes 49160 | tf_op jit(solution)/shard_map/ppermute | solution.py:238
  20.0 3.7 %collective-permute-start.8 = (f32[32,128]{1,0:T(8,128)S(1)}, f32[32,128]{1,0:T(8,128)S(1)}, u32[]{:S(2)}, u32[]{:S(2)}) collective-permute-start(f32[32,128]{1,0:T(8,128)S(1)} %fusion), channel_id=1, source_target_pairs={{0,2},{1,3},{2,0},{3,1},{4,6},{5,7},{6,4},{7,5},{8,10},{9,11},{10,... | collective-permute-start | bytes 49160 | tf_op jit(solution)/shard_map/ppermute | solution.py:238
  23.9 9.5 %collective-permute-start.11 = (bf16[32,2688]{1,0:T(8,128)(2,1)S(1)}, bf16[32,2688]{1,0:T(8,128)(2,1)S(1)}, u32[]{:S(2)}, u32[]{:S(2)}) collective-permute-start(bf16[32,2688]{1,0:T(8,128)(2,1)S(1)} %shard_map.116.mine_ref), channel_id=1, source_target_pairs={{0,12},{4,8},{8,4},{12,0},{1,13},{5,9},{9,5},{13,1},{2,14},{6,10},... | collective-permute-start | bytes 516104 | tf_op jit(solution)/shard_map/ppermute | solution.py:238
  28.0 13.3 %collective-permute-start.10 = (bf16[32,2688]{1,0:T(8,128)(2,1)S(1)}, bf16[32,2688]{1,0:T(8,128)(2,1)S(1)}, u32[]{:S(2)}, u32[]{:S(2)}) collective-permute-start(bf16[32,2688]{1,0:T(8,128)(2,1)S(1)} %shard_map.116.mine_ref), channel_id=1, source_target_pairs={{0,8},{4,12},{8,0},{12,4},{1,9},{5,13},{9,1},{13,5},{2,10},{6,14},... | collective-permute-start | bytes 516104 | tf_op jit(solution)/shard_map/ppermute | solution.py:238
  28.0 13.3 %collective-permute-start.9 = (bf16[32,2688]{1,0:T(8,128)(2,1)S(1)}, bf16[32,2688]{1,0:T(8,128)(2,1)S(1)}, u32[]{:S(2)}, u32[]{:S(2)}) collective-permute-start(bf16[32,2688]{1,0:T(8,128)(2,1)S(1)} %shard_map.116.mine_ref), channel_id=1, source_target_pairs={{0,4},{4,0},{8,12},{12,8},{1,5},{5,1},{9,13},{13,9},{2,6},{6,2},{1... | collective-permute-start | bytes 516104 | tf_op jit(solution)/shard_map/ppermute | solution.py:238

commit v7 on v6

--- a/solution.py
+++ b/solution.py
@@ -18,7 +18,7 @@
 F32 = jnp.float32
 BF16 = jnp.bfloat16
 LIMIT = 40 * 1024 * 1024
-FULL = 55136 * 1024
+FULL = 55080 * 1024
 
 
 def dot(left, right, left_dim, right_dim):
@@ -197,27 +197,32 @@
     part_ref[...] = dot(dl_ref[...], x_ref[...], 1, 0)
 
 
-def partial_kernel(own_ref, x_ref, up_ref, send_ref):
-    part = dot(own_ref[...], x_ref[...], 1, 0).astype(BF16)
-    wide, size = part.shape[1], up_ref.shape[1]
-    half = send_ref.shape[1] - wide
-    send_ref[:, :wide] = part
-    send_ref[:RANK, wide:] = up_ref[:, :half]
-    send_ref[RANK:, wide : wide + size - half] = up_ref[:, half:]
-    if 2 * half > size:
-        send_ref[RANK:, wide + size - half :] = jnp.zeros((RANK, 2 * half - size), BF16)
-
-
-def final_kernel(mine_ref, one_ref, two_ref, three_ref, down_ref, upq_ref, upv_ref):
-    near = mine_ref[...].astype(F32) + one_ref[...].astype(F32)
-    far = two_ref[...].astype(F32) + three_ref[...].astype(F32)
-    total = near + far
+def partial_kernel(own_ref, x_ref, *refs):
+    send_ref = refs[-1]
+    wide = x_ref.shape[1]
+    send_ref[:, :wide] = dot(own_ref[...], x_ref[...], 1, 0).astype(BF16)
+    if len(refs) == 2:
+        send_ref[:, wide:] = refs[0][...]
+
+
+def add_four(refs):
+    first, second, third, fourth = [ref[...].astype(F32) for ref in refs]
+    return (first + second) + (third + fourth)
+
+
+def queries_kernel(*refs):
+    down_ref, upq_ref, upv_ref = refs[4:]
+    total = add_four(refs[:4])
     wide, size = down_ref.shape[1], upq_ref.shape[1]
-    half = total.shape[1] - wide
     down_ref[...] = total[:, :wide]
-    upq_ref[:, :half] = total[:RANK, wide:]
-    upq_ref[:, half:] = total[RANK:, wide : wide + size - half]
-    upv_ref[...] = total[RANK:, wide + size - half : wide + size - half + HEAD]
+    upq_ref[...] = total[:, wide : wide + size]
+    upv_ref[...] = total[:, wide + size :]
+
+
+def values_kernel(*refs):
+    down_ref = refs[5]
+    down_ref[:RANK] = refs[4][...]
+    down_ref[RANK:] = add_four(refs[:4])
 
 
 def body(x, q, k, v, o, segment, a, wq, wv):
@@ -240,19 +245,6 @@
     def shift(array, by):
         moves = [(i, (i + by) % seq_count) for i in range(seq_count)]
         return lax.ppermute(array, "seq", moves)
-
-    def near(array, bit):
-        moves = []
-        for i in range(seq_count):
-            for f in range(fsdp_count):
-                if f % 2 == 0:
-                    to, flip = i ^ 1, bit
-                elif i in (1, 2):
-                    to, flip = 3 - i, bit
-                else:
-                    to, flip = i, 2
-                moves.append((i * fsdp_count + f, to * fsdp_count + (f ^ flip)))
-        return lax.ppermute(array, ("seq", "fsdp"), moves)
 
     def sum_fsdp(array):
         if fsdp_count & (fsdp_count - 1):
@@ -291,17 +283,9 @@
     angles = positions[:, None] * freqs[None, :]
     cos, sin = jnp.cos(angles), jnp.sin(angles)
     packs = jnp.stack([shift(pack, d) for d in range(blocks, 0, -1)])
-    if direct:
-        part = part + swap(part, "fsdp", 1)
-        low = part + swap(part, "fsdp", 2)
-        far = (near(part[RANK:], 0) + near(part[RANK:], 2)).astype(BF16)
-        early = (low, cos, sin, far, packs, wv)
-        low, cos, sin, far, packs, wv = lax.optimization_barrier(early)
-        mine = (seq_index == 2) == (lax.axis_index("fsdp") % 2 == 1)
-        lows = jnp.where(mine, far, swap(far, "fsdp", 1))[None]
-    else:
-        low = sum_fsdp(part)
-        lows = jnp.stack([shift(low[RANK:].astype(BF16), d) for d in range(blocks, 0, -1)])
+    low = sum_fsdp(part)
+    low, cos, sin, wv = lax.optimization_barrier((low, cos, sin, wv))
+    lows = jnp.stack([shift(low[RANK:].astype(BF16), d) for d in range(blocks, 0, -1)])
     count = heads if blocks == 1 else 1
     qr, kt, s, dp, cos_t, sin_t = call(
         functools.partial(project_kernel, count, heads),
@@ -330,28 +314,36 @@
     )(qr, s, o, seg_rows, packs, base, cos[:halo], sin[:halo], wv)
     codes_v, lows = lax.optimization_barrier((codes_v, lows))
     code_v = codes_v[:RANK]
+    backs = []
     for b, d in enumerate(range(blocks, 0, -1)):
-        code_v = code_v + shift(codes_v[(b + 1) * RANK : (b + 2) * RANK], -d)
+        backs.append(shift(codes_v[(b + 1) * RANK : (b + 2) * RANK], -d))
     code_q, up = call(
         functools.partial(grads_kernel, count, send, blocks, heads),
         [((RANK, tok), F32), ((RANK, (heads + 1) * HEAD), BF16 if direct else F32)],
         [pltpu.VMEM((heads * HEAD, tok), BF16)],
         cost=6 << 20,
     )(low, lows, packs, o, w, dp, kt, kt_far, dv, cos_t, sin_t, wq, wv)
-    codes = jnp.concatenate([code_q, code_v], axis=0)
     if not direct:
-        dlow = sum_fsdp(codes).astype(BF16)
+        code_v = sum(backs, code_v)
+        dlow = sum_fsdp(jnp.concatenate([code_q, code_v], axis=0)).astype(BF16)
         (down,) = call(down_kernel, [((2 * RANK, wide), F32)])(dlow, x)
         down, up = lax.psum((down, up), "seq")
         return down.T, up[:, : heads * HEAD], up[:, heads * HEAD :]
 
-    dlow = sum_fsdp(codes).astype(BF16)
-    half = -(-(heads + 1) // 2) * HEAD
-    (mine,) = call(partial_kernel, [((2 * RANK, wide + half), BF16)])(dlow, x, up)
-    down, up_q, up_v = call(
-        final_kernel,
-        [((2 * RANK, wide), F32), ((RANK, heads * HEAD), F32), ((RANK, HEAD), F32)],
-    )(mine, *[swap(mine, "seq", bit) for bit in (1, 2, 3)])
+    up_size = (heads + 1) * HEAD
+    dlow_q = sum_fsdp(code_q).astype(BF16)
+    (mine_q,) = call(partial_kernel, [((RANK, wide + up_size), BF16)])(dlow_q, x, up)
+    all_q = [mine_q] + [swap(mine_q, "seq", bit) for bit in (1, 2, 3)]
+    code_v, mine_q = lax.optimization_barrier((code_v, mine_q))
+    dlow_v = sum_fsdp(code_v + backs[0]).astype(BF16)
+    (mine_v,) = call(partial_kernel, [((RANK, wide), BF16)])(dlow_v, x)
+    all_v = [mine_v] + [swap(mine_v, "seq", bit) for bit in (1, 2, 3)]
+    down_q, up_q, up_v = call(
+        queries_kernel,
+        [((RANK, wide), F32), ((RANK, heads * HEAD), F32), ((RANK, HEAD), F32)],
+        cost=64 << 20,
+    )(*all_q)
+    (down,) = call(values_kernel, [((2 * RANK, wide), F32)])(*all_v, down_q)
     return down.T, up_q, up_v
 
 

time: 42.3 us -> 42.6 us (level)
  waiting for transfers between devices: 20.8 us -> 18.3 us
  starting transfers between devices: 14.8 us -> 17.2 us
  Pallas kernels: 5 us -> 5.43 us
    ppermute x8 -> x12, starting transfers between devices: 6.42 us -> 12.1 us  [swap(): return lax.ppermute(array, axis, [(i, i ^ bit) for i in range(size)])]
    ppermute x2 -> x3, waiting for transfers between devices: 0.54 us -> 3.64 us  [shift(): return lax.ppermute(array, 'seq', moves)]
    ppermute x2 -> x0, starting transfers between devices: 3.02 us -> none  [near(): return lax.ppermute(array, ('seq', 'fsdp'), moves)]
    ppermute x8 -> x12, waiting for transfers between devices: 17.6 us -> 14.6 us  [swap(): return lax.ppermute(array, axis, [(i, i ^ bit) for i in range(size)])]
    ppermute x2 -> x0, waiting for transfers between devices: 2.66 us -> none  [near(): return lax.ppermute(array, ('seq', 'fsdp'), moves)]
    pallas_call x2 -> x4, Pallas kernels: 0.98 us -> 1.74 us  [the longest x1 0.75 us: body(): down, = call(values_kernel, [((2 * RANK, wide), F32)])(*all_v, down_q)]
    ppermute x2 -> x3, starting transfers between devices: 5.38 us -> 5.14 us  [shift(): return lax.ppermute(array, 'seq', moves)]
  transfers between devices with their start and end apart: 12 -> 15, of which waited for: 8 -> 8; matrix products, arithmetic and copies ran while one was open for 1% -> 1% of each run, Pallas kernels for 5% -> 6%
where the time goes in v7:
time: 42.6 us; the launch traced here: 42.4 us
  waiting for transfers between devices  18.3 us (43%)
  starting transfers between devices  17.2 us (40%)
  Pallas kernels  5.43 us (13%)
  between operations  0.79 us (2%)
  other arithmetic  0.48 us (1%)
    ppermute x12, waiting for transfers between devices, swap(): return lax.ppermute(array, axis, [(i, i ^ bit) for i in range(size)])  14.6 us
    ppermute x12, starting transfers between devices, swap(): return lax.ppermute(array, axis, [(i, i ^ bit) for i in range(size)])  12.1 us
    ppermute x3, starting transfers between devices, shift(): return lax.ppermute(array, 'seq', moves)  5.14 us
    ppermute x3, waiting for transfers between devices, shift(): return lax.ppermute(array, 'seq', moves)  3.64 us
    pallas_call x1, Pallas kernels, body(): call(functools.partial(lowrank_kernel, send), [((2 * RANK, tok), F32), ((...  1.4 us
    pallas_call x1, Pallas kernels, body(): call(functools.partial(grads_kernel, count, send, blocks, heads), [((RANK...  0.86 us
  transfers between devices with their start and end apart: 15, of which 8 were waited for; matrix products, arithmetic and copies ran while one was open for 1% of the time, Pallas kernels for 6%

profile of v7, /device:TPU:0, one launch (start us, length us, event | category | flops | bytes accessed | tf_op | source)
XLA Modules:
  0.0 42.4 jit_solution(9459317871273080596)
XLA Ops:
  0.6 1.4 %shard_map.112 = (f32[32,128]{1,0:T(8,128)S(1)}, bf16[128,128]{1,0:T(8,128)(2,1)S(1)}, bf16[128,128]{1,0:T(8,128)(2,1)S(1)}, bf16[128,128]{1,0:T(8,128)(2,1)S(1)}, bf16[16,1024]{1,0:T(8,128)(2,1)S(1)}) custom-call(bf16[128,2048]{1,0:T(8,128)(2,1)} %x_ref.3, bf16[32,2048]{1,0:T(8,128)(2,1)} %bitcast.9, bf16[128,128]{1,0:T(8,128)(2,1)} %refs_2_.1, ...), custom_call_target="tpu_custom_call" | custom-call | flops 1 | bytes 1 | tf_op jit(solution)/shard_map/pallas_call | solution.py:259
  2.1 0.5 %collective-permute-start = (f32[32,128]{1,0:T(8,128)S(1)}, f32[32,128]{1,0:T(8,128)S(1)}, u32[]{:S(2)}, u32[]{:S(2)}) collective-permute-start(f32[32,128]{1,0:T(8,128)S(1)} %get-tuple-element.30), channel_id=1, source_target_pairs={{0,1},{1,0},{2,3},{3,2},{4,5},{5,4},{6,7},{7,6},{8,9},{9,8},{10,11... | collective-permute-start | bytes 49160 | tf_op jit(solution)/shard_map/ppermute | solution.py:243
  2.6 0.1 copy-done.4
  2.7 3.1 %collective-permute-start.2 = (bf16[144,128]{1,0:T(8,128)(2,1)S(1)}, bf16[144,128]{1,0:T(8,128)(2,1)S(1)}, u32[]{:S(2)}, u32[]{:S(2)}) collective-permute-start(bf16[144,128]{1,0:T(8,128)(2,1)S(1)} %pad_maximum_fusion), channel_id=1, source_target_pairs={{0,4},{4,8},{8,12},{12,0},{1,5},{5,9},{9,13},{13,1},{2,6},{6,10},{... | collective-permute-start | bytes 110600 | tf_op jit(solution)/shard_map/ppermute | solution.py:247
  5.8 0.0 copy-start.2
  5.8 0.4 multiply_sine_fusion
  6.3 1.6 %collective-permute-start.1 = (f32[32,128]{1,0:T(8,128)S(1)}, f32[32,128]{1,0:T(8,128)S(1)}, u32[]{:S(2)}, u32[]{:S(2)}) collective-permute-start(f32[32,128]{1,0:T(8,128)S(1)} %add.32), channel_id=1, source_target_pairs={{0,2},{1,3},{2,0},{3,1},{4,6},{5,7},{6,4},{7,5},{8,10},{9,11},{10,... | collective-permute-start | bytes 49160 | tf_op jit(solution)/shard_map/ppermute | solution.py:243
  7.9 2.2 %collective-permute-done.1 = f32[32,128]{1,0:T(8,128)S(1)} collective-permute-done((f32[32,128]{1,0:T(8,128)S(1)}, f32[32,128]{1,0:T(8,128)S(1)}, u32[]{:S(2)}, u32[]{:S(2)}) %collective-permute-start.1) | collective-permute-done | bytes 16416 | tf_op jit(solution)/shard_map/ppermute | solution.py:243
  10.1 1.6 %collective-permute-start.3 = (bf16[16,128]{1,0:T(8,128)(2,1)S(1)}, bf16[16,128]{1,0:T(8,128)(2,1)S(1)}, u32[]{:S(2)}, u32[]{:S(2)}) collective-permute-start(bf16[16,128]{1,0:T(8,128)(2,1)S(1)} %slice.31), channel_id=1, source_target_pairs={{0,4},{4,8},{8,12},{12,0},{1,5},{5,9},{9,13},{13,1},{2,6},{6,10},{... | collective-permute-start | bytes 12296 | tf_op jit(solution)/shard_map/ppermute | solution.py:247
  11.8 0.7 %shard_map.113 = (bf16[1024,128]{1,0:T(8,128)(2,1)S(1)}, bf16[128,128]{1,0:T(8,128)(2,1)S(1)}, f32[128,1024]{1,0:T(8,128)S(1)}, f32[128,1024]{1,0:T(8,128)S(1)},...) custom-call(f32[32,128]{1,0:T(8,128)S(1)} %add.33.low_ref, bf16[128,1024]{1,0:T(8,128)(2,1)S(1)} %copy-done.2, ...), custom_call_target="tpu_custom_call" | custom-call | flops 3145728 | bytes 3145728 | tf_op jit(solution)/shard_map/pallas_call | solution.py:290
  12.5 0.8 %shard_map.114 = (f32[192,1024]{1,0:T(8,128)S(1)}, bf16[128,64]{1,0:T(8,128)(2,1)S(1)}, f32[192,128]{1,0:T(8,128)S(1)}, f32[32,128]{1,0:T(8,128)S(1)}) custom-call(bf16[1024,128]{1,0:T(8,128)(2,1)S(1)} %get-tuple-element.38.qr_ref, f32[128,1024]{1,0:T(8,128)S(1)} %get-tuple-element.39.s_ref, bf16[128,1024]{1,0:T(8,128)(2,1)S(1)} %copy-done.1, ...), custom_call_target="tpu_custom_call" | custom-call | flops 5242880 | bytes 5242880 | tf_op jit(solution)/shard_map/pallas_call | solution.py:304
  13.2 2.3 %collective-permute-done.3 = bf16[16,128]{1,0:T(8,128)(2,1)S(1)} collective-permute-done((bf16[16,128]{1,0:T(8,128)(2,1)S(1)}, bf16[16,128]{1,0:T(8,128)(2,1)S(1)}, u32[]{:S(2)}, u32[]{:S(2)}) %collective-permute-start.3) | collective-permute-done | bytes 4128 | tf_op jit(solution)/shard_map/ppermute | solution.py:247
  15.6 0.9 %shard_map.115 = (f32[16,128]{1,0:T(8,128)S(1)}, bf16[16,1152]{1,0:T(8,128)(2,1)S(1)}) custom-call(f32[32,128]{1,0:T(8,128)S(1)} %add.33.low_ref, bf16[1,16,128]{2,1,0:T(8,128)(2,1)S(1)} %bitcast.7, bf16[1,144,128]{2,1,0:T(8,128)(2,1)S(1)} %bitcast.6, bf16[128,1024]{1,0:T(8,128)(2,1)S(1)} %copy-done.1, f32[192,1024]{1,0:T(8,128)S(1)} %get-tuple-element.44.w_ref, ...), custom_call_target="tpu_custom_call" | custom-call | flops 6291456 | bytes 6291456 | tf_op jit(solution)/shard_map/pallas_call | solution.py:320
  16.4 0.1 collective-permute-start.4
  16.5 1.2 %collective-permute-done.4 = f32[16,128]{1,0:T(8,128)S(1)} collective-permute-done((f32[16,128]{1,0:T(8,128)S(1)}, f32[16,128]{1,0:T(8,128)S(1)}, u32[]{:S(2)}, u32[]{:S(2)}) %collective-permute-start.4) | collective-permute-done | bytes 8224 | tf_op jit(solution)/shard_map/ppermute | solution.py:243
  17.7 1.5 %collective-permute-start.5 = (f32[16,128]{1,0:T(8,128)S(1)}, f32[16,128]{1,0:T(8,128)S(1)}, u32[]{:S(2)}, u32[]{:S(2)}) collective-permute-start(f32[16,128]{1,0:T(8,128)S(1)} %add.36), channel_id=1, source_target_pairs={{0,2},{1,3},{2,0},{3,1},{4,6},{5,7},{6,4},{7,5},{8,10},{9,11},{10,... | collective-permute-start | bytes 24584 | tf_op jit(solution)/shard_map/ppermute | solution.py:243
  19.2 0.4 %collective-permute-start.6 = (f32[16,128]{1,0:T(8,128)S(1)}, f32[16,128]{1,0:T(8,128)S(1)}, u32[]{:S(2)}, u32[]{:S(2)}) collective-permute-start(f32[16,128]{1,0:T(8,128)S(1)} %get-tuple-element.57), channel_id=1, source_target_pairs={{0,12},{4,0},{8,4},{12,8},{1,13},{5,1},{9,5},{13,9},{2,14},{6,2},{... | collective-permute-start | bytes 24584 | tf_op jit(solution)/shard_map/ppermute | solution.py:247
  19.6 1.7 %collective-permute-done.5 = f32[16,128]{1,0:T(8,128)S(1)} collective-permute-done((f32[16,128]{1,0:T(8,128)S(1)}, f32[16,128]{1,0:T(8,128)S(1)}, u32[]{:S(2)}, u32[]{:S(2)}) %collective-permute-start.5) | collective-permute-done | bytes 8224 | tf_op jit(solution)/shard_map/ppermute | solution.py:243
  21.3 0.2 shard_map.116.refs_0_
  21.5 1.3 %collective-permute-done.6 = f32[16,128]{1,0:T(8,128)S(1)} collective-permute-done((f32[16,128]{1,0:T(8,128)S(1)}, f32[16,128]{1,0:T(8,128)S(1)}, u32[]{:S(2)}, u32[]{:S(2)}) %collective-permute-start.6) | collective-permute-done | bytes 8224 | tf_op jit(solution)/shard_map/ppermute | solution.py:247
  22.8 1.2 %collective-permute-done.7 = f32[16,128]{1,0:T(8,128)S(1)} collective-permute-done((f32[16,128]{1,0:T(8,128)S(1)}, f32[16,128]{1,0:T(8,128)S(1)}, u32[]{:S(2)}, u32[]{:S(2)}) %collective-permute-start.7) | collective-permute-done | bytes 8224 | tf_op jit(solution)/shard_map/ppermute | solution.py:243
  24.0 0.5 %collective-permute-start.8 = (f32[16,128]{1,0:T(8,128)S(1)}, f32[16,128]{1,0:T(8,128)S(1)}, u32[]{:S(2)}, u32[]{:S(2)}) collective-permute-start(f32[16,128]{1,0:T(8,128)S(1)} %add.39), channel_id=1, source_target_pairs={{0,2},{1,3},{2,0},{3,1},{4,6},{5,7},{6,4},{7,5},{8,10},{9,11},{10,... | collective-permute-start | bytes 24584 | tf_op jit(solution)/shard_map/ppermute | solution.py:243
  24.5 2.6 %collective-permute-start.13 = (bf16[16,3200]{1,0:T(8,128)(2,1)S(1)}, bf16[16,3200]{1,0:T(8,128)(2,1)S(1)}, u32[]{:S(2)}, u32[]{:S(2)}) collective-permute-start(bf16[16,3200]{1,0:T(8,128)(2,1)S(1)} %shard_map.116.refs_0_), channel_id=1, source_target_pairs={{0,8},{4,12},{8,0},{12,4},{1,9},{5,13},{9,1},{13,5},{2,10},{6,14},... | collective-permute-start | bytes 307208 | tf_op jit(solution)/shard_map/ppermute | solution.py:243
  27.1 1.8 %collective-permute-start.14 = (bf16[16,3200]{1,0:T(8,128)(2,1)S(1)}, bf16[16,3200]{1,0:T(8,128)(2,1)S(1)}, u32[]{:S(2)}, u32[]{:S(2)}) collective-permute-start(bf16[16,3200]{1,0:T(8,128)(2,1)S(1)} %shard_map.116.refs_0_), channel_id=1, source_target_pairs={{0,12},{4,8},{8,4},{12,0},{1,13},{5,9},{9,5},{13,1},{2,14},{6,10},... | collective-permute-start | bytes 307208 | tf_op jit(solution)/shard_map/ppermute | solution.py:243
  28.9 0.2 shard_map.117.refs_0_
  29.1 0.1 collective-permute-start.10
  29.2 2.1 %collective-permute-start.11 = (bf16[16,2048]{1,0:T(8,128)(2,1)S(1)}, bf16[16,2048]{1,0:T(8,128)(2,1)S(1)}, u32[]{:S(2)}, u32[]{:S(2)}) collective-permute-start(bf16[16,2048]{1,0:T(8,128)(2,1)S(1)} %shard_map.117.refs_0_), channel_id=1, source_target_pairs={{0,12},{4,8},{8,4},{12,0},{1,13},{5,9},{9,5},{13,1},{2,14},{6,10},... | collective-permute-start | bytes 196616 | tf_op jit(solution)/shard_map/ppermute | solution.py:243
  31.3 1.4 %collective-permute-start.9 = (bf16[16,2048]{1,0:T(8,128)(2,1)S(1)}, bf16[16,2048]{1,0:T(8,128)(2,1)S(1)}, u32[]{:S(2)}, u32[]{:S(2)}) collective-permute-start(bf16[16,2048]{1,0:T(8,128)(2,1)S(1)} %shard_map.117.refs_0_), channel_id=1, source_target_pairs={{0,4},{4,0},{8,12},{12,8},{1,5},{5,1},{9,13},{13,9},{2,6},{6,2},{1... | collective-permute-start | bytes 196616 | tf_op jit(solution)/shard_map/ppermute | solution.py:243
  32.6 5.8 %collective-permute-done.13.refs_2_ = bf16[16,3200]{1,0:T(8,128)(2,1)S(1)} collective-permute-done((bf16[16,3200]{1,0:T(8,128)(2,1)S(1)}, bf16[16,3200]{1,0:T(8,128)(2,1)S(1)}, u32[]{:S(2)}, u32[]{:S(2)}) %collective-permute-start.13) | collective-permute-done | bytes 102432 | tf_op jit(solution)/shard_map/ppermute | solution.py:243
  38.4 0.7 %shard_map.118 = (f32[16,2048]{1,0:T(8,128)S(1)}, f32[16,1024]{1,0:T(8,128)}, f32[16,128]{1,0:T(8,128)}) custom-call(bf16[16,3200]{1,0:T(8,128)(2,1)S(1)} %shard_map.116.refs_0_, bf16[16,3200]{1,0:T(8,128)(2,1)S(1)} %collective-permute-done.12.refs_1_, bf16[16,3200]{1,0:T(8,128)(2,1)S(1)} %collective-permute-done.13.refs_2_, ...), custom_call_target="tpu_custom_call" | custom-call | flops 67108864 | bytes 67108864 | tf_op jit(solution)/shard_map/pallas_call | solution.py:341
  39.1 2.6 %collective-permute-done.10.refs_2_ = bf16[16,2048]{1,0:T(8,128)(2,1)S(1)} collective-permute-done((bf16[16,2048]{1,0:T(8,128)(2,1)S(1)}, bf16[16,2048]{1,0:T(8,128)(2,1)S(1)}, u32[]{:S(2)}, u32[]{:S(2)}) %collective-permute-start.10) | collective-permute-done | bytes 65568 | tf_op jit(solution)/shard_map/ppermute | solution.py:243
  41.7 0.7 %shard_map.119 = f32[32,2048]{1,0:T(8,128)} custom-call(bf16[16,2048]{1,0:T(8,128)(2,1)S(1)} %shard_map.117.refs_0_, bf16[16,2048]{1,0:T(8,128)(2,1)S(1)} %collective-permute-done.9.refs_1_, bf16[16,2048]{1,0:T(8,128)(2,1)S(1)} %collective-permute-done.10.refs_2_, bf16[16,2048]{1,0:T(8,128)(2,1)S(1)} %collective-permute-done.11.refs_3_, ...), custom_call_target="tpu_custom_call" | custom-call | flops 1 | bytes 1 | tf_op jit(solution)/shard_map/pallas_call | solution.py:346
  (36 shorter events, 0.1 us)
Async XLA Ops:
  2.0 0.7 %copy-start.4 = (s32[128]{0:T(128)S(1)}, s32[128]{0:T(128)}, u32[]{:S(2)}) copy-start(s32[128]{0:T(128)} %param.14) | copy-start | bytes 1540
  2.1 4.2 %collective-permute-start = (f32[32,128]{1,0:T(8,128)S(1)}, f32[32,128]{1,0:T(8,128)S(1)}, u32[]{:S(2)}, u32[]{:S(2)}) collective-permute-start(f32[32,128]{1,0:T(8,128)S(1)} %get-tuple-element.30), channel_id=1, source_target_pairs={{0,1},{1,0},{2,3},{3,2},{4,5},{5,4},{6,7},{7,6},{8,9},{9,8},{10,11... | collective-permute-start | bytes 49160 | tf_op jit(solution)/shard_map/ppermute | solution.py:243
  2.7 9.8 %collective-permute-start.2 = (bf16[144,128]{1,0:T(8,128)(2,1)S(1)}, bf16[144,128]{1,0:T(8,128)(2,1)S(1)}, u32[]{:S(2)}, u32[]{:S(2)}) collective-permute-start(bf16[144,128]{1,0:T(8,128)(2,1)S(1)} %pad_maximum_fusion), channel_id=1, source_target_pairs={{0,4},{4,8},{8,12},{12,0},{1,5},{5,9},{9,13},{13,1},{2,6},{6,10},{... | collective-permute-start | bytes 110600 | tf_op jit(solution)/shard_map/ppermute | solution.py:247
  5.8 2.1 %copy-start.3 = (bf16[16,128]{1,0:T(8,128)(2,1)S(1)}, bf16[16,128]{1,0:T(8,128)(2,1)}, u32[]{:S(2)}) copy-start(bf16[16,128]{1,0:T(8,128)(2,1)} %param.17) | copy-start | bytes 12292
  5.8 6.0 %copy-start.2 = (bf16[128,1024]{1,0:T(8,128)(2,1)S(1)}, bf16[128,1024]{1,0:T(8,128)(2,1)}, u32[]{:S(2)}) copy-start(bf16[128,1024]{1,0:T(8,128)(2,1)} %q_ref.1) | copy-start | bytes 786436
  6.3 5.5 %copy-start.1 = (bf16[128,1024]{1,0:T(8,128)(2,1)S(1)}, bf16[128,1024]{1,0:T(8,128)(2,1)}, u32[]{:S(2)}) copy-start(bf16[128,1024]{1,0:T(8,128)(2,1)} %o_ref.5) | copy-start | bytes 786436
  6.3 3.8 %collective-permute-start.1 = (f32[32,128]{1,0:T(8,128)S(1)}, f32[32,128]{1,0:T(8,128)S(1)}, u32[]{:S(2)}, u32[]{:S(2)}) collective-permute-start(f32[32,128]{1,0:T(8,128)S(1)} %add.32), channel_id=1, source_target_pairs={{0,2},{1,3},{2,0},{3,1},{4,6},{5,7},{6,4},{7,5},{8,10},{9,11},{10,... | collective-permute-start | bytes 49160 | tf_op jit(solution)/shard_map/ppermute | solution.py:243
  10.1 5.4 %collective-permute-start.3 = (bf16[16,128]{1,0:T(8,128)(2,1)S(1)}, bf16[16,128]{1,0:T(8,128)(2,1)S(1)}, u32[]{:S(2)}, u32[]{:S(2)}) collective-permute-start(bf16[16,128]{1,0:T(8,128)(2,1)S(1)} %slice.31), channel_id=1, source_target_pairs={{0,4},{4,8},{8,12},{12,0},{1,5},{5,9},{9,13},{13,1},{2,6},{6,10},{... | collective-permute-start | bytes 12296 | tf_op jit(solution)/shard_map/ppermute | solution.py:247
  15.6 5.8 %copy-start = (bf16[128,2048]{1,0:T(8,128)(2,1)S(1)}, bf16[128,2048]{1,0:T(8,128)(2,1)}, u32[]{:S(2)}) copy-start(bf16[128,2048]{1,0:T(8,128)(2,1)} %x_ref.3) | copy-start | bytes 1572868
  16.4 1.2 %collective-permute-start.4 = (f32[16,128]{1,0:T(8,128)S(1)}, f32[16,128]{1,0:T(8,128)S(1)}, u32[]{:S(2)}, u32[]{:S(2)}) collective-permute-start(f32[16,128]{1,0:T(8,128)S(1)} %get-tuple-element.51), channel_id=1, source_target_pairs={{0,1},{1,0},{2,3},{3,2},{4,5},{5,4},{6,7},{7,6},{8,9},{9,8},{10,11... | collective-permute-start | bytes 24584 | tf_op jit(solution)/shard_map/ppermute | solution.py:243
  17.7 3.7 %collective-permute-start.5 = (f32[16,128]{1,0:T(8,128)S(1)}, f32[16,128]{1,0:T(8,128)S(1)}, u32[]{:S(2)}, u32[]{:S(2)}) collective-permute-start(f32[16,128]{1,0:T(8,128)S(1)} %add.36), channel_id=1, source_target_pairs={{0,2},{1,3},{2,0},{3,1},{4,6},{5,7},{6,4},{7,5},{8,10},{9,11},{10,... | collective-permute-start | bytes 24584 | tf_op jit(solution)/shard_map/ppermute | solution.py:243
  19.2 3.7 %collective-permute-start.6 = (f32[16,128]{1,0:T(8,128)S(1)}, f32[16,128]{1,0:T(8,128)S(1)}, u32[]{:S(2)}, u32[]{:S(2)}) collective-permute-start(f32[16,128]{1,0:T(8,128)S(1)} %get-tuple-element.57), channel_id=1, source_target_pairs={{0,12},{4,0},{8,4},{12,8},{1,13},{5,1},{9,5},{13,9},{2,14},{6,2},{... | collective-permute-start | bytes 24584 | tf_op jit(solution)/shard_map/ppermute | solution.py:247
  22.8 1.2 %collective-permute-start.7 = (f32[16,128]{1,0:T(8,128)S(1)}, f32[16,128]{1,0:T(8,128)S(1)}, u32[]{:S(2)}, u32[]{:S(2)}) collective-permute-start(f32[16,128]{1,0:T(8,128)S(1)} %add.38), channel_id=1, source_target_pairs={{0,1},{1,0},{2,3},{3,2},{4,5},{5,4},{6,7},{7,6},{8,9},{9,8},{10,11... | collective-permute-start | bytes 24584 | tf_op jit(solution)/shard_map/ppermute | solution.py:243
  24.0 4.9 %collective-permute-start.8 = (f32[16,128]{1,0:T(8,128)S(1)}, f32[16,128]{1,0:T(8,128)S(1)}, u32[]{:S(2)}, u32[]{:S(2)}) collective-permute-start(f32[16,128]{1,0:T(8,128)S(1)} %add.39), channel_id=1, source_target_pairs={{0,2},{1,3},{2,0},{3,1},{4,6},{5,7},{6,4},{7,5},{8,10},{9,11},{10,... | collective-permute-start | bytes 24584 | tf_op jit(solution)/shard_map/ppermute | solution.py:243
  24.5 6.8 %collective-permute-start.12 = (bf16[16,3200]{1,0:T(8,128)(2,1)S(1)}, bf16[16,3200]{1,0:T(8,128)(2,1)S(1)}, u32[]{:S(2)}, u32[]{:S(2)}) collective-permute-start(bf16[16,3200]{1,0:T(8,128)(2,1)S(1)} %shard_map.116.refs_0_), channel_id=1, source_target_pairs={{0,4},{4,0},{8,12},{12,8},{1,5},{5,1},{9,13},{13,9},{2,6},{6,2},{1... | collective-permute-start | bytes 307208 | tf_op jit(solution)/shard_map/ppermute | solution.py:243
  24.5 13.9 %collective-permute-start.13 = (bf16[16,3200]{1,0:T(8,128)(2,1)S(1)}, bf16[16,3200]{1,0:T(8,128)(2,1)S(1)}, u32[]{:S(2)}, u32[]{:S(2)}) collective-permute-start(bf16[16,3200]{1,0:T(8,128)(2,1)S(1)} %shard_map.116.refs_0_), channel_id=1, source_target_pairs={{0,8},{4,12},{8,0},{12,4},{1,9},{5,13},{9,1},{13,5},{2,10},{6,14},... | collective-permute-start | bytes 307208 | tf_op jit(solution)/shard_map/ppermute | solution.py:243
  27.1 11.3 %collective-permute-start.14 = (bf16[16,3200]{1,0:T(8,128)(2,1)S(1)}, bf16[16,3200]{1,0:T(8,128)(2,1)S(1)}, u32[]{:S(2)}, u32[]{:S(2)}) collective-permute-start(bf16[16,3200]{1,0:T(8,128)(2,1)S(1)} %shard_map.116.refs_0_), channel_id=1, source_target_pairs={{0,12},{4,8},{8,4},{12,0},{1,13},{5,9},{9,5},{13,1},{2,14},{6,10},... | collective-permute-start | bytes 307208 | tf_op jit(solution)/shard_map/ppermute | solution.py:243
  29.1 12.6 %collective-permute-start.10 = (bf16[16,2048]{1,0:T(8,128)(2,1)S(1)}, bf16[16,2048]{1,0:T(8,128)(2,1)S(1)}, u32[]{:S(2)}, u32[]{:S(2)}) collective-permute-start(bf16[16,2048]{1,0:T(8,128)(2,1)S(1)} %shard_map.117.refs_0_), channel_id=1, source_target_pairs={{0,8},{4,12},{8,0},{12,4},{1,9},{5,13},{9,1},{13,5},{2,10},{6,14},... | collective-permute-start | bytes 196616 | tf_op jit(solution)/shard_map/ppermute | solution.py:243
  29.2 12.5 %collective-permute-start.11 = (bf16[16,2048]{1,0:T(8,128)(2,1)S(1)}, bf16[16,2048]{1,0:T(8,128)(2,1)S(1)}, u32[]{:S(2)}, u32[]{:S(2)}) collective-permute-start(bf16[16,2048]{1,0:T(8,128)(2,1)S(1)} %shard_map.117.refs_0_), channel_id=1, source_target_pairs={{0,12},{4,8},{8,4},{12,0},{1,13},{5,9},{9,5},{13,1},{2,14},{6,10},... | collective-permute-start | bytes 196616 | tf_op jit(solution)/shard_map/ppermute | solution.py:243
  31.3 10.4 %collective-permute-start.9 = (bf16[16,2048]{1,0:T(8,128)(2,1)S(1)}, bf16[16,2048]{1,0:T(8,128)(2,1)S(1)}, u32[]{:S(2)}, u32[]{:S(2)}) collective-permute-start(bf16[16,2048]{1,0:T(8,128)(2,1)S(1)} %shard_map.117.refs_0_), channel_id=1, source_target_pairs={{0,4},{4,0},{8,12},{12,8},{1,5},{5,1},{9,13},{13,9},{2,6},{6,2},{1... | collective-permute-start | bytes 196616 | tf_op jit(solution)/shard_map/ppermute | solution.py:243

commit v8 on v6

--- a/solution.py
+++ b/solution.py
@@ -18,7 +18,7 @@
 F32 = jnp.float32
 BF16 = jnp.bfloat16
 LIMIT = 40 * 1024 * 1024
-FULL = 55136 * 1024
+FULL = 55080 * 1024
 
 
 def dot(left, right, left_dim, right_dim):
@@ -197,27 +197,29 @@
     part_ref[...] = dot(dl_ref[...], x_ref[...], 1, 0)
 
 
-def partial_kernel(own_ref, x_ref, up_ref, send_ref):
+def partial_kernel(own_ref, x_ref, up_ref, near_ref, part_ref, both_ref):
     part = dot(own_ref[...], x_ref[...], 1, 0).astype(BF16)
     wide, size = part.shape[1], up_ref.shape[1]
-    half = send_ref.shape[1] - wide
-    send_ref[:, :wide] = part
-    send_ref[:RANK, wide:] = up_ref[:, :half]
-    send_ref[RANK:, wide : wide + size - half] = up_ref[:, half:]
+    half = both_ref.shape[1] - wide
+    part_ref[...] = part
+    both_ref[:, :wide] = part
+    up = (up_ref[...].astype(F32) + near_ref[...].astype(F32)).astype(BF16)
+    both_ref[:RANK, wide:] = up[:, :half]
+    both_ref[RANK:, wide : wide + size - half] = up[:, half:]
     if 2 * half > size:
-        send_ref[RANK:, wide + size - half :] = jnp.zeros((RANK, 2 * half - size), BF16)
+        both_ref[RANK:, wide + size - half :] = jnp.zeros((RANK, 2 * half - size), BF16)
 
 
 def final_kernel(mine_ref, one_ref, two_ref, three_ref, down_ref, upq_ref, upv_ref):
-    near = mine_ref[...].astype(F32) + one_ref[...].astype(F32)
-    far = two_ref[...].astype(F32) + three_ref[...].astype(F32)
-    total = near + far
-    wide, size = down_ref.shape[1], upq_ref.shape[1]
-    half = total.shape[1] - wide
-    down_ref[...] = total[:, :wide]
-    upq_ref[:, :half] = total[:RANK, wide:]
-    upq_ref[:, half:] = total[RANK:, wide : wide + size - half]
-    upv_ref[...] = total[RANK:, wide + size - half : wide + size - half + HEAD]
+    wide = one_ref.shape[1]
+    near = mine_ref[:, :wide].astype(F32) + one_ref[...].astype(F32)
+    far = two_ref[:, :wide].astype(F32) + three_ref[...].astype(F32)
+    down_ref[...] = near + far
+    up = mine_ref[:, wide:].astype(F32) + two_ref[:, wide:].astype(F32)
+    half, size = up.shape[1], upq_ref.shape[1]
+    upq_ref[:, :half] = up[:RANK]
+    upq_ref[:, half:] = up[RANK:, : size - half]
+    upv_ref[...] = up[RANK:, size - half : size - half + HEAD]
 
 
 def body(x, q, k, v, o, segment, a, wq, wv):
@@ -241,14 +243,14 @@
         moves = [(i, (i + by) % seq_count) for i in range(seq_count)]
         return lax.ppermute(array, "seq", moves)
 
-    def near(array, bit):
+    def near(array):
         moves = []
         for i in range(seq_count):
             for f in range(fsdp_count):
                 if f % 2 == 0:
-                    to, flip = i ^ 1, bit
+                    to, flip = i ^ 1, 0
                 elif i in (1, 2):
-                    to, flip = 3 - i, bit
+                    to, flip = 3 - i, 0
                 else:
                     to, flip = i, 2
                 moves.append((i * fsdp_count + f, to * fsdp_count + (f ^ flip)))
@@ -291,17 +293,13 @@
     angles = positions[:, None] * freqs[None, :]
     cos, sin = jnp.cos(angles), jnp.sin(angles)
     packs = jnp.stack([shift(pack, d) for d in range(blocks, 0, -1)])
+    low = sum_fsdp(part)
+    low, cos, sin, wv = lax.optimization_barrier((low, cos, sin, wv))
+    low_v = low[RANK:].astype(BF16)
     if direct:
-        part = part + swap(part, "fsdp", 1)
-        low = part + swap(part, "fsdp", 2)
-        far = (near(part[RANK:], 0) + near(part[RANK:], 2)).astype(BF16)
-        early = (low, cos, sin, far, packs, wv)
-        low, cos, sin, far, packs, wv = lax.optimization_barrier(early)
-        mine = (seq_index == 2) == (lax.axis_index("fsdp") % 2 == 1)
-        lows = jnp.where(mine, far, swap(far, "fsdp", 1))[None]
+        far = near(low_v)
     else:
-        low = sum_fsdp(part)
-        lows = jnp.stack([shift(low[RANK:].astype(BF16), d) for d in range(blocks, 0, -1)])
+        lows = jnp.stack([shift(low_v, d) for d in range(blocks, 0, -1)])
     count = heads if blocks == 1 else 1
     qr, kt, s, dp, cos_t, sin_t = call(
         functools.partial(project_kernel, count, heads),
@@ -328,30 +326,40 @@
         in_specs=specs,
         cost=5 << 20,
     )(qr, s, o, seg_rows, packs, base, cos[:halo], sin[:halo], wv)
-    codes_v, lows = lax.optimization_barrier((codes_v, lows))
+    if direct:
+        w, far = lax.optimization_barrier((w, far))
+        mine = (seq_index == 2) == (lax.axis_index("fsdp") % 2 == 1)
+        lows = jnp.where(mine, far, swap(far, "fsdp", 1))[None]
     code_v = codes_v[:RANK]
+    backs = []
     for b, d in enumerate(range(blocks, 0, -1)):
-        code_v = code_v + shift(codes_v[(b + 1) * RANK : (b + 2) * RANK], -d)
+        backs.append(shift(codes_v[(b + 1) * RANK : (b + 2) * RANK], -d))
     code_q, up = call(
         functools.partial(grads_kernel, count, send, blocks, heads),
         [((RANK, tok), F32), ((RANK, (heads + 1) * HEAD), BF16 if direct else F32)],
         [pltpu.VMEM((heads * HEAD, tok), BF16)],
-        cost=6 << 20,
+        cost=24 << 20,
     )(low, lows, packs, o, w, dp, kt, kt_far, dv, cos_t, sin_t, wq, wv)
-    codes = jnp.concatenate([code_q, code_v], axis=0)
     if not direct:
-        dlow = sum_fsdp(codes).astype(BF16)
+        code_v = sum(backs, code_v)
+        dlow = sum_fsdp(jnp.concatenate([code_q, code_v], axis=0)).astype(BF16)
         (down,) = call(down_kernel, [((2 * RANK, wide), F32)])(dlow, x)
         down, up = lax.psum((down, up), "seq")
         return down.T, up[:, : heads * HEAD], up[:, heads * HEAD :]
 
-    dlow = sum_fsdp(codes).astype(BF16)
+    codes = jnp.concatenate([code_q, code_v + backs[0]], axis=0)
+    near_up = swap(up, "seq", 1)
+    codes = codes + swap(codes, "fsdp", 1)
+    codes, near_up = lax.optimization_barrier((codes, near_up))
+    dlow = (codes + swap(codes, "fsdp", 2)).astype(BF16)
     half = -(-(heads + 1) // 2) * HEAD
-    (mine,) = call(partial_kernel, [((2 * RANK, wide + half), BF16)])(dlow, x, up)
+    part, both = call(
+        partial_kernel, [((2 * RANK, wide), BF16), ((2 * RANK, wide + half), BF16)]
+    )(dlow, x, up, near_up)
     down, up_q, up_v = call(
         final_kernel,
         [((2 * RANK, wide), F32), ((RANK, heads * HEAD), F32), ((RANK, HEAD), F32)],
-    )(mine, *[swap(mine, "seq", bit) for bit in (1, 2, 3)])
+    )(both, swap(part, "seq", 1), swap(both, "seq", 2), swap(part, "seq", 3))
     return down.T, up_q, up_v
 
 

time: 42.3 us -> 40.2 us (0.950); the launches traced: 42.2 us -> 39.5 us
  waiting for transfers between devices: 20.8 us -> 16.9 us
  starting transfers between devices: 14.8 us -> 16.5 us
    ppermute x8 -> x9, starting transfers between devices: 6.42 us -> 9.71 us  [swap(): return lax.ppermute(array, axis, [(i, i ^ bit) for i in range(size)])]
    ppermute x2 -> x1, waiting for transfers between devices: 2.66 us -> 0.54 us  [near(): return lax.ppermute(array, ('seq', 'fsdp'), moves)]
    ppermute x8 -> x9, waiting for transfers between devices: 17.6 us -> 15.6 us  [swap(): return lax.ppermute(array, axis, [(i, i ^ bit) for i in range(size)])]
    ppermute x2 -> x1, starting transfers between devices: 3.02 us -> 1.63 us  [near(): return lax.ppermute(array, ('seq', 'fsdp'), moves)]
  transfers between devices with their start and end apart: 12 -> 12, of which waited for: 8 -> 8; matrix products, arithmetic and copies ran while one was open for 1% -> 1% of each run, Pallas kernels for 5% -> 6%
where the time goes in v8:
time: 40.2 us; the launch traced here: 39.5 us
  waiting for transfers between devices  16.9 us (42%)
  starting transfers between devices  16.5 us (41%)
  Pallas kernels  4.65 us (12%)
  between operations  0.79 us (2%)
  other arithmetic  0.48 us (1%)
    ppermute x9, waiting for transfers between devices, swap(): return lax.ppermute(array, axis, [(i, i ^ bit) for i in range(size)])  15.6 us
    ppermute x9, starting transfers between devices, swap(): return lax.ppermute(array, axis, [(i, i ^ bit) for i in range(size)])  9.71 us
    ppermute x2, starting transfers between devices, shift(): return lax.ppermute(array, 'seq', moves)  5.14 us
    ppermute x1, starting transfers between devices, near(): return lax.ppermute(array, ('seq', 'fsdp'), moves)  1.63 us
    pallas_call x1, Pallas kernels, body(): call(functools.partial(lowrank_kernel, send), [((2 * RANK, tok), F32), ((...  1.4 us
    pallas_call x1, Pallas kernels, body(): call(functools.partial(grads_kernel, count, send, blocks, heads), [((RANK...  0.85 us
  transfers between devices with their start and end apart: 12, of which 8 were waited for; matrix products, arithmetic and copies ran while one was open for 1% of the time, Pallas kernels for 6%

profile of v8, /device:TPU:0, one launch (start us, length us, event | category | flops | bytes accessed | tf_op | source)
XLA Modules:
  0.0 39.5 jit_solution(6608066492068262564)
XLA Ops:
  0.6 1.4 %shard_map.112 = (f32[32,128]{1,0:T(8,128)S(1)}, bf16[128,128]{1,0:T(8,128)(2,1)S(1)}, bf16[128,128]{1,0:T(8,128)(2,1)S(1)}, bf16[128,128]{1,0:T(8,128)(2,1)S(1)}, bf16[16,1024]{1,0:T(8,128)(2,1)S(1)}) custom-call(bf16[128,2048]{1,0:T(8,128)(2,1)} %x_ref.1, bf16[32,2048]{1,0:T(8,128)(2,1)} %bitcast.8, bf16[128,128]{1,0:T(8,128)(2,1)} %refs_2_.1, ...), custom_call_target="tpu_custom_call" | custom-call | flops 1 | bytes 1 | tf_op jit(solution)/shard_map/pallas_call | solution.py:269
  2.0 0.0 copy-start.4
  2.1 0.5 %collective-permute-start = (f32[32,128]{1,0:T(8,128)S(1)}, f32[32,128]{1,0:T(8,128)S(1)}, u32[]{:S(2)}, u32[]{:S(2)}) collective-permute-start(f32[32,128]{1,0:T(8,128)S(1)} %get-tuple-element.33), channel_id=1, source_target_pairs={{0,1},{1,0},{2,3},{3,2},{4,5},{5,4},{6,7},{7,6},{8,9},{9,8},{10,11... | collective-permute-start | bytes 49160 | tf_op jit(solution)/shard_map/ppermute | solution.py:240
  2.6 0.1 copy-done.4
  2.7 3.1 %collective-permute-start.2 = (bf16[144,128]{1,0:T(8,128)(2,1)S(1)}, bf16[144,128]{1,0:T(8,128)(2,1)S(1)}, u32[]{:S(2)}, u32[]{:S(2)}) collective-permute-start(bf16[144,128]{1,0:T(8,128)(2,1)S(1)} %pad_maximum_fusion), channel_id=1, source_target_pairs={{0,4},{4,8},{8,12},{12,0},{1,5},{5,9},{9,13},{13,1},{2,6},{6,10},{... | collective-permute-start | bytes 110600 | tf_op jit(solution)/shard_map/ppermute | solution.py:244
  5.8 0.0 copy-start.2
  5.8 0.4 %multiply_sine_fusion = (f32[192,64]{1,0:T(8,128)S(1)}, f32[192,64]{1,0:T(8,128)S(1)}) fusion(f32[64]{0:T(128)S(1)} %multiply_power_fusion, f32[192]{0:T(256)S(1)} %add_convert_fusion.1), kind=kLoop, calls=%fused_computation | loop fusion | flops 12288 | bytes 99328 | tf_op jit(solution)/shard_map/sin | solution.py:294
  6.3 0.0 copy-start
  6.3 1.6 %collective-permute-start.1 = (f32[32,128]{1,0:T(8,128)S(1)}, f32[32,128]{1,0:T(8,128)S(1)}, u32[]{:S(2)}, u32[]{:S(2)}) collective-permute-start(f32[32,128]{1,0:T(8,128)S(1)} %add.30), channel_id=1, source_target_pairs={{0,2},{1,3},{2,0},{3,1},{4,6},{5,7},{6,4},{7,5},{8,10},{9,11},{10,... | collective-permute-start | bytes 49160 | tf_op jit(solution)/shard_map/ppermute | solution.py:240
  7.9 2.2 %collective-permute-done.1 = f32[32,128]{1,0:T(8,128)S(1)} collective-permute-done((f32[32,128]{1,0:T(8,128)S(1)}, f32[32,128]{1,0:T(8,128)S(1)}, u32[]{:S(2)}, u32[]{:S(2)}) %collective-permute-start.1) | collective-permute-done | bytes 16416 | tf_op jit(solution)/shard_map/ppermute | solution.py:240
  10.1 1.6 %collective-permute-start.3 = (bf16[16,128]{1,0:T(8,128)(2,1)S(1)}, bf16[16,128]{1,0:T(8,128)(2,1)S(1)}, u32[]{:S(2)}, u32[]{:S(2)}) collective-permute-start(bf16[16,128]{1,0:T(8,128)(2,1)S(1)} %slice.32), channel_id=1, source_target_pairs={{0,4},{1,3},{2,6},{3,1},{4,0},{5,9},{6,2},{7,11},{8,12},{9,5},{10,... | collective-permute-start | bytes 12296 | tf_op jit(solution)/shard_map/ppermute | solution.py:257
  11.8 0.7 %shard_map.113 = (bf16[1024,128]{1,0:T(8,128)(2,1)S(1)}, bf16[128,128]{1,0:T(8,128)(2,1)S(1)}, f32[128,1024]{1,0:T(8,128)S(1)}, f32[128,1024]{1,0:T(8,128)S(1)},...) custom-call(f32[32,128]{1,0:T(8,128)S(1)} %add.31.low_ref, bf16[128,1024]{1,0:T(8,128)(2,1)S(1)} %copy-done.2, ...), custom_call_target="tpu_custom_call" | custom-call | flops 3145728 | bytes 3145728 | tf_op jit(solution)/shard_map/pallas_call | solution.py:304
  12.5 0.0 collective-permute-done.2
  12.5 0.8 %shard_map.114 = (f32[192,1024]{1,0:T(8,128)S(1)}, bf16[128,64]{1,0:T(8,128)(2,1)S(1)}, f32[192,128]{1,0:T(8,128)S(1)}, f32[32,128]{1,0:T(8,128)S(1)}) custom-call(bf16[1024,128]{1,0:T(8,128)(2,1)S(1)} %get-tuple-element.41.qr_ref, f32[128,1024]{1,0:T(8,128)S(1)} %get-tuple-element.42.s_ref, bf16[128,1024]{1,0:T(8,128)(2,1)S(1)} %copy-done, ...), custom_call_target="tpu_custom_call" | custom-call | flops 5242880 | bytes 5242880 | tf_op jit(solution)/shard_map/pallas_call | solution.py:318
  13.2 0.5 %collective-permute-done.3 = bf16[16,128]{1,0:T(8,128)(2,1)S(1)} collective-permute-done((bf16[16,128]{1,0:T(8,128)(2,1)S(1)}, bf16[16,128]{1,0:T(8,128)(2,1)S(1)}, u32[]{:S(2)}, u32[]{:S(2)}) %collective-permute-start.3) | collective-permute-done | bytes 4128 | tf_op jit(solution)/shard_map/ppermute | solution.py:257
  13.8 0.0 collective-permute-start.4
  13.8 2.1 %collective-permute-start.5 = (f32[16,128]{1,0:T(8,128)S(1)}, f32[16,128]{1,0:T(8,128)S(1)}, u32[]{:S(2)}, u32[]{:S(2)}) collective-permute-start(f32[16,128]{1,0:T(8,128)S(1)} %slice.28), channel_id=1, source_target_pairs={{0,12},{4,0},{8,4},{12,8},{1,13},{5,1},{9,5},{13,9},{2,14},{6,2},{... | collective-permute-start | bytes 24584 | tf_op jit(solution)/shard_map/ppermute | solution.py:244
  15.9 0.0 collective-permute-done.4
  15.9 0.9 %shard_map.115 = (f32[16,128]{1,0:T(8,128)S(1)}, bf16[16,1152]{1,0:T(8,128)(2,1)S(1)}) custom-call(f32[32,128]{1,0:T(8,128)S(1)} %add.31.low_ref, bf16[1,16,128]{2,1,0:T(8,128)(2,1)S(1)} %select_bitcast_fusion.far_ref, bf16[1,144,128]{2,1,0:T(8,128)(2,1)S(1)} %bitcast.7, bf16[128,1024]{1,0:T(8,128)(2,1)S(1)} %copy-done, ...), custom_call_target="tpu_custom_call" | custom-call | flops 25165824 | bytes 25165824 | tf_op jit(solution)/shard_map/pallas_call | solution.py:337
  16.7 0.7 %collective-permute-done.5 = f32[16,128]{1,0:T(8,128)S(1)} collective-permute-done((f32[16,128]{1,0:T(8,128)S(1)}, f32[16,128]{1,0:T(8,128)S(1)}, u32[]{:S(2)}, u32[]{:S(2)}) %collective-permute-start.5) | collective-permute-done | bytes 8224 | tf_op jit(solution)/shard_map/ppermute | solution.py:244
  17.4 1.6 %collective-permute-start.7 = (bf16[16,1152]{1,0:T(8,128)(2,1)S(1)}, bf16[16,1152]{1,0:T(8,128)(2,1)S(1)}, u32[]{:S(2)}, u32[]{:S(2)}) collective-permute-start(bf16[16,1152]{1,0:T(8,128)(2,1)S(1)} %get-tuple-element.55.up_ref), channel_id=1, source_target_pairs={{0,4},{4,0},{8,12},{12,8},{1,5},{5,1},{9,13},{13,9},{2,6},{6,2},{1... | collective-permute-start | bytes 110600 | tf_op jit(solution)/shard_map/ppermute | solution.py:240
  19.1 2.4 %collective-permute-done.7.near_ref = bf16[16,1152]{1,0:T(8,128)(2,1)S(1)} collective-permute-done((bf16[16,1152]{1,0:T(8,128)(2,1)S(1)}, bf16[16,1152]{1,0:T(8,128)(2,1)S(1)}, u32[]{:S(2)}, u32[]{:S(2)}) %collective-permute-start.7) | collective-permute-done | bytes 36896 | tf_op jit(solution)/shard_map/ppermute | solution.py:240
  21.5 1.5 %collective-permute-start.8 = (f32[32,128]{1,0:T(8,128)S(1)}, f32[32,128]{1,0:T(8,128)S(1)}, u32[]{:S(2)}, u32[]{:S(2)}) collective-permute-start(f32[32,128]{1,0:T(8,128)S(1)} %fusion), channel_id=1, source_target_pairs={{0,2},{1,3},{2,0},{3,1},{4,6},{5,7},{6,4},{7,5},{8,10},{9,11},{10,... | collective-permute-start | bytes 49160 | tf_op jit(solution)/shard_map/ppermute | solution.py:240
  23.0 2.2 %collective-permute-done.8 = f32[32,128]{1,0:T(8,128)S(1)} collective-permute-done((f32[32,128]{1,0:T(8,128)S(1)}, f32[32,128]{1,0:T(8,128)S(1)}, u32[]{:S(2)}, u32[]{:S(2)}) %collective-permute-start.8) | collective-permute-done | bytes 16416 | tf_op jit(solution)/shard_map/ppermute | solution.py:240
  25.2 0.2 shard_map.116
  25.4 2.7 %collective-permute-start.10 = (bf16[32,2688]{1,0:T(8,128)(2,1)S(1)}, bf16[32,2688]{1,0:T(8,128)(2,1)S(1)}, u32[]{:S(2)}, u32[]{:S(2)}) collective-permute-start(bf16[32,2688]{1,0:T(8,128)(2,1)S(1)} %get-tuple-element.58.mine_ref), channel_id=1, source_target_pairs={{0,8},{4,12},{8,0},{12,4},{1,9},{5,13},{9,1},{13,5},{2,10},{6,14},... | collective-permute-start | bytes 516104 | tf_op jit(solution)/shard_map/ppermute | solution.py:240
  28.1 1.4 %collective-permute-start.11 = (bf16[32,2048]{1,0:T(8,128)(2,1)S(1)}, bf16[32,2048]{1,0:T(8,128)(2,1)S(1)}, u32[]{:S(2)}, u32[]{:S(2)}) collective-permute-start(bf16[32,2048]{1,0:T(8,128)(2,1)S(1)} %get-tuple-element.59), channel_id=1, source_target_pairs={{0,12},{4,8},{8,4},{12,0},{1,13},{5,9},{9,5},{13,1},{2,14},{6,10},... | collective-permute-start | bytes 393224 | tf_op jit(solution)/shard_map/ppermute | solution.py:240
  29.4 0.5 %collective-permute-start.9 = (bf16[32,2048]{1,0:T(8,128)(2,1)S(1)}, bf16[32,2048]{1,0:T(8,128)(2,1)S(1)}, u32[]{:S(2)}, u32[]{:S(2)}) collective-permute-start(bf16[32,2048]{1,0:T(8,128)(2,1)S(1)} %get-tuple-element.59), channel_id=1, source_target_pairs={{0,4},{4,0},{8,12},{12,8},{1,5},{5,1},{9,13},{13,9},{2,6},{6,2},{1... | collective-permute-start | bytes 393224 | tf_op jit(solution)/shard_map/ppermute | solution.py:240
  29.9 7.0 %collective-permute-done.11.three_ref = bf16[32,2048]{1,0:T(8,128)(2,1)S(1)} collective-permute-done((bf16[32,2048]{1,0:T(8,128)(2,1)S(1)}, bf16[32,2048]{1,0:T(8,128)(2,1)S(1)}, u32[]{:S(2)}, u32[]{:S(2)}) %collective-permute-start.11) | collective-permute-done | bytes 131104 | tf_op jit(solution)/shard_map/ppermute | solution.py:240
  36.9 0.9 %collective-permute-done.9.one_ref = bf16[32,2048]{1,0:T(8,128)(2,1)S(1)} collective-permute-done((bf16[32,2048]{1,0:T(8,128)(2,1)S(1)}, bf16[32,2048]{1,0:T(8,128)(2,1)S(1)}, u32[]{:S(2)}, u32[]{:S(2)}) %collective-permute-start.9) | collective-permute-done | bytes 131104 | tf_op jit(solution)/shard_map/ppermute | solution.py:240
  37.9 0.8 %collective-permute-done.10.two_ref = bf16[32,2688]{1,0:T(8,128)(2,1)S(1)} collective-permute-done((bf16[32,2688]{1,0:T(8,128)(2,1)S(1)}, bf16[32,2688]{1,0:T(8,128)(2,1)S(1)}, u32[]{:S(2)}, u32[]{:S(2)}) %collective-permute-start.10) | collective-permute-done | bytes 172064 | tf_op jit(solution)/shard_map/ppermute | solution.py:240
  38.7 0.8 %shard_map.117 = (f32[32,2048]{1,0:T(8,128)}, f32[16,1024]{1,0:T(8,128)}, f32[16,128]{1,0:T(8,128)}) custom-call(bf16[32,2688]{1,0:T(8,128)(2,1)S(1)} %get-tuple-element.58.mine_ref, bf16[32,2048]{1,0:T(8,128)(2,1)S(1)} %collective-permute-done.9.one_ref, bf16[32,2688]{1,0:T(8,128)(2,1)S(1)} %collective-permute-done.10.two_ref, ...), custom_call_target="tpu_custom_call" | custom-call | flops 1 | bytes 1 | tf_op jit(solution)/shard_map/pallas_call | solution.py:359
  (28 shorter events, 0.1 us)
Async XLA Ops:
  2.0 0.7 %copy-start.4 = (s32[128]{0:T(128)S(1)}, s32[128]{0:T(128)}, u32[]{:S(2)}) copy-start(s32[128]{0:T(128)} %param.14) | copy-start | bytes 1540
  2.1 4.2 %collective-permute-start = (f32[32,128]{1,0:T(8,128)S(1)}, f32[32,128]{1,0:T(8,128)S(1)}, u32[]{:S(2)}, u32[]{:S(2)}) collective-permute-start(f32[32,128]{1,0:T(8,128)S(1)} %get-tuple-element.33), channel_id=1, source_target_pairs={{0,1},{1,0},{2,3},{3,2},{4,5},{5,4},{6,7},{7,6},{8,9},{9,8},{10,11... | collective-permute-start | bytes 49160 | tf_op jit(solution)/shard_map/ppermute | solution.py:240
  2.7 9.8 %collective-permute-start.2 = (bf16[144,128]{1,0:T(8,128)(2,1)S(1)}, bf16[144,128]{1,0:T(8,128)(2,1)S(1)}, u32[]{:S(2)}, u32[]{:S(2)}) collective-permute-start(bf16[144,128]{1,0:T(8,128)(2,1)S(1)} %pad_maximum_fusion), channel_id=1, source_target_pairs={{0,4},{4,8},{8,12},{12,0},{1,5},{5,9},{9,13},{13,1},{2,6},{6,10},{... | collective-permute-start | bytes 110600 | tf_op jit(solution)/shard_map/ppermute | solution.py:244
  5.8 2.1 %copy-start.3 = (bf16[16,128]{1,0:T(8,128)(2,1)S(1)}, bf16[16,128]{1,0:T(8,128)(2,1)}, u32[]{:S(2)}) copy-start(bf16[16,128]{1,0:T(8,128)(2,1)} %param.17) | copy-start | bytes 12292
  5.8 6.0 %copy-start.2 = (bf16[128,1024]{1,0:T(8,128)(2,1)S(1)}, bf16[128,1024]{1,0:T(8,128)(2,1)}, u32[]{:S(2)}) copy-start(bf16[128,1024]{1,0:T(8,128)(2,1)} %q_ref.1) | copy-start | bytes 786436
  6.3 5.5 %copy-start = (bf16[128,1024]{1,0:T(8,128)(2,1)S(1)}, bf16[128,1024]{1,0:T(8,128)(2,1)}, u32[]{:S(2)}) copy-start(bf16[128,1024]{1,0:T(8,128)(2,1)} %o_ref.5) | copy-start | bytes 786436
  6.3 3.8 %collective-permute-start.1 = (f32[32,128]{1,0:T(8,128)S(1)}, f32[32,128]{1,0:T(8,128)S(1)}, u32[]{:S(2)}, u32[]{:S(2)}) collective-permute-start(f32[32,128]{1,0:T(8,128)S(1)} %add.30), channel_id=1, source_target_pairs={{0,2},{1,3},{2,0},{3,1},{4,6},{5,7},{6,4},{7,5},{8,10},{9,11},{10,... | collective-permute-start | bytes 49160 | tf_op jit(solution)/shard_map/ppermute | solution.py:240
  10.1 3.7 %collective-permute-start.3 = (bf16[16,128]{1,0:T(8,128)(2,1)S(1)}, bf16[16,128]{1,0:T(8,128)(2,1)S(1)}, u32[]{:S(2)}, u32[]{:S(2)}) collective-permute-start(bf16[16,128]{1,0:T(8,128)(2,1)S(1)} %slice.32), channel_id=1, source_target_pairs={{0,4},{1,3},{2,6},{3,1},{4,0},{5,9},{6,2},{7,11},{8,12},{9,5},{10,... | collective-permute-start | bytes 12296 | tf_op jit(solution)/shard_map/ppermute | solution.py:257
  13.8 2.1 %collective-permute-start.4 = (bf16[16,128]{1,0:T(8,128)(2,1)S(1)}, bf16[16,128]{1,0:T(8,128)(2,1)S(1)}, u32[]{:S(2)}, u32[]{:S(2)}) collective-permute-start(bf16[16,128]{1,0:T(8,128)(2,1)S(1)} %collective-permute-done.3), channel_id=1, source_target_pairs={{0,1},{1,0},{2,3},{3,2},{4,5},{5,4},{6,7},{7,6},{8,9},{9,8},{10,11... | collective-permute-start | bytes 12296 | tf_op jit(solution)/shard_map/ppermute | solution.py:240
  13.8 3.7 %collective-permute-start.5 = (f32[16,128]{1,0:T(8,128)S(1)}, f32[16,128]{1,0:T(8,128)S(1)}, u32[]{:S(2)}, u32[]{:S(2)}) collective-permute-start(f32[16,128]{1,0:T(8,128)S(1)} %slice.28), channel_id=1, source_target_pairs={{0,12},{4,0},{8,4},{12,8},{1,13},{5,1},{9,5},{13,9},{2,14},{6,2},{... | collective-permute-start | bytes 24584 | tf_op jit(solution)/shard_map/ppermute | solution.py:244
  15.9 9.4 %copy-start.1 = (bf16[128,2048]{1,0:T(8,128)(2,1)S(1)}, bf16[128,2048]{1,0:T(8,128)(2,1)}, u32[]{:S(2)}) copy-start(bf16[128,2048]{1,0:T(8,128)(2,1)} %x_ref.1) | copy-start | bytes 1572868
  17.4 1.7 %collective-permute-start.6 = (f32[32,128]{1,0:T(8,128)S(1)}, f32[32,128]{1,0:T(8,128)S(1)}, u32[]{:S(2)}, u32[]{:S(2)}) collective-permute-start(f32[32,128]{1,0:T(8,128)S(1)} %pad_maximum_fusion.1), channel_id=1, source_target_pairs={{0,1},{1,0},{2,3},{3,2},{4,5},{5,4},{6,7},{7,6},{8,9},{9,8},{10,11... | collective-permute-start | bytes 49160 | tf_op jit(solution)/shard_map/ppermute | solution.py:240
  17.4 4.0 %collective-permute-start.7 = (bf16[16,1152]{1,0:T(8,128)(2,1)S(1)}, bf16[16,1152]{1,0:T(8,128)(2,1)S(1)}, u32[]{:S(2)}, u32[]{:S(2)}) collective-permute-start(bf16[16,1152]{1,0:T(8,128)(2,1)S(1)} %get-tuple-element.55.up_ref), channel_id=1, source_target_pairs={{0,4},{4,0},{8,12},{12,8},{1,5},{5,1},{9,13},{13,9},{2,6},{6,2},{1... | collective-permute-start | bytes 110600 | tf_op jit(solution)/shard_map/ppermute | solution.py:240
  21.5 3.7 %collective-permute-start.8 = (f32[32,128]{1,0:T(8,128)S(1)}, f32[32,128]{1,0:T(8,128)S(1)}, u32[]{:S(2)}, u32[]{:S(2)}) collective-permute-start(f32[32,128]{1,0:T(8,128)S(1)} %fusion), channel_id=1, source_target_pairs={{0,2},{1,3},{2,0},{3,1},{4,6},{5,7},{6,4},{7,5},{8,10},{9,11},{10,... | collective-permute-start | bytes 49160 | tf_op jit(solution)/shard_map/ppermute | solution.py:240
  25.4 13.3 %collective-permute-start.10 = (bf16[32,2688]{1,0:T(8,128)(2,1)S(1)}, bf16[32,2688]{1,0:T(8,128)(2,1)S(1)}, u32[]{:S(2)}, u32[]{:S(2)}) collective-permute-start(bf16[32,2688]{1,0:T(8,128)(2,1)S(1)} %get-tuple-element.58.mine_ref), channel_id=1, source_target_pairs={{0,8},{4,12},{8,0},{12,4},{1,9},{5,13},{9,1},{13,5},{2,10},{6,14},... | collective-permute-start | bytes 516104 | tf_op jit(solution)/shard_map/ppermute | solution.py:240
  28.1 8.9 %collective-permute-start.11 = (bf16[32,2048]{1,0:T(8,128)(2,1)S(1)}, bf16[32,2048]{1,0:T(8,128)(2,1)S(1)}, u32[]{:S(2)}, u32[]{:S(2)}) collective-permute-start(bf16[32,2048]{1,0:T(8,128)(2,1)S(1)} %get-tuple-element.59), channel_id=1, source_target_pairs={{0,12},{4,8},{8,4},{12,0},{1,13},{5,9},{9,5},{13,1},{2,14},{6,10},... | collective-permute-start | bytes 393224 | tf_op jit(solution)/shard_map/ppermute | solution.py:240
  29.4 8.4 %collective-permute-start.9 = (bf16[32,2048]{1,0:T(8,128)(2,1)S(1)}, bf16[32,2048]{1,0:T(8,128)(2,1)S(1)}, u32[]{:S(2)}, u32[]{:S(2)}) collective-permute-start(bf16[32,2048]{1,0:T(8,128)(2,1)S(1)} %get-tuple-element.59), channel_id=1, source_target_pairs={{0,4},{4,0},{8,12},{12,8},{1,5},{5,1},{9,13},{13,9},{2,6},{6,2},{1... | collective-permute-start | bytes 393224 | tf_op jit(solution)/shard_map/ppermute | solution.py:240

commit v9 on v6

--- a/solution.py
+++ b/solution.py
@@ -18,7 +18,7 @@
 F32 = jnp.float32
 BF16 = jnp.bfloat16
 LIMIT = 40 * 1024 * 1024
-FULL = 55136 * 1024
+FULL = 55080 * 1024
 
 
 def dot(left, right, left_dim, right_dim):
@@ -208,7 +208,7 @@
         send_ref[RANK:, wide + size - half :] = jnp.zeros((RANK, 2 * half - size), BF16)
 
 
-def final_kernel(mine_ref, one_ref, two_ref, three_ref, down_ref, upq_ref, upv_ref):
+def final_kernel(mine_ref, three_ref, two_ref, one_ref, down_ref, upq_ref, upv_ref):
     near = mine_ref[...].astype(F32) + one_ref[...].astype(F32)
     far = two_ref[...].astype(F32) + three_ref[...].astype(F32)
     total = near + far
@@ -241,27 +241,24 @@
         moves = [(i, (i + by) % seq_count) for i in range(seq_count)]
         return lax.ppermute(array, "seq", moves)
 
-    def near(array, bit):
+    def near(array):
         moves = []
         for i in range(seq_count):
             for f in range(fsdp_count):
                 if f % 2 == 0:
-                    to, flip = i ^ 1, bit
+                    to, flip = i ^ 1, 0
                 elif i in (1, 2):
-                    to, flip = 3 - i, bit
+                    to, flip = 3 - i, 0
                 else:
                     to, flip = i, 2
                 moves.append((i * fsdp_count + f, to * fsdp_count + (f ^ flip)))
         return lax.ppermute(array, ("seq", "fsdp"), moves)
 
     def sum_fsdp(array):
-        if fsdp_count & (fsdp_count - 1):
+        if fsdp_count != 4:
             return lax.psum(array, "fsdp")
-        bit = 1
-        while bit < fsdp_count:
-            array = array + swap(array, "fsdp", bit)
-            bit *= 2
-        return array
+        one, two, three = [swap(array, "fsdp", bit) for bit in (1, 2, 3)]
+        return (array + one) + (two + three)
 
     seg_row = segment.reshape(1, tok)
     part, tails, k, v, wq = call(
@@ -291,17 +288,13 @@
     angles = positions[:, None] * freqs[None, :]
     cos, sin = jnp.cos(angles), jnp.sin(angles)
     packs = jnp.stack([shift(pack, d) for d in range(blocks, 0, -1)])
+    low = sum_fsdp(part)
+    low, cos, sin, wv = lax.optimization_barrier((low, cos, sin, wv))
+    low_v = low[RANK:].astype(BF16)
     if direct:
-        part = part + swap(part, "fsdp", 1)
-        low = part + swap(part, "fsdp", 2)
-        far = (near(part[RANK:], 0) + near(part[RANK:], 2)).astype(BF16)
-        early = (low, cos, sin, far, packs, wv)
-        low, cos, sin, far, packs, wv = lax.optimization_barrier(early)
-        mine = (seq_index == 2) == (lax.axis_index("fsdp") % 2 == 1)
-        lows = jnp.where(mine, far, swap(far, "fsdp", 1))[None]
+        far = near(low_v)
     else:
-        low = sum_fsdp(part)
-        lows = jnp.stack([shift(low[RANK:].astype(BF16), d) for d in range(blocks, 0, -1)])
+        lows = jnp.stack([shift(low_v, d) for d in range(blocks, 0, -1)])
     count = heads if blocks == 1 else 1
     qr, kt, s, dp, cos_t, sin_t = call(
         functools.partial(project_kernel, count, heads),
@@ -328,30 +321,36 @@
         in_specs=specs,
         cost=5 << 20,
     )(qr, s, o, seg_rows, packs, base, cos[:halo], sin[:halo], wv)
-    codes_v, lows = lax.optimization_barrier((codes_v, lows))
+    if direct:
+        w, far = lax.optimization_barrier((w, far))
+        mine = (seq_index == 2) == (lax.axis_index("fsdp") % 2 == 1)
+        lows = jnp.where(mine, far, swap(far, "fsdp", 1))[None]
     code_v = codes_v[:RANK]
+    backs = []
     for b, d in enumerate(range(blocks, 0, -1)):
-        code_v = code_v + shift(codes_v[(b + 1) * RANK : (b + 2) * RANK], -d)
+        backs.append(shift(codes_v[(b + 1) * RANK : (b + 2) * RANK], -d))
     code_q, up = call(
         functools.partial(grads_kernel, count, send, blocks, heads),
         [((RANK, tok), F32), ((RANK, (heads + 1) * HEAD), BF16 if direct else F32)],
         [pltpu.VMEM((heads * HEAD, tok), BF16)],
-        cost=6 << 20,
+        cost=24 << 20,
     )(low, lows, packs, o, w, dp, kt, kt_far, dv, cos_t, sin_t, wq, wv)
-    codes = jnp.concatenate([code_q, code_v], axis=0)
     if not direct:
-        dlow = sum_fsdp(codes).astype(BF16)
+        code_v = sum(backs, code_v)
+        dlow = sum_fsdp(jnp.concatenate([code_q, code_v], axis=0)).astype(BF16)
         (down,) = call(down_kernel, [((2 * RANK, wide), F32)])(dlow, x)
         down, up = lax.psum((down, up), "seq")
         return down.T, up[:, : heads * HEAD], up[:, heads * HEAD :]
 
+    codes = jnp.concatenate([code_q, code_v + backs[0]], axis=0)
     dlow = sum_fsdp(codes).astype(BF16)
     half = -(-(heads + 1) // 2) * HEAD
     (mine,) = call(partial_kernel, [((2 * RANK, wide + half), BF16)])(dlow, x, up)
+    three, two, one = [swap(mine, "seq", bit) for bit in (3, 2, 1)]
     down, up_q, up_v = call(
         final_kernel,
         [((2 * RANK, wide), F32), ((RANK, heads * HEAD), F32), ((RANK, HEAD), F32)],
-    )(mine, *[swap(mine, "seq", bit) for bit in (1, 2, 3)])
+    )(mine, three, two, one)
     return down.T, up_q, up_v
 
 

time: 42.3 us -> 39.7 us (0.939)
  waiting for transfers between devices: 20.8 us -> 16.4 us
  starting transfers between devices: 14.8 us -> 16.9 us
    ppermute x8 -> x10, starting transfers between devices: 6.42 us -> 9.81 us  [swap(): return lax.ppermute(array, axis, [(i, i ^ bit) for i in range(size)])]
    ppermute x2 -> x1, waiting for transfers between devices: 2.66 us -> 0.13 us  [near(): return lax.ppermute(array, ('seq', 'fsdp'), moves)]
    ppermute x8 -> x10, waiting for transfers between devices: 17.6 us -> 15.4 us  [swap(): return lax.ppermute(array, axis, [(i, i ^ bit) for i in range(size)])]
    ppermute x2 -> x1, starting transfers between devices: 3.02 us -> 1.64 us  [near(): return lax.ppermute(array, ('seq', 'fsdp'), moves)]
  transfers between devices with their start and end apart: 12 -> 13, of which waited for: 8 -> 8; matrix products, arithmetic and copies ran while one was open for 1% -> 1% of each run, Pallas kernels for 5% -> 6%
where the time goes in v9:
time: 39.7 us; the launch traced here: 39.5 us
  starting transfers between devices  16.9 us (43%)
  waiting for transfers between devices  16.4 us (41%)
  Pallas kernels  4.64 us (12%)
  between operations  0.77 us (2%)
  other arithmetic  0.48 us (1%)
    ppermute x10, waiting for transfers between devices, swap(): return lax.ppermute(array, axis, [(i, i ^ bit) for i in range(size)])  15.4 us
    ppermute x10, starting transfers between devices, swap(): return lax.ppermute(array, axis, [(i, i ^ bit) for i in range(size)])  9.81 us
    ppermute x2, starting transfers between devices, shift(): return lax.ppermute(array, 'seq', moves)  5.47 us
    ppermute x1, starting transfers between devices, near(): return lax.ppermute(array, ('seq', 'fsdp'), moves)  1.64 us
    pallas_call x1, Pallas kernels, body(): call(functools.partial(lowrank_kernel, send), [((2 * RANK, tok), F32), ((...  1.4 us
    ppermute x2, waiting for transfers between devices, shift(): return lax.ppermute(array, 'seq', moves)  0.92 us
    pallas_call x1, Pallas kernels, body(): call(functools.partial(grads_kernel, count, send, blocks, heads), [((RANK...  0.85 us
  transfers between devices with their start and end apart: 13, of which 8 were waited for; matrix products, arithmetic and copies ran while one was open for 1% of the time, Pallas kernels for 6%

profile of v9, /device:TPU:0, one launch (start us, length us, event | category | flops | bytes accessed | tf_op | source)
XLA Modules:
  0.0 39.5 jit_solution(3906892959912508015)
XLA Ops:
  0.6 1.4 %shard_map.112 = (f32[32,128]{1,0:T(8,128)S(1)}, bf16[128,128]{1,0:T(8,128)(2,1)S(1)}, bf16[128,128]{1,0:T(8,128)(2,1)S(1)}, bf16[128,128]{1,0:T(8,128)(2,1)S(1)}, bf16[16,1024]{1,0:T(8,128)(2,1)S(1)}) custom-call(bf16[128,2048]{1,0:T(8,128)(2,1)} %x_ref.1, bf16[32,2048]{1,0:T(8,128)(2,1)} %bitcast.8, bf16[128,128]{1,0:T(8,128)(2,1)} %refs_2_.1, ...), custom_call_target="tpu_custom_call" | custom-call | flops 1 | bytes 1 | tf_op jit(solution)/shard_map/pallas_call | solution.py:264
  2.0 0.0 copy-start.4
  2.1 0.5 %collective-permute-start = (f32[32,128]{1,0:T(8,128)S(1)}, f32[32,128]{1,0:T(8,128)S(1)}, u32[]{:S(2)}, u32[]{:S(2)}) collective-permute-start(f32[32,128]{1,0:T(8,128)S(1)} %get-tuple-element.29), channel_id=1, source_target_pairs={{0,1},{1,0},{2,3},{3,2},{4,5},{5,4},{6,7},{7,6},{8,9},{9,8},{10,11... | collective-permute-start | bytes 49160 | tf_op jit(solution)/shard_map/ppermute | solution.py:238
  2.6 2.6 %collective-permute-start.1 = (f32[32,128]{1,0:T(8,128)S(1)}, f32[32,128]{1,0:T(8,128)S(1)}, u32[]{:S(2)}, u32[]{:S(2)}) collective-permute-start(f32[32,128]{1,0:T(8,128)S(1)} %get-tuple-element.29), channel_id=1, source_target_pairs={{0,2},{1,3},{2,0},{3,1},{4,6},{5,7},{6,4},{7,5},{8,10},{9,11},{10,... | collective-permute-start | bytes 49160 | tf_op jit(solution)/shard_map/ppermute | solution.py:238
  5.1 0.1 collective-permute-start.2
  5.2 1.9 %collective-permute-start.3 = (bf16[144,128]{1,0:T(8,128)(2,1)S(1)}, bf16[144,128]{1,0:T(8,128)(2,1)S(1)}, u32[]{:S(2)}, u32[]{:S(2)}) collective-permute-start(bf16[144,128]{1,0:T(8,128)(2,1)S(1)} %pad_maximum_fusion), channel_id=1, source_target_pairs={{0,4},{4,8},{8,12},{12,0},{1,5},{5,9},{9,13},{13,1},{2,6},{6,10},{... | collective-permute-start | bytes 110600 | tf_op jit(solution)/shard_map/ppermute | solution.py:242
  7.1 0.0 copy-start.2
  7.1 0.4 %multiply_sine_fusion = (f32[192,64]{1,0:T(8,128)S(1)}, f32[192,64]{1,0:T(8,128)S(1)}) fusion(f32[64]{0:T(128)S(1)} %multiply_power_fusion, f32[192]{0:T(256)S(1)} %add_convert_fusion.1), kind=kLoop, calls=%fused_computation | loop fusion | flops 12288 | bytes 99328 | tf_op jit(solution)/shard_map/sin | solution.py:289
  7.6 0.2 copy-done.3
  7.8 0.0 collective-permute-done
  7.8 0.0 collective-permute-done.1
  7.8 0.5 %collective-permute-done.2 = f32[32,128]{1,0:T(8,128)S(1)} collective-permute-done((f32[32,128]{1,0:T(8,128)S(1)}, f32[32,128]{1,0:T(8,128)S(1)}, u32[]{:S(2)}, u32[]{:S(2)}) %collective-permute-start.2) | collective-permute-done | bytes 16416 | tf_op jit(solution)/shard_map/ppermute | solution.py:238
  8.3 1.6 %collective-permute-start.4 = (bf16[16,128]{1,0:T(8,128)(2,1)S(1)}, bf16[16,128]{1,0:T(8,128)(2,1)S(1)}, u32[]{:S(2)}, u32[]{:S(2)}) collective-permute-start(bf16[16,128]{1,0:T(8,128)(2,1)S(1)} %slice.32), channel_id=1, source_target_pairs={{0,4},{1,3},{2,6},{3,1},{4,0},{5,9},{6,2},{7,11},{8,12},{9,5},{10,... | collective-permute-start | bytes 12296 | tf_op jit(solution)/shard_map/ppermute | solution.py:255
  10.0 0.7 %shard_map.113 = (bf16[1024,128]{1,0:T(8,128)(2,1)S(1)}, bf16[128,128]{1,0:T(8,128)(2,1)S(1)}, f32[128,1024]{1,0:T(8,128)S(1)}, f32[128,1024]{1,0:T(8,128)S(1)},...) custom-call(f32[32,128]{1,0:T(8,128)S(1)} %add_add_fusion.low_ref, bf16[128,1024]{1,0:T(8,128)(2,1)S(1)} %copy-done.2, ...), custom_call_target="tpu_custom_call" | custom-call | flops 3145728 | bytes 3145728 | tf_op jit(solution)/shard_map/pallas_call | solution.py:299
  10.7 0.4 %collective-permute-done.3 = bf16[144,128]{1,0:T(8,128)(2,1)S(1)} collective-permute-done((bf16[144,128]{1,0:T(8,128)(2,1)S(1)}, bf16[144,128]{1,0:T(8,128)(2,1)S(1)}, u32[]{:S(2)}, u32[]{:S(2)}) %collective-permute-start.3) | collective-permute-done | bytes 36896 | tf_op jit(solution)/shard_map/ppermute | solution.py:242
  11.1 0.7 %shard_map.114 = (f32[192,1024]{1,0:T(8,128)S(1)}, bf16[128,64]{1,0:T(8,128)(2,1)S(1)}, f32[192,128]{1,0:T(8,128)S(1)}, f32[32,128]{1,0:T(8,128)S(1)}) custom-call(bf16[1024,128]{1,0:T(8,128)(2,1)S(1)} %get-tuple-element.37.qr_ref, f32[128,1024]{1,0:T(8,128)S(1)} %get-tuple-element.38.s_ref, bf16[128,1024]{1,0:T(8,128)(2,1)S(1)} %copy-done, ...), custom_call_target="tpu_custom_call" | custom-call | flops 5242880 | bytes 5242880 | tf_op jit(solution)/shard_map/pallas_call | solution.py:313
  11.9 0.1 collective-permute-done.4
  12.0 0.0 collective-permute-start.5
  12.0 3.6 %collective-permute-start.6 = (f32[16,128]{1,0:T(8,128)S(1)}, f32[16,128]{1,0:T(8,128)S(1)}, u32[]{:S(2)}, u32[]{:S(2)}) collective-permute-start(f32[16,128]{1,0:T(8,128)S(1)} %slice.28), channel_id=1, source_target_pairs={{0,12},{4,0},{8,4},{12,8},{1,13},{5,1},{9,5},{13,9},{2,14},{6,2},{... | collective-permute-start | bytes 24584 | tf_op jit(solution)/shard_map/ppermute | solution.py:242
  15.6 0.9 %shard_map.115 = (f32[16,128]{1,0:T(8,128)S(1)}, bf16[16,1152]{1,0:T(8,128)(2,1)S(1)}) custom-call(f32[32,128]{1,0:T(8,128)S(1)} %add_add_fusion.low_ref, bf16[1,16,128]{2,1,0:T(8,128)(2,1)S(1)} %select_bitcast_fusion.far_ref, bf16[1,144,128]{2,1,0:T(8,128)(2,1)S(1)} %bitcast.7, bf16[128,1024]{1,0:T(8,128)(2,1)S(1)} %copy-done, ...), custom_call_target="tpu_custom_call" | custom-call | flops 25165824 | bytes 25165824 | tf_op jit(solution)/shard_map/pallas_call | solution.py:332
  16.5 0.5 %collective-permute-done.6 = f32[16,128]{1,0:T(8,128)S(1)} collective-permute-done((f32[16,128]{1,0:T(8,128)S(1)}, f32[16,128]{1,0:T(8,128)S(1)}, u32[]{:S(2)}, u32[]{:S(2)}) %collective-permute-start.6) | collective-permute-done | bytes 8224 | tf_op jit(solution)/shard_map/ppermute | solution.py:242
  17.0 0.8 %collective-permute-start.8 = (f32[32,128]{1,0:T(8,128)S(1)}, f32[32,128]{1,0:T(8,128)S(1)}, u32[]{:S(2)}, u32[]{:S(2)}) collective-permute-start(f32[32,128]{1,0:T(8,128)S(1)} %pad_maximum_fusion.1), channel_id=1, source_target_pairs={{0,2},{1,3},{2,0},{3,1},{4,6},{5,7},{6,4},{7,5},{8,10},{9,11},{10,... | collective-permute-start | bytes 49160 | tf_op jit(solution)/shard_map/ppermute | solution.py:238
  17.8 1.1 %collective-permute-start.9 = (f32[32,128]{1,0:T(8,128)S(1)}, f32[32,128]{1,0:T(8,128)S(1)}, u32[]{:S(2)}, u32[]{:S(2)}) collective-permute-start(f32[32,128]{1,0:T(8,128)S(1)} %pad_maximum_fusion.1), channel_id=1, source_target_pairs={{0,3},{1,2},{2,1},{3,0},{4,7},{5,6},{6,5},{7,4},{8,11},{9,10},{10,... | collective-permute-start | bytes 49160 | tf_op jit(solution)/shard_map/ppermute | solution.py:238
  18.8 0.0 collective-permute-done.7
  18.8 2.0 %collective-permute-done.8 = f32[32,128]{1,0:T(8,128)S(1)} collective-permute-done((f32[32,128]{1,0:T(8,128)S(1)}, f32[32,128]{1,0:T(8,128)S(1)}, u32[]{:S(2)}, u32[]{:S(2)}) %collective-permute-start.8) | collective-permute-done | bytes 16416 | tf_op jit(solution)/shard_map/ppermute | solution.py:238
  20.8 0.1 collective-permute-done.9
  21.0 0.2 shard_map.116.mine_ref
  21.2 4.2 %collective-permute-start.10 = (bf16[32,2688]{1,0:T(8,128)(2,1)S(1)}, bf16[32,2688]{1,0:T(8,128)(2,1)S(1)}, u32[]{:S(2)}, u32[]{:S(2)}) collective-permute-start(bf16[32,2688]{1,0:T(8,128)(2,1)S(1)} %shard_map.116.mine_ref), channel_id=1, source_target_pairs={{0,12},{4,8},{8,4},{12,0},{1,13},{5,9},{9,5},{13,1},{2,14},{6,10},... | collective-permute-start | bytes 516104 | tf_op jit(solution)/shard_map/ppermute | solution.py:238
  25.3 0.6 %collective-permute-start.12 = (bf16[32,2688]{1,0:T(8,128)(2,1)S(1)}, bf16[32,2688]{1,0:T(8,128)(2,1)S(1)}, u32[]{:S(2)}, u32[]{:S(2)}) collective-permute-start(bf16[32,2688]{1,0:T(8,128)(2,1)S(1)} %shard_map.116.mine_ref), channel_id=1, source_target_pairs={{0,4},{4,0},{8,12},{12,8},{1,5},{5,1},{9,13},{13,9},{2,6},{6,2},{1... | collective-permute-start | bytes 516104 | tf_op jit(solution)/shard_map/ppermute | solution.py:238
  26.0 4.7 %collective-permute-done.10.three_ref = bf16[32,2688]{1,0:T(8,128)(2,1)S(1)} collective-permute-done((bf16[32,2688]{1,0:T(8,128)(2,1)S(1)}, bf16[32,2688]{1,0:T(8,128)(2,1)S(1)}, u32[]{:S(2)}, u32[]{:S(2)}) %collective-permute-start.10) | collective-permute-done | bytes 172064 | tf_op jit(solution)/shard_map/ppermute | solution.py:238
  30.6 8.1 %collective-permute-done.11.two_ref = bf16[32,2688]{1,0:T(8,128)(2,1)S(1)} collective-permute-done((bf16[32,2688]{1,0:T(8,128)(2,1)S(1)}, bf16[32,2688]{1,0:T(8,128)(2,1)S(1)}, u32[]{:S(2)}, u32[]{:S(2)}) %collective-permute-start.11) | collective-permute-done | bytes 172064 | tf_op jit(solution)/shard_map/ppermute | solution.py:238
  38.7 0.8 %shard_map.117 = (f32[32,2048]{1,0:T(8,128)}, f32[16,1024]{1,0:T(8,128)}, f32[16,128]{1,0:T(8,128)}) custom-call(bf16[32,2688]{1,0:T(8,128)(2,1)S(1)} %shard_map.116.mine_ref, bf16[32,2688]{1,0:T(8,128)(2,1)S(1)} %collective-permute-done.10.three_ref, bf16[32,2688]{1,0:T(8,128)(2,1)S(1)} %collective-permute-done.11.two_ref, ...), custom_call_target="tpu_custom_call" | custom-call | flops 1 | bytes 1 | tf_op jit(solution)/shard_map/pallas_call | solution.py:350
  (28 shorter events, 0.1 us)
Async XLA Ops:
  2.0 3.2 %copy-start.4 = (s32[128]{0:T(128)S(1)}, s32[128]{0:T(128)}, u32[]{:S(2)}) copy-start(s32[128]{0:T(128)} %param.14) | copy-start | bytes 1540
  2.1 5.8 %collective-permute-start = (f32[32,128]{1,0:T(8,128)S(1)}, f32[32,128]{1,0:T(8,128)S(1)}, u32[]{:S(2)}, u32[]{:S(2)}) collective-permute-start(f32[32,128]{1,0:T(8,128)S(1)} %get-tuple-element.29), channel_id=1, source_target_pairs={{0,1},{1,0},{2,3},{3,2},{4,5},{5,4},{6,7},{7,6},{8,9},{9,8},{10,11... | collective-permute-start | bytes 49160 | tf_op jit(solution)/shard_map/ppermute | solution.py:238
  2.6 5.2 %collective-permute-start.1 = (f32[32,128]{1,0:T(8,128)S(1)}, f32[32,128]{1,0:T(8,128)S(1)}, u32[]{:S(2)}, u32[]{:S(2)}) collective-permute-start(f32[32,128]{1,0:T(8,128)S(1)} %get-tuple-element.29), channel_id=1, source_target_pairs={{0,2},{1,3},{2,0},{3,1},{4,6},{5,7},{6,4},{7,5},{8,10},{9,11},{10,... | collective-permute-start | bytes 49160 | tf_op jit(solution)/shard_map/ppermute | solution.py:238
  5.1 3.2 %collective-permute-start.2 = (f32[32,128]{1,0:T(8,128)S(1)}, f32[32,128]{1,0:T(8,128)S(1)}, u32[]{:S(2)}, u32[]{:S(2)}) collective-permute-start(f32[32,128]{1,0:T(8,128)S(1)} %get-tuple-element.29), channel_id=1, source_target_pairs={{0,3},{1,2},{2,1},{3,0},{4,7},{5,6},{6,5},{7,4},{8,11},{9,10},{10,... | collective-permute-start | bytes 49160 | tf_op jit(solution)/shard_map/ppermute | solution.py:238
  5.2 5.9 %collective-permute-start.3 = (bf16[144,128]{1,0:T(8,128)(2,1)S(1)}, bf16[144,128]{1,0:T(8,128)(2,1)S(1)}, u32[]{:S(2)}, u32[]{:S(2)}) collective-permute-start(bf16[144,128]{1,0:T(8,128)(2,1)S(1)} %pad_maximum_fusion), channel_id=1, source_target_pairs={{0,4},{4,8},{8,12},{12,0},{1,5},{5,9},{9,13},{13,1},{2,6},{6,10},{... | collective-permute-start | bytes 110600 | tf_op jit(solution)/shard_map/ppermute | solution.py:242
  7.1 0.7 %copy-start.3 = (bf16[16,128]{1,0:T(8,128)(2,1)S(1)}, bf16[16,128]{1,0:T(8,128)(2,1)}, u32[]{:S(2)}) copy-start(bf16[16,128]{1,0:T(8,128)(2,1)} %param.17) | copy-start | bytes 12292
  7.1 2.9 %copy-start.2 = (bf16[128,1024]{1,0:T(8,128)(2,1)S(1)}, bf16[128,1024]{1,0:T(8,128)(2,1)}, u32[]{:S(2)}) copy-start(bf16[128,1024]{1,0:T(8,128)(2,1)} %q_ref.1) | copy-start | bytes 786436
  7.8 2.2 %copy-start = (bf16[128,1024]{1,0:T(8,128)(2,1)S(1)}, bf16[128,1024]{1,0:T(8,128)(2,1)}, u32[]{:S(2)}) copy-start(bf16[128,1024]{1,0:T(8,128)(2,1)} %o_ref.5) | copy-start | bytes 786436
  8.3 3.7 %collective-permute-start.4 = (bf16[16,128]{1,0:T(8,128)(2,1)S(1)}, bf16[16,128]{1,0:T(8,128)(2,1)S(1)}, u32[]{:S(2)}, u32[]{:S(2)}) collective-permute-start(bf16[16,128]{1,0:T(8,128)(2,1)S(1)} %slice.32), channel_id=1, source_target_pairs={{0,4},{1,3},{2,6},{3,1},{4,0},{5,9},{6,2},{7,11},{8,12},{9,5},{10,... | collective-permute-start | bytes 12296 | tf_op jit(solution)/shard_map/ppermute | solution.py:255
  12.0 3.6 %collective-permute-start.5 = (bf16[16,128]{1,0:T(8,128)(2,1)S(1)}, bf16[16,128]{1,0:T(8,128)(2,1)S(1)}, u32[]{:S(2)}, u32[]{:S(2)}) collective-permute-start(bf16[16,128]{1,0:T(8,128)(2,1)S(1)} %collective-permute-done.4), channel_id=1, source_target_pairs={{0,1},{1,0},{2,3},{3,2},{4,5},{5,4},{6,7},{7,6},{8,9},{9,8},{10,11... | collective-permute-start | bytes 12296 | tf_op jit(solution)/shard_map/ppermute | solution.py:238
  12.0 5.0 %collective-permute-start.6 = (f32[16,128]{1,0:T(8,128)S(1)}, f32[16,128]{1,0:T(8,128)S(1)}, u32[]{:S(2)}, u32[]{:S(2)}) collective-permute-start(f32[16,128]{1,0:T(8,128)S(1)} %slice.28), channel_id=1, source_target_pairs={{0,12},{4,0},{8,4},{12,8},{1,13},{5,1},{9,5},{13,9},{2,14},{6,2},{... | collective-permute-start | bytes 24584 | tf_op jit(solution)/shard_map/ppermute | solution.py:242
  15.6 5.4 %copy-start.1 = (bf16[128,2048]{1,0:T(8,128)(2,1)S(1)}, bf16[128,2048]{1,0:T(8,128)(2,1)}, u32[]{:S(2)}) copy-start(bf16[128,2048]{1,0:T(8,128)(2,1)} %x_ref.1) | copy-start | bytes 1572868
  17.0 1.9 %collective-permute-start.7 = (f32[32,128]{1,0:T(8,128)S(1)}, f32[32,128]{1,0:T(8,128)S(1)}, u32[]{:S(2)}, u32[]{:S(2)}) collective-permute-start(f32[32,128]{1,0:T(8,128)S(1)} %pad_maximum_fusion.1), channel_id=1, source_target_pairs={{0,1},{1,0},{2,3},{3,2},{4,5},{5,4},{6,7},{7,6},{8,9},{9,8},{10,11... | collective-permute-start | bytes 49160 | tf_op jit(solution)/shard_map/ppermute | solution.py:238
  17.0 3.8 %collective-permute-start.8 = (f32[32,128]{1,0:T(8,128)S(1)}, f32[32,128]{1,0:T(8,128)S(1)}, u32[]{:S(2)}, u32[]{:S(2)}) collective-permute-start(f32[32,128]{1,0:T(8,128)S(1)} %pad_maximum_fusion.1), channel_id=1, source_target_pairs={{0,2},{1,3},{2,0},{3,1},{4,6},{5,7},{6,4},{7,5},{8,10},{9,11},{10,... | collective-permute-start | bytes 49160 | tf_op jit(solution)/shard_map/ppermute | solution.py:238
  17.8 3.2 %collective-permute-start.9 = (f32[32,128]{1,0:T(8,128)S(1)}, f32[32,128]{1,0:T(8,128)S(1)}, u32[]{:S(2)}, u32[]{:S(2)}) collective-permute-start(f32[32,128]{1,0:T(8,128)S(1)} %pad_maximum_fusion.1), channel_id=1, source_target_pairs={{0,3},{1,2},{2,1},{3,0},{4,7},{5,6},{6,5},{7,4},{8,11},{9,10},{10,... | collective-permute-start | bytes 49160 | tf_op jit(solution)/shard_map/ppermute | solution.py:238
  21.2 9.4 %collective-permute-start.10 = (bf16[32,2688]{1,0:T(8,128)(2,1)S(1)}, bf16[32,2688]{1,0:T(8,128)(2,1)S(1)}, u32[]{:S(2)}, u32[]{:S(2)}) collective-permute-start(bf16[32,2688]{1,0:T(8,128)(2,1)S(1)} %shard_map.116.mine_ref), channel_id=1, source_target_pairs={{0,12},{4,8},{8,4},{12,0},{1,13},{5,9},{9,5},{13,1},{2,14},{6,10},... | collective-permute-start | bytes 516104 | tf_op jit(solution)/shard_map/ppermute | solution.py:238
  25.3 13.4 %collective-permute-start.11 = (bf16[32,2688]{1,0:T(8,128)(2,1)S(1)}, bf16[32,2688]{1,0:T(8,128)(2,1)S(1)}, u32[]{:S(2)}, u32[]{:S(2)}) collective-permute-start(bf16[32,2688]{1,0:T(8,128)(2,1)S(1)} %shard_map.116.mine_ref), channel_id=1, source_target_pairs={{0,8},{4,12},{8,0},{12,4},{1,9},{5,13},{9,1},{13,5},{2,10},{6,14},... | collective-permute-start | bytes 516104 | tf_op jit(solution)/shard_map/ppermute | solution.py:238
  25.3 13.4 %collective-permute-start.12 = (bf16[32,2688]{1,0:T(8,128)(2,1)S(1)}, bf16[32,2688]{1,0:T(8,128)(2,1)S(1)}, u32[]{:S(2)}, u32[]{:S(2)}) collective-permute-start(bf16[32,2688]{1,0:T(8,128)(2,1)S(1)} %shard_map.116.mine_ref), channel_id=1, source_target_pairs={{0,4},{4,0},{8,12},{12,8},{1,5},{5,1},{9,13},{13,9},{2,6},{6,2},{1... | collective-permute-start | bytes 516104 | tf_op jit(solution)/shard_map/ppermute | solution.py:238

commit v10 on v9

--- a/solution.py
+++ b/solution.py
@@ -241,11 +241,11 @@
         moves = [(i, (i + by) % seq_count) for i in range(seq_count)]
         return lax.ppermute(array, "seq", moves)
 
-    def near(array):
+    def inner(array, even):
         moves = []
         for i in range(seq_count):
             for f in range(fsdp_count):
-                if f % 2 == 0:
+                if even and f % 2 == 0:
                     to, flip = i ^ 1, 0
                 elif i in (1, 2):
                     to, flip = 3 - i, 0
@@ -292,7 +292,7 @@
     low, cos, sin, wv = lax.optimization_barrier((low, cos, sin, wv))
     low_v = low[RANK:].astype(BF16)
     if direct:
-        far = near(low_v)
+        far = inner(low_v, True)
     else:
         lows = jnp.stack([shift(low_v, d) for d in range(blocks, 0, -1)])
     count = heads if blocks == 1 else 1
@@ -326,9 +326,9 @@
         mine = (seq_index == 2) == (lax.axis_index("fsdp") % 2 == 1)
         lows = jnp.where(mine, far, swap(far, "fsdp", 1))[None]
     code_v = codes_v[:RANK]
-    backs = []
-    for b, d in enumerate(range(blocks, 0, -1)):
-        backs.append(shift(codes_v[(b + 1) * RANK : (b + 2) * RANK], -d))
+    if direct:
+        above, below = swap(codes_v[RANK:], "seq", 1), inner(codes_v[RANK:], False)
+        backs = jnp.where(seq_index % 2 == 0, above, jnp.where(seq_index == 1, below, 0.0))
     code_q, up = call(
         functools.partial(grads_kernel, count, send, blocks, heads),
         [((RANK, tok), F32), ((RANK, (heads + 1) * HEAD), BF16 if direct else F32)],
@@ -336,13 +336,14 @@
         cost=24 << 20,
     )(low, lows, packs, o, w, dp, kt, kt_far, dv, cos_t, sin_t, wq, wv)
     if not direct:
-        code_v = sum(backs, code_v)
+        for b, d in enumerate(range(blocks, 0, -1)):
+            code_v = code_v + shift(codes_v[(b + 1) * RANK : (b + 2) * RANK], -d)
         dlow = sum_fsdp(jnp.concatenate([code_q, code_v], axis=0)).astype(BF16)
         (down,) = call(down_kernel, [((2 * RANK, wide), F32)])(dlow, x)
         down, up = lax.psum((down, up), "seq")
         return down.T, up[:, : heads * HEAD], up[:, heads * HEAD :]
 
-    codes = jnp.concatenate([code_q, code_v + backs[0]], axis=0)
+    codes = jnp.concatenate([code_q, code_v + backs], axis=0)
     dlow = sum_fsdp(codes).astype(BF16)
     half = -(-(heads + 1) // 2) * HEAD
     (mine,) = call(partial_kernel, [((2 * RANK, wide + half), BF16)])(dlow, x, up)

time: 39.7 us -> 40.2 us (1.013)
  waiting for transfers between devices: 16.4 us -> 17.9 us
  starting transfers between devices: 16.9 us -> 15.9 us
    ppermute x2 -> x1, starting transfers between devices: 5.47 us -> 1.87 us  [shift(): return lax.ppermute(array, 'seq', moves)]
    ppermute x10 -> x11, starting transfers between devices: 9.81 us -> 11.4 us  [swap(): return lax.ppermute(array, axis, [(i, i ^ bit) for i in range(size)])]
    ppermute x1 -> x2, waiting for transfers between devices: 0.13 us -> 1.68 us  [inner(): return lax.ppermute(array, ('seq', 'fsdp'), moves)]
    ppermute x1 -> x2, starting transfers between devices: 1.64 us -> 2.67 us  [inner(): return lax.ppermute(array, ('seq', 'fsdp'), moves)]
    ppermute x2 -> x1, waiting for transfers between devices: 0.92 us -> 0.42 us  [shift(): return lax.ppermute(array, 'seq', moves)]
    ppermute x10 -> x11, waiting for transfers between devices: 15.4 us -> 15.8 us  [swap(): return lax.ppermute(array, axis, [(i, i ^ bit) for i in range(size)])]
  transfers between devices with their start and end apart: 13 -> 14, of which waited for: 8 -> 9; matrix products, arithmetic and copies ran while one was open for 1% -> 1% of each run, Pallas kernels for 6% -> 6%
where the time goes in v10:
time: 40.2 us; the launch traced here: 40 us
  waiting for transfers between devices  17.9 us (45%)
  starting transfers between devices  15.9 us (40%)
  Pallas kernels  4.64 us (12%)
  between operations  0.78 us (2%)
  other arithmetic  0.48 us (1%)
    ppermute x11, waiting for transfers between devices, swap(): return lax.ppermute(array, axis, [(i, i ^ bit) for i in range(size)])  15.8 us
    ppermute x11, starting transfers between devices, swap(): return lax.ppermute(array, axis, [(i, i ^ bit) for i in range(size)])  11.4 us
    ppermute x2, starting transfers between devices, inner(): return lax.ppermute(array, ('seq', 'fsdp'), moves)  2.67 us
    ppermute x1, starting transfers between devices, shift(): return lax.ppermute(array, 'seq', moves)  1.87 us
    ppermute x2, waiting for transfers between devices, inner(): return lax.ppermute(array, ('seq', 'fsdp'), moves)  1.68 us
    pallas_call x1, Pallas kernels, body(): call(functools.partial(lowrank_kernel, send), [((2 * RANK, tok), F32), ((...  1.4 us
    pallas_call x1, Pallas kernels, body(): call(functools.partial(grads_kernel, count, send, blocks, heads), [((RANK...  0.85 us
  transfers between devices with their start and end apart: 14, of which 9 were waited for; matrix products, arithmetic and copies ran while one was open for 1% of the time, Pallas kernels for 6%

profile of v10, /device:TPU:0, one launch (start us, length us, event | category | flops | bytes accessed | tf_op | source)
XLA Modules:
  0.0 40.0 jit_solution(11672921713205283940)
XLA Ops:
  0.6 1.4 %shard_map.112 = (f32[32,128]{1,0:T(8,128)S(1)}, bf16[128,128]{1,0:T(8,128)(2,1)S(1)}, bf16[128,128]{1,0:T(8,128)(2,1)S(1)}, bf16[128,128]{1,0:T(8,128)(2,1)S(1)}, bf16[16,1024]{1,0:T(8,128)(2,1)S(1)}) custom-call(bf16[128,2048]{1,0:T(8,128)(2,1)} %x_ref.1, bf16[32,2048]{1,0:T(8,128)(2,1)} %bitcast.8, bf16[128,128]{1,0:T(8,128)(2,1)} %refs_2_.1, ...), custom_call_target="tpu_custom_call" | custom-call | flops 1 | bytes 1 | tf_op jit(solution)/shard_map/pallas_call | solution.py:264
  2.0 0.0 copy-start.4
  2.1 0.5 %collective-permute-start = (f32[32,128]{1,0:T(8,128)S(1)}, f32[32,128]{1,0:T(8,128)S(1)}, u32[]{:S(2)}, u32[]{:S(2)}) collective-permute-start(f32[32,128]{1,0:T(8,128)S(1)} %get-tuple-element.29), channel_id=1, source_target_pairs={{0,1},{1,0},{2,3},{3,2},{4,5},{5,4},{6,7},{7,6},{8,9},{9,8},{10,11... | collective-permute-start | bytes 49160 | tf_op jit(solution)/shard_map/ppermute | solution.py:238
  2.6 2.6 %collective-permute-start.1 = (f32[32,128]{1,0:T(8,128)S(1)}, f32[32,128]{1,0:T(8,128)S(1)}, u32[]{:S(2)}, u32[]{:S(2)}) collective-permute-start(f32[32,128]{1,0:T(8,128)S(1)} %get-tuple-element.29), channel_id=1, source_target_pairs={{0,2},{1,3},{2,0},{3,1},{4,6},{5,7},{6,4},{7,5},{8,10},{9,11},{10,... | collective-permute-start | bytes 49160 | tf_op jit(solution)/shard_map/ppermute | solution.py:238
  5.1 0.1 collective-permute-start.2
  5.2 1.9 %collective-permute-start.3 = (bf16[144,128]{1,0:T(8,128)(2,1)S(1)}, bf16[144,128]{1,0:T(8,128)(2,1)S(1)}, u32[]{:S(2)}, u32[]{:S(2)}) collective-permute-start(bf16[144,128]{1,0:T(8,128)(2,1)S(1)} %pad_maximum_fusion), channel_id=1, source_target_pairs={{0,4},{4,8},{8,12},{12,0},{1,5},{5,9},{9,13},{13,1},{2,6},{6,10},{... | collective-permute-start | bytes 110600 | tf_op jit(solution)/shard_map/ppermute | solution.py:242
  7.1 0.0 copy-start.2
  7.1 0.4 %multiply_sine_fusion = (f32[192,64]{1,0:T(8,128)S(1)}, f32[192,64]{1,0:T(8,128)S(1)}) fusion(f32[64]{0:T(128)S(1)} %multiply_power_fusion, f32[192]{0:T(256)S(1)} %add_convert_fusion.1), kind=kLoop, calls=%fused_computation | loop fusion | flops 12288 | bytes 99328 | tf_op jit(solution)/shard_map/sin | solution.py:289
  7.6 0.2 copy-done.3
  7.8 0.5 %collective-permute-done.2 = f32[32,128]{1,0:T(8,128)S(1)} collective-permute-done((f32[32,128]{1,0:T(8,128)S(1)}, f32[32,128]{1,0:T(8,128)S(1)}, u32[]{:S(2)}, u32[]{:S(2)}) %collective-permute-start.2) | collective-permute-done | bytes 16416 | tf_op jit(solution)/shard_map/ppermute | solution.py:238
  8.3 1.6 %collective-permute-start.4 = (bf16[16,128]{1,0:T(8,128)(2,1)S(1)}, bf16[16,128]{1,0:T(8,128)(2,1)S(1)}, u32[]{:S(2)}, u32[]{:S(2)}) collective-permute-start(bf16[16,128]{1,0:T(8,128)(2,1)S(1)} %slice.33), channel_id=1, source_target_pairs={{0,4},{1,3},{2,6},{3,1},{4,0},{5,9},{6,2},{7,11},{8,12},{9,5},{10,... | collective-permute-start | bytes 12296 | tf_op jit(solution)/shard_map/ppermute | solution.py:255
  10.0 0.7 %shard_map.113 = (bf16[1024,128]{1,0:T(8,128)(2,1)S(1)}, bf16[128,128]{1,0:T(8,128)(2,1)S(1)}, f32[128,1024]{1,0:T(8,128)S(1)}, f32[128,1024]{1,0:T(8,128)S(1)},...) custom-call(f32[32,128]{1,0:T(8,128)S(1)} %add_add_fusion.low_ref, bf16[128,1024]{1,0:T(8,128)(2,1)S(1)} %copy-done.2, ...), custom_call_target="tpu_custom_call" | custom-call | flops 3145728 | bytes 3145728 | tf_op jit(solution)/shard_map/pallas_call | solution.py:299
  10.7 0.4 %collective-permute-done.3 = bf16[144,128]{1,0:T(8,128)(2,1)S(1)} collective-permute-done((bf16[144,128]{1,0:T(8,128)(2,1)S(1)}, bf16[144,128]{1,0:T(8,128)(2,1)S(1)}, u32[]{:S(2)}, u32[]{:S(2)}) %collective-permute-start.3) | collective-permute-done | bytes 36896 | tf_op jit(solution)/shard_map/ppermute | solution.py:242
  11.1 0.7 %shard_map.114 = (f32[192,1024]{1,0:T(8,128)S(1)}, bf16[128,64]{1,0:T(8,128)(2,1)S(1)}, f32[192,128]{1,0:T(8,128)S(1)}, f32[32,128]{1,0:T(8,128)S(1)}) custom-call(bf16[1024,128]{1,0:T(8,128)(2,1)S(1)} %get-tuple-element.37.qr_ref, f32[128,1024]{1,0:T(8,128)S(1)} %get-tuple-element.38.s_ref, bf16[128,1024]{1,0:T(8,128)(2,1)S(1)} %copy-done, ...), custom_call_target="tpu_custom_call" | custom-call | flops 5242880 | bytes 5242880 | tf_op jit(solution)/shard_map/pallas_call | solution.py:313
  11.9 0.1 collective-permute-done.4
  12.0 1.6 %collective-permute-start.6 = (f32[16,128]{1,0:T(8,128)S(1)}, f32[16,128]{1,0:T(8,128)S(1)}, u32[]{:S(2)}, u32[]{:S(2)}) collective-permute-start(f32[16,128]{1,0:T(8,128)S(1)} %slice.29), channel_id=1, source_target_pairs={{0,4},{4,0},{8,12},{12,8},{1,5},{5,1},{9,13},{13,9},{2,6},{6,2},{1... | collective-permute-start | bytes 24584 | tf_op jit(solution)/shard_map/ppermute | solution.py:238
  13.6 1.0 %collective-permute-start.7 = (f32[16,128]{1,0:T(8,128)S(1)}, f32[16,128]{1,0:T(8,128)S(1)}, u32[]{:S(2)}, u32[]{:S(2)}) collective-permute-start(f32[16,128]{1,0:T(8,128)S(1)} %slice.29), channel_id=1, source_target_pairs={{0,2},{1,3},{2,0},{3,1},{4,8},{5,9},{6,10},{7,11},{8,4},{9,5},{10,... | collective-permute-start | bytes 24584 | tf_op jit(solution)/shard_map/ppermute | solution.py:255
  14.6 0.9 %shard_map.115 = (f32[16,128]{1,0:T(8,128)S(1)}, bf16[16,1152]{1,0:T(8,128)(2,1)S(1)}) custom-call(f32[32,128]{1,0:T(8,128)S(1)} %add_add_fusion.low_ref, bf16[1,16,128]{2,1,0:T(8,128)(2,1)S(1)} %select_bitcast_fusion.far_ref, bf16[1,144,128]{2,1,0:T(8,128)(2,1)S(1)} %bitcast.7, bf16[128,1024]{1,0:T(8,128)(2,1)S(1)} %copy-done, ...), custom_call_target="tpu_custom_call" | custom-call | flops 25165824 | bytes 25165824 | tf_op jit(solution)/shard_map/pallas_call | solution.py:332
  15.5 0.2 collective-permute-done.6
  15.7 1.6 %collective-permute-done.7 = f32[16,128]{1,0:T(8,128)S(1)} collective-permute-done((f32[16,128]{1,0:T(8,128)S(1)}, f32[16,128]{1,0:T(8,128)S(1)}, u32[]{:S(2)}, u32[]{:S(2)}) %collective-permute-start.7) | collective-permute-done | bytes 8224 | tf_op jit(solution)/shard_map/ppermute | solution.py:255
  17.2 0.1 collective-permute-start.10
  17.3 1.1 %collective-permute-start.8 = (f32[32,128]{1,0:T(8,128)S(1)}, f32[32,128]{1,0:T(8,128)S(1)}, u32[]{:S(2)}, u32[]{:S(2)}) collective-permute-start(f32[32,128]{1,0:T(8,128)S(1)} %pad_maximum_fusion.1), channel_id=1, source_target_pairs={{0,1},{1,0},{2,3},{3,2},{4,5},{5,4},{6,7},{7,6},{8,9},{9,8},{10,11... | collective-permute-start | bytes 49160 | tf_op jit(solution)/shard_map/ppermute | solution.py:238
  18.4 1.0 %collective-permute-start.9 = (f32[32,128]{1,0:T(8,128)S(1)}, f32[32,128]{1,0:T(8,128)S(1)}, u32[]{:S(2)}, u32[]{:S(2)}) collective-permute-start(f32[32,128]{1,0:T(8,128)S(1)} %pad_maximum_fusion.1), channel_id=1, source_target_pairs={{0,2},{1,3},{2,0},{3,1},{4,6},{5,7},{6,4},{7,5},{8,10},{9,11},{10,... | collective-permute-start | bytes 49160 | tf_op jit(solution)/shard_map/ppermute | solution.py:238
  19.4 1.0 %collective-permute-done.10 = f32[32,128]{1,0:T(8,128)S(1)} collective-permute-done((f32[32,128]{1,0:T(8,128)S(1)}, f32[32,128]{1,0:T(8,128)S(1)}, u32[]{:S(2)}, u32[]{:S(2)}) %collective-permute-start.10) | collective-permute-done | bytes 16416 | tf_op jit(solution)/shard_map/ppermute | solution.py:238
  20.5 1.7 %collective-permute-done.9 = f32[32,128]{1,0:T(8,128)S(1)} collective-permute-done((f32[32,128]{1,0:T(8,128)S(1)}, f32[32,128]{1,0:T(8,128)S(1)}, u32[]{:S(2)}, u32[]{:S(2)}) %collective-permute-start.9) | collective-permute-done | bytes 16416 | tf_op jit(solution)/shard_map/ppermute | solution.py:238
  22.2 0.2 shard_map.116.mine_ref
  22.4 2.5 %collective-permute-start.11 = (bf16[32,2688]{1,0:T(8,128)(2,1)S(1)}, bf16[32,2688]{1,0:T(8,128)(2,1)S(1)}, u32[]{:S(2)}, u32[]{:S(2)}) collective-permute-start(bf16[32,2688]{1,0:T(8,128)(2,1)S(1)} %shard_map.116.mine_ref), channel_id=1, source_target_pairs={{0,12},{4,8},{8,4},{12,0},{1,13},{5,9},{9,5},{13,1},{2,14},{6,10},... | collective-permute-start | bytes 516104 | tf_op jit(solution)/shard_map/ppermute | solution.py:238
  24.9 0.1 collective-permute-start.12
  25.1 1.8 %collective-permute-start.13 = (bf16[32,2688]{1,0:T(8,128)(2,1)S(1)}, bf16[32,2688]{1,0:T(8,128)(2,1)S(1)}, u32[]{:S(2)}, u32[]{:S(2)}) collective-permute-start(bf16[32,2688]{1,0:T(8,128)(2,1)S(1)} %shard_map.116.mine_ref), channel_id=1, source_target_pairs={{0,4},{4,0},{8,12},{12,8},{1,5},{5,1},{9,13},{13,9},{2,6},{6,2},{1... | collective-permute-start | bytes 516104 | tf_op jit(solution)/shard_map/ppermute | solution.py:238
  26.9 4.7 %collective-permute-done.11.three_ref = bf16[32,2688]{1,0:T(8,128)(2,1)S(1)} collective-permute-done((bf16[32,2688]{1,0:T(8,128)(2,1)S(1)}, bf16[32,2688]{1,0:T(8,128)(2,1)S(1)}, u32[]{:S(2)}, u32[]{:S(2)}) %collective-permute-start.11) | collective-permute-done | bytes 172064 | tf_op jit(solution)/shard_map/ppermute | solution.py:238
  31.6 7.6 %collective-permute-done.12.two_ref = bf16[32,2688]{1,0:T(8,128)(2,1)S(1)} collective-permute-done((bf16[32,2688]{1,0:T(8,128)(2,1)S(1)}, bf16[32,2688]{1,0:T(8,128)(2,1)S(1)}, u32[]{:S(2)}, u32[]{:S(2)}) %collective-permute-start.12) | collective-permute-done | bytes 172064 | tf_op jit(solution)/shard_map/ppermute | solution.py:238
  39.2 0.8 %shard_map.117 = (f32[32,2048]{1,0:T(8,128)}, f32[16,1024]{1,0:T(8,128)}, f32[16,128]{1,0:T(8,128)}) custom-call(bf16[32,2688]{1,0:T(8,128)(2,1)S(1)} %shard_map.116.mine_ref, bf16[32,2688]{1,0:T(8,128)(2,1)S(1)} %collective-permute-done.11.three_ref, bf16[32,2688]{1,0:T(8,128)(2,1)S(1)} %collective-permute-done.12.two_ref, ...), custom_call_target="tpu_custom_call" | custom-call | flops 1 | bytes 1 | tf_op jit(solution)/shard_map/pallas_call | solution.py:351
  (30 shorter events, 0.1 us)
Async XLA Ops:
  2.0 3.2 %copy-start.4 = (s32[128]{0:T(128)S(1)}, s32[128]{0:T(128)}, u32[]{:S(2)}) copy-start(s32[128]{0:T(128)} %param.14) | copy-start | bytes 1540
  2.1 5.8 %collective-permute-start = (f32[32,128]{1,0:T(8,128)S(1)}, f32[32,128]{1,0:T(8,128)S(1)}, u32[]{:S(2)}, u32[]{:S(2)}) collective-permute-start(f32[32,128]{1,0:T(8,128)S(1)} %get-tuple-element.29), channel_id=1, source_target_pairs={{0,1},{1,0},{2,3},{3,2},{4,5},{5,4},{6,7},{7,6},{8,9},{9,8},{10,11... | collective-permute-start | bytes 49160 | tf_op jit(solution)/shard_map/ppermute | solution.py:238
  2.6 5.2 %collective-permute-start.1 = (f32[32,128]{1,0:T(8,128)S(1)}, f32[32,128]{1,0:T(8,128)S(1)}, u32[]{:S(2)}, u32[]{:S(2)}) collective-permute-start(f32[32,128]{1,0:T(8,128)S(1)} %get-tuple-element.29), channel_id=1, source_target_pairs={{0,2},{1,3},{2,0},{3,1},{4,6},{5,7},{6,4},{7,5},{8,10},{9,11},{10,... | collective-permute-start | bytes 49160 | tf_op jit(solution)/shard_map/ppermute | solution.py:238
  5.1 3.2 %collective-permute-start.2 = (f32[32,128]{1,0:T(8,128)S(1)}, f32[32,128]{1,0:T(8,128)S(1)}, u32[]{:S(2)}, u32[]{:S(2)}) collective-permute-start(f32[32,128]{1,0:T(8,128)S(1)} %get-tuple-element.29), channel_id=1, source_target_pairs={{0,3},{1,2},{2,1},{3,0},{4,7},{5,6},{6,5},{7,4},{8,11},{9,10},{10,... | collective-permute-start | bytes 49160 | tf_op jit(solution)/shard_map/ppermute | solution.py:238
  5.2 5.9 %collective-permute-start.3 = (bf16[144,128]{1,0:T(8,128)(2,1)S(1)}, bf16[144,128]{1,0:T(8,128)(2,1)S(1)}, u32[]{:S(2)}, u32[]{:S(2)}) collective-permute-start(bf16[144,128]{1,0:T(8,128)(2,1)S(1)} %pad_maximum_fusion), channel_id=1, source_target_pairs={{0,4},{4,8},{8,12},{12,0},{1,5},{5,9},{9,13},{13,1},{2,6},{6,10},{... | collective-permute-start | bytes 110600 | tf_op jit(solution)/shard_map/ppermute | solution.py:242
  7.1 0.7 %copy-start.3 = (bf16[16,128]{1,0:T(8,128)(2,1)S(1)}, bf16[16,128]{1,0:T(8,128)(2,1)}, u32[]{:S(2)}) copy-start(bf16[16,128]{1,0:T(8,128)(2,1)} %param.17) | copy-start | bytes 12292
  7.1 2.9 %copy-start.2 = (bf16[128,1024]{1,0:T(8,128)(2,1)S(1)}, bf16[128,1024]{1,0:T(8,128)(2,1)}, u32[]{:S(2)}) copy-start(bf16[128,1024]{1,0:T(8,128)(2,1)} %q_ref.1) | copy-start | bytes 786436
  7.8 2.2 %copy-start = (bf16[128,1024]{1,0:T(8,128)(2,1)S(1)}, bf16[128,1024]{1,0:T(8,128)(2,1)}, u32[]{:S(2)}) copy-start(bf16[128,1024]{1,0:T(8,128)(2,1)} %o_ref.5) | copy-start | bytes 786436
  8.3 3.7 %collective-permute-start.4 = (bf16[16,128]{1,0:T(8,128)(2,1)S(1)}, bf16[16,128]{1,0:T(8,128)(2,1)S(1)}, u32[]{:S(2)}, u32[]{:S(2)}) collective-permute-start(bf16[16,128]{1,0:T(8,128)(2,1)S(1)} %slice.33), channel_id=1, source_target_pairs={{0,4},{1,3},{2,6},{3,1},{4,0},{5,9},{6,2},{7,11},{8,12},{9,5},{10,... | collective-permute-start | bytes 12296 | tf_op jit(solution)/shard_map/ppermute | solution.py:255
  12.0 2.6 %collective-permute-start.5 = (bf16[16,128]{1,0:T(8,128)(2,1)S(1)}, bf16[16,128]{1,0:T(8,128)(2,1)S(1)}, u32[]{:S(2)}, u32[]{:S(2)}) collective-permute-start(bf16[16,128]{1,0:T(8,128)(2,1)S(1)} %collective-permute-done.4), channel_id=1, source_target_pairs={{0,1},{1,0},{2,3},{3,2},{4,5},{5,4},{6,7},{7,6},{8,9},{9,8},{10,11... | collective-permute-start | bytes 12296 | tf_op jit(solution)/shard_map/ppermute | solution.py:238
  12.0 3.7 %collective-permute-start.6 = (f32[16,128]{1,0:T(8,128)S(1)}, f32[16,128]{1,0:T(8,128)S(1)}, u32[]{:S(2)}, u32[]{:S(2)}) collective-permute-start(f32[16,128]{1,0:T(8,128)S(1)} %slice.29), channel_id=1, source_target_pairs={{0,4},{4,0},{8,12},{12,8},{1,5},{5,1},{9,13},{13,9},{2,6},{6,2},{1... | collective-permute-start | bytes 24584 | tf_op jit(solution)/shard_map/ppermute | solution.py:238
  13.6 3.7 %collective-permute-start.7 = (f32[16,128]{1,0:T(8,128)S(1)}, f32[16,128]{1,0:T(8,128)S(1)}, u32[]{:S(2)}, u32[]{:S(2)}) collective-permute-start(f32[16,128]{1,0:T(8,128)S(1)} %slice.29), channel_id=1, source_target_pairs={{0,2},{1,3},{2,0},{3,1},{4,8},{5,9},{6,10},{7,11},{8,4},{9,5},{10,... | collective-permute-start | bytes 24584 | tf_op jit(solution)/shard_map/ppermute | solution.py:255
  14.6 7.6 %copy-start.1 = (bf16[128,2048]{1,0:T(8,128)(2,1)S(1)}, bf16[128,2048]{1,0:T(8,128)(2,1)}, u32[]{:S(2)}) copy-start(bf16[128,2048]{1,0:T(8,128)(2,1)} %x_ref.1) | copy-start | bytes 1572868
  17.2 3.2 %collective-permute-start.10 = (f32[32,128]{1,0:T(8,128)S(1)}, f32[32,128]{1,0:T(8,128)S(1)}, u32[]{:S(2)}, u32[]{:S(2)}) collective-permute-start(f32[32,128]{1,0:T(8,128)S(1)} %pad_maximum_fusion.1), channel_id=1, source_target_pairs={{0,3},{1,2},{2,1},{3,0},{4,7},{5,6},{6,5},{7,4},{8,11},{9,10},{10,... | collective-permute-start | bytes 49160 | tf_op jit(solution)/shard_map/ppermute | solution.py:238
  17.3 3.2 %collective-permute-start.8 = (f32[32,128]{1,0:T(8,128)S(1)}, f32[32,128]{1,0:T(8,128)S(1)}, u32[]{:S(2)}, u32[]{:S(2)}) collective-permute-start(f32[32,128]{1,0:T(8,128)S(1)} %pad_maximum_fusion.1), channel_id=1, source_target_pairs={{0,1},{1,0},{2,3},{3,2},{4,5},{5,4},{6,7},{7,6},{8,9},{9,8},{10,11... | collective-permute-start | bytes 49160 | tf_op jit(solution)/shard_map/ppermute | solution.py:238
  18.4 3.7 %collective-permute-start.9 = (f32[32,128]{1,0:T(8,128)S(1)}, f32[32,128]{1,0:T(8,128)S(1)}, u32[]{:S(2)}, u32[]{:S(2)}) collective-permute-start(f32[32,128]{1,0:T(8,128)S(1)} %pad_maximum_fusion.1), channel_id=1, source_target_pairs={{0,2},{1,3},{2,0},{3,1},{4,6},{5,7},{6,4},{7,5},{8,10},{9,11},{10,... | collective-permute-start | bytes 49160 | tf_op jit(solution)/shard_map/ppermute | solution.py:238
  22.4 9.2 %collective-permute-start.11 = (bf16[32,2688]{1,0:T(8,128)(2,1)S(1)}, bf16[32,2688]{1,0:T(8,128)(2,1)S(1)}, u32[]{:S(2)}, u32[]{:S(2)}) collective-permute-start(bf16[32,2688]{1,0:T(8,128)(2,1)S(1)} %shard_map.116.mine_ref), channel_id=1, source_target_pairs={{0,12},{4,8},{8,4},{12,0},{1,13},{5,9},{9,5},{13,1},{2,14},{6,10},... | collective-permute-start | bytes 516104 | tf_op jit(solution)/shard_map/ppermute | solution.py:238
  24.9 14.3 %collective-permute-start.12 = (bf16[32,2688]{1,0:T(8,128)(2,1)S(1)}, bf16[32,2688]{1,0:T(8,128)(2,1)S(1)}, u32[]{:S(2)}, u32[]{:S(2)}) collective-permute-start(bf16[32,2688]{1,0:T(8,128)(2,1)S(1)} %shard_map.116.mine_ref), channel_id=1, source_target_pairs={{0,8},{4,12},{8,0},{12,4},{1,9},{5,13},{9,1},{13,5},{2,10},{6,14},... | collective-permute-start | bytes 516104 | tf_op jit(solution)/shard_map/ppermute | solution.py:238
  25.1 14.2 %collective-permute-start.13 = (bf16[32,2688]{1,0:T(8,128)(2,1)S(1)}, bf16[32,2688]{1,0:T(8,128)(2,1)S(1)}, u32[]{:S(2)}, u32[]{:S(2)}) collective-permute-start(bf16[32,2688]{1,0:T(8,128)(2,1)S(1)} %shard_map.116.mine_ref), channel_id=1, source_target_pairs={{0,4},{4,0},{8,12},{12,8},{1,5},{5,1},{9,13},{13,9},{2,6},{6,2},{1... | collective-permute-start | bytes 516104 | tf_op jit(solution)/shard_map/ppermute | solution.py:238

commit v11 on v10

--- a/solution.py
+++ b/solution.py
@@ -197,27 +197,25 @@
     part_ref[...] = dot(dl_ref[...], x_ref[...], 1, 0)
 
 
-def partial_kernel(own_ref, x_ref, up_ref, send_ref):
+def partial_kernel(own_ref, x_ref, up_ref, near_ref, part_ref, both_ref):
     part = dot(own_ref[...], x_ref[...], 1, 0).astype(BF16)
-    wide, size = part.shape[1], up_ref.shape[1]
-    half = send_ref.shape[1] - wide
-    send_ref[:, :wide] = part
-    send_ref[:RANK, wide:] = up_ref[:, :half]
-    send_ref[RANK:, wide : wide + size - half] = up_ref[:, half:]
-    if 2 * half > size:
-        send_ref[RANK:, wide + size - half :] = jnp.zeros((RANK, 2 * half - size), BF16)
+    wide = part.shape[1]
+    part_ref[...] = part
+    both_ref[:, :wide] = part[:RANK]
+    both_ref[:, wide : 2 * wide] = part[RANK:]
+    both_ref[:, 2 * wide :] = (up_ref[...].astype(F32) + near_ref[...].astype(F32)).astype(BF16)
 
 
 def final_kernel(mine_ref, three_ref, two_ref, one_ref, down_ref, upq_ref, upv_ref):
-    near = mine_ref[...].astype(F32) + one_ref[...].astype(F32)
-    far = two_ref[...].astype(F32) + three_ref[...].astype(F32)
-    total = near + far
     wide, size = down_ref.shape[1], upq_ref.shape[1]
-    half = total.shape[1] - wide
-    down_ref[...] = total[:, :wide]
-    upq_ref[:, :half] = total[:RANK, wide:]
-    upq_ref[:, half:] = total[RANK:, wide : wide + size - half]
-    upv_ref[...] = total[RANK:, wide + size - half : wide + size - half + HEAD]
+    for i in range(2):
+        rows, cut = slice(i * RANK, (i + 1) * RANK), slice(i * wide, (i + 1) * wide)
+        near = mine_ref[:, cut].astype(F32) + one_ref[rows].astype(F32)
+        far = two_ref[:, cut].astype(F32) + three_ref[rows].astype(F32)
+        down_ref[rows] = near + far
+    up = mine_ref[:, 2 * wide :].astype(F32) + two_ref[:, 2 * wide :].astype(F32)
+    upq_ref[...] = up[:, :size]
+    upv_ref[...] = up[:, size:]
 
 
 def body(x, q, k, v, o, segment, a, wq, wv):
@@ -344,14 +342,16 @@
         return down.T, up[:, : heads * HEAD], up[:, heads * HEAD :]
 
     codes = jnp.concatenate([code_q, code_v + backs], axis=0)
-    dlow = sum_fsdp(codes).astype(BF16)
-    half = -(-(heads + 1) // 2) * HEAD
-    (mine,) = call(partial_kernel, [((2 * RANK, wide + half), BF16)])(dlow, x, up)
-    three, two, one = [swap(mine, "seq", bit) for bit in (3, 2, 1)]
+    dlow, near_up = lax.optimization_barrier((sum_fsdp(codes), swap(up, "seq", 1)))
+    part, both = call(
+        partial_kernel,
+        [((2 * RANK, wide), BF16), ((RANK, 2 * wide + (heads + 1) * HEAD), BF16)],
+    )(dlow.astype(BF16), x, up, near_up)
+    three, two, one = swap(part, "seq", 3), swap(both, "seq", 2), swap(part, "seq", 1)
     down, up_q, up_v = call(
         final_kernel,
         [((2 * RANK, wide), F32), ((RANK, heads * HEAD), F32), ((RANK, HEAD), F32)],
-    )(mine, three, two, one)
+    )(both, three, two, one)
     return down.T, up_q, up_v
 
 

time: 40.2 us -> 37.7 us (0.938)
  waiting for transfers between devices: 17.9 us -> 15.2 us
    ppermute x11 -> x12, waiting for transfers between devices: 15.8 us -> 13.1 us  [swap(): return lax.ppermute(array, axis, [(i, i ^ bit) for i in range(size)])]
    ppermute x11 -> x12, starting transfers between devices: 11.4 us -> 11.6 us  [swap(): return lax.ppermute(array, axis, [(i, i ^ bit) for i in range(size)])]
  transfers between devices with their start and end apart: 14 -> 15, of which waited for: 9 -> 9; matrix products, arithmetic and copies ran while one was open for 1% -> 1% of each run, Pallas kernels for 6% -> 6%
where the time goes in v11:
time: 37.7 us; the launch traced here: 37.6 us
  starting transfers between devices  16.2 us (43%)
  waiting for transfers between devices  15.2 us (40%)
  Pallas kernels  4.64 us (12%)
  between operations  0.77 us (2%)
  other arithmetic  0.48 us (1%)
    ppermute x12, waiting for transfers between devices, swap(): return lax.ppermute(array, axis, [(i, i ^ bit) for i in range(size)])  13.1 us
    ppermute x12, starting transfers between devices, swap(): return lax.ppermute(array, axis, [(i, i ^ bit) for i in range(size)])  11.6 us
    ppermute x2, starting transfers between devices, inner(): return lax.ppermute(array, ('seq', 'fsdp'), moves)  2.67 us
    ppermute x1, starting transfers between devices, shift(): return lax.ppermute(array, 'seq', moves)  1.87 us
    ppermute x2, waiting for transfers between devices, inner(): return lax.ppermute(array, ('seq', 'fsdp'), moves)  1.68 us
    pallas_call x1, Pallas kernels, body(): call(functools.partial(lowrank_kernel, send), [((2 * RANK, tok), F32), ((...  1.4 us
    pallas_call x1, Pallas kernels, body(): call(functools.partial(grads_kernel, count, send, blocks, heads), [((RANK...  0.85 us
    pallas_call x1, Pallas kernels, body(): call(final_kernel, [((2 * RANK, wide), F32), ((RANK, heads * HEAD), F32),...  0.78 us
  transfers between devices with their start and end apart: 15, of which 9 were waited for; matrix products, arithmetic and copies ran while one was open for 1% of the time, Pallas kernels for 6%

profile of v11, /device:TPU:0, one launch (start us, length us, event | category | flops | bytes accessed | tf_op | source)
XLA Modules:
  0.0 37.6 jit_solution(9096873469315260572)
XLA Ops:
  0.6 1.4 %shard_map.112 = (f32[32,128]{1,0:T(8,128)S(1)}, bf16[128,128]{1,0:T(8,128)(2,1)S(1)}, bf16[128,128]{1,0:T(8,128)(2,1)S(1)}, bf16[128,128]{1,0:T(8,128)(2,1)S(1)}, bf16[16,1024]{1,0:T(8,128)(2,1)S(1)}) custom-call(bf16[128,2048]{1,0:T(8,128)(2,1)} %x_ref.1, bf16[32,2048]{1,0:T(8,128)(2,1)} %bitcast.8, bf16[128,128]{1,0:T(8,128)(2,1)} %refs_2_.1, ...), custom_call_target="tpu_custom_call" | custom-call | flops 1 | bytes 1 | tf_op jit(solution)/shard_map/pallas_call | solution.py:262
  2.0 0.0 copy-start.4
  2.1 0.5 %collective-permute-start = (f32[32,128]{1,0:T(8,128)S(1)}, f32[32,128]{1,0:T(8,128)S(1)}, u32[]{:S(2)}, u32[]{:S(2)}) collective-permute-start(f32[32,128]{1,0:T(8,128)S(1)} %get-tuple-element.33), channel_id=1, source_target_pairs={{0,1},{1,0},{2,3},{3,2},{4,5},{5,4},{6,7},{7,6},{8,9},{9,8},{10,11... | collective-permute-start | bytes 49160 | tf_op jit(solution)/shard_map/ppermute | solution.py:236
  2.6 2.6 %collective-permute-start.1 = (f32[32,128]{1,0:T(8,128)S(1)}, f32[32,128]{1,0:T(8,128)S(1)}, u32[]{:S(2)}, u32[]{:S(2)}) collective-permute-start(f32[32,128]{1,0:T(8,128)S(1)} %get-tuple-element.33), channel_id=1, source_target_pairs={{0,2},{1,3},{2,0},{3,1},{4,6},{5,7},{6,4},{7,5},{8,10},{9,11},{10,... | collective-permute-start | bytes 49160 | tf_op jit(solution)/shard_map/ppermute | solution.py:236
  5.1 0.1 collective-permute-start.2
  5.2 1.9 %collective-permute-start.3 = (bf16[144,128]{1,0:T(8,128)(2,1)S(1)}, bf16[144,128]{1,0:T(8,128)(2,1)S(1)}, u32[]{:S(2)}, u32[]{:S(2)}) collective-permute-start(bf16[144,128]{1,0:T(8,128)(2,1)S(1)} %pad_maximum_fusion), channel_id=1, source_target_pairs={{0,4},{4,8},{8,12},{12,0},{1,5},{5,9},{9,13},{13,1},{2,6},{6,10},{... | collective-permute-start | bytes 110600 | tf_op jit(solution)/shard_map/ppermute | solution.py:240
  7.1 0.0 copy-start.2
  7.1 0.4 %multiply_sine_fusion = (f32[192,64]{1,0:T(8,128)S(1)}, f32[192,64]{1,0:T(8,128)S(1)}) fusion(f32[64]{0:T(128)S(1)} %multiply_power_fusion, f32[192]{0:T(256)S(1)} %add_convert_fusion), kind=kLoop, calls=%fused_computation | loop fusion | flops 12288 | bytes 99328 | tf_op jit(solution)/shard_map/sin | solution.py:287
  7.6 0.2 copy-done.3
  7.8 0.5 %collective-permute-done.2 = f32[32,128]{1,0:T(8,128)S(1)} collective-permute-done((f32[32,128]{1,0:T(8,128)S(1)}, f32[32,128]{1,0:T(8,128)S(1)}, u32[]{:S(2)}, u32[]{:S(2)}) %collective-permute-start.2) | collective-permute-done | bytes 16416 | tf_op jit(solution)/shard_map/ppermute | solution.py:236
  8.3 1.6 %collective-permute-start.4 = (bf16[16,128]{1,0:T(8,128)(2,1)S(1)}, bf16[16,128]{1,0:T(8,128)(2,1)S(1)}, u32[]{:S(2)}, u32[]{:S(2)}) collective-permute-start(bf16[16,128]{1,0:T(8,128)(2,1)S(1)} %slice.33), channel_id=1, source_target_pairs={{0,4},{1,3},{2,6},{3,1},{4,0},{5,9},{6,2},{7,11},{8,12},{9,5},{10,... | collective-permute-start | bytes 12296 | tf_op jit(solution)/shard_map/ppermute | solution.py:253
  10.0 0.7 %shard_map.113 = (bf16[1024,128]{1,0:T(8,128)(2,1)S(1)}, bf16[128,128]{1,0:T(8,128)(2,1)S(1)}, f32[128,1024]{1,0:T(8,128)S(1)}, f32[128,1024]{1,0:T(8,128)S(1)},...) custom-call(f32[32,128]{1,0:T(8,128)S(1)} %add_add_fusion.1.low_ref, bf16[128,1024]{1,0:T(8,128)(2,1)S(1)} %copy-done.2, ...), custom_call_target="tpu_custom_call" | custom-call | flops 3145728 | bytes 3145728 | tf_op jit(solution)/shard_map/pallas_call | solution.py:297
  10.7 0.4 %collective-permute-done.3 = bf16[144,128]{1,0:T(8,128)(2,1)S(1)} collective-permute-done((bf16[144,128]{1,0:T(8,128)(2,1)S(1)}, bf16[144,128]{1,0:T(8,128)(2,1)S(1)}, u32[]{:S(2)}, u32[]{:S(2)}) %collective-permute-start.3) | collective-permute-done | bytes 36896 | tf_op jit(solution)/shard_map/ppermute | solution.py:240
  11.1 0.7 %shard_map.114 = (f32[192,1024]{1,0:T(8,128)S(1)}, bf16[128,64]{1,0:T(8,128)(2,1)S(1)}, f32[192,128]{1,0:T(8,128)S(1)}, f32[32,128]{1,0:T(8,128)S(1)}) custom-call(bf16[1024,128]{1,0:T(8,128)(2,1)S(1)} %get-tuple-element.41.qr_ref, f32[128,1024]{1,0:T(8,128)S(1)} %get-tuple-element.42.s_ref, bf16[128,1024]{1,0:T(8,128)(2,1)S(1)} %copy-done, ...), custom_call_target="tpu_custom_call" | custom-call | flops 5242880 | bytes 5242880 | tf_op jit(solution)/shard_map/pallas_call | solution.py:311
  11.9 0.1 collective-permute-done.4
  12.0 1.6 %collective-permute-start.6 = (f32[16,128]{1,0:T(8,128)S(1)}, f32[16,128]{1,0:T(8,128)S(1)}, u32[]{:S(2)}, u32[]{:S(2)}) collective-permute-start(f32[16,128]{1,0:T(8,128)S(1)} %slice.29), channel_id=1, source_target_pairs={{0,4},{4,0},{8,12},{12,8},{1,5},{5,1},{9,13},{13,9},{2,6},{6,2},{1... | collective-permute-start | bytes 24584 | tf_op jit(solution)/shard_map/ppermute | solution.py:236
  13.6 1.0 %collective-permute-start.7 = (f32[16,128]{1,0:T(8,128)S(1)}, f32[16,128]{1,0:T(8,128)S(1)}, u32[]{:S(2)}, u32[]{:S(2)}) collective-permute-start(f32[16,128]{1,0:T(8,128)S(1)} %slice.29), channel_id=1, source_target_pairs={{0,2},{1,3},{2,0},{3,1},{4,8},{5,9},{6,10},{7,11},{8,4},{9,5},{10,... | collective-permute-start | bytes 24584 | tf_op jit(solution)/shard_map/ppermute | solution.py:253
  14.6 0.9 %shard_map.115 = (f32[16,128]{1,0:T(8,128)S(1)}, bf16[16,1152]{1,0:T(8,128)(2,1)S(1)}) custom-call(f32[32,128]{1,0:T(8,128)S(1)} %add_add_fusion.1.low_ref, bf16[1,16,128]{2,1,0:T(8,128)(2,1)S(1)} %select_bitcast_fusion.far_ref, bf16[1,144,128]{2,1,0:T(8,128)(2,1)S(1)} %bitcast.7, bf16[128,1024]{1,0:T(8,128)(2,1)S(1)} %copy-done, ...), custom_call_target="tpu_custom_call" | custom-call | flops 25165824 | bytes 25165824 | tf_op jit(solution)/shard_map/pallas_call | solution.py:330
  15.5 0.2 collective-permute-done.6
  15.7 1.6 %collective-permute-done.7 = f32[16,128]{1,0:T(8,128)S(1)} collective-permute-done((f32[16,128]{1,0:T(8,128)S(1)}, f32[16,128]{1,0:T(8,128)S(1)}, u32[]{:S(2)}, u32[]{:S(2)}) %collective-permute-start.7) | collective-permute-done | bytes 8224 | tf_op jit(solution)/shard_map/ppermute | solution.py:253
  17.2 0.1 collective-permute-start.10
  17.3 1.1 %collective-permute-start.8 = (f32[32,128]{1,0:T(8,128)S(1)}, f32[32,128]{1,0:T(8,128)S(1)}, u32[]{:S(2)}, u32[]{:S(2)}) collective-permute-start(f32[32,128]{1,0:T(8,128)S(1)} %pad_maximum_fusion.1), channel_id=1, source_target_pairs={{0,1},{1,0},{2,3},{3,2},{4,5},{5,4},{6,7},{7,6},{8,9},{9,8},{10,11... | collective-permute-start | bytes 49160 | tf_op jit(solution)/shard_map/ppermute | solution.py:236
  18.4 1.0 %collective-permute-start.9 = (f32[32,128]{1,0:T(8,128)S(1)}, f32[32,128]{1,0:T(8,128)S(1)}, u32[]{:S(2)}, u32[]{:S(2)}) collective-permute-start(f32[32,128]{1,0:T(8,128)S(1)} %pad_maximum_fusion.1), channel_id=1, source_target_pairs={{0,2},{1,3},{2,0},{3,1},{4,6},{5,7},{6,4},{7,5},{8,10},{9,11},{10,... | collective-permute-start | bytes 49160 | tf_op jit(solution)/shard_map/ppermute | solution.py:236
  19.4 1.1 %collective-permute-start.11 = (bf16[16,1152]{1,0:T(8,128)(2,1)S(1)}, bf16[16,1152]{1,0:T(8,128)(2,1)S(1)}, u32[]{:S(2)}, u32[]{:S(2)}) collective-permute-start(bf16[16,1152]{1,0:T(8,128)(2,1)S(1)} %get-tuple-element.55.up_ref), channel_id=1, source_target_pairs={{0,4},{4,0},{8,12},{12,8},{1,5},{5,1},{9,13},{13,9},{2,6},{6,2},{1... | collective-permute-start | bytes 110600 | tf_op jit(solution)/shard_map/ppermute | solution.py:236
  20.6 1.6 %collective-permute-done.9 = f32[32,128]{1,0:T(8,128)S(1)} collective-permute-done((f32[32,128]{1,0:T(8,128)S(1)}, f32[32,128]{1,0:T(8,128)S(1)}, u32[]{:S(2)}, u32[]{:S(2)}) %collective-permute-start.9) | collective-permute-done | bytes 16416 | tf_op jit(solution)/shard_map/ppermute | solution.py:236
  22.2 1.2 %collective-permute-done.11.near_ref = bf16[16,1152]{1,0:T(8,128)(2,1)S(1)} collective-permute-done((bf16[16,1152]{1,0:T(8,128)(2,1)S(1)}, bf16[16,1152]{1,0:T(8,128)(2,1)S(1)}, u32[]{:S(2)}, u32[]{:S(2)}) %collective-permute-start.11) | collective-permute-done | bytes 36896 | tf_op jit(solution)/shard_map/ppermute | solution.py:236
  23.4 0.2 shard_map.116
  23.6 2.7 %collective-permute-start.13 = (bf16[16,5248]{1,0:T(8,128)(2,1)S(1)}, bf16[16,5248]{1,0:T(8,128)(2,1)S(1)}, u32[]{:S(2)}, u32[]{:S(2)}) collective-permute-start(bf16[16,5248]{1,0:T(8,128)(2,1)S(1)} %get-tuple-element.58.mine_ref), channel_id=1, source_target_pairs={{0,8},{4,12},{8,0},{12,4},{1,9},{5,13},{9,1},{13,5},{2,10},{6,14},... | collective-permute-start | bytes 503816 | tf_op jit(solution)/shard_map/ppermute | solution.py:236
  26.3 0.9 %collective-permute-start.12 = (bf16[32,2048]{1,0:T(8,128)(2,1)S(1)}, bf16[32,2048]{1,0:T(8,128)(2,1)S(1)}, u32[]{:S(2)}, u32[]{:S(2)}) collective-permute-start(bf16[32,2048]{1,0:T(8,128)(2,1)S(1)} %get-tuple-element.59), channel_id=1, source_target_pairs={{0,12},{4,8},{8,4},{12,0},{1,13},{5,9},{9,5},{13,1},{2,14},{6,10},... | collective-permute-start | bytes 393224 | tf_op jit(solution)/shard_map/ppermute | solution.py:236
  27.2 7.6 %collective-permute-done.12.three_ref = bf16[32,2048]{1,0:T(8,128)(2,1)S(1)} collective-permute-done((bf16[32,2048]{1,0:T(8,128)(2,1)S(1)}, bf16[32,2048]{1,0:T(8,128)(2,1)S(1)}, u32[]{:S(2)}, u32[]{:S(2)}) %collective-permute-start.12) | collective-permute-done | bytes 131104 | tf_op jit(solution)/shard_map/ppermute | solution.py:236
  34.8 2.0 %collective-permute-done.14.one_ref = bf16[32,2048]{1,0:T(8,128)(2,1)S(1)} collective-permute-done((bf16[32,2048]{1,0:T(8,128)(2,1)S(1)}, bf16[32,2048]{1,0:T(8,128)(2,1)S(1)}, u32[]{:S(2)}, u32[]{:S(2)}) %collective-permute-start.14) | collective-permute-done | bytes 131104 | tf_op jit(solution)/shard_map/ppermute | solution.py:236
  36.8 0.8 %shard_map.117 = (f32[32,2048]{1,0:T(8,128)}, f32[16,1024]{1,0:T(8,128)}, f32[16,128]{1,0:T(8,128)}) custom-call(bf16[16,5248]{1,0:T(8,128)(2,1)S(1)} %get-tuple-element.58.mine_ref, bf16[32,2048]{1,0:T(8,128)(2,1)S(1)} %collective-permute-done.12.three_ref, bf16[16,5248]{1,0:T(8,128)(2,1)S(1)} %collective-permute-done.13.two_ref, ...), custom_call_target="tpu_custom_call" | custom-call | flops 1 | bytes 1 | tf_op jit(solution)/shard_map/pallas_call | solution.py:351
  (32 shorter events, 0.1 us)
Async XLA Ops:
  2.0 3.2 %copy-start.4 = (s32[128]{0:T(128)S(1)}, s32[128]{0:T(128)}, u32[]{:S(2)}) copy-start(s32[128]{0:T(128)} %param.14) | copy-start | bytes 1540
  2.1 5.8 %collective-permute-start = (f32[32,128]{1,0:T(8,128)S(1)}, f32[32,128]{1,0:T(8,128)S(1)}, u32[]{:S(2)}, u32[]{:S(2)}) collective-permute-start(f32[32,128]{1,0:T(8,128)S(1)} %get-tuple-element.33), channel_id=1, source_target_pairs={{0,1},{1,0},{2,3},{3,2},{4,5},{5,4},{6,7},{7,6},{8,9},{9,8},{10,11... | collective-permute-start | bytes 49160 | tf_op jit(solution)/shard_map/ppermute | solution.py:236
  2.6 5.2 %collective-permute-start.1 = (f32[32,128]{1,0:T(8,128)S(1)}, f32[32,128]{1,0:T(8,128)S(1)}, u32[]{:S(2)}, u32[]{:S(2)}) collective-permute-start(f32[32,128]{1,0:T(8,128)S(1)} %get-tuple-element.33), channel_id=1, source_target_pairs={{0,2},{1,3},{2,0},{3,1},{4,6},{5,7},{6,4},{7,5},{8,10},{9,11},{10,... | collective-permute-start | bytes 49160 | tf_op jit(solution)/shard_map/ppermute | solution.py:236
  5.1 3.2 %collective-permute-start.2 = (f32[32,128]{1,0:T(8,128)S(1)}, f32[32,128]{1,0:T(8,128)S(1)}, u32[]{:S(2)}, u32[]{:S(2)}) collective-permute-start(f32[32,128]{1,0:T(8,128)S(1)} %get-tuple-element.33), channel_id=1, source_target_pairs={{0,3},{1,2},{2,1},{3,0},{4,7},{5,6},{6,5},{7,4},{8,11},{9,10},{10,... | collective-permute-start | bytes 49160 | tf_op jit(solution)/shard_map/ppermute | solution.py:236
  5.2 5.9 %collective-permute-start.3 = (bf16[144,128]{1,0:T(8,128)(2,1)S(1)}, bf16[144,128]{1,0:T(8,128)(2,1)S(1)}, u32[]{:S(2)}, u32[]{:S(2)}) collective-permute-start(bf16[144,128]{1,0:T(8,128)(2,1)S(1)} %pad_maximum_fusion), channel_id=1, source_target_pairs={{0,4},{4,8},{8,12},{12,0},{1,5},{5,9},{9,13},{13,1},{2,6},{6,10},{... | collective-permute-start | bytes 110600 | tf_op jit(solution)/shard_map/ppermute | solution.py:240
  7.1 0.7 %copy-start.3 = (bf16[16,128]{1,0:T(8,128)(2,1)S(1)}, bf16[16,128]{1,0:T(8,128)(2,1)}, u32[]{:S(2)}) copy-start(bf16[16,128]{1,0:T(8,128)(2,1)} %param.17) | copy-start | bytes 12292
  7.1 2.9 %copy-start.2 = (bf16[128,1024]{1,0:T(8,128)(2,1)S(1)}, bf16[128,1024]{1,0:T(8,128)(2,1)}, u32[]{:S(2)}) copy-start(bf16[128,1024]{1,0:T(8,128)(2,1)} %q_ref.1) | copy-start | bytes 786436
  7.8 2.2 %copy-start = (bf16[128,1024]{1,0:T(8,128)(2,1)S(1)}, bf16[128,1024]{1,0:T(8,128)(2,1)}, u32[]{:S(2)}) copy-start(bf16[128,1024]{1,0:T(8,128)(2,1)} %o_ref.5) | copy-start | bytes 786436
  8.3 3.7 %collective-permute-start.4 = (bf16[16,128]{1,0:T(8,128)(2,1)S(1)}, bf16[16,128]{1,0:T(8,128)(2,1)S(1)}, u32[]{:S(2)}, u32[]{:S(2)}) collective-permute-start(bf16[16,128]{1,0:T(8,128)(2,1)S(1)} %slice.33), channel_id=1, source_target_pairs={{0,4},{1,3},{2,6},{3,1},{4,0},{5,9},{6,2},{7,11},{8,12},{9,5},{10,... | collective-permute-start | bytes 12296 | tf_op jit(solution)/shard_map/ppermute | solution.py:253
  12.0 2.6 %collective-permute-start.5 = (bf16[16,128]{1,0:T(8,128)(2,1)S(1)}, bf16[16,128]{1,0:T(8,128)(2,1)S(1)}, u32[]{:S(2)}, u32[]{:S(2)}) collective-permute-start(bf16[16,128]{1,0:T(8,128)(2,1)S(1)} %collective-permute-done.4), channel_id=1, source_target_pairs={{0,1},{1,0},{2,3},{3,2},{4,5},{5,4},{6,7},{7,6},{8,9},{9,8},{10,11... | collective-permute-start | bytes 12296 | tf_op jit(solution)/shard_map/ppermute | solution.py:236
  12.0 3.7 %collective-permute-start.6 = (f32[16,128]{1,0:T(8,128)S(1)}, f32[16,128]{1,0:T(8,128)S(1)}, u32[]{:S(2)}, u32[]{:S(2)}) collective-permute-start(f32[16,128]{1,0:T(8,128)S(1)} %slice.29), channel_id=1, source_target_pairs={{0,4},{4,0},{8,12},{12,8},{1,5},{5,1},{9,13},{13,9},{2,6},{6,2},{1... | collective-permute-start | bytes 24584 | tf_op jit(solution)/shard_map/ppermute | solution.py:236
  13.6 3.7 %collective-permute-start.7 = (f32[16,128]{1,0:T(8,128)S(1)}, f32[16,128]{1,0:T(8,128)S(1)}, u32[]{:S(2)}, u32[]{:S(2)}) collective-permute-start(f32[16,128]{1,0:T(8,128)S(1)} %slice.29), channel_id=1, source_target_pairs={{0,2},{1,3},{2,0},{3,1},{4,8},{5,9},{6,10},{7,11},{8,4},{9,5},{10,... | collective-permute-start | bytes 24584 | tf_op jit(solution)/shard_map/ppermute | solution.py:253
  14.6 8.8 %copy-start.1 = (bf16[128,2048]{1,0:T(8,128)(2,1)S(1)}, bf16[128,2048]{1,0:T(8,128)(2,1)}, u32[]{:S(2)}) copy-start(bf16[128,2048]{1,0:T(8,128)(2,1)} %x_ref.1) | copy-start | bytes 1572868
  17.2 3.3 %collective-permute-start.10 = (f32[32,128]{1,0:T(8,128)S(1)}, f32[32,128]{1,0:T(8,128)S(1)}, u32[]{:S(2)}, u32[]{:S(2)}) collective-permute-start(f32[32,128]{1,0:T(8,128)S(1)} %pad_maximum_fusion.1), channel_id=1, source_target_pairs={{0,3},{1,2},{2,1},{3,0},{4,7},{5,6},{6,5},{7,4},{8,11},{9,10},{10,... | collective-permute-start | bytes 49160 | tf_op jit(solution)/shard_map/ppermute | solution.py:236
  17.3 3.3 %collective-permute-start.8 = (f32[32,128]{1,0:T(8,128)S(1)}, f32[32,128]{1,0:T(8,128)S(1)}, u32[]{:S(2)}, u32[]{:S(2)}) collective-permute-start(f32[32,128]{1,0:T(8,128)S(1)} %pad_maximum_fusion.1), channel_id=1, source_target_pairs={{0,1},{1,0},{2,3},{3,2},{4,5},{5,4},{6,7},{7,6},{8,9},{9,8},{10,11... | collective-permute-start | bytes 49160 | tf_op jit(solution)/shard_map/ppermute | solution.py:236
  18.4 3.7 %collective-permute-start.9 = (f32[32,128]{1,0:T(8,128)S(1)}, f32[32,128]{1,0:T(8,128)S(1)}, u32[]{:S(2)}, u32[]{:S(2)}) collective-permute-start(f32[32,128]{1,0:T(8,128)S(1)} %pad_maximum_fusion.1), channel_id=1, source_target_pairs={{0,2},{1,3},{2,0},{3,1},{4,6},{5,7},{6,4},{7,5},{8,10},{9,11},{10,... | collective-permute-start | bytes 49160 | tf_op jit(solution)/shard_map/ppermute | solution.py:236
  19.4 4.0 %collective-permute-start.11 = (bf16[16,1152]{1,0:T(8,128)(2,1)S(1)}, bf16[16,1152]{1,0:T(8,128)(2,1)S(1)}, u32[]{:S(2)}, u32[]{:S(2)}) collective-permute-start(bf16[16,1152]{1,0:T(8,128)(2,1)S(1)} %get-tuple-element.55.up_ref), channel_id=1, source_target_pairs={{0,4},{4,0},{8,12},{12,8},{1,5},{5,1},{9,13},{13,9},{2,6},{6,2},{1... | collective-permute-start | bytes 110600 | tf_op jit(solution)/shard_map/ppermute | solution.py:236
  23.6 13.2 %collective-permute-start.13 = (bf16[16,5248]{1,0:T(8,128)(2,1)S(1)}, bf16[16,5248]{1,0:T(8,128)(2,1)S(1)}, u32[]{:S(2)}, u32[]{:S(2)}) collective-permute-start(bf16[16,5248]{1,0:T(8,128)(2,1)S(1)} %get-tuple-element.58.mine_ref), channel_id=1, source_target_pairs={{0,8},{4,12},{8,0},{12,4},{1,9},{5,13},{9,1},{13,5},{2,10},{6,14},... | collective-permute-start | bytes 503816 | tf_op jit(solution)/shard_map/ppermute | solution.py:236
  26.3 8.5 %collective-permute-start.12 = (bf16[32,2048]{1,0:T(8,128)(2,1)S(1)}, bf16[32,2048]{1,0:T(8,128)(2,1)S(1)}, u32[]{:S(2)}, u32[]{:S(2)}) collective-permute-start(bf16[32,2048]{1,0:T(8,128)(2,1)S(1)} %get-tuple-element.59), channel_id=1, source_target_pairs={{0,12},{4,8},{8,4},{12,0},{1,13},{5,9},{9,5},{13,1},{2,14},{6,10},... | collective-permute-start | bytes 393224 | tf_op jit(solution)/shard_map/ppermute | solution.py:236
  27.2 9.6 %collective-permute-start.14 = (bf16[32,2048]{1,0:T(8,128)(2,1)S(1)}, bf16[32,2048]{1,0:T(8,128)(2,1)S(1)}, u32[]{:S(2)}, u32[]{:S(2)}) collective-permute-start(bf16[32,2048]{1,0:T(8,128)(2,1)S(1)} %get-tuple-element.59), channel_id=1, source_target_pairs={{0,4},{4,0},{8,12},{12,8},{1,5},{5,1},{9,13},{13,9},{2,6},{6,2},{1... | collective-permute-start | bytes 393224 | tf_op jit(solution)/shard_map/ppermute | solution.py:236

commit v12 on v11

--- a/solution.py
+++ b/solution.py
@@ -197,23 +197,30 @@
     part_ref[...] = dot(dl_ref[...], x_ref[...], 1, 0)
 
 
-def partial_kernel(own_ref, x_ref, up_ref, near_ref, part_ref, both_ref):
+def partial_kernel(own_ref, x_ref, both_ref, query_ref, value_ref):
     part = dot(own_ref[...], x_ref[...], 1, 0).astype(BF16)
-    wide = part.shape[1]
-    part_ref[...] = part
-    both_ref[:, :wide] = part[:RANK]
-    both_ref[:, wide : 2 * wide] = part[RANK:]
-    both_ref[:, 2 * wide :] = (up_ref[...].astype(F32) + near_ref[...].astype(F32)).astype(BF16)
-
-
-def final_kernel(mine_ref, three_ref, two_ref, one_ref, down_ref, upq_ref, upv_ref):
+    both_ref[...] = part
+    query_ref[...] = part[:RANK]
+    value_ref[...] = part[RANK:]
+
+
+def combine_kernel(query_ref, up_ref, near_ref, send_ref):
+    wide = query_ref.shape[1]
+    send_ref[:, :wide] = query_ref[...]
+    send_ref[:, wide:] = (up_ref[...].astype(F32) + near_ref[...].astype(F32)).astype(BF16)
+
+
+def final_kernel(
+    mine_ref, one_ref, query_ref, query_two_ref, query_three_ref, value_two_ref, value_three_ref,
+    down_ref, upq_ref, upv_ref,
+):
     wide, size = down_ref.shape[1], upq_ref.shape[1]
-    for i in range(2):
-        rows, cut = slice(i * RANK, (i + 1) * RANK), slice(i * wide, (i + 1) * wide)
-        near = mine_ref[:, cut].astype(F32) + one_ref[rows].astype(F32)
-        far = two_ref[:, cut].astype(F32) + three_ref[rows].astype(F32)
-        down_ref[rows] = near + far
-    up = mine_ref[:, 2 * wide :].astype(F32) + two_ref[:, 2 * wide :].astype(F32)
+    near = mine_ref[...].astype(F32) + one_ref[...].astype(F32)
+    far = query_two_ref[:, :wide].astype(F32) + query_three_ref[...].astype(F32)
+    down_ref[:RANK] = near[:RANK] + far
+    far = value_two_ref[...].astype(F32) + value_three_ref[...].astype(F32)
+    down_ref[RANK:] = near[RANK:] + far
+    up = query_ref[:, wide:].astype(F32) + query_two_ref[:, wide:].astype(F32)
     upq_ref[...] = up[:, :size]
     upv_ref[...] = up[:, size:]
 
@@ -342,16 +349,19 @@
         return down.T, up[:, : heads * HEAD], up[:, heads * HEAD :]
 
     codes = jnp.concatenate([code_q, code_v + backs], axis=0)
-    dlow, near_up = lax.optimization_barrier((sum_fsdp(codes), swap(up, "seq", 1)))
-    part, both = call(
-        partial_kernel,
-        [((2 * RANK, wide), BF16), ((RANK, 2 * wide + (heads + 1) * HEAD), BF16)],
-    )(dlow.astype(BF16), x, up, near_up)
-    three, two, one = swap(part, "seq", 3), swap(both, "seq", 2), swap(part, "seq", 1)
+    near_up = swap(up, "seq", 1)
+    both, part_q, part_v = call(
+        partial_kernel, [((2 * RANK, wide), BF16), ((RANK, wide), BF16), ((RANK, wide), BF16)]
+    )(sum_fsdp(codes).astype(BF16), x)
+    (send_q,) = call(combine_kernel, [((RANK, wide + up.shape[1]), BF16)])(part_q, up, near_up)
+    value_two = swap(part_v, "seq", 2)
+    value_three = swap(value_two, "seq", 1)
+    query_two, query_three = swap(send_q, "seq", 2), swap(part_q, "seq", 3)
+    one = swap(both, "seq", 1)
     down, up_q, up_v = call(
         final_kernel,
         [((2 * RANK, wide), F32), ((RANK, heads * HEAD), F32), ((RANK, HEAD), F32)],
-    )(both, three, two, one)
+    )(both, one, send_q, query_two, query_three, value_two, value_three)
     return down.T, up_q, up_v
 
 

time: 37.7 us -> 35.8 us (0.950)
  waiting for transfers between devices: 15.2 us -> 9.73 us
  starting transfers between devices: 16.2 us -> 19.7 us
    ppermute x12 -> x14, waiting for transfers between devices: 13.1 us -> 7.62 us  [swap(): return lax.ppermute(array, axis, [(i, i ^ bit) for i in range(size)])]
    ppermute x12 -> x14, starting transfers between devices: 11.6 us -> 15.2 us  [swap(): return lax.ppermute(array, axis, [(i, i ^ bit) for i in range(size)])]
  transfers between devices with their start and end apart: 15 -> 17, of which waited for: 9 -> 9; matrix products, arithmetic and copies ran while one was open for 1% -> 1% of each run, Pallas kernels for 6% -> 7%
where the time goes in v12:
time: 35.8 us; the launch traced here: 35.7 us
  starting transfers between devices  19.7 us (55%)
  waiting for transfers between devices  9.73 us (27%)
  Pallas kernels  4.65 us (13%)
  between operations  0.79 us (2%)
  other arithmetic  0.48 us (1%)
    ppermute x14, starting transfers between devices, swap(): return lax.ppermute(array, axis, [(i, i ^ bit) for i in range(size)])  15.2 us
    ppermute x14, waiting for transfers between devices, swap(): return lax.ppermute(array, axis, [(i, i ^ bit) for i in range(size)])  7.62 us
    ppermute x2, starting transfers between devices, inner(): return lax.ppermute(array, ('seq', 'fsdp'), moves)  2.67 us
    ppermute x1, starting transfers between devices, shift(): return lax.ppermute(array, 'seq', moves)  1.87 us
    ppermute x2, waiting for transfers between devices, inner(): return lax.ppermute(array, ('seq', 'fsdp'), moves)  1.68 us
    pallas_call x1, Pallas kernels, body(): call(functools.partial(lowrank_kernel, send), [((2 * RANK, tok), F32), ((...  1.4 us
    pallas_call x1, Pallas kernels, body(): call(functools.partial(grads_kernel, count, send, blocks, heads), [((RANK...  0.85 us
    pallas_call x1, Pallas kernels, body(): call(final_kernel, [((2 * RANK, wide), F32), ((RANK, heads * HEAD), F32),...  0.78 us
  transfers between devices with their start and end apart: 17, of which 9 were waited for; matrix products, arithmetic and copies ran while one was open for 1% of the time, Pallas kernels for 7%

profile of v12, /device:TPU:0, one launch (start us, length us, event | category | flops | bytes accessed | tf_op | source)
XLA Modules:
  0.0 35.7 jit_solution(2502452363189691037)
XLA Ops:
  0.6 1.4 %shard_map.112 = (f32[32,128]{1,0:T(8,128)S(1)}, bf16[128,128]{1,0:T(8,128)(2,1)S(1)}, bf16[128,128]{1,0:T(8,128)(2,1)S(1)}, bf16[128,128]{1,0:T(8,128)(2,1)S(1)}, bf16[16,1024]{1,0:T(8,128)(2,1)S(1)}) custom-call(bf16[128,2048]{1,0:T(8,128)(2,1)} %x_ref.1, bf16[32,2048]{1,0:T(8,128)(2,1)} %bitcast.8, bf16[128,128]{1,0:T(8,128)(2,1)} %refs_2_.1, ...), custom_call_target="tpu_custom_call" | custom-call | flops 1 | bytes 1 | tf_op jit(solution)/shard_map/pallas_call | solution.py:269
  2.1 0.5 %collective-permute-start = (f32[32,128]{1,0:T(8,128)S(1)}, f32[32,128]{1,0:T(8,128)S(1)}, u32[]{:S(2)}, u32[]{:S(2)}) collective-permute-start(f32[32,128]{1,0:T(8,128)S(1)} %get-tuple-element.32), channel_id=1, source_target_pairs={{0,1},{1,0},{2,3},{3,2},{4,5},{5,4},{6,7},{7,6},{8,9},{9,8},{10,11... | collective-permute-start | bytes 49160 | tf_op jit(solution)/shard_map/ppermute | solution.py:243
  2.6 2.6 %collective-permute-start.1 = (f32[32,128]{1,0:T(8,128)S(1)}, f32[32,128]{1,0:T(8,128)S(1)}, u32[]{:S(2)}, u32[]{:S(2)}) collective-permute-start(f32[32,128]{1,0:T(8,128)S(1)} %get-tuple-element.32), channel_id=1, source_target_pairs={{0,2},{1,3},{2,0},{3,1},{4,6},{5,7},{6,4},{7,5},{8,10},{9,11},{10,... | collective-permute-start | bytes 49160 | tf_op jit(solution)/shard_map/ppermute | solution.py:243
  5.1 0.1 collective-permute-start.2
  5.2 1.9 %collective-permute-start.3 = (bf16[144,128]{1,0:T(8,128)(2,1)S(1)}, bf16[144,128]{1,0:T(8,128)(2,1)S(1)}, u32[]{:S(2)}, u32[]{:S(2)}) collective-permute-start(bf16[144,128]{1,0:T(8,128)(2,1)S(1)} %pad_maximum_fusion), channel_id=1, source_target_pairs={{0,4},{4,8},{8,12},{12,0},{1,5},{5,9},{9,13},{13,1},{2,6},{6,10},{... | collective-permute-start | bytes 110600 | tf_op jit(solution)/shard_map/ppermute | solution.py:247
  7.1 0.4 %multiply_sine_fusion = (f32[192,64]{1,0:T(8,128)S(1)}, f32[192,64]{1,0:T(8,128)S(1)}) fusion(f32[64]{0:T(128)S(1)} %multiply_power_fusion, f32[192]{0:T(256)S(1)} %add_convert_fusion.1), kind=kLoop, calls=%fused_computation | loop fusion | flops 12288 | bytes 99328 | tf_op jit(solution)/shard_map/sin | solution.py:294
  7.6 0.2 copy-done.3
  7.8 0.5 %collective-permute-done.2 = f32[32,128]{1,0:T(8,128)S(1)} collective-permute-done((f32[32,128]{1,0:T(8,128)S(1)}, f32[32,128]{1,0:T(8,128)S(1)}, u32[]{:S(2)}, u32[]{:S(2)}) %collective-permute-start.2) | collective-permute-done | bytes 16416 | tf_op jit(solution)/shard_map/ppermute | solution.py:243
  8.3 1.6 %collective-permute-start.4 = (bf16[16,128]{1,0:T(8,128)(2,1)S(1)}, bf16[16,128]{1,0:T(8,128)(2,1)S(1)}, u32[]{:S(2)}, u32[]{:S(2)}) collective-permute-start(bf16[16,128]{1,0:T(8,128)(2,1)S(1)} %slice.33), channel_id=1, source_target_pairs={{0,4},{1,3},{2,6},{3,1},{4,0},{5,9},{6,2},{7,11},{8,12},{9,5},{10,... | collective-permute-start | bytes 12296 | tf_op jit(solution)/shard_map/ppermute | solution.py:260
  10.0 0.7 %shard_map.113 = (bf16[1024,128]{1,0:T(8,128)(2,1)S(1)}, bf16[128,128]{1,0:T(8,128)(2,1)S(1)}, f32[128,1024]{1,0:T(8,128)S(1)}, f32[128,1024]{1,0:T(8,128)S(1)},...) custom-call(f32[32,128]{1,0:T(8,128)S(1)} %add_add_fusion.low_ref, bf16[128,1024]{1,0:T(8,128)(2,1)S(1)} %copy-done.2, ...), custom_call_target="tpu_custom_call" | custom-call | flops 3145728 | bytes 3145728 | tf_op jit(solution)/shard_map/pallas_call | solution.py:304
  10.7 0.4 %collective-permute-done.3 = bf16[144,128]{1,0:T(8,128)(2,1)S(1)} collective-permute-done((bf16[144,128]{1,0:T(8,128)(2,1)S(1)}, bf16[144,128]{1,0:T(8,128)(2,1)S(1)}, u32[]{:S(2)}, u32[]{:S(2)}) %collective-permute-start.3) | collective-permute-done | bytes 36896 | tf_op jit(solution)/shard_map/ppermute | solution.py:247
  11.1 0.7 %shard_map.114 = (f32[192,1024]{1,0:T(8,128)S(1)}, bf16[128,64]{1,0:T(8,128)(2,1)S(1)}, f32[192,128]{1,0:T(8,128)S(1)}, f32[32,128]{1,0:T(8,128)S(1)}) custom-call(bf16[1024,128]{1,0:T(8,128)(2,1)S(1)} %get-tuple-element.40.qr_ref, f32[128,1024]{1,0:T(8,128)S(1)} %get-tuple-element.41.s_ref, bf16[128,1024]{1,0:T(8,128)(2,1)S(1)} %copy-done, ...), custom_call_target="tpu_custom_call" | custom-call | flops 5242880 | bytes 5242880 | tf_op jit(solution)/shard_map/pallas_call | solution.py:318
  11.9 0.1 collective-permute-done.4
  12.0 1.6 %collective-permute-start.6 = (f32[16,128]{1,0:T(8,128)S(1)}, f32[16,128]{1,0:T(8,128)S(1)}, u32[]{:S(2)}, u32[]{:S(2)}) collective-permute-start(f32[16,128]{1,0:T(8,128)S(1)} %slice.29), channel_id=1, source_target_pairs={{0,4},{4,0},{8,12},{12,8},{1,5},{5,1},{9,13},{13,9},{2,6},{6,2},{1... | collective-permute-start | bytes 24584 | tf_op jit(solution)/shard_map/ppermute | solution.py:243
  13.6 1.0 %collective-permute-start.7 = (f32[16,128]{1,0:T(8,128)S(1)}, f32[16,128]{1,0:T(8,128)S(1)}, u32[]{:S(2)}, u32[]{:S(2)}) collective-permute-start(f32[16,128]{1,0:T(8,128)S(1)} %slice.29), channel_id=1, source_target_pairs={{0,2},{1,3},{2,0},{3,1},{4,8},{5,9},{6,10},{7,11},{8,4},{9,5},{10,... | collective-permute-start | bytes 24584 | tf_op jit(solution)/shard_map/ppermute | solution.py:260
  14.6 0.9 %shard_map.115 = (f32[16,128]{1,0:T(8,128)S(1)}, bf16[16,1152]{1,0:T(8,128)(2,1)S(1)}) custom-call(f32[32,128]{1,0:T(8,128)S(1)} %add_add_fusion.low_ref, bf16[1,16,128]{2,1,0:T(8,128)(2,1)S(1)} %select_bitcast_fusion.far_ref, bf16[1,144,128]{2,1,0:T(8,128)(2,1)S(1)} %bitcast.7, bf16[128,1024]{1,0:T(8,128)(2,1)S(1)} %copy-done, ...), custom_call_target="tpu_custom_call" | custom-call | flops 25165824 | bytes 25165824 | tf_op jit(solution)/shard_map/pallas_call | solution.py:337
  15.5 0.2 collective-permute-done.6
  15.7 1.6 %collective-permute-done.7 = f32[16,128]{1,0:T(8,128)S(1)} collective-permute-done((f32[16,128]{1,0:T(8,128)S(1)}, f32[16,128]{1,0:T(8,128)S(1)}, u32[]{:S(2)}, u32[]{:S(2)}) %collective-permute-start.7) | collective-permute-done | bytes 8224 | tf_op jit(solution)/shard_map/ppermute | solution.py:260
  17.2 0.1 collective-permute-start.10
  17.3 1.1 %collective-permute-start.8 = (f32[32,128]{1,0:T(8,128)S(1)}, f32[32,128]{1,0:T(8,128)S(1)}, u32[]{:S(2)}, u32[]{:S(2)}) collective-permute-start(f32[32,128]{1,0:T(8,128)S(1)} %pad_maximum_fusion.1), channel_id=1, source_target_pairs={{0,1},{1,0},{2,3},{3,2},{4,5},{5,4},{6,7},{7,6},{8,9},{9,8},{10,11... | collective-permute-start | bytes 49160 | tf_op jit(solution)/shard_map/ppermute | solution.py:243
  18.4 1.0 %collective-permute-start.9 = (f32[32,128]{1,0:T(8,128)S(1)}, f32[32,128]{1,0:T(8,128)S(1)}, u32[]{:S(2)}, u32[]{:S(2)}) collective-permute-start(f32[32,128]{1,0:T(8,128)S(1)} %pad_maximum_fusion.1), channel_id=1, source_target_pairs={{0,2},{1,3},{2,0},{3,1},{4,6},{5,7},{6,4},{7,5},{8,10},{9,11},{10,... | collective-permute-start | bytes 49160 | tf_op jit(solution)/shard_map/ppermute | solution.py:243
  19.4 1.1 %collective-permute-start.12 = (bf16[16,1152]{1,0:T(8,128)(2,1)S(1)}, bf16[16,1152]{1,0:T(8,128)(2,1)S(1)}, u32[]{:S(2)}, u32[]{:S(2)}) collective-permute-start(bf16[16,1152]{1,0:T(8,128)(2,1)S(1)} %get-tuple-element.56.up_ref), channel_id=1, source_target_pairs={{0,4},{4,0},{8,12},{12,8},{1,5},{5,1},{9,13},{13,9},{2,6},{6,2},{1... | collective-permute-start | bytes 110600 | tf_op jit(solution)/shard_map/ppermute | solution.py:243
  20.6 1.6 %collective-permute-done.9 = f32[32,128]{1,0:T(8,128)S(1)} collective-permute-done((f32[32,128]{1,0:T(8,128)S(1)}, f32[32,128]{1,0:T(8,128)S(1)}, u32[]{:S(2)}, u32[]{:S(2)}) %collective-permute-start.9) | collective-permute-done | bytes 16416 | tf_op jit(solution)/shard_map/ppermute | solution.py:243
  22.2 0.2 shard_map.116
  22.4 2.3 %collective-permute-start.15 = (bf16[16,2048]{1,0:T(8,128)(2,1)S(1)}, bf16[16,2048]{1,0:T(8,128)(2,1)S(1)}, u32[]{:S(2)}, u32[]{:S(2)}) collective-permute-start(bf16[16,2048]{1,0:T(8,128)(2,1)S(1)} %get-tuple-element.57), channel_id=1, source_target_pairs={{0,8},{4,12},{8,0},{12,4},{1,9},{5,13},{9,1},{13,5},{2,10},{6,14},... | collective-permute-start | bytes 196616 | tf_op jit(solution)/shard_map/ppermute | solution.py:243
  24.8 0.8 %collective-permute-start.11 = (bf16[32,2048]{1,0:T(8,128)(2,1)S(1)}, bf16[32,2048]{1,0:T(8,128)(2,1)S(1)}, u32[]{:S(2)}, u32[]{:S(2)}) collective-permute-start(bf16[32,2048]{1,0:T(8,128)(2,1)S(1)} %get-tuple-element.54.mine_ref), channel_id=1, source_target_pairs={{0,4},{4,0},{8,12},{12,8},{1,5},{5,1},{9,13},{13,9},{2,6},{6,2},{1... | collective-permute-start | bytes 393224 | tf_op jit(solution)/shard_map/ppermute | solution.py:243
  25.5 1.1 %collective-permute-start.13 = (bf16[16,3200]{1,0:T(8,128)(2,1)S(1)}, bf16[16,3200]{1,0:T(8,128)(2,1)S(1)}, u32[]{:S(2)}, u32[]{:S(2)}) collective-permute-start(bf16[16,3200]{1,0:T(8,128)(2,1)S(1)} %shard_map.117.query_ref), channel_id=1, source_target_pairs={{0,8},{4,12},{8,0},{12,4},{1,9},{5,13},{9,1},{13,5},{2,10},{6,14},... | collective-permute-start | bytes 307208 | tf_op jit(solution)/shard_map/ppermute | solution.py:243
  26.6 2.6 %collective-permute-start.14 = (bf16[16,2048]{1,0:T(8,128)(2,1)S(1)}, bf16[16,2048]{1,0:T(8,128)(2,1)S(1)}, u32[]{:S(2)}, u32[]{:S(2)}) collective-permute-start(bf16[16,2048]{1,0:T(8,128)(2,1)S(1)} %get-tuple-element.55.query_ref), channel_id=1, source_target_pairs={{0,12},{4,8},{8,4},{12,0},{1,13},{5,9},{9,5},{13,1},{2,14},{6,10},... | collective-permute-start | bytes 196616 | tf_op jit(solution)/shard_map/ppermute | solution.py:243
  29.3 0.3 collective-permute-start.16
  29.6 4.4 %collective-permute-done.14.query_three_ref = bf16[16,2048]{1,0:T(8,128)(2,1)S(1)} collective-permute-done((bf16[16,2048]{1,0:T(8,128)(2,1)S(1)}, bf16[16,2048]{1,0:T(8,128)(2,1)S(1)}, u32[]{:S(2)}, u32[]{:S(2)}) %collective-permute-start.14) | collective-permute-done | bytes 65568 | tf_op jit(solution)/shard_map/ppermute | solution.py:243
  34.0 0.9 %collective-permute-done.13.query_two_ref = bf16[16,3200]{1,0:T(8,128)(2,1)S(1)} collective-permute-done((bf16[16,3200]{1,0:T(8,128)(2,1)S(1)}, bf16[16,3200]{1,0:T(8,128)(2,1)S(1)}, u32[]{:S(2)}, u32[]{:S(2)}) %collective-permute-start.13) | collective-permute-done | bytes 102432 | tf_op jit(solution)/shard_map/ppermute | solution.py:243
  34.9 0.8 %shard_map.118 = (f32[32,2048]{1,0:T(8,128)}, f32[16,1024]{1,0:T(8,128)}, f32[16,128]{1,0:T(8,128)}) custom-call(bf16[32,2048]{1,0:T(8,128)(2,1)S(1)} %get-tuple-element.54.mine_ref, bf16[32,2048]{1,0:T(8,128)(2,1)S(1)} %collective-permute-done.11.one_ref, bf16[16,3200]{1,0:T(8,128)(2,1)S(1)} %shard_map.117.query_ref, ...), custom_call_target="tpu_custom_call" | custom-call | flops 1 | bytes 1 | tf_op jit(solution)/shard_map/pallas_call | solution.py:361
  (37 shorter events, 0.2 us)
Async XLA Ops:
  2.0 3.2 %copy-start.4 = (s32[128]{0:T(128)S(1)}, s32[128]{0:T(128)}, u32[]{:S(2)}) copy-start(s32[128]{0:T(128)} %param.14) | copy-start | bytes 1540
  2.1 5.8 %collective-permute-start = (f32[32,128]{1,0:T(8,128)S(1)}, f32[32,128]{1,0:T(8,128)S(1)}, u32[]{:S(2)}, u32[]{:S(2)}) collective-permute-start(f32[32,128]{1,0:T(8,128)S(1)} %get-tuple-element.32), channel_id=1, source_target_pairs={{0,1},{1,0},{2,3},{3,2},{4,5},{5,4},{6,7},{7,6},{8,9},{9,8},{10,11... | collective-permute-start | bytes 49160 | tf_op jit(solution)/shard_map/ppermute | solution.py:243
  2.6 5.2 %collective-permute-start.1 = (f32[32,128]{1,0:T(8,128)S(1)}, f32[32,128]{1,0:T(8,128)S(1)}, u32[]{:S(2)}, u32[]{:S(2)}) collective-permute-start(f32[32,128]{1,0:T(8,128)S(1)} %get-tuple-element.32), channel_id=1, source_target_pairs={{0,2},{1,3},{2,0},{3,1},{4,6},{5,7},{6,4},{7,5},{8,10},{9,11},{10,... | collective-permute-start | bytes 49160 | tf_op jit(solution)/shard_map/ppermute | solution.py:243
  5.1 3.2 %collective-permute-start.2 = (f32[32,128]{1,0:T(8,128)S(1)}, f32[32,128]{1,0:T(8,128)S(1)}, u32[]{:S(2)}, u32[]{:S(2)}) collective-permute-start(f32[32,128]{1,0:T(8,128)S(1)} %get-tuple-element.32), channel_id=1, source_target_pairs={{0,3},{1,2},{2,1},{3,0},{4,7},{5,6},{6,5},{7,4},{8,11},{9,10},{10,... | collective-permute-start | bytes 49160 | tf_op jit(solution)/shard_map/ppermute | solution.py:243
  5.2 5.9 %collective-permute-start.3 = (bf16[144,128]{1,0:T(8,128)(2,1)S(1)}, bf16[144,128]{1,0:T(8,128)(2,1)S(1)}, u32[]{:S(2)}, u32[]{:S(2)}) collective-permute-start(bf16[144,128]{1,0:T(8,128)(2,1)S(1)} %pad_maximum_fusion), channel_id=1, source_target_pairs={{0,4},{4,8},{8,12},{12,0},{1,5},{5,9},{9,13},{13,1},{2,6},{6,10},{... | collective-permute-start | bytes 110600 | tf_op jit(solution)/shard_map/ppermute | solution.py:247
  7.1 0.7 %copy-start.3 = (bf16[16,128]{1,0:T(8,128)(2,1)S(1)}, bf16[16,128]{1,0:T(8,128)(2,1)}, u32[]{:S(2)}) copy-start(bf16[16,128]{1,0:T(8,128)(2,1)} %param.17) | copy-start | bytes 12292
  7.1 2.9 %copy-start.2 = (bf16[128,1024]{1,0:T(8,128)(2,1)S(1)}, bf16[128,1024]{1,0:T(8,128)(2,1)}, u32[]{:S(2)}) copy-start(bf16[128,1024]{1,0:T(8,128)(2,1)} %q_ref.1) | copy-start | bytes 786436
  7.8 2.2 %copy-start = (bf16[128,1024]{1,0:T(8,128)(2,1)S(1)}, bf16[128,1024]{1,0:T(8,128)(2,1)}, u32[]{:S(2)}) copy-start(bf16[128,1024]{1,0:T(8,128)(2,1)} %o_ref.5) | copy-start | bytes 786436
  8.3 3.7 %collective-permute-start.4 = (bf16[16,128]{1,0:T(8,128)(2,1)S(1)}, bf16[16,128]{1,0:T(8,128)(2,1)S(1)}, u32[]{:S(2)}, u32[]{:S(2)}) collective-permute-start(bf16[16,128]{1,0:T(8,128)(2,1)S(1)} %slice.33), channel_id=1, source_target_pairs={{0,4},{1,3},{2,6},{3,1},{4,0},{5,9},{6,2},{7,11},{8,12},{9,5},{10,... | collective-permute-start | bytes 12296 | tf_op jit(solution)/shard_map/ppermute | solution.py:260
  12.0 2.6 %collective-permute-start.5 = (bf16[16,128]{1,0:T(8,128)(2,1)S(1)}, bf16[16,128]{1,0:T(8,128)(2,1)S(1)}, u32[]{:S(2)}, u32[]{:S(2)}) collective-permute-start(bf16[16,128]{1,0:T(8,128)(2,1)S(1)} %collective-permute-done.4), channel_id=1, source_target_pairs={{0,1},{1,0},{2,3},{3,2},{4,5},{5,4},{6,7},{7,6},{8,9},{9,8},{10,11... | collective-permute-start | bytes 12296 | tf_op jit(solution)/shard_map/ppermute | solution.py:243
  12.0 3.7 %collective-permute-start.6 = (f32[16,128]{1,0:T(8,128)S(1)}, f32[16,128]{1,0:T(8,128)S(1)}, u32[]{:S(2)}, u32[]{:S(2)}) collective-permute-start(f32[16,128]{1,0:T(8,128)S(1)} %slice.29), channel_id=1, source_target_pairs={{0,4},{4,0},{8,12},{12,8},{1,5},{5,1},{9,13},{13,9},{2,6},{6,2},{1... | collective-permute-start | bytes 24584 | tf_op jit(solution)/shard_map/ppermute | solution.py:243
  13.6 3.7 %collective-permute-start.7 = (f32[16,128]{1,0:T(8,128)S(1)}, f32[16,128]{1,0:T(8,128)S(1)}, u32[]{:S(2)}, u32[]{:S(2)}) collective-permute-start(f32[16,128]{1,0:T(8,128)S(1)} %slice.29), channel_id=1, source_target_pairs={{0,2},{1,3},{2,0},{3,1},{4,8},{5,9},{6,10},{7,11},{8,4},{9,5},{10,... | collective-permute-start | bytes 24584 | tf_op jit(solution)/shard_map/ppermute | solution.py:260
  14.6 7.6 %copy-start.1 = (bf16[128,2048]{1,0:T(8,128)(2,1)S(1)}, bf16[128,2048]{1,0:T(8,128)(2,1)}, u32[]{:S(2)}) copy-start(bf16[128,2048]{1,0:T(8,128)(2,1)} %x_ref.1) | copy-start | bytes 1572868
  17.2 3.3 %collective-permute-start.10 = (f32[32,128]{1,0:T(8,128)S(1)}, f32[32,128]{1,0:T(8,128)S(1)}, u32[]{:S(2)}, u32[]{:S(2)}) collective-permute-start(f32[32,128]{1,0:T(8,128)S(1)} %pad_maximum_fusion.1), channel_id=1, source_target_pairs={{0,3},{1,2},{2,1},{3,0},{4,7},{5,6},{6,5},{7,4},{8,11},{9,10},{10,... | collective-permute-start | bytes 49160 | tf_op jit(solution)/shard_map/ppermute | solution.py:243
  17.3 3.3 %collective-permute-start.8 = (f32[32,128]{1,0:T(8,128)S(1)}, f32[32,128]{1,0:T(8,128)S(1)}, u32[]{:S(2)}, u32[]{:S(2)}) collective-permute-start(f32[32,128]{1,0:T(8,128)S(1)} %pad_maximum_fusion.1), channel_id=1, source_target_pairs={{0,1},{1,0},{2,3},{3,2},{4,5},{5,4},{6,7},{7,6},{8,9},{9,8},{10,11... | collective-permute-start | bytes 49160 | tf_op jit(solution)/shard_map/ppermute | solution.py:243
  18.4 3.7 %collective-permute-start.9 = (f32[32,128]{1,0:T(8,128)S(1)}, f32[32,128]{1,0:T(8,128)S(1)}, u32[]{:S(2)}, u32[]{:S(2)}) collective-permute-start(f32[32,128]{1,0:T(8,128)S(1)} %pad_maximum_fusion.1), channel_id=1, source_target_pairs={{0,2},{1,3},{2,0},{3,1},{4,6},{5,7},{6,4},{7,5},{8,10},{9,11},{10,... | collective-permute-start | bytes 49160 | tf_op jit(solution)/shard_map/ppermute | solution.py:243
  19.4 6.1 %collective-permute-start.12 = (bf16[16,1152]{1,0:T(8,128)(2,1)S(1)}, bf16[16,1152]{1,0:T(8,128)(2,1)S(1)}, u32[]{:S(2)}, u32[]{:S(2)}) collective-permute-start(bf16[16,1152]{1,0:T(8,128)(2,1)S(1)} %get-tuple-element.56.up_ref), channel_id=1, source_target_pairs={{0,4},{4,0},{8,12},{12,8},{1,5},{5,1},{9,13},{13,9},{2,6},{6,2},{1... | collective-permute-start | bytes 110600 | tf_op jit(solution)/shard_map/ppermute | solution.py:243
  22.4 6.9 %collective-permute-start.15 = (bf16[16,2048]{1,0:T(8,128)(2,1)S(1)}, bf16[16,2048]{1,0:T(8,128)(2,1)S(1)}, u32[]{:S(2)}, u32[]{:S(2)}) collective-permute-start(bf16[16,2048]{1,0:T(8,128)(2,1)S(1)} %get-tuple-element.57), channel_id=1, source_target_pairs={{0,8},{4,12},{8,0},{12,4},{1,9},{5,13},{9,1},{13,5},{2,10},{6,14},... | collective-permute-start | bytes 196616 | tf_op jit(solution)/shard_map/ppermute | solution.py:243
  24.8 10.1 %collective-permute-start.11 = (bf16[32,2048]{1,0:T(8,128)(2,1)S(1)}, bf16[32,2048]{1,0:T(8,128)(2,1)S(1)}, u32[]{:S(2)}, u32[]{:S(2)}) collective-permute-start(bf16[32,2048]{1,0:T(8,128)(2,1)S(1)} %get-tuple-element.54.mine_ref), channel_id=1, source_target_pairs={{0,4},{4,0},{8,12},{12,8},{1,5},{5,1},{9,13},{13,9},{2,6},{6,2},{1... | collective-permute-start | bytes 393224 | tf_op jit(solution)/shard_map/ppermute | solution.py:243
  25.5 9.3 %collective-permute-start.13 = (bf16[16,3200]{1,0:T(8,128)(2,1)S(1)}, bf16[16,3200]{1,0:T(8,128)(2,1)S(1)}, u32[]{:S(2)}, u32[]{:S(2)}) collective-permute-start(bf16[16,3200]{1,0:T(8,128)(2,1)S(1)} %shard_map.117.query_ref), channel_id=1, source_target_pairs={{0,8},{4,12},{8,0},{12,4},{1,9},{5,13},{9,1},{13,5},{2,10},{6,14},... | collective-permute-start | bytes 307208 | tf_op jit(solution)/shard_map/ppermute | solution.py:243
  26.6 7.4 %collective-permute-start.14 = (bf16[16,2048]{1,0:T(8,128)(2,1)S(1)}, bf16[16,2048]{1,0:T(8,128)(2,1)S(1)}, u32[]{:S(2)}, u32[]{:S(2)}) collective-permute-start(bf16[16,2048]{1,0:T(8,128)(2,1)S(1)} %get-tuple-element.55.query_ref), channel_id=1, source_target_pairs={{0,12},{4,8},{8,4},{12,0},{1,13},{5,9},{9,5},{13,1},{2,14},{6,10},... | collective-permute-start | bytes 196616 | tf_op jit(solution)/shard_map/ppermute | solution.py:243
  29.3 5.6 %collective-permute-start.16 = (bf16[16,2048]{1,0:T(8,128)(2,1)S(1)}, bf16[16,2048]{1,0:T(8,128)(2,1)S(1)}, u32[]{:S(2)}, u32[]{:S(2)}) collective-permute-start(bf16[16,2048]{1,0:T(8,128)(2,1)S(1)} %collective-permute-done.15.value_two_ref), channel_id=1, source_target_pairs={{0,4},{4,0},{8,12},{12,8},{1,5},{5,1},{9,13},{13,9},{2,6},{6,2},{1... | collective-permute-start | bytes 196616 | tf_op jit(solution)/shard_map/ppermute | solution.py:243

commit v13 on v11

--- a/solution.py
+++ b/solution.py
@@ -197,25 +197,35 @@
     part_ref[...] = dot(dl_ref[...], x_ref[...], 1, 0)
 
 
-def partial_kernel(own_ref, x_ref, up_ref, near_ref, part_ref, both_ref):
+def partial_kernel(own_ref, x_ref, up_ref, both_ref, relay_ref, rest_ref):
     part = dot(own_ref[...], x_ref[...], 1, 0).astype(BF16)
-    wide = part.shape[1]
-    part_ref[...] = part
+    wide, up = part.shape[1], up_ref[...]
+    cut = wide - rest_ref.shape[1]
     both_ref[:, :wide] = part[:RANK]
     both_ref[:, wide : 2 * wide] = part[RANK:]
-    both_ref[:, 2 * wide :] = (up_ref[...].astype(F32) + near_ref[...].astype(F32)).astype(BF16)
-
-
-def final_kernel(mine_ref, three_ref, two_ref, one_ref, down_ref, upq_ref, upv_ref):
+    both_ref[:, 2 * wide :] = up
+    relay_ref[:, :cut] = part[:RANK, :cut]
+    relay_ref[:, cut : cut + wide] = part[RANK:]
+    relay_ref[:, cut + wide :] = up
+    rest_ref[...] = part[:RANK, cut:]
+
+
+def final_kernel(
+    mine_ref, one_ref, rest_two_ref, rest_three_ref, relay_two_ref, first_three_ref, second_three_ref,
+    down_ref, upq_ref, upv_ref,
+):
     wide, size = down_ref.shape[1], upq_ref.shape[1]
-    for i in range(2):
-        rows, cut = slice(i * RANK, (i + 1) * RANK), slice(i * wide, (i + 1) * wide)
-        near = mine_ref[:, cut].astype(F32) + one_ref[rows].astype(F32)
-        far = two_ref[:, cut].astype(F32) + three_ref[rows].astype(F32)
-        down_ref[rows] = near + far
-    up = mine_ref[:, 2 * wide :].astype(F32) + two_ref[:, 2 * wide :].astype(F32)
-    upq_ref[...] = up[:, :size]
-    upv_ref[...] = up[:, size:]
+    cut = wide - rest_three_ref.shape[1]
+    near = mine_ref[...].astype(F32) + one_ref[...].astype(F32)
+    relay = jnp.concatenate([first_three_ref[...], second_three_ref[...]], axis=1)
+    relay = relay_two_ref[...].astype(F32) + relay.astype(F32)
+    down_ref[:RANK, :cut] = near[:, :cut] + relay[:, :cut]
+    rest = rest_two_ref[...].astype(F32) + rest_three_ref[...].astype(F32)
+    down_ref[:RANK, cut:] = near[:, cut:wide] + rest
+    others = near[:, wide:] + relay[:, cut:]
+    down_ref[RANK:] = others[:, :wide]
+    upq_ref[...] = others[:, wide : wide + size]
+    upv_ref[...] = others[:, wide + size :]
 
 
 def body(x, q, k, v, o, segment, a, wq, wv):
@@ -342,16 +352,20 @@
         return down.T, up[:, : heads * HEAD], up[:, heads * HEAD :]
 
     codes = jnp.concatenate([code_q, code_v + backs], axis=0)
-    dlow, near_up = lax.optimization_barrier((sum_fsdp(codes), swap(up, "seq", 1)))
-    part, both = call(
+    cut, size = HEAD, (heads + 1) * HEAD
+    half = (cut + wide + size) // 2 // HEAD * HEAD
+    both, relay, rest = call(
         partial_kernel,
-        [((2 * RANK, wide), BF16), ((RANK, 2 * wide + (heads + 1) * HEAD), BF16)],
-    )(dlow.astype(BF16), x, up, near_up)
-    three, two, one = swap(part, "seq", 3), swap(both, "seq", 2), swap(part, "seq", 1)
+        [((RANK, 2 * wide + size), BF16), ((RANK, cut + wide + size), BF16), ((RANK, wide - cut), BF16)],
+    )(sum_fsdp(codes).astype(BF16), x, up)
+    relay_two = swap(relay, "seq", 2)
+    relay_three = [swap(part, "seq", 1) for part in (relay_two[:, :half], relay_two[:, half:])]
+    rest_two, rest_three = swap(rest, "seq", 2), swap(rest, "seq", 3)
+    one = swap(both, "seq", 1)
     down, up_q, up_v = call(
         final_kernel,
         [((2 * RANK, wide), F32), ((RANK, heads * HEAD), F32), ((RANK, HEAD), F32)],
-    )(both, three, two, one)
+    )(both, one, rest_two, rest_three, relay_two, *relay_three)
     return down.T, up_q, up_v
 
 

time: 37.7 us -> 39 us (1.034)
  starting transfers between devices: 16.2 us -> 19.4 us
  waiting for transfers between devices: 15.2 us -> 13.2 us
    ppermute x12 -> x14, starting transfers between devices: 11.6 us -> 14.8 us  [swap(): return lax.ppermute(array, axis, [(i, i ^ bit) for i in range(size)])]
    ppermute x12 -> x14, waiting for transfers between devices: 13.1 us -> 11.1 us  [swap(): return lax.ppermute(array, axis, [(i, i ^ bit) for i in range(size)])]
  transfers between devices with their start and end apart: 15 -> 17, of which waited for: 9 -> 10; matrix products, arithmetic and copies ran while one was open for 1% -> 1% of each run, Pallas kernels for 6% -> 6%
where the time goes in v13:
time: 39 us; the launch traced here: 38.8 us
  starting transfers between devices  19.4 us (50%)
  waiting for transfers between devices  13.2 us (34%)
  Pallas kernels  4.65 us (12%)
  between operations  0.79 us (2%)
  other arithmetic  0.48 us (1%)
    ppermute x14, starting transfers between devices, swap(): return lax.ppermute(array, axis, [(i, i ^ bit) for i in range(size)])  14.8 us
    ppermute x14, waiting for transfers between devices, swap(): return lax.ppermute(array, axis, [(i, i ^ bit) for i in range(size)])  11.1 us
    ppermute x2, starting transfers between devices, inner(): return lax.ppermute(array, ('seq', 'fsdp'), moves)  2.67 us
    ppermute x1, starting transfers between devices, shift(): return lax.ppermute(array, 'seq', moves)  1.87 us
    ppermute x2, waiting for transfers between devices, inner(): return lax.ppermute(array, ('seq', 'fsdp'), moves)  1.68 us
    pallas_call x1, Pallas kernels, body(): call(functools.partial(lowrank_kernel, send), [((2 * RANK, tok), F32), ((...  1.4 us
    pallas_call x1, Pallas kernels, body(): call(functools.partial(grads_kernel, count, send, blocks, heads), [((RANK...  0.85 us
    pallas_call x1, Pallas kernels, body(): call(final_kernel, [((2 * RANK, wide), F32), ((RANK, heads * HEAD), F32),...  0.79 us
  transfers between devices with their start and end apart: 17, of which 10 were waited for; matrix products, arithmetic and copies ran while one was open for 1% of the time, Pallas kernels for 6%

profile of v13, /device:TPU:0, one launch (start us, length us, event | category | flops | bytes accessed | tf_op | source)
XLA Modules:
  0.0 38.8 jit_solution(15386993020209601044)
XLA Ops:
  0.6 1.4 %shard_map.112 = (f32[32,128]{1,0:T(8,128)S(1)}, bf16[128,128]{1,0:T(8,128)(2,1)S(1)}, bf16[128,128]{1,0:T(8,128)(2,1)S(1)}, bf16[128,128]{1,0:T(8,128)(2,1)S(1)}, bf16[16,1024]{1,0:T(8,128)(2,1)S(1)}) custom-call(bf16[128,2048]{1,0:T(8,128)(2,1)} %x_ref.1, bf16[32,2048]{1,0:T(8,128)(2,1)} %bitcast.8, bf16[128,128]{1,0:T(8,128)(2,1)} %refs_2_.1, ...), custom_call_target="tpu_custom_call" | custom-call | flops 1 | bytes 1 | tf_op jit(solution)/shard_map/pallas_call | solution.py:272
  2.1 0.5 %collective-permute-start = (f32[32,128]{1,0:T(8,128)S(1)}, f32[32,128]{1,0:T(8,128)S(1)}, u32[]{:S(2)}, u32[]{:S(2)}) collective-permute-start(f32[32,128]{1,0:T(8,128)S(1)} %get-tuple-element.32), channel_id=1, source_target_pairs={{0,1},{1,0},{2,3},{3,2},{4,5},{5,4},{6,7},{7,6},{8,9},{9,8},{10,11... | collective-permute-start | bytes 49160 | tf_op jit(solution)/shard_map/ppermute | solution.py:246
  2.6 2.6 %collective-permute-start.1 = (f32[32,128]{1,0:T(8,128)S(1)}, f32[32,128]{1,0:T(8,128)S(1)}, u32[]{:S(2)}, u32[]{:S(2)}) collective-permute-start(f32[32,128]{1,0:T(8,128)S(1)} %get-tuple-element.32), channel_id=1, source_target_pairs={{0,2},{1,3},{2,0},{3,1},{4,6},{5,7},{6,4},{7,5},{8,10},{9,11},{10,... | collective-permute-start | bytes 49160 | tf_op jit(solution)/shard_map/ppermute | solution.py:246
  5.2 1.9 %collective-permute-start.3 = (bf16[144,128]{1,0:T(8,128)(2,1)S(1)}, bf16[144,128]{1,0:T(8,128)(2,1)S(1)}, u32[]{:S(2)}, u32[]{:S(2)}) collective-permute-start(bf16[144,128]{1,0:T(8,128)(2,1)S(1)} %pad_maximum_fusion), channel_id=1, source_target_pairs={{0,4},{4,8},{8,12},{12,0},{1,5},{5,9},{9,13},{13,1},{2,6},{6,10},{... | collective-permute-start | bytes 110600 | tf_op jit(solution)/shard_map/ppermute | solution.py:250
  7.1 0.4 %multiply_sine_fusion = (f32[192,64]{1,0:T(8,128)S(1)}, f32[192,64]{1,0:T(8,128)S(1)}) fusion(f32[64]{0:T(128)S(1)} %multiply_power_fusion, f32[192]{0:T(256)S(1)} %add_convert_fusion.1), kind=kLoop, calls=%fused_computation | loop fusion | flops 12288 | bytes 99328 | tf_op jit(solution)/shard_map/sin | solution.py:297
  7.6 0.2 copy-done.3
  7.8 0.5 %collective-permute-done.2 = f32[32,128]{1,0:T(8,128)S(1)} collective-permute-done((f32[32,128]{1,0:T(8,128)S(1)}, f32[32,128]{1,0:T(8,128)S(1)}, u32[]{:S(2)}, u32[]{:S(2)}) %collective-permute-start.2) | collective-permute-done | bytes 16416 | tf_op jit(solution)/shard_map/ppermute | solution.py:246
  8.3 1.6 %collective-permute-start.4 = (bf16[16,128]{1,0:T(8,128)(2,1)S(1)}, bf16[16,128]{1,0:T(8,128)(2,1)S(1)}, u32[]{:S(2)}, u32[]{:S(2)}) collective-permute-start(bf16[16,128]{1,0:T(8,128)(2,1)S(1)} %slice.43), channel_id=1, source_target_pairs={{0,4},{1,3},{2,6},{3,1},{4,0},{5,9},{6,2},{7,11},{8,12},{9,5},{10,... | collective-permute-start | bytes 12296 | tf_op jit(solution)/shard_map/ppermute | solution.py:263
  10.0 0.7 %shard_map.113 = (bf16[1024,128]{1,0:T(8,128)(2,1)S(1)}, bf16[128,128]{1,0:T(8,128)(2,1)S(1)}, f32[128,1024]{1,0:T(8,128)S(1)}, f32[128,1024]{1,0:T(8,128)S(1)},...) custom-call(f32[32,128]{1,0:T(8,128)S(1)} %add_add_fusion.low_ref, bf16[128,1024]{1,0:T(8,128)(2,1)S(1)} %copy-done.2, ...), custom_call_target="tpu_custom_call" | custom-call | flops 3145728 | bytes 3145728 | tf_op jit(solution)/shard_map/pallas_call | solution.py:307
  10.7 0.4 %collective-permute-done.3 = bf16[144,128]{1,0:T(8,128)(2,1)S(1)} collective-permute-done((bf16[144,128]{1,0:T(8,128)(2,1)S(1)}, bf16[144,128]{1,0:T(8,128)(2,1)S(1)}, u32[]{:S(2)}, u32[]{:S(2)}) %collective-permute-start.3) | collective-permute-done | bytes 36896 | tf_op jit(solution)/shard_map/ppermute | solution.py:250
  11.1 0.7 %shard_map.114 = (f32[192,1024]{1,0:T(8,128)S(1)}, bf16[128,64]{1,0:T(8,128)(2,1)S(1)}, f32[192,128]{1,0:T(8,128)S(1)}, f32[32,128]{1,0:T(8,128)S(1)}) custom-call(bf16[1024,128]{1,0:T(8,128)(2,1)S(1)} %get-tuple-element.40.qr_ref, f32[128,1024]{1,0:T(8,128)S(1)} %get-tuple-element.41.s_ref, bf16[128,1024]{1,0:T(8,128)(2,1)S(1)} %copy-done, ...), custom_call_target="tpu_custom_call" | custom-call | flops 5242880 | bytes 5242880 | tf_op jit(solution)/shard_map/pallas_call | solution.py:321
  11.9 0.1 collective-permute-done.4
  12.0 1.6 %collective-permute-start.6 = (f32[16,128]{1,0:T(8,128)S(1)}, f32[16,128]{1,0:T(8,128)S(1)}, u32[]{:S(2)}, u32[]{:S(2)}) collective-permute-start(f32[16,128]{1,0:T(8,128)S(1)} %slice.35), channel_id=1, source_target_pairs={{0,4},{4,0},{8,12},{12,8},{1,5},{5,1},{9,13},{13,9},{2,6},{6,2},{1... | collective-permute-start | bytes 24584 | tf_op jit(solution)/shard_map/ppermute | solution.py:246
  13.6 1.0 %collective-permute-start.7 = (f32[16,128]{1,0:T(8,128)S(1)}, f32[16,128]{1,0:T(8,128)S(1)}, u32[]{:S(2)}, u32[]{:S(2)}) collective-permute-start(f32[16,128]{1,0:T(8,128)S(1)} %slice.35), channel_id=1, source_target_pairs={{0,2},{1,3},{2,0},{3,1},{4,8},{5,9},{6,10},{7,11},{8,4},{9,5},{10,... | collective-permute-start | bytes 24584 | tf_op jit(solution)/shard_map/ppermute | solution.py:263
  14.6 0.9 %shard_map.115 = (f32[16,128]{1,0:T(8,128)S(1)}, bf16[16,1152]{1,0:T(8,128)(2,1)S(1)}) custom-call(f32[32,128]{1,0:T(8,128)S(1)} %add_add_fusion.low_ref, bf16[1,16,128]{2,1,0:T(8,128)(2,1)S(1)} %select_bitcast_fusion.far_ref, bf16[1,144,128]{2,1,0:T(8,128)(2,1)S(1)} %bitcast.7, bf16[128,1024]{1,0:T(8,128)(2,1)S(1)} %copy-done, ...), custom_call_target="tpu_custom_call" | custom-call | flops 25165824 | bytes 25165824 | tf_op jit(solution)/shard_map/pallas_call | solution.py:340
  15.5 0.2 collective-permute-done.6
  15.7 1.6 %collective-permute-done.7 = f32[16,128]{1,0:T(8,128)S(1)} collective-permute-done((f32[16,128]{1,0:T(8,128)S(1)}, f32[16,128]{1,0:T(8,128)S(1)}, u32[]{:S(2)}, u32[]{:S(2)}) %collective-permute-start.7) | collective-permute-done | bytes 8224 | tf_op jit(solution)/shard_map/ppermute | solution.py:263
  17.3 1.1 %collective-permute-start.8 = (f32[32,128]{1,0:T(8,128)S(1)}, f32[32,128]{1,0:T(8,128)S(1)}, u32[]{:S(2)}, u32[]{:S(2)}) collective-permute-start(f32[32,128]{1,0:T(8,128)S(1)} %pad_maximum_fusion.1), channel_id=1, source_target_pairs={{0,1},{1,0},{2,3},{3,2},{4,5},{5,4},{6,7},{7,6},{8,9},{9,8},{10,11... | collective-permute-start | bytes 49160 | tf_op jit(solution)/shard_map/ppermute | solution.py:246
  18.4 1.0 %collective-permute-start.9 = (f32[32,128]{1,0:T(8,128)S(1)}, f32[32,128]{1,0:T(8,128)S(1)}, u32[]{:S(2)}, u32[]{:S(2)}) collective-permute-start(f32[32,128]{1,0:T(8,128)S(1)} %pad_maximum_fusion.1), channel_id=1, source_target_pairs={{0,2},{1,3},{2,0},{3,1},{4,6},{5,7},{6,4},{7,5},{8,10},{9,11},{10,... | collective-permute-start | bytes 49160 | tf_op jit(solution)/shard_map/ppermute | solution.py:246
  19.4 1.0 %collective-permute-done.10 = f32[32,128]{1,0:T(8,128)S(1)} collective-permute-done((f32[32,128]{1,0:T(8,128)S(1)}, f32[32,128]{1,0:T(8,128)S(1)}, u32[]{:S(2)}, u32[]{:S(2)}) %collective-permute-start.10) | collective-permute-done | bytes 16416 | tf_op jit(solution)/shard_map/ppermute | solution.py:246
  20.5 1.7 %collective-permute-done.9 = f32[32,128]{1,0:T(8,128)S(1)} collective-permute-done((f32[32,128]{1,0:T(8,128)S(1)}, f32[32,128]{1,0:T(8,128)S(1)}, u32[]{:S(2)}, u32[]{:S(2)}) %collective-permute-start.9) | collective-permute-done | bytes 16416 | tf_op jit(solution)/shard_map/ppermute | solution.py:246
  22.2 0.2 shard_map.116
  22.4 2.3 %collective-permute-start.14 = (bf16[16,3328]{1,0:T(8,128)(2,1)S(1)}, bf16[16,3328]{1,0:T(8,128)(2,1)S(1)}, u32[]{:S(2)}, u32[]{:S(2)}) collective-permute-start(bf16[16,3328]{1,0:T(8,128)(2,1)S(1)} %get-tuple-element.57), channel_id=1, source_target_pairs={{0,8},{4,12},{8,0},{12,4},{1,9},{5,13},{9,1},{13,5},{2,10},{6,14},... | collective-permute-start | bytes 319496 | tf_op jit(solution)/shard_map/ppermute | solution.py:246
  24.8 0.6 %collective-permute-start.12 = (bf16[16,1920]{1,0:T(8,128)(2,1)S(1)}, bf16[16,1920]{1,0:T(8,128)(2,1)S(1)}, u32[]{:S(2)}, u32[]{:S(2)}) collective-permute-start(bf16[16,1920]{1,0:T(8,128)(2,1)S(1)} %get-tuple-element.56), channel_id=1, source_target_pairs={{0,8},{4,12},{8,0},{12,4},{1,9},{5,13},{9,1},{13,5},{2,10},{6,14},... | collective-permute-start | bytes 184328 | tf_op jit(solution)/shard_map/ppermute | solution.py:246
  25.4 2.5 %collective-permute-start.13 = (bf16[16,1920]{1,0:T(8,128)(2,1)S(1)}, bf16[16,1920]{1,0:T(8,128)(2,1)S(1)}, u32[]{:S(2)}, u32[]{:S(2)}) collective-permute-start(bf16[16,1920]{1,0:T(8,128)(2,1)S(1)} %get-tuple-element.56), channel_id=1, source_target_pairs={{0,12},{4,8},{8,4},{12,0},{1,13},{5,9},{9,5},{13,1},{2,14},{6,10},... | collective-permute-start | bytes 184328 | tf_op jit(solution)/shard_map/ppermute | solution.py:246
  27.9 0.4 collective-permute-start.11
  28.2 4.9 %collective-permute-done.14.relay_two_ref = bf16[16,3328]{1,0:T(8,128)(2,1)S(1)} collective-permute-done((bf16[16,3328]{1,0:T(8,128)(2,1)S(1)}, bf16[16,3328]{1,0:T(8,128)(2,1)S(1)}, u32[]{:S(2)}, u32[]{:S(2)}) %collective-permute-start.14) | collective-permute-done | bytes 106528 | tf_op jit(solution)/shard_map/ppermute | solution.py:246
  33.1 0.1 collective-permute-start.15
  33.2 2.0 %collective-permute-start.16 = (bf16[16,1664]{1,0:T(8,128)(2,1)S(1)}, bf16[16,1664]{1,0:T(8,128)(2,1)S(1)}, u32[]{:S(2)}, u32[]{:S(2)}) collective-permute-start(bf16[16,1664]{1,0:T(8,128)(2,1)S(1)} %get-tuple-element.61), channel_id=1, source_target_pairs={{0,4},{4,0},{8,12},{12,8},{1,5},{5,1},{9,13},{13,9},{2,6},{6,2},{1... | collective-permute-start | bytes 159752 | tf_op jit(solution)/shard_map/ppermute | solution.py:246
  35.2 2.2 %collective-permute-done.15.first_three_ref = bf16[16,1664]{1,0:T(8,128)(2,1)S(1)} collective-permute-done((bf16[16,1664]{1,0:T(8,128)(2,1)S(1)}, bf16[16,1664]{1,0:T(8,128)(2,1)S(1)}, u32[]{:S(2)}, u32[]{:S(2)}) %collective-permute-start.15) | collective-permute-done | bytes 53280 | tf_op jit(solution)/shard_map/ppermute | solution.py:246
  37.4 0.6 %collective-permute-done.16.second_three_ref = bf16[16,1664]{1,0:T(8,128)(2,1)S(1)} collective-permute-done((bf16[16,1664]{1,0:T(8,128)(2,1)S(1)}, bf16[16,1664]{1,0:T(8,128)(2,1)S(1)}, u32[]{:S(2)}, u32[]{:S(2)}) %collective-permute-start.16) | collective-permute-done | bytes 53280 | tf_op jit(solution)/shard_map/ppermute | solution.py:246
  38.0 0.8 %shard_map.117 = (f32[32,2048]{1,0:T(8,128)}, f32[16,1024]{1,0:T(8,128)}, f32[16,128]{1,0:T(8,128)}) custom-call(bf16[16,5248]{1,0:T(8,128)(2,1)S(1)} %get-tuple-element.55.mine_ref, bf16[16,5248]{1,0:T(8,128)(2,1)S(1)} %collective-permute-done.11.one_ref, bf16[16,1920]{1,0:T(8,128)(2,1)S(1)} %collective-permute-done.12.rest_two_ref, ...), custom_call_target="tpu_custom_call" | custom-call | flops 1 | bytes 1 | tf_op jit(solution)/shard_map/pallas_call | solution.py:365
  (37 shorter events, 0.3 us)
Async XLA Ops:
  2.0 3.2 %copy-start.4 = (s32[128]{0:T(128)S(1)}, s32[128]{0:T(128)}, u32[]{:S(2)}) copy-start(s32[128]{0:T(128)} %param.14) | copy-start | bytes 1540
  2.1 5.8 %collective-permute-start = (f32[32,128]{1,0:T(8,128)S(1)}, f32[32,128]{1,0:T(8,128)S(1)}, u32[]{:S(2)}, u32[]{:S(2)}) collective-permute-start(f32[32,128]{1,0:T(8,128)S(1)} %get-tuple-element.32), channel_id=1, source_target_pairs={{0,1},{1,0},{2,3},{3,2},{4,5},{5,4},{6,7},{7,6},{8,9},{9,8},{10,11... | collective-permute-start | bytes 49160 | tf_op jit(solution)/shard_map/ppermute | solution.py:246
  2.6 5.2 %collective-permute-start.1 = (f32[32,128]{1,0:T(8,128)S(1)}, f32[32,128]{1,0:T(8,128)S(1)}, u32[]{:S(2)}, u32[]{:S(2)}) collective-permute-start(f32[32,128]{1,0:T(8,128)S(1)} %get-tuple-element.32), channel_id=1, source_target_pairs={{0,2},{1,3},{2,0},{3,1},{4,6},{5,7},{6,4},{7,5},{8,10},{9,11},{10,... | collective-permute-start | bytes 49160 | tf_op jit(solution)/shard_map/ppermute | solution.py:246
  5.1 3.2 %collective-permute-start.2 = (f32[32,128]{1,0:T(8,128)S(1)}, f32[32,128]{1,0:T(8,128)S(1)}, u32[]{:S(2)}, u32[]{:S(2)}) collective-permute-start(f32[32,128]{1,0:T(8,128)S(1)} %get-tuple-element.32), channel_id=1, source_target_pairs={{0,3},{1,2},{2,1},{3,0},{4,7},{5,6},{6,5},{7,4},{8,11},{9,10},{10,... | collective-permute-start | bytes 49160 | tf_op jit(solution)/shard_map/ppermute | solution.py:246
  5.2 5.9 %collective-permute-start.3 = (bf16[144,128]{1,0:T(8,128)(2,1)S(1)}, bf16[144,128]{1,0:T(8,128)(2,1)S(1)}, u32[]{:S(2)}, u32[]{:S(2)}) collective-permute-start(bf16[144,128]{1,0:T(8,128)(2,1)S(1)} %pad_maximum_fusion), channel_id=1, source_target_pairs={{0,4},{4,8},{8,12},{12,0},{1,5},{5,9},{9,13},{13,1},{2,6},{6,10},{... | collective-permute-start | bytes 110600 | tf_op jit(solution)/shard_map/ppermute | solution.py:250
  7.1 0.7 %copy-start.3 = (bf16[16,128]{1,0:T(8,128)(2,1)S(1)}, bf16[16,128]{1,0:T(8,128)(2,1)}, u32[]{:S(2)}) copy-start(bf16[16,128]{1,0:T(8,128)(2,1)} %param.17) | copy-start | bytes 12292
  7.1 2.9 %copy-start.2 = (bf16[128,1024]{1,0:T(8,128)(2,1)S(1)}, bf16[128,1024]{1,0:T(8,128)(2,1)}, u32[]{:S(2)}) copy-start(bf16[128,1024]{1,0:T(8,128)(2,1)} %q_ref.1) | copy-start | bytes 786436
  7.8 2.2 %copy-start = (bf16[128,1024]{1,0:T(8,128)(2,1)S(1)}, bf16[128,1024]{1,0:T(8,128)(2,1)}, u32[]{:S(2)}) copy-start(bf16[128,1024]{1,0:T(8,128)(2,1)} %o_ref.5) | copy-start | bytes 786436
  8.3 3.7 %collective-permute-start.4 = (bf16[16,128]{1,0:T(8,128)(2,1)S(1)}, bf16[16,128]{1,0:T(8,128)(2,1)S(1)}, u32[]{:S(2)}, u32[]{:S(2)}) collective-permute-start(bf16[16,128]{1,0:T(8,128)(2,1)S(1)} %slice.43), channel_id=1, source_target_pairs={{0,4},{1,3},{2,6},{3,1},{4,0},{5,9},{6,2},{7,11},{8,12},{9,5},{10,... | collective-permute-start | bytes 12296 | tf_op jit(solution)/shard_map/ppermute | solution.py:263
  12.0 2.6 %collective-permute-start.5 = (bf16[16,128]{1,0:T(8,128)(2,1)S(1)}, bf16[16,128]{1,0:T(8,128)(2,1)S(1)}, u32[]{:S(2)}, u32[]{:S(2)}) collective-permute-start(bf16[16,128]{1,0:T(8,128)(2,1)S(1)} %collective-permute-done.4), channel_id=1, source_target_pairs={{0,1},{1,0},{2,3},{3,2},{4,5},{5,4},{6,7},{7,6},{8,9},{9,8},{10,11... | collective-permute-start | bytes 12296 | tf_op jit(solution)/shard_map/ppermute | solution.py:246
  12.0 3.7 %collective-permute-start.6 = (f32[16,128]{1,0:T(8,128)S(1)}, f32[16,128]{1,0:T(8,128)S(1)}, u32[]{:S(2)}, u32[]{:S(2)}) collective-permute-start(f32[16,128]{1,0:T(8,128)S(1)} %slice.35), channel_id=1, source_target_pairs={{0,4},{4,0},{8,12},{12,8},{1,5},{5,1},{9,13},{13,9},{2,6},{6,2},{1... | collective-permute-start | bytes 24584 | tf_op jit(solution)/shard_map/ppermute | solution.py:246
  13.6 3.7 %collective-permute-start.7 = (f32[16,128]{1,0:T(8,128)S(1)}, f32[16,128]{1,0:T(8,128)S(1)}, u32[]{:S(2)}, u32[]{:S(2)}) collective-permute-start(f32[16,128]{1,0:T(8,128)S(1)} %slice.35), channel_id=1, source_target_pairs={{0,2},{1,3},{2,0},{3,1},{4,8},{5,9},{6,10},{7,11},{8,4},{9,5},{10,... | collective-permute-start | bytes 24584 | tf_op jit(solution)/shard_map/ppermute | solution.py:263
  14.6 7.6 %copy-start.1 = (bf16[128,2048]{1,0:T(8,128)(2,1)S(1)}, bf16[128,2048]{1,0:T(8,128)(2,1)}, u32[]{:S(2)}) copy-start(bf16[128,2048]{1,0:T(8,128)(2,1)} %x_ref.1) | copy-start | bytes 1572868
  17.2 3.2 %collective-permute-start.10 = (f32[32,128]{1,0:T(8,128)S(1)}, f32[32,128]{1,0:T(8,128)S(1)}, u32[]{:S(2)}, u32[]{:S(2)}) collective-permute-start(f32[32,128]{1,0:T(8,128)S(1)} %pad_maximum_fusion.1), channel_id=1, source_target_pairs={{0,3},{1,2},{2,1},{3,0},{4,7},{5,6},{6,5},{7,4},{8,11},{9,10},{10,... | collective-permute-start | bytes 49160 | tf_op jit(solution)/shard_map/ppermute | solution.py:246
  17.3 3.2 %collective-permute-start.8 = (f32[32,128]{1,0:T(8,128)S(1)}, f32[32,128]{1,0:T(8,128)S(1)}, u32[]{:S(2)}, u32[]{:S(2)}) collective-permute-start(f32[32,128]{1,0:T(8,128)S(1)} %pad_maximum_fusion.1), channel_id=1, source_target_pairs={{0,1},{1,0},{2,3},{3,2},{4,5},{5,4},{6,7},{7,6},{8,9},{9,8},{10,11... | collective-permute-start | bytes 49160 | tf_op jit(solution)/shard_map/ppermute | solution.py:246
  18.4 3.7 %collective-permute-start.9 = (f32[32,128]{1,0:T(8,128)S(1)}, f32[32,128]{1,0:T(8,128)S(1)}, u32[]{:S(2)}, u32[]{:S(2)}) collective-permute-start(f32[32,128]{1,0:T(8,128)S(1)} %pad_maximum_fusion.1), channel_id=1, source_target_pairs={{0,2},{1,3},{2,0},{3,1},{4,6},{5,7},{6,4},{7,5},{8,10},{9,11},{10,... | collective-permute-start | bytes 49160 | tf_op jit(solution)/shard_map/ppermute | solution.py:246
  22.4 10.7 %collective-permute-start.14 = (bf16[16,3328]{1,0:T(8,128)(2,1)S(1)}, bf16[16,3328]{1,0:T(8,128)(2,1)S(1)}, u32[]{:S(2)}, u32[]{:S(2)}) collective-permute-start(bf16[16,3328]{1,0:T(8,128)(2,1)S(1)} %get-tuple-element.57), channel_id=1, source_target_pairs={{0,8},{4,12},{8,0},{12,4},{1,9},{5,13},{9,1},{13,5},{2,10},{6,14},... | collective-permute-start | bytes 319496 | tf_op jit(solution)/shard_map/ppermute | solution.py:246
  24.8 10.5 %collective-permute-start.12 = (bf16[16,1920]{1,0:T(8,128)(2,1)S(1)}, bf16[16,1920]{1,0:T(8,128)(2,1)S(1)}, u32[]{:S(2)}, u32[]{:S(2)}) collective-permute-start(bf16[16,1920]{1,0:T(8,128)(2,1)S(1)} %get-tuple-element.56), channel_id=1, source_target_pairs={{0,8},{4,12},{8,0},{12,4},{1,9},{5,13},{9,1},{13,5},{2,10},{6,14},... | collective-permute-start | bytes 184328 | tf_op jit(solution)/shard_map/ppermute | solution.py:246
  25.4 9.8 %collective-permute-start.13 = (bf16[16,1920]{1,0:T(8,128)(2,1)S(1)}, bf16[16,1920]{1,0:T(8,128)(2,1)S(1)}, u32[]{:S(2)}, u32[]{:S(2)}) collective-permute-start(bf16[16,1920]{1,0:T(8,128)(2,1)S(1)} %get-tuple-element.56), channel_id=1, source_target_pairs={{0,12},{4,8},{8,4},{12,0},{1,13},{5,9},{9,5},{13,1},{2,14},{6,10},... | collective-permute-start | bytes 184328 | tf_op jit(solution)/shard_map/ppermute | solution.py:246
  27.9 10.1 %collective-permute-start.11 = (bf16[16,5248]{1,0:T(8,128)(2,1)S(1)}, bf16[16,5248]{1,0:T(8,128)(2,1)S(1)}, u32[]{:S(2)}, u32[]{:S(2)}) collective-permute-start(bf16[16,5248]{1,0:T(8,128)(2,1)S(1)} %get-tuple-element.55.mine_ref), channel_id=1, source_target_pairs={{0,4},{4,0},{8,12},{12,8},{1,5},{5,1},{9,13},{13,9},{2,6},{6,2},{1... | collective-permute-start | bytes 503816 | tf_op jit(solution)/shard_map/ppermute | solution.py:246
  33.1 4.3 %collective-permute-start.15 = (bf16[16,1664]{1,0:T(8,128)(2,1)S(1)}, bf16[16,1664]{1,0:T(8,128)(2,1)S(1)}, u32[]{:S(2)}, u32[]{:S(2)}) collective-permute-start(bf16[16,1664]{1,0:T(8,128)(2,1)S(1)} %get-tuple-element.62), channel_id=1, source_target_pairs={{0,4},{4,0},{8,12},{12,8},{1,5},{5,1},{9,13},{13,9},{2,6},{6,2},{1... | collective-permute-start | bytes 159752 | tf_op jit(solution)/shard_map/ppermute | solution.py:246
  33.2 4.8 %collective-permute-start.16 = (bf16[16,1664]{1,0:T(8,128)(2,1)S(1)}, bf16[16,1664]{1,0:T(8,128)(2,1)S(1)}, u32[]{:S(2)}, u32[]{:S(2)}) collective-permute-start(bf16[16,1664]{1,0:T(8,128)(2,1)S(1)} %get-tuple-element.61), channel_id=1, source_target_pairs={{0,4},{4,0},{8,12},{12,8},{1,5},{5,1},{9,13},{13,9},{2,6},{6,2},{1... | collective-permute-start | bytes 159752 | tf_op jit(solution)/shard_map/ppermute | solution.py:246

commit v14 on v12

--- a/solution.py
+++ b/solution.py
@@ -246,17 +246,17 @@
         moves = [(i, (i + by) % seq_count) for i in range(seq_count)]
         return lax.ppermute(array, "seq", moves)
 
-    def inner(array, even):
+    def inner(array, bit):
         moves = []
         for i in range(seq_count):
             for f in range(fsdp_count):
-                if even and f % 2 == 0:
-                    to, flip = i ^ 1, 0
+                if f % 2 == 0:
+                    source = (i ^ 1, f ^ bit)
                 elif i in (1, 2):
-                    to, flip = 3 - i, 0
+                    source = (3 - i, f ^ bit)
                 else:
-                    to, flip = i, 2
-                moves.append((i * fsdp_count + f, to * fsdp_count + (f ^ flip)))
+                    source = (i, f ^ bit if bit % 2 else f ^ 2)
+                moves.append((source[0] * fsdp_count + source[1], i * fsdp_count + f))
         return lax.ppermute(array, ("seq", "fsdp"), moves)
 
     def sum_fsdp(array):
@@ -297,7 +297,7 @@
     low, cos, sin, wv = lax.optimization_barrier((low, cos, sin, wv))
     low_v = low[RANK:].astype(BF16)
     if direct:
-        far = inner(low_v, True)
+        far = inner(low_v, 0)
     else:
         lows = jnp.stack([shift(low_v, d) for d in range(blocks, 0, -1)])
     count = heads if blocks == 1 else 1
@@ -332,8 +332,12 @@
         lows = jnp.where(mine, far, swap(far, "fsdp", 1))[None]
     code_v = codes_v[:RANK]
     if direct:
-        above, below = swap(codes_v[RANK:], "seq", 1), inner(codes_v[RANK:], False)
-        backs = jnp.where(seq_index % 2 == 0, above, jnp.where(seq_index == 1, below, 0.0))
+        parts = [inner(codes_v[RANK:], bit) for bit in range(4)]
+        back = (parts[0] + parts[1]) + (parts[2] + parts[3])
+        even = lax.axis_index("fsdp") % 2 == 0
+        mine = even == (seq_index % 2 == 0)
+        back = jnp.where(mine, back, swap(back, "fsdp", 1))
+        back = jnp.where(seq_index < seq_count - 1, back, 0.0)
     code_q, up = call(
         functools.partial(grads_kernel, count, send, blocks, heads),
         [((RANK, tok), F32), ((RANK, (heads + 1) * HEAD), BF16 if direct else F32)],
@@ -348,11 +352,12 @@
         down, up = lax.psum((down, up), "seq")
         return down.T, up[:, : heads * HEAD], up[:, heads * HEAD :]
 
-    codes = jnp.concatenate([code_q, code_v + backs], axis=0)
+    codes = sum_fsdp(jnp.concatenate([code_q, code_v], axis=0))
+    dlow = jnp.concatenate([codes[:RANK], codes[RANK:] + back], axis=0).astype(BF16)
     near_up = swap(up, "seq", 1)
     both, part_q, part_v = call(
         partial_kernel, [((2 * RANK, wide), BF16), ((RANK, wide), BF16), ((RANK, wide), BF16)]
-    )(sum_fsdp(codes).astype(BF16), x)
+    )(dlow, x)
     (send_q,) = call(combine_kernel, [((RANK, wide + up.shape[1]), BF16)])(part_q, up, near_up)
     value_two = swap(part_v, "seq", 2)
     value_three = swap(value_two, "seq", 1)

time: 35.8 us -> 36.8 us (1.028)
  starting transfers between devices: 19.7 us -> 22.3 us
  waiting for transfers between devices: 9.73 us -> 8.04 us
    ppermute x2 -> x5, starting transfers between devices: 2.67 us -> 6.28 us  [inner(): return lax.ppermute(array, ('seq', 'fsdp'), moves)]
    ppermute x2 -> x5, waiting for transfers between devices: 1.68 us -> 0.39 us  [inner(): return lax.ppermute(array, ('seq', 'fsdp'), moves)]
    ppermute x14, starting transfers between devices: 15.2 us -> 14.2 us  [swap(): return lax.ppermute(array, axis, [(i, i ^ bit) for i in range(size)])]
    ppermute x14, waiting for transfers between devices: 7.62 us -> 7.23 us  [swap(): return lax.ppermute(array, axis, [(i, i ^ bit) for i in range(size)])]
  transfers between devices with their start and end apart: 17 -> 20, of which waited for: 9 -> 8; matrix products, arithmetic and copies ran while one was open for 1% -> 1% of each run, Pallas kernels for 7% -> 7%
where the time goes in v14:
time: 36.8 us; the launch traced here: 36.6 us
  starting transfers between devices  22.3 us (61%)
  waiting for transfers between devices  8.04 us (22%)
  Pallas kernels  4.67 us (13%)
  between operations  0.8 us (2%)
  other arithmetic  0.49 us (1%)
    ppermute x14, starting transfers between devices, swap(): return lax.ppermute(array, axis, [(i, i ^ bit) for i in range(size)])  14.2 us
    ppermute x14, waiting for transfers between devices, swap(): return lax.ppermute(array, axis, [(i, i ^ bit) for i in range(size)])  7.23 us
    ppermute x5, starting transfers between devices, inner(): return lax.ppermute(array, ('seq', 'fsdp'), moves)  6.28 us
    ppermute x1, starting transfers between devices, shift(): return lax.ppermute(array, 'seq', moves)  1.87 us
    pallas_call x1, Pallas kernels, body(): call(functools.partial(lowrank_kernel, send), [((2 * RANK, tok), F32), ((...  1.4 us
    pallas_call x1, Pallas kernels, body(): call(functools.partial(grads_kernel, count, send, blocks, heads), [((RANK...  0.87 us
    pallas_call x1, Pallas kernels, body(): call(final_kernel, [((2 * RANK, wide), F32), ((RANK, heads * HEAD), F32),...  0.77 us
    pallas_call x1, Pallas kernels, body(): call(functools.partial(softmax_kernel, count, send, blocks, heads), [((ke...  0.75 us
  transfers between devices with their start and end apart: 20, of which 8 were waited for; matrix products, arithmetic and copies ran while one was open for 1% of the time, Pallas kernels for 7%

profile of v14, /device:TPU:0, one launch (start us, length us, event | category | flops | bytes accessed | tf_op | source)
XLA Modules:
  0.0 36.6 jit_solution(10696265115438397594)
XLA Ops:
  0.6 1.4 %shard_map.112 = (f32[32,128]{1,0:T(8,128)S(1)}, bf16[128,128]{1,0:T(8,128)(2,1)S(1)}, bf16[128,128]{1,0:T(8,128)(2,1)S(1)}, bf16[128,128]{1,0:T(8,128)(2,1)S(1)}, bf16[16,1024]{1,0:T(8,128)(2,1)S(1)}) custom-call(bf16[128,2048]{1,0:T(8,128)(2,1)} %x_ref.1, bf16[32,2048]{1,0:T(8,128)(2,1)} %bitcast.8, bf16[128,128]{1,0:T(8,128)(2,1)} %refs_2_.1, ...), custom_call_target="tpu_custom_call" | custom-call | flops 1 | bytes 1 | tf_op jit(solution)/shard_map/pallas_call | solution.py:269
  2.1 0.5 %collective-permute-start = (f32[32,128]{1,0:T(8,128)S(1)}, f32[32,128]{1,0:T(8,128)S(1)}, u32[]{:S(2)}, u32[]{:S(2)}) collective-permute-start(f32[32,128]{1,0:T(8,128)S(1)} %get-tuple-element.32), channel_id=1, source_target_pairs={{0,1},{1,0},{2,3},{3,2},{4,5},{5,4},{6,7},{7,6},{8,9},{9,8},{10,11... | collective-permute-start | bytes 49160 | tf_op jit(solution)/shard_map/ppermute | solution.py:243
  2.6 2.6 %collective-permute-start.1 = (f32[32,128]{1,0:T(8,128)S(1)}, f32[32,128]{1,0:T(8,128)S(1)}, u32[]{:S(2)}, u32[]{:S(2)}) collective-permute-start(f32[32,128]{1,0:T(8,128)S(1)} %get-tuple-element.32), channel_id=1, source_target_pairs={{0,2},{1,3},{2,0},{3,1},{4,6},{5,7},{6,4},{7,5},{8,10},{9,11},{10,... | collective-permute-start | bytes 49160 | tf_op jit(solution)/shard_map/ppermute | solution.py:243
  5.2 1.9 %collective-permute-start.3 = (bf16[144,128]{1,0:T(8,128)(2,1)S(1)}, bf16[144,128]{1,0:T(8,128)(2,1)S(1)}, u32[]{:S(2)}, u32[]{:S(2)}) collective-permute-start(bf16[144,128]{1,0:T(8,128)(2,1)S(1)} %pad_maximum_fusion), channel_id=1, source_target_pairs={{0,4},{4,8},{8,12},{12,0},{1,5},{5,9},{9,13},{13,1},{2,6},{6,10},{... | collective-permute-start | bytes 110600 | tf_op jit(solution)/shard_map/ppermute | solution.py:247
  7.1 0.4 %multiply_sine_fusion = (f32[192,64]{1,0:T(8,128)S(1)}, f32[192,64]{1,0:T(8,128)S(1)}) fusion(f32[64]{0:T(128)S(1)} %multiply_power_fusion, f32[192]{0:T(256)S(1)} %add_convert_fusion), kind=kLoop, calls=%fused_computation | loop fusion | flops 12288 | bytes 99328 | tf_op jit(solution)/shard_map/sin | solution.py:294
  7.5 0.3 copy-done.3
  7.8 0.5 %collective-permute-done.2 = f32[32,128]{1,0:T(8,128)S(1)} collective-permute-done((f32[32,128]{1,0:T(8,128)S(1)}, f32[32,128]{1,0:T(8,128)S(1)}, u32[]{:S(2)}, u32[]{:S(2)}) %collective-permute-start.2) | collective-permute-done | bytes 16416 | tf_op jit(solution)/shard_map/ppermute | solution.py:243
  8.3 1.6 %collective-permute-start.4 = (bf16[16,128]{1,0:T(8,128)(2,1)S(1)}, bf16[16,128]{1,0:T(8,128)(2,1)S(1)}, u32[]{:S(2)}, u32[]{:S(2)}) collective-permute-start(bf16[16,128]{1,0:T(8,128)(2,1)S(1)} %slice.50), channel_id=1, source_target_pairs={{4,0},{3,1},{6,2},{1,3},{0,4},{9,5},{2,6},{11,7},{12,8},{5,9},{14,... | collective-permute-start | bytes 12296 | tf_op jit(solution)/shard_map/ppermute | solution.py:260
  10.0 0.7 %shard_map.113 = (bf16[1024,128]{1,0:T(8,128)(2,1)S(1)}, bf16[128,128]{1,0:T(8,128)(2,1)S(1)}, f32[128,1024]{1,0:T(8,128)S(1)}, f32[128,1024]{1,0:T(8,128)S(1)},...) custom-call(f32[32,128]{1,0:T(8,128)S(1)} %add_add_fusion.1.low_ref, bf16[128,1024]{1,0:T(8,128)(2,1)S(1)} %copy-done.2, ...), custom_call_target="tpu_custom_call" | custom-call | flops 3145728 | bytes 3145728 | tf_op jit(solution)/shard_map/pallas_call | solution.py:304
  10.7 0.4 %collective-permute-done.3 = bf16[144,128]{1,0:T(8,128)(2,1)S(1)} collective-permute-done((bf16[144,128]{1,0:T(8,128)(2,1)S(1)}, bf16[144,128]{1,0:T(8,128)(2,1)S(1)}, u32[]{:S(2)}, u32[]{:S(2)}) %collective-permute-start.3) | collective-permute-done | bytes 36896 | tf_op jit(solution)/shard_map/ppermute | solution.py:247
  11.1 0.7 %shard_map.114 = (f32[192,1024]{1,0:T(8,128)S(1)}, bf16[128,64]{1,0:T(8,128)(2,1)S(1)}, f32[192,128]{1,0:T(8,128)S(1)}, f32[32,128]{1,0:T(8,128)S(1)}) custom-call(bf16[1024,128]{1,0:T(8,128)(2,1)S(1)} %get-tuple-element.40.qr_ref, f32[128,1024]{1,0:T(8,128)S(1)} %get-tuple-element.41.s_ref, bf16[128,1024]{1,0:T(8,128)(2,1)S(1)} %copy-done, ...), custom_call_target="tpu_custom_call" | custom-call | flops 5242880 | bytes 5242880 | tf_op jit(solution)/shard_map/pallas_call | solution.py:318
  11.9 0.1 collective-permute-done.4
  12.0 0.5 %collective-permute-start.10 = (f32[16,128]{1,0:T(8,128)S(1)}, f32[16,128]{1,0:T(8,128)S(1)}, u32[]{:S(2)}, u32[]{:S(2)}) collective-permute-start(f32[16,128]{1,0:T(8,128)S(1)} %get-tuple-element.61), channel_id=1, source_target_pairs={{5,0},{0,1},{7,2},{2,3},{1,4},{8,5},{3,6},{10,7},{13,8},{4,9},{15,... | collective-permute-start | bytes 24584 | tf_op jit(solution)/shard_map/ppermute | solution.py:260
  12.5 3.2 %collective-permute-start.11 = (f32[16,128]{1,0:T(8,128)S(1)}, f32[16,128]{1,0:T(8,128)S(1)}, u32[]{:S(2)}, u32[]{:S(2)}) collective-permute-start(f32[16,128]{1,0:T(8,128)S(1)} %get-tuple-element.61), channel_id=1, source_target_pairs={{6,0},{3,1},{4,2},{1,3},{2,4},{11,5},{0,6},{9,7},{14,8},{7,9},{12,... | collective-permute-start | bytes 24584 | tf_op jit(solution)/shard_map/ppermute | solution.py:260
  15.7 0.9 %collective-permute-start.9 = (f32[16,128]{1,0:T(8,128)S(1)}, f32[16,128]{1,0:T(8,128)S(1)}, u32[]{:S(2)}, u32[]{:S(2)}) collective-permute-start(f32[16,128]{1,0:T(8,128)S(1)} %get-tuple-element.61), channel_id=1, source_target_pairs={{4,0},{3,1},{6,2},{1,3},{0,4},{9,5},{2,6},{11,7},{12,8},{5,9},{14,... | collective-permute-start | bytes 24584 | tf_op jit(solution)/shard_map/ppermute | solution.py:260
  16.7 0.9 %shard_map.115 = (f32[16,128]{1,0:T(8,128)S(1)}, bf16[16,1152]{1,0:T(8,128)(2,1)S(1)}) custom-call(f32[32,128]{1,0:T(8,128)S(1)} %add_add_fusion.1.low_ref, bf16[1,16,128]{2,1,0:T(8,128)(2,1)S(1)} %select_bitcast_fusion.far_ref, bf16[1,144,128]{2,1,0:T(8,128)(2,1)S(1)} %bitcast.7, bf16[128,1024]{1,0:T(8,128)(2,1)S(1)} %copy-done, ...), custom_call_target="tpu_custom_call" | custom-call | flops 25165824 | bytes 25165824 | tf_op jit(solution)/shard_map/pallas_call | solution.py:341
  17.5 0.3 collective-permute-start.6
  17.8 1.3 %collective-permute-start.7 = (f32[32,128]{1,0:T(8,128)S(1)}, f32[32,128]{1,0:T(8,128)S(1)}, u32[]{:S(2)}, u32[]{:S(2)}) collective-permute-start(f32[32,128]{1,0:T(8,128)S(1)} %pad_maximum_fusion.1), channel_id=1, source_target_pairs={{0,2},{1,3},{2,0},{3,1},{4,6},{5,7},{6,4},{7,5},{8,10},{9,11},{10,... | collective-permute-start | bytes 49160 | tf_op jit(solution)/shard_map/ppermute | solution.py:243
  19.1 0.4 %collective-permute-start.8 = (f32[32,128]{1,0:T(8,128)S(1)}, f32[32,128]{1,0:T(8,128)S(1)}, u32[]{:S(2)}, u32[]{:S(2)}) collective-permute-start(f32[32,128]{1,0:T(8,128)S(1)} %pad_maximum_fusion.1), channel_id=1, source_target_pairs={{0,3},{1,2},{2,1},{3,0},{4,7},{5,6},{6,5},{7,4},{8,11},{9,10},{10,... | collective-permute-start | bytes 49160 | tf_op jit(solution)/shard_map/ppermute | solution.py:243
  19.5 0.2 collective-permute-done.12
  19.7 1.2 %collective-permute-start.15 = (bf16[16,1152]{1,0:T(8,128)(2,1)S(1)}, bf16[16,1152]{1,0:T(8,128)(2,1)S(1)}, u32[]{:S(2)}, u32[]{:S(2)}) collective-permute-start(bf16[16,1152]{1,0:T(8,128)(2,1)S(1)} %get-tuple-element.56.up_ref), channel_id=1, source_target_pairs={{0,4},{4,0},{8,12},{12,8},{1,5},{5,1},{9,13},{13,9},{2,6},{6,2},{1... | collective-permute-start | bytes 110600 | tf_op jit(solution)/shard_map/ppermute | solution.py:243
  20.9 0.5 %collective-permute-start.13 = (f32[16,128]{1,0:T(8,128)S(1)}, f32[16,128]{1,0:T(8,128)S(1)}, u32[]{:S(2)}, u32[]{:S(2)}) collective-permute-start(f32[16,128]{1,0:T(8,128)S(1)} %add_add_fusion.2), channel_id=1, source_target_pairs={{0,1},{1,0},{2,3},{3,2},{4,5},{5,4},{6,7},{7,6},{8,9},{9,8},{10,11... | collective-permute-start | bytes 24584 | tf_op jit(solution)/shard_map/ppermute | solution.py:243
  21.4 0.2 collective-permute-done.7
  21.5 0.7 %collective-permute-done.8 = f32[32,128]{1,0:T(8,128)S(1)} collective-permute-done((f32[32,128]{1,0:T(8,128)S(1)}, f32[32,128]{1,0:T(8,128)S(1)}, u32[]{:S(2)}, u32[]{:S(2)}) %collective-permute-start.8) | collective-permute-done | bytes 16416 | tf_op jit(solution)/shard_map/ppermute | solution.py:243
  22.3 0.2 shard_map.116
  22.5 2.6 %collective-permute-start.18 = (bf16[16,2048]{1,0:T(8,128)(2,1)S(1)}, bf16[16,2048]{1,0:T(8,128)(2,1)S(1)}, u32[]{:S(2)}, u32[]{:S(2)}) collective-permute-start(bf16[16,2048]{1,0:T(8,128)(2,1)S(1)} %get-tuple-element.57), channel_id=1, source_target_pairs={{0,8},{4,12},{8,0},{12,4},{1,9},{5,13},{9,1},{13,5},{2,10},{6,14},... | collective-permute-start | bytes 196616 | tf_op jit(solution)/shard_map/ppermute | solution.py:243
  25.2 0.8 %collective-permute-start.14 = (bf16[32,2048]{1,0:T(8,128)(2,1)S(1)}, bf16[32,2048]{1,0:T(8,128)(2,1)S(1)}, u32[]{:S(2)}, u32[]{:S(2)}) collective-permute-start(bf16[32,2048]{1,0:T(8,128)(2,1)S(1)} %get-tuple-element.54.mine_ref), channel_id=1, source_target_pairs={{0,4},{4,0},{8,12},{12,8},{1,5},{5,1},{9,13},{13,9},{2,6},{6,2},{1... | collective-permute-start | bytes 393224 | tf_op jit(solution)/shard_map/ppermute | solution.py:243
  25.9 1.2 %collective-permute-start.16 = (bf16[16,3200]{1,0:T(8,128)(2,1)S(1)}, bf16[16,3200]{1,0:T(8,128)(2,1)S(1)}, u32[]{:S(2)}, u32[]{:S(2)}) collective-permute-start(bf16[16,3200]{1,0:T(8,128)(2,1)S(1)} %shard_map.117.query_ref), channel_id=1, source_target_pairs={{0,8},{4,12},{8,0},{12,4},{1,9},{5,13},{9,1},{13,5},{2,10},{6,14},... | collective-permute-start | bytes 307208 | tf_op jit(solution)/shard_map/ppermute | solution.py:243
  27.2 2.5 %collective-permute-start.17 = (bf16[16,2048]{1,0:T(8,128)(2,1)S(1)}, bf16[16,2048]{1,0:T(8,128)(2,1)S(1)}, u32[]{:S(2)}, u32[]{:S(2)}) collective-permute-start(bf16[16,2048]{1,0:T(8,128)(2,1)S(1)} %get-tuple-element.55.query_ref), channel_id=1, source_target_pairs={{0,12},{4,8},{8,4},{12,0},{1,13},{5,9},{9,5},{13,1},{2,14},{6,10},... | collective-permute-start | bytes 196616 | tf_op jit(solution)/shard_map/ppermute | solution.py:243
  29.6 0.3 collective-permute-start.19
  30.0 5.8 %collective-permute-done.17.query_three_ref = bf16[16,2048]{1,0:T(8,128)(2,1)S(1)} collective-permute-done((bf16[16,2048]{1,0:T(8,128)(2,1)S(1)}, bf16[16,2048]{1,0:T(8,128)(2,1)S(1)}, u32[]{:S(2)}, u32[]{:S(2)}) %collective-permute-start.17) | collective-permute-done | bytes 65568 | tf_op jit(solution)/shard_map/ppermute | solution.py:243
  35.9 0.8 %shard_map.118 = (f32[32,2048]{1,0:T(8,128)}, f32[16,1024]{1,0:T(8,128)}, f32[16,128]{1,0:T(8,128)}) custom-call(bf16[32,2048]{1,0:T(8,128)(2,1)S(1)} %get-tuple-element.54.mine_ref, bf16[32,2048]{1,0:T(8,128)(2,1)S(1)} %collective-permute-done.14.one_ref, bf16[16,3200]{1,0:T(8,128)(2,1)S(1)} %shard_map.117.query_ref, ...), custom_call_target="tpu_custom_call" | custom-call | flops 1 | bytes 1 | tf_op jit(solution)/shard_map/pallas_call | solution.py:366
  (46 shorter events, 0.3 us)
Async XLA Ops:
  2.0 3.2 %copy-start.4 = (s32[128]{0:T(128)S(1)}, s32[128]{0:T(128)}, u32[]{:S(2)}) copy-start(s32[128]{0:T(128)} %param.14) | copy-start | bytes 1540
  2.1 5.8 %collective-permute-start = (f32[32,128]{1,0:T(8,128)S(1)}, f32[32,128]{1,0:T(8,128)S(1)}, u32[]{:S(2)}, u32[]{:S(2)}) collective-permute-start(f32[32,128]{1,0:T(8,128)S(1)} %get-tuple-element.32), channel_id=1, source_target_pairs={{0,1},{1,0},{2,3},{3,2},{4,5},{5,4},{6,7},{7,6},{8,9},{9,8},{10,11... | collective-permute-start | bytes 49160 | tf_op jit(solution)/shard_map/ppermute | solution.py:243
  2.6 5.3 %collective-permute-start.1 = (f32[32,128]{1,0:T(8,128)S(1)}, f32[32,128]{1,0:T(8,128)S(1)}, u32[]{:S(2)}, u32[]{:S(2)}) collective-permute-start(f32[32,128]{1,0:T(8,128)S(1)} %get-tuple-element.32), channel_id=1, source_target_pairs={{0,2},{1,3},{2,0},{3,1},{4,6},{5,7},{6,4},{7,5},{8,10},{9,11},{10,... | collective-permute-start | bytes 49160 | tf_op jit(solution)/shard_map/ppermute | solution.py:243
  5.1 3.2 %collective-permute-start.2 = (f32[32,128]{1,0:T(8,128)S(1)}, f32[32,128]{1,0:T(8,128)S(1)}, u32[]{:S(2)}, u32[]{:S(2)}) collective-permute-start(f32[32,128]{1,0:T(8,128)S(1)} %get-tuple-element.32), channel_id=1, source_target_pairs={{0,3},{1,2},{2,1},{3,0},{4,7},{5,6},{6,5},{7,4},{8,11},{9,10},{10,... | collective-permute-start | bytes 49160 | tf_op jit(solution)/shard_map/ppermute | solution.py:243
  5.2 5.9 %collective-permute-start.3 = (bf16[144,128]{1,0:T(8,128)(2,1)S(1)}, bf16[144,128]{1,0:T(8,128)(2,1)S(1)}, u32[]{:S(2)}, u32[]{:S(2)}) collective-permute-start(bf16[144,128]{1,0:T(8,128)(2,1)S(1)} %pad_maximum_fusion), channel_id=1, source_target_pairs={{0,4},{4,8},{8,12},{12,0},{1,5},{5,9},{9,13},{13,1},{2,6},{6,10},{... | collective-permute-start | bytes 110600 | tf_op jit(solution)/shard_map/ppermute | solution.py:247
  7.1 0.7 %copy-start.3 = (bf16[16,128]{1,0:T(8,128)(2,1)S(1)}, bf16[16,128]{1,0:T(8,128)(2,1)}, u32[]{:S(2)}) copy-start(bf16[16,128]{1,0:T(8,128)(2,1)} %param.17) | copy-start | bytes 12292
  7.8 2.2 %copy-start = (bf16[128,1024]{1,0:T(8,128)(2,1)S(1)}, bf16[128,1024]{1,0:T(8,128)(2,1)}, u32[]{:S(2)}) copy-start(bf16[128,1024]{1,0:T(8,128)(2,1)} %o_ref.5) | copy-start | bytes 786436
  7.8 2.2 %copy-start.2 = (bf16[128,1024]{1,0:T(8,128)(2,1)S(1)}, bf16[128,1024]{1,0:T(8,128)(2,1)}, u32[]{:S(2)}) copy-start(bf16[128,1024]{1,0:T(8,128)(2,1)} %q_ref.1) | copy-start | bytes 786436
  8.3 3.7 %collective-permute-start.4 = (bf16[16,128]{1,0:T(8,128)(2,1)S(1)}, bf16[16,128]{1,0:T(8,128)(2,1)S(1)}, u32[]{:S(2)}, u32[]{:S(2)}) collective-permute-start(bf16[16,128]{1,0:T(8,128)(2,1)S(1)} %slice.50), channel_id=1, source_target_pairs={{4,0},{3,1},{6,2},{1,3},{0,4},{9,5},{2,6},{11,7},{12,8},{5,9},{14,... | collective-permute-start | bytes 12296 | tf_op jit(solution)/shard_map/ppermute | solution.py:260
  12.0 4.7 %collective-permute-start.5 = (bf16[16,128]{1,0:T(8,128)(2,1)S(1)}, bf16[16,128]{1,0:T(8,128)(2,1)S(1)}, u32[]{:S(2)}, u32[]{:S(2)}) collective-permute-start(bf16[16,128]{1,0:T(8,128)(2,1)S(1)} %collective-permute-done.4), channel_id=1, source_target_pairs={{0,1},{1,0},{2,3},{3,2},{4,5},{5,4},{6,7},{7,6},{8,9},{9,8},{10,11... | collective-permute-start | bytes 12296 | tf_op jit(solution)/shard_map/ppermute | solution.py:243
  12.0 5.8 %collective-permute-start.10 = (f32[16,128]{1,0:T(8,128)S(1)}, f32[16,128]{1,0:T(8,128)S(1)}, u32[]{:S(2)}, u32[]{:S(2)}) collective-permute-start(f32[16,128]{1,0:T(8,128)S(1)} %get-tuple-element.61), channel_id=1, source_target_pairs={{5,0},{0,1},{7,2},{2,3},{1,4},{8,5},{3,6},{10,7},{13,8},{4,9},{15,... | collective-permute-start | bytes 24584 | tf_op jit(solution)/shard_map/ppermute | solution.py:260
  12.5 6.6 %collective-permute-start.11 = (f32[16,128]{1,0:T(8,128)S(1)}, f32[16,128]{1,0:T(8,128)S(1)}, u32[]{:S(2)}, u32[]{:S(2)}) collective-permute-start(f32[16,128]{1,0:T(8,128)S(1)} %get-tuple-element.61), channel_id=1, source_target_pairs={{6,0},{3,1},{4,2},{1,3},{2,4},{11,5},{0,6},{9,7},{14,8},{7,9},{12,... | collective-permute-start | bytes 24584 | tf_op jit(solution)/shard_map/ppermute | solution.py:260
  15.7 4.0 %collective-permute-start.12 = (f32[16,128]{1,0:T(8,128)S(1)}, f32[16,128]{1,0:T(8,128)S(1)}, u32[]{:S(2)}, u32[]{:S(2)}) collective-permute-start(f32[16,128]{1,0:T(8,128)S(1)} %get-tuple-element.61), channel_id=1, source_target_pairs={{7,0},{2,1},{5,2},{0,3},{3,4},{10,5},{1,6},{8,7},{15,8},{6,9},{13,... | collective-permute-start | bytes 24584 | tf_op jit(solution)/shard_map/ppermute | solution.py:260
  15.7 5.1 %collective-permute-start.9 = (f32[16,128]{1,0:T(8,128)S(1)}, f32[16,128]{1,0:T(8,128)S(1)}, u32[]{:S(2)}, u32[]{:S(2)}) collective-permute-start(f32[16,128]{1,0:T(8,128)S(1)} %get-tuple-element.61), channel_id=1, source_target_pairs={{4,0},{3,1},{6,2},{1,3},{0,4},{9,5},{2,6},{11,7},{12,8},{5,9},{14,... | collective-permute-start | bytes 24584 | tf_op jit(solution)/shard_map/ppermute | solution.py:260
  16.6 5.7 %copy-start.1 = (bf16[128,2048]{1,0:T(8,128)(2,1)S(1)}, bf16[128,2048]{1,0:T(8,128)(2,1)}, u32[]{:S(2)}) copy-start(bf16[128,2048]{1,0:T(8,128)(2,1)} %x_ref.1) | copy-start | bytes 1572868
  17.5 3.8 %collective-permute-start.6 = (f32[32,128]{1,0:T(8,128)S(1)}, f32[32,128]{1,0:T(8,128)S(1)}, u32[]{:S(2)}, u32[]{:S(2)}) collective-permute-start(f32[32,128]{1,0:T(8,128)S(1)} %pad_maximum_fusion.1), channel_id=1, source_target_pairs={{0,1},{1,0},{2,3},{3,2},{4,5},{5,4},{6,7},{7,6},{8,9},{9,8},{10,11... | collective-permute-start | bytes 49160 | tf_op jit(solution)/shard_map/ppermute | solution.py:243
  17.8 3.7 %collective-permute-start.7 = (f32[32,128]{1,0:T(8,128)S(1)}, f32[32,128]{1,0:T(8,128)S(1)}, u32[]{:S(2)}, u32[]{:S(2)}) collective-permute-start(f32[32,128]{1,0:T(8,128)S(1)} %pad_maximum_fusion.1), channel_id=1, source_target_pairs={{0,2},{1,3},{2,0},{3,1},{4,6},{5,7},{6,4},{7,5},{8,10},{9,11},{10,... | collective-permute-start | bytes 49160 | tf_op jit(solution)/shard_map/ppermute | solution.py:243
  19.1 3.2 %collective-permute-start.8 = (f32[32,128]{1,0:T(8,128)S(1)}, f32[32,128]{1,0:T(8,128)S(1)}, u32[]{:S(2)}, u32[]{:S(2)}) collective-permute-start(f32[32,128]{1,0:T(8,128)S(1)} %pad_maximum_fusion.1), channel_id=1, source_target_pairs={{0,3},{1,2},{2,1},{3,0},{4,7},{5,6},{6,5},{7,4},{8,11},{9,10},{10,... | collective-permute-start | bytes 49160 | tf_op jit(solution)/shard_map/ppermute | solution.py:243
  19.7 6.2 %collective-permute-start.15 = (bf16[16,1152]{1,0:T(8,128)(2,1)S(1)}, bf16[16,1152]{1,0:T(8,128)(2,1)S(1)}, u32[]{:S(2)}, u32[]{:S(2)}) collective-permute-start(bf16[16,1152]{1,0:T(8,128)(2,1)S(1)} %get-tuple-element.56.up_ref), channel_id=1, source_target_pairs={{0,4},{4,0},{8,12},{12,8},{1,5},{5,1},{9,13},{13,9},{2,6},{6,2},{1... | collective-permute-start | bytes 110600 | tf_op jit(solution)/shard_map/ppermute | solution.py:243
  20.9 1.4 %collective-permute-start.13 = (f32[16,128]{1,0:T(8,128)S(1)}, f32[16,128]{1,0:T(8,128)S(1)}, u32[]{:S(2)}, u32[]{:S(2)}) collective-permute-start(f32[16,128]{1,0:T(8,128)S(1)} %add_add_fusion.2), channel_id=1, source_target_pairs={{0,1},{1,0},{2,3},{3,2},{4,5},{5,4},{6,7},{7,6},{8,9},{9,8},{10,11... | collective-permute-start | bytes 24584 | tf_op jit(solution)/shard_map/ppermute | solution.py:243
  22.5 7.1 %collective-permute-start.18 = (bf16[16,2048]{1,0:T(8,128)(2,1)S(1)}, bf16[16,2048]{1,0:T(8,128)(2,1)S(1)}, u32[]{:S(2)}, u32[]{:S(2)}) collective-permute-start(bf16[16,2048]{1,0:T(8,128)(2,1)S(1)} %get-tuple-element.57), channel_id=1, source_target_pairs={{0,8},{4,12},{8,0},{12,4},{1,9},{5,13},{9,1},{13,5},{2,10},{6,14},... | collective-permute-start | bytes 196616 | tf_op jit(solution)/shard_map/ppermute | solution.py:243
  25.2 10.7 %collective-permute-start.14 = (bf16[32,2048]{1,0:T(8,128)(2,1)S(1)}, bf16[32,2048]{1,0:T(8,128)(2,1)S(1)}, u32[]{:S(2)}, u32[]{:S(2)}) collective-permute-start(bf16[32,2048]{1,0:T(8,128)(2,1)S(1)} %get-tuple-element.54.mine_ref), channel_id=1, source_target_pairs={{0,4},{4,0},{8,12},{12,8},{1,5},{5,1},{9,13},{13,9},{2,6},{6,2},{1... | collective-permute-start | bytes 393224 | tf_op jit(solution)/shard_map/ppermute | solution.py:243
  25.9 9.9 %collective-permute-start.16 = (bf16[16,3200]{1,0:T(8,128)(2,1)S(1)}, bf16[16,3200]{1,0:T(8,128)(2,1)S(1)}, u32[]{:S(2)}, u32[]{:S(2)}) collective-permute-start(bf16[16,3200]{1,0:T(8,128)(2,1)S(1)} %shard_map.117.query_ref), channel_id=1, source_target_pairs={{0,8},{4,12},{8,0},{12,4},{1,9},{5,13},{9,1},{13,5},{2,10},{6,14},... | collective-permute-start | bytes 307208 | tf_op jit(solution)/shard_map/ppermute | solution.py:243
  27.2 8.6 %collective-permute-start.17 = (bf16[16,2048]{1,0:T(8,128)(2,1)S(1)}, bf16[16,2048]{1,0:T(8,128)(2,1)S(1)}, u32[]{:S(2)}, u32[]{:S(2)}) collective-permute-start(bf16[16,2048]{1,0:T(8,128)(2,1)S(1)} %get-tuple-element.55.query_ref), channel_id=1, source_target_pairs={{0,12},{4,8},{8,4},{12,0},{1,13},{5,9},{9,5},{13,1},{2,14},{6,10},... | collective-permute-start | bytes 196616 | tf_op jit(solution)/shard_map/ppermute | solution.py:243
  29.6 6.2 %collective-permute-start.19 = (bf16[16,2048]{1,0:T(8,128)(2,1)S(1)}, bf16[16,2048]{1,0:T(8,128)(2,1)S(1)}, u32[]{:S(2)}, u32[]{:S(2)}) collective-permute-start(bf16[16,2048]{1,0:T(8,128)(2,1)S(1)} %collective-permute-done.18.value_two_ref), channel_id=1, source_target_pairs={{0,4},{4,0},{8,12},{12,8},{1,5},{5,1},{9,13},{13,9},{2,6},{6,2},{1... | collective-permute-start | bytes 196616 | tf_op jit(solution)/shard_map/ppermute | solution.py:243

commit v15 on v12

--- a/solution.py
+++ b/solution.py
@@ -93,8 +93,8 @@
 
 def project_kernel(
     count, heads,
-    low_ref, q_ref, k_ref, v_ref, o_ref, seg_ref, cos_ref, sin_ref, wq_ref, wv_ref,
-    qr_ref, kt_ref, s_ref, dp_ref, cost_ref, sint_ref,
+    low_ref, q_ref, k_ref, seg_ref, cos_ref, sin_ref, wq_ref,
+    qr_ref, kt_ref, s_ref, cost_ref, sint_ref,
 ):
     tok = q_ref.shape[0]
     low = low_ref[...].astype(BF16)
@@ -104,7 +104,6 @@
     keys = rotate_rows(k_ref[...].astype(F32), cos, sin)
     kt_ref[...] = keys.T.astype(BF16)
     keys = keys.astype(BF16)
-    vals = (v_ref[...].astype(F32) + dot(low[RANK:], wv_ref[...], 0, 0)).astype(BF16)
     seg_here = seg_ref[...].astype(F32)[0:1]
     key = lax.broadcasted_iota(jnp.int32, (tok, tok), 0)
     query = lax.broadcasted_iota(jnp.int32, (tok, tok), 1)
@@ -117,12 +116,20 @@
         qr = jnp.concatenate([rotate_rows(u, cos, sin).astype(BF16) for u in parts], axis=0)
         qr_ref[cut] = qr
         s_ref[:, cut] = dot(keys, qr, 1, 1) * INV_ROOT + bias
+
+
+def own_kernel(count, heads, low_ref, v_ref, o_ref, wv_ref, dp_ref):
+    low_v = low_ref[RANK:].astype(BF16)
+    vals = (v_ref[...].astype(F32) + dot(low_v, wv_ref[...], 0, 0)).astype(BF16)
+    tok = o_ref.shape[0]
+    for g in range(0, heads, count):
+        cut = slice(g * tok, (g + count) * tok)
         dp_ref[:, cut] = dot(vals, head_rows(o_ref, g, count), 1, 1)
 
 
 def softmax_kernel(
     count, send, blocks, heads,
-    qr_ref, s_ref, o_ref, seg_ref, pack_ref, base_ref, cos_ref, sin_ref, wv_ref,
+    qr_ref, s_ref, o_ref, seg_ref, pack_ref, base_ref, cos_ref, sin_ref, wv_ref, low_ref,
     w_ref, kt_ref, dv_ref, code_ref,
 ):
     tok = o_ref.shape[0]
@@ -154,6 +161,7 @@
     codes = split_dot(wv_ref[...], by_token(dv, send, tok), 1, 1)
     for b in range(blocks + 1):
         code_ref[b * RANK : (b + 1) * RANK] = codes[:, b * tok : (b + 1) * tok]
+    code_ref[(blocks + 1) * RANK :] = low_ref[RANK:].astype(BF16).astype(F32)
 
 
 def grads_kernel(
@@ -246,16 +254,11 @@
         moves = [(i, (i + by) % seq_count) for i in range(seq_count)]
         return lax.ppermute(array, "seq", moves)
 
-    def inner(array, even):
+    def inner(array):
         moves = []
         for i in range(seq_count):
             for f in range(fsdp_count):
-                if even and f % 2 == 0:
-                    to, flip = i ^ 1, 0
-                elif i in (1, 2):
-                    to, flip = 3 - i, 0
-                else:
-                    to, flip = i, 2
+                to, flip = (3 - i, 0) if i in (1, 2) else (i, 2)
                 moves.append((i * fsdp_count + f, to * fsdp_count + (f ^ flip)))
         return lax.ppermute(array, ("seq", "fsdp"), moves)
 
@@ -295,25 +298,19 @@
     packs = jnp.stack([shift(pack, d) for d in range(blocks, 0, -1)])
     low = sum_fsdp(part)
     low, cos, sin, wv = lax.optimization_barrier((low, cos, sin, wv))
-    low_v = low[RANK:].astype(BF16)
-    if direct:
-        far = inner(low_v, True)
-    else:
-        lows = jnp.stack([shift(low_v, d) for d in range(blocks, 0, -1)])
     count = heads if blocks == 1 else 1
-    qr, kt, s, dp, cos_t, sin_t = call(
+    qr, kt, s, cos_t, sin_t = call(
         functools.partial(project_kernel, count, heads),
         [
             ((heads * tok, HEAD), BF16),
             ((HEAD, tok), BF16),
             ((tok, heads * tok), F32),
-            ((tok, heads * tok), F32),
             ((HALF, tok), F32),
             ((HALF, tok), F32),
         ],
         cost=3 << 20,
-    )(low, q, k, v, o, seg_rows, cos[halo:], sin[halo:], wq, wv)
-    specs = [pl.BlockSpec(memory_space=pltpu.VMEM)] * 9
+    )(low, q, k, seg_rows, cos[halo:], sin[halo:], wq)
+    specs = [pl.BlockSpec(memory_space=pltpu.VMEM)] * 10
     specs[5] = pl.BlockSpec(memory_space=pltpu.SMEM)
     w, kt_far, dv, codes_v = call(
         functools.partial(softmax_kernel, count, send, blocks, heads),
@@ -321,19 +318,26 @@
             ((keys, heads * tok), F32),
             ((HEAD, halo), BF16),
             ((keys, HEAD), F32),
-            (((blocks + 1) * RANK, tok), F32),
+            (((blocks + 2) * RANK, tok), F32),
         ],
         in_specs=specs,
         cost=5 << 20,
-    )(qr, s, o, seg_rows, packs, base, cos[:halo], sin[:halo], wv)
+    )(qr, s, o, seg_rows, packs, base, cos[:halo], sin[:halo], wv, low)
+    code_v = codes_v[:RANK]
+    low_v, dv = lax.optimization_barrier((low, dv))
+    (dp,) = call(
+        functools.partial(own_kernel, count, heads), [((tok, heads * tok), F32)], cost=24 << 20
+    )(low_v, v, o, wv)
     if direct:
-        w, far = lax.optimization_barrier((w, far))
-        mine = (seq_index == 2) == (lax.axis_index("fsdp") % 2 == 1)
-        lows = jnp.where(mine, far, swap(far, "fsdp", 1))[None]
-    code_v = codes_v[:RANK]
-    if direct:
-        above, below = swap(codes_v[RANK:], "seq", 1), inner(codes_v[RANK:], False)
-        backs = jnp.where(seq_index % 2 == 0, above, jnp.where(seq_index == 1, below, 0.0))
+        outer, middle = swap(codes_v[RANK:], "seq", 1), inner(codes_v[RANK:])
+        lows = jnp.where(seq_index == 2, middle[RANK:], outer[RANK:]).astype(BF16)[None]
+        back = jnp.where(seq_index == 1, middle[:RANK], 0.0)
+        code_v = code_v + jnp.where(seq_index % 2 == 0, outer[:RANK], back)
+    else:
+        low_v = low[RANK:].astype(BF16)
+        lows = jnp.stack([shift(low_v, d) for d in range(blocks, 0, -1)])
+        for b, d in enumerate(range(blocks, 0, -1)):
+            code_v = code_v + shift(codes_v[(b + 1) * RANK : (b + 2) * RANK], -d)
     code_q, up = call(
         functools.partial(grads_kernel, count, send, blocks, heads),
         [((RANK, tok), F32), ((RANK, (heads + 1) * HEAD), BF16 if direct else F32)],
@@ -341,14 +345,12 @@
         cost=24 << 20,
     )(low, lows, packs, o, w, dp, kt, kt_far, dv, cos_t, sin_t, wq, wv)
     if not direct:
-        for b, d in enumerate(range(blocks, 0, -1)):
-            code_v = code_v + shift(codes_v[(b + 1) * RANK : (b + 2) * RANK], -d)
         dlow = sum_fsdp(jnp.concatenate([code_q, code_v], axis=0)).astype(BF16)
         (down,) = call(down_kernel, [((2 * RANK, wide), F32)])(dlow, x)
         down, up = lax.psum((down, up), "seq")
         return down.T, up[:, : heads * HEAD], up[:, heads * HEAD :]
 
-    codes = jnp.concatenate([code_q, code_v + backs], axis=0)
+    codes = jnp.concatenate([code_q, code_v], axis=0)
     near_up = swap(up, "seq", 1)
     both, part_q, part_v = call(
         partial_kernel, [((2 * RANK, wide), BF16), ((RANK, wide), BF16), ((RANK, wide), BF16)]

time: 35.8 us -> 36.2 us (1.011)
  starting transfers between devices: 19.7 us -> 13.8 us
  waiting for transfers between devices: 9.73 us -> 15.3 us
  local copies, waits for them, and re-layouts: 0.29 us -> 0.7 us
    ppermute x14 -> x13, starting transfers between devices: 15.2 us -> 10.3 us  [swap(): return lax.ppermute(array, axis, [(i, i ^ bit) for i in range(size)])]
    ppermute x14 -> x13, waiting for transfers between devices: 7.62 us -> 11.9 us  [swap(): return lax.ppermute(array, axis, [(i, i ^ bit) for i in range(size)])]
    ppermute x1, waiting for transfers between devices: 0.42 us -> 1.76 us  [shift(): return lax.ppermute(array, 'seq', moves)]
    ppermute x2 -> x1, starting transfers between devices: 2.67 us -> 1.67 us  [inner(): return lax.ppermute(array, ('seq', 'fsdp'), moves)]
    unnamed x10, local copies, waits for them, and re-layouts: 0.26 us -> 0.66 us
    ppermute x2 -> x1, waiting for transfers between devices: 1.68 us -> 1.71 us  [inner(): return lax.ppermute(array, ('seq', 'fsdp'), moves)]
  transfers between devices with their start and end apart: 17 -> 15, of which waited for: 9 -> 8; matrix products, arithmetic and copies ran while one was open for 1% -> 1% of each run, Pallas kernels for 7% -> 3%
where the time goes in v15:
time: 36.2 us; the launch traced here: 36.1 us
  waiting for transfers between devices  15.3 us (42%)
  starting transfers between devices  13.8 us (38%)
  Pallas kernels  4.96 us (14%)
  between operations  0.79 us (2%)
  local copies, waits for them, and re-layouts  0.7 us (2%)
  other arithmetic  0.48 us (1%)
    ppermute x13, waiting for transfers between devices, swap(): return lax.ppermute(array, axis, [(i, i ^ bit) for i in range(size)])  11.9 us
    ppermute x13, starting transfers between devices, swap(): return lax.ppermute(array, axis, [(i, i ^ bit) for i in range(size)])  10.3 us
    ppermute x1, starting transfers between devices, shift(): return lax.ppermute(array, 'seq', moves)  1.87 us
    ppermute x1, waiting for transfers between devices, shift(): return lax.ppermute(array, 'seq', moves)  1.76 us
    ppermute x1, waiting for transfers between devices, inner(): return lax.ppermute(array, ('seq', 'fsdp'), moves)  1.71 us
    ppermute x1, starting transfers between devices, inner(): return lax.ppermute(array, ('seq', 'fsdp'), moves)  1.67 us
    pallas_call x1, Pallas kernels, body(): call(functools.partial(lowrank_kernel, send), [((2 * RANK, tok), F32), ((...  1.4 us
    pallas_call x1, Pallas kernels, body(): call(functools.partial(grads_kernel, count, send, blocks, heads), [((RANK...  0.87 us
  transfers between devices with their start and end apart: 15, of which 8 were waited for; matrix products, arithmetic and copies ran while one was open for 1% of the time, Pallas kernels for 3%

profile of v15, /device:TPU:0, one launch (start us, length us, event | category | flops | bytes accessed | tf_op | source)
XLA Modules:
  0.0 36.1 jit_solution(5203254730862078284)
XLA Ops:
  0.6 1.4 %shard_map.112 = (f32[32,128]{1,0:T(8,128)S(1)}, bf16[128,128]{1,0:T(8,128)(2,1)S(1)}, bf16[128,128]{1,0:T(8,128)(2,1)S(1)}, bf16[128,128]{1,0:T(8,128)(2,1)S(1)}, bf16[16,1024]{1,0:T(8,128)(2,1)S(1)}) custom-call(bf16[128,2048]{1,0:T(8,128)(2,1)} %x_ref.1, bf16[32,2048]{1,0:T(8,128)(2,1)} %bitcast.8, bf16[128,128]{1,0:T(8,128)(2,1)} %refs_2_.1, ...), custom_call_target="tpu_custom_call" | custom-call | flops 1 | bytes 1 | tf_op jit(solution)/shard_map/pallas_call | solution.py:272
  2.0 0.0 copy-start.4
  2.1 0.5 %collective-permute-start = (f32[32,128]{1,0:T(8,128)S(1)}, f32[32,128]{1,0:T(8,128)S(1)}, u32[]{:S(2)}, u32[]{:S(2)}) collective-permute-start(f32[32,128]{1,0:T(8,128)S(1)} %get-tuple-element.31), channel_id=1, source_target_pairs={{0,1},{1,0},{2,3},{3,2},{4,5},{5,4},{6,7},{7,6},{8,9},{9,8},{10,11... | collective-permute-start | bytes 49160 | tf_op jit(solution)/shard_map/ppermute | solution.py:251
  2.6 2.6 %collective-permute-start.1 = (f32[32,128]{1,0:T(8,128)S(1)}, f32[32,128]{1,0:T(8,128)S(1)}, u32[]{:S(2)}, u32[]{:S(2)}) collective-permute-start(f32[32,128]{1,0:T(8,128)S(1)} %get-tuple-element.31), channel_id=1, source_target_pairs={{0,2},{1,3},{2,0},{3,1},{4,6},{5,7},{6,4},{7,5},{8,10},{9,11},{10,... | collective-permute-start | bytes 49160 | tf_op jit(solution)/shard_map/ppermute | solution.py:251
  5.1 0.1 collective-permute-start.2
  5.2 1.9 %collective-permute-start.3 = (bf16[144,128]{1,0:T(8,128)(2,1)S(1)}, bf16[144,128]{1,0:T(8,128)(2,1)S(1)}, u32[]{:S(2)}, u32[]{:S(2)}) collective-permute-start(bf16[144,128]{1,0:T(8,128)(2,1)S(1)} %pad_maximum_fusion), channel_id=1, source_target_pairs={{0,4},{4,8},{8,12},{12,0},{1,5},{5,9},{9,13},{13,1},{2,6},{6,10},{... | collective-permute-start | bytes 110600 | tf_op jit(solution)/shard_map/ppermute | solution.py:255
  7.1 0.4 %multiply_sine_fusion = (f32[192,64]{1,0:T(8,128)S(1)}, f32[192,64]{1,0:T(8,128)S(1)}) fusion(f32[64]{0:T(128)S(1)} %multiply_power_fusion, f32[192]{0:T(256)S(1)} %add_convert_fusion.1), kind=kLoop, calls=%fused_computation | loop fusion | flops 12288 | bytes 99328 | tf_op jit(solution)/shard_map/sin | solution.py:297
  7.5 0.3 copy-done.3
  7.8 0.5 %collective-permute-done.2 = f32[32,128]{1,0:T(8,128)S(1)} collective-permute-done((f32[32,128]{1,0:T(8,128)S(1)}, f32[32,128]{1,0:T(8,128)S(1)}, u32[]{:S(2)}, u32[]{:S(2)}) %collective-permute-start.2) | collective-permute-done | bytes 16416 | tf_op jit(solution)/shard_map/ppermute | solution.py:251
  8.3 0.0 copy-start
  8.4 0.4 %copy-done.2 = bf16[128,1024]{1,0:T(8,128)(2,1)S(1)} copy-done((bf16[128,1024]{1,0:T(8,128)(2,1)S(1)}, bf16[128,1024]{1,0:T(8,128)(2,1)}, u32[]{:S(2)}) %copy-start.2) | copy-done | bytes 262168
  8.8 0.6 %shard_map.113 = (bf16[1024,128]{1,0:T(8,128)(2,1)S(1)}, bf16[128,128]{1,0:T(8,128)(2,1)S(1)}, f32[128,1024]{1,0:T(8,128)S(1)}, f32[64,128]{1,0:T(8,128)S(1)}, f32[64,128]{1,0:T(8,128)S(1)}) custom-call(f32[32,128]{1,0:T(8,128)S(1)} %add_add_fusion.low_ref, bf16[128,1024]{1,0:T(8,128)(2,1)S(1)} %copy-done.2, bf16[128,128]{1,0:T(8,128)(2,1)S(1)} %get-tuple-element.33.k_ref, ...), custom_call_target="tpu_custom_call" | custom-call | flops 3145728 | bytes 3145728 | tf_op jit(solution)/shard_map/pallas_call | solution.py:302
  9.4 1.8 %collective-permute-done.3 = bf16[144,128]{1,0:T(8,128)(2,1)S(1)} collective-permute-done((bf16[144,128]{1,0:T(8,128)(2,1)S(1)}, bf16[144,128]{1,0:T(8,128)(2,1)S(1)}, u32[]{:S(2)}, u32[]{:S(2)}) %collective-permute-start.3) | collective-permute-done | bytes 36896 | tf_op jit(solution)/shard_map/ppermute | solution.py:255
  11.1 0.8 %shard_map.114 = (f32[192,1024]{1,0:T(8,128)S(1)}, bf16[128,64]{1,0:T(8,128)(2,1)S(1)}, f32[192,128]{1,0:T(8,128)S(1)}, f32[48,128]{1,0:T(8,128)S(1)}) custom-call(bf16[1024,128]{1,0:T(8,128)(2,1)S(1)} %get-tuple-element.37.qr_ref, f32[128,1024]{1,0:T(8,128)S(1)} %get-tuple-element.38.s_ref, bf16[128,1024]{1,0:T(8,128)(2,1)S(1)} %copy-done, ...), custom_call_target="tpu_custom_call" | custom-call | flops 5242880 | bytes 5242880 | tf_op jit(solution)/shard_map/pallas_call | solution.py:315
  11.9 1.7 %collective-permute-start.4 = (f32[32,128]{1,0:T(8,128)S(1)}, f32[32,128]{1,0:T(8,128)S(1)}, u32[]{:S(2)}, u32[]{:S(2)}) collective-permute-start(f32[32,128]{1,0:T(8,128)S(1)} %slice.35), channel_id=1, source_target_pairs={{0,2},{1,3},{2,0},{3,1},{4,8},{5,9},{6,10},{7,11},{8,4},{9,5},{10,... | collective-permute-start | bytes 49160 | tf_op jit(solution)/shard_map/ppermute | solution.py:263
  13.5 0.4 %shard_map.115.dp_ref = f32[128,1024]{1,0:T(8,128)S(1)} custom-call(f32[32,128]{1,0:T(8,128)S(1)} %add_add_fusion.low_ref, bf16[128,128]{1,0:T(8,128)(2,1)S(1)} %get-tuple-element.45.v_ref, bf16[128,1024]{1,0:T(8,128)(2,1)S(1)} %copy-done, bf16[16,128]{1,0:T(8,128)(2,1)S(1)} %broadcast_multiply_fusion.wv_ref), custom_call_target="tpu_custom_call" | custom-call | flops 25165824 | bytes 25165824 | tf_op jit(solution)/shard_map/pallas_call | solution.py:328
  13.9 1.7 %collective-permute-done.4 = f32[32,128]{1,0:T(8,128)S(1)} collective-permute-done((f32[32,128]{1,0:T(8,128)S(1)}, f32[32,128]{1,0:T(8,128)S(1)}, u32[]{:S(2)}, u32[]{:S(2)}) %collective-permute-start.4) | collective-permute-done | bytes 16416 | tf_op jit(solution)/shard_map/ppermute | solution.py:263
  15.6 1.7 %collective-permute-done.5 = f32[32,128]{1,0:T(8,128)S(1)} collective-permute-done((f32[32,128]{1,0:T(8,128)S(1)}, f32[32,128]{1,0:T(8,128)S(1)}, u32[]{:S(2)}, u32[]{:S(2)}) %collective-permute-start.5) | collective-permute-done | bytes 16416 | tf_op jit(solution)/shard_map/ppermute | solution.py:251
  17.3 0.9 %shard_map.116 = (f32[16,128]{1,0:T(8,128)S(1)}, bf16[16,1152]{1,0:T(8,128)(2,1)S(1)}) custom-call(f32[32,128]{1,0:T(8,128)S(1)} %add_add_fusion.low_ref, bf16[1,16,128]{2,1,0:T(8,128)(2,1)S(1)} %fusion.3.far_ref, bf16[1,144,128]{2,1,0:T(8,128)(2,1)S(1)} %bitcast.7, bf16[128,1024]{1,0:T(8,128)(2,1)S(1)} %copy-done, f32[192,1024]{1,0:T(8,128)S(1)} %get-tuple-element.42.w_ref, ...), custom_call_target="tpu_custom_call" | custom-call | flops 25165824 | bytes 25165824 | tf_op jit(solution)/shard_map/pallas_call | solution.py:341
  18.2 0.1 collective-permute-start.6
  18.3 0.4 %collective-permute-start.7 = (f32[32,128]{1,0:T(8,128)S(1)}, f32[32,128]{1,0:T(8,128)S(1)}, u32[]{:S(2)}, u32[]{:S(2)}) collective-permute-start(f32[32,128]{1,0:T(8,128)S(1)} %pad_maximum_fusion.1), channel_id=1, source_target_pairs={{0,2},{1,3},{2,0},{3,1},{4,6},{5,7},{6,4},{7,5},{8,10},{9,11},{10,... | collective-permute-start | bytes 49160 | tf_op jit(solution)/shard_map/ppermute | solution.py:251
  18.7 1.4 %collective-permute-start.8 = (f32[32,128]{1,0:T(8,128)S(1)}, f32[32,128]{1,0:T(8,128)S(1)}, u32[]{:S(2)}, u32[]{:S(2)}) collective-permute-start(f32[32,128]{1,0:T(8,128)S(1)} %pad_maximum_fusion.1), channel_id=1, source_target_pairs={{0,3},{1,2},{2,1},{3,0},{4,7},{5,6},{6,5},{7,4},{8,11},{9,10},{10,... | collective-permute-start | bytes 49160 | tf_op jit(solution)/shard_map/ppermute | solution.py:251
  20.1 1.9 %collective-permute-done.7 = f32[32,128]{1,0:T(8,128)S(1)} collective-permute-done((f32[32,128]{1,0:T(8,128)S(1)}, f32[32,128]{1,0:T(8,128)S(1)}, u32[]{:S(2)}, u32[]{:S(2)}) %collective-permute-start.7) | collective-permute-done | bytes 16416 | tf_op jit(solution)/shard_map/ppermute | solution.py:251
  22.1 0.2 shard_map.117
  22.3 0.7 %collective-permute-start.13 = (bf16[16,2048]{1,0:T(8,128)(2,1)S(1)}, bf16[16,2048]{1,0:T(8,128)(2,1)S(1)}, u32[]{:S(2)}, u32[]{:S(2)}) collective-permute-start(bf16[16,2048]{1,0:T(8,128)(2,1)S(1)} %get-tuple-element.55), channel_id=1, source_target_pairs={{0,8},{4,12},{8,0},{12,4},{1,9},{5,13},{9,1},{13,5},{2,10},{6,14},... | collective-permute-start | bytes 196616 | tf_op jit(solution)/shard_map/ppermute | solution.py:251
  23.0 1.8 %collective-permute-start.9 = (bf16[32,2048]{1,0:T(8,128)(2,1)S(1)}, bf16[32,2048]{1,0:T(8,128)(2,1)S(1)}, u32[]{:S(2)}, u32[]{:S(2)}) collective-permute-start(bf16[32,2048]{1,0:T(8,128)(2,1)S(1)} %get-tuple-element.52.mine_ref), channel_id=1, source_target_pairs={{0,4},{4,0},{8,12},{12,8},{1,5},{5,1},{9,13},{13,9},{2,6},{6,2},{1... | collective-permute-start | bytes 393224 | tf_op jit(solution)/shard_map/ppermute | solution.py:251
  24.9 1.3 %collective-permute-start.11 = (bf16[16,3200]{1,0:T(8,128)(2,1)S(1)}, bf16[16,3200]{1,0:T(8,128)(2,1)S(1)}, u32[]{:S(2)}, u32[]{:S(2)}) collective-permute-start(bf16[16,3200]{1,0:T(8,128)(2,1)S(1)} %shard_map.118.query_ref), channel_id=1, source_target_pairs={{0,8},{4,12},{8,0},{12,4},{1,9},{5,13},{9,1},{13,5},{2,10},{6,14},... | collective-permute-start | bytes 307208 | tf_op jit(solution)/shard_map/ppermute | solution.py:251
  26.2 1.3 %collective-permute-start.12 = (bf16[16,2048]{1,0:T(8,128)(2,1)S(1)}, bf16[16,2048]{1,0:T(8,128)(2,1)S(1)}, u32[]{:S(2)}, u32[]{:S(2)}) collective-permute-start(bf16[16,2048]{1,0:T(8,128)(2,1)S(1)} %get-tuple-element.53.query_ref), channel_id=1, source_target_pairs={{0,12},{4,8},{8,4},{12,0},{1,13},{5,9},{9,5},{13,1},{2,14},{6,10},... | collective-permute-start | bytes 196616 | tf_op jit(solution)/shard_map/ppermute | solution.py:251
  27.5 1.7 %collective-permute-done.13.value_two_ref = bf16[16,2048]{1,0:T(8,128)(2,1)S(1)} collective-permute-done((bf16[16,2048]{1,0:T(8,128)(2,1)S(1)}, bf16[16,2048]{1,0:T(8,128)(2,1)S(1)}, u32[]{:S(2)}, u32[]{:S(2)}) %collective-permute-start.13) | collective-permute-done | bytes 65568 | tf_op jit(solution)/shard_map/ppermute | solution.py:251
  29.2 5.6 %collective-permute-done.12.query_three_ref = bf16[16,2048]{1,0:T(8,128)(2,1)S(1)} collective-permute-done((bf16[16,2048]{1,0:T(8,128)(2,1)S(1)}, bf16[16,2048]{1,0:T(8,128)(2,1)S(1)}, u32[]{:S(2)}, u32[]{:S(2)}) %collective-permute-start.12) | collective-permute-done | bytes 65568 | tf_op jit(solution)/shard_map/ppermute | solution.py:251
  34.8 0.5 %collective-permute-done.11.query_two_ref = bf16[16,3200]{1,0:T(8,128)(2,1)S(1)} collective-permute-done((bf16[16,3200]{1,0:T(8,128)(2,1)S(1)}, bf16[16,3200]{1,0:T(8,128)(2,1)S(1)}, u32[]{:S(2)}, u32[]{:S(2)}) %collective-permute-start.11) | collective-permute-done | bytes 102432 | tf_op jit(solution)/shard_map/ppermute | solution.py:251
  35.3 0.8 %shard_map.119 = (f32[32,2048]{1,0:T(8,128)}, f32[16,1024]{1,0:T(8,128)}, f32[16,128]{1,0:T(8,128)}) custom-call(bf16[32,2048]{1,0:T(8,128)(2,1)S(1)} %get-tuple-element.52.mine_ref, bf16[32,2048]{1,0:T(8,128)(2,1)S(1)} %collective-permute-done.9.one_ref, bf16[16,3200]{1,0:T(8,128)(2,1)S(1)} %shard_map.118.query_ref, ...), custom_call_target="tpu_custom_call" | custom-call | flops 1 | bytes 1 | tf_op jit(solution)/shard_map/pallas_call | solution.py:363
  (33 shorter events, 0.1 us)
Async XLA Ops:
  2.0 3.2 %copy-start.4 = (s32[128]{0:T(128)S(1)}, s32[128]{0:T(128)}, u32[]{:S(2)}) copy-start(s32[128]{0:T(128)} %param.14) | copy-start | bytes 1540
  2.1 5.8 %collective-permute-start = (f32[32,128]{1,0:T(8,128)S(1)}, f32[32,128]{1,0:T(8,128)S(1)}, u32[]{:S(2)}, u32[]{:S(2)}) collective-permute-start(f32[32,128]{1,0:T(8,128)S(1)} %get-tuple-element.31), channel_id=1, source_target_pairs={{0,1},{1,0},{2,3},{3,2},{4,5},{5,4},{6,7},{7,6},{8,9},{9,8},{10,11... | collective-permute-start | bytes 49160 | tf_op jit(solution)/shard_map/ppermute | solution.py:251
  2.6 5.2 %collective-permute-start.1 = (f32[32,128]{1,0:T(8,128)S(1)}, f32[32,128]{1,0:T(8,128)S(1)}, u32[]{:S(2)}, u32[]{:S(2)}) collective-permute-start(f32[32,128]{1,0:T(8,128)S(1)} %get-tuple-element.31), channel_id=1, source_target_pairs={{0,2},{1,3},{2,0},{3,1},{4,6},{5,7},{6,4},{7,5},{8,10},{9,11},{10,... | collective-permute-start | bytes 49160 | tf_op jit(solution)/shard_map/ppermute | solution.py:251
  5.1 3.2 %collective-permute-start.2 = (f32[32,128]{1,0:T(8,128)S(1)}, f32[32,128]{1,0:T(8,128)S(1)}, u32[]{:S(2)}, u32[]{:S(2)}) collective-permute-start(f32[32,128]{1,0:T(8,128)S(1)} %get-tuple-element.31), channel_id=1, source_target_pairs={{0,3},{1,2},{2,1},{3,0},{4,7},{5,6},{6,5},{7,4},{8,11},{9,10},{10,... | collective-permute-start | bytes 49160 | tf_op jit(solution)/shard_map/ppermute | solution.py:251
  5.2 5.9 %collective-permute-start.3 = (bf16[144,128]{1,0:T(8,128)(2,1)S(1)}, bf16[144,128]{1,0:T(8,128)(2,1)S(1)}, u32[]{:S(2)}, u32[]{:S(2)}) collective-permute-start(bf16[144,128]{1,0:T(8,128)(2,1)S(1)} %pad_maximum_fusion), channel_id=1, source_target_pairs={{0,4},{4,8},{8,12},{12,0},{1,5},{5,9},{9,13},{13,1},{2,6},{6,10},{... | collective-permute-start | bytes 110600 | tf_op jit(solution)/shard_map/ppermute | solution.py:255
  7.1 0.7 %copy-start.3 = (bf16[16,128]{1,0:T(8,128)(2,1)S(1)}, bf16[16,128]{1,0:T(8,128)(2,1)}, u32[]{:S(2)}) copy-start(bf16[16,128]{1,0:T(8,128)(2,1)} %param.17) | copy-start | bytes 12292
  7.8 0.9 %copy-start.2 = (bf16[128,1024]{1,0:T(8,128)(2,1)S(1)}, bf16[128,1024]{1,0:T(8,128)(2,1)}, u32[]{:S(2)}) copy-start(bf16[128,1024]{1,0:T(8,128)(2,1)} %q_ref.1) | copy-start | bytes 786436
  8.3 2.8 %copy-start = (bf16[128,1024]{1,0:T(8,128)(2,1)S(1)}, bf16[128,1024]{1,0:T(8,128)(2,1)}, u32[]{:S(2)}) copy-start(bf16[128,1024]{1,0:T(8,128)(2,1)} %o_ref.5) | copy-start | bytes 786436
  11.9 3.8 %collective-permute-start.4 = (f32[32,128]{1,0:T(8,128)S(1)}, f32[32,128]{1,0:T(8,128)S(1)}, u32[]{:S(2)}, u32[]{:S(2)}) collective-permute-start(f32[32,128]{1,0:T(8,128)S(1)} %slice.35), channel_id=1, source_target_pairs={{0,2},{1,3},{2,0},{3,1},{4,8},{5,9},{6,10},{7,11},{8,4},{9,5},{10,... | collective-permute-start | bytes 49160 | tf_op jit(solution)/shard_map/ppermute | solution.py:263
  13.5 3.7 %collective-permute-start.5 = (f32[32,128]{1,0:T(8,128)S(1)}, f32[32,128]{1,0:T(8,128)S(1)}, u32[]{:S(2)}, u32[]{:S(2)}) collective-permute-start(f32[32,128]{1,0:T(8,128)S(1)} %slice.35), channel_id=1, source_target_pairs={{0,4},{4,0},{8,12},{12,8},{1,5},{5,1},{9,13},{13,9},{2,6},{6,2},{1... | collective-permute-start | bytes 49160 | tf_op jit(solution)/shard_map/ppermute | solution.py:251
  17.3 4.8 %copy-start.1 = (bf16[128,2048]{1,0:T(8,128)(2,1)S(1)}, bf16[128,2048]{1,0:T(8,128)(2,1)}, u32[]{:S(2)}) copy-start(bf16[128,2048]{1,0:T(8,128)(2,1)} %x_ref.1) | copy-start | bytes 1572868
  18.2 1.9 %collective-permute-start.6 = (f32[32,128]{1,0:T(8,128)S(1)}, f32[32,128]{1,0:T(8,128)S(1)}, u32[]{:S(2)}, u32[]{:S(2)}) collective-permute-start(f32[32,128]{1,0:T(8,128)S(1)} %pad_maximum_fusion.1), channel_id=1, source_target_pairs={{0,1},{1,0},{2,3},{3,2},{4,5},{5,4},{6,7},{7,6},{8,9},{9,8},{10,11... | collective-permute-start | bytes 49160 | tf_op jit(solution)/shard_map/ppermute | solution.py:251
  18.3 3.8 %collective-permute-start.7 = (f32[32,128]{1,0:T(8,128)S(1)}, f32[32,128]{1,0:T(8,128)S(1)}, u32[]{:S(2)}, u32[]{:S(2)}) collective-permute-start(f32[32,128]{1,0:T(8,128)S(1)} %pad_maximum_fusion.1), channel_id=1, source_target_pairs={{0,2},{1,3},{2,0},{3,1},{4,6},{5,7},{6,4},{7,5},{8,10},{9,11},{10,... | collective-permute-start | bytes 49160 | tf_op jit(solution)/shard_map/ppermute | solution.py:251
  18.7 3.4 %collective-permute-start.8 = (f32[32,128]{1,0:T(8,128)S(1)}, f32[32,128]{1,0:T(8,128)S(1)}, u32[]{:S(2)}, u32[]{:S(2)}) collective-permute-start(f32[32,128]{1,0:T(8,128)S(1)} %pad_maximum_fusion.1), channel_id=1, source_target_pairs={{0,3},{1,2},{2,1},{3,0},{4,7},{5,6},{6,5},{7,4},{8,11},{9,10},{10,... | collective-permute-start | bytes 49160 | tf_op jit(solution)/shard_map/ppermute | solution.py:251
  20.1 4.7 %collective-permute-start.10 = (bf16[16,1152]{1,0:T(8,128)(2,1)S(1)}, bf16[16,1152]{1,0:T(8,128)(2,1)S(1)}, u32[]{:S(2)}, u32[]{:S(2)}) collective-permute-start(bf16[16,1152]{1,0:T(8,128)(2,1)S(1)} %get-tuple-element.54.up_ref), channel_id=1, source_target_pairs={{0,4},{4,0},{8,12},{12,8},{1,5},{5,1},{9,13},{13,9},{2,6},{6,2},{1... | collective-permute-start | bytes 110600 | tf_op jit(solution)/shard_map/ppermute | solution.py:251
  22.3 6.9 %collective-permute-start.13 = (bf16[16,2048]{1,0:T(8,128)(2,1)S(1)}, bf16[16,2048]{1,0:T(8,128)(2,1)S(1)}, u32[]{:S(2)}, u32[]{:S(2)}) collective-permute-start(bf16[16,2048]{1,0:T(8,128)(2,1)S(1)} %get-tuple-element.55), channel_id=1, source_target_pairs={{0,8},{4,12},{8,0},{12,4},{1,9},{5,13},{9,1},{13,5},{2,10},{6,14},... | collective-permute-start | bytes 196616 | tf_op jit(solution)/shard_map/ppermute | solution.py:251
  23.0 12.3 %collective-permute-start.9 = (bf16[32,2048]{1,0:T(8,128)(2,1)S(1)}, bf16[32,2048]{1,0:T(8,128)(2,1)S(1)}, u32[]{:S(2)}, u32[]{:S(2)}) collective-permute-start(bf16[32,2048]{1,0:T(8,128)(2,1)S(1)} %get-tuple-element.52.mine_ref), channel_id=1, source_target_pairs={{0,4},{4,0},{8,12},{12,8},{1,5},{5,1},{9,13},{13,9},{2,6},{6,2},{1... | collective-permute-start | bytes 393224 | tf_op jit(solution)/shard_map/ppermute | solution.py:251
  24.9 10.4 %collective-permute-start.11 = (bf16[16,3200]{1,0:T(8,128)(2,1)S(1)}, bf16[16,3200]{1,0:T(8,128)(2,1)S(1)}, u32[]{:S(2)}, u32[]{:S(2)}) collective-permute-start(bf16[16,3200]{1,0:T(8,128)(2,1)S(1)} %shard_map.118.query_ref), channel_id=1, source_target_pairs={{0,8},{4,12},{8,0},{12,4},{1,9},{5,13},{9,1},{13,5},{2,10},{6,14},... | collective-permute-start | bytes 307208 | tf_op jit(solution)/shard_map/ppermute | solution.py:251
  26.2 8.6 %collective-permute-start.12 = (bf16[16,2048]{1,0:T(8,128)(2,1)S(1)}, bf16[16,2048]{1,0:T(8,128)(2,1)S(1)}, u32[]{:S(2)}, u32[]{:S(2)}) collective-permute-start(bf16[16,2048]{1,0:T(8,128)(2,1)S(1)} %get-tuple-element.53.query_ref), channel_id=1, source_target_pairs={{0,12},{4,8},{8,4},{12,0},{1,13},{5,9},{9,5},{13,1},{2,14},{6,10},... | collective-permute-start | bytes 196616 | tf_op jit(solution)/shard_map/ppermute | solution.py:251
  29.2 6.1 %collective-permute-start.14 = (bf16[16,2048]{1,0:T(8,128)(2,1)S(1)}, bf16[16,2048]{1,0:T(8,128)(2,1)S(1)}, u32[]{:S(2)}, u32[]{:S(2)}) collective-permute-start(bf16[16,2048]{1,0:T(8,128)(2,1)S(1)} %collective-permute-done.13.value_two_ref), channel_id=1, source_target_pairs={{0,4},{4,0},{8,12},{12,8},{1,5},{5,1},{9,13},{13,9},{2,6},{6,2},{1... | collective-permute-start | bytes 196616 | tf_op jit(solution)/shard_map/ppermute | solution.py:251

commit v16 on v15

--- a/solution.py
+++ b/solution.py
@@ -219,11 +219,12 @@
 
 
 def final_kernel(
-    mine_ref, one_ref, query_ref, query_two_ref, query_three_ref, value_two_ref, value_three_ref,
+    mine_ref, query_ref, query_two_ref, query_three_ref, value_two_ref, value_three_ref, query_one_ref, value_one_ref,
     down_ref, upq_ref, upv_ref,
 ):
     wide, size = down_ref.shape[1], upq_ref.shape[1]
-    near = mine_ref[...].astype(F32) + one_ref[...].astype(F32)
+    one = jnp.concatenate([query_one_ref[...], value_one_ref[...]], axis=0)
+    near = mine_ref[...].astype(F32) + one.astype(F32)
     far = query_two_ref[:, :wide].astype(F32) + query_three_ref[...].astype(F32)
     down_ref[:RANK] = near[:RANK] + far
     far = value_two_ref[...].astype(F32) + value_three_ref[...].astype(F32)
@@ -356,14 +357,15 @@
         partial_kernel, [((2 * RANK, wide), BF16), ((RANK, wide), BF16), ((RANK, wide), BF16)]
     )(sum_fsdp(codes).astype(BF16), x)
     (send_q,) = call(combine_kernel, [((RANK, wide + up.shape[1]), BF16)])(part_q, up, near_up)
+    send_q, late = lax.optimization_barrier((send_q, both))
     value_two = swap(part_v, "seq", 2)
     value_three = swap(value_two, "seq", 1)
     query_two, query_three = swap(send_q, "seq", 2), swap(part_q, "seq", 3)
-    one = swap(both, "seq", 1)
+    ones = [swap(late[i * RANK : (i + 1) * RANK], "seq", 1) for i in range(2)]
     down, up_q, up_v = call(
         final_kernel,
         [((2 * RANK, wide), F32), ((RANK, heads * HEAD), F32), ((RANK, HEAD), F32)],
-    )(both, one, send_q, query_two, query_three, value_two, value_three)
+    )(both, send_q, query_two, query_three, value_two, value_three, *ones)
     return down.T, up_q, up_v
 
 

time: 36.2 us -> 38.3 us (1.058)
  waiting for transfers between devices: 15.3 us -> 16.4 us
  starting transfers between devices: 13.8 us -> 14.8 us
    ppermute x13 -> x14, waiting for transfers between devices: 11.9 us -> 12.9 us  [swap(): return lax.ppermute(array, axis, [(i, i ^ bit) for i in range(size)])]
    ppermute x13 -> x14, starting transfers between devices: 10.3 us -> 11.3 us  [swap(): return lax.ppermute(array, axis, [(i, i ^ bit) for i in range(size)])]
  transfers between devices with their start and end apart: 15 -> 16, of which waited for: 8 -> 9; matrix products, arithmetic and copies ran while one was open for 1% -> 1% of each run, Pallas kernels for 3% -> 3%
where the time goes in v16:
time: 38.3 us; the launch traced here: 38.2 us
  waiting for transfers between devices  16.4 us (43%)
  starting transfers between devices  14.8 us (39%)
  Pallas kernels  4.97 us (13%)
  between operations  0.8 us (2%)
  local copies, waits for them, and re-layouts  0.71 us (2%)
  other arithmetic  0.48 us (1%)
    ppermute x14, waiting for transfers between devices, swap(): return lax.ppermute(array, axis, [(i, i ^ bit) for i in range(size)])  12.9 us
    ppermute x14, starting transfers between devices, swap(): return lax.ppermute(array, axis, [(i, i ^ bit) for i in range(size)])  11.3 us
    ppermute x1, starting transfers between devices, shift(): return lax.ppermute(array, 'seq', moves)  1.87 us
    ppermute x1, waiting for transfers between devices, shift(): return lax.ppermute(array, 'seq', moves)  1.76 us
    ppermute x1, waiting for transfers between devices, inner(): return lax.ppermute(array, ('seq', 'fsdp'), moves)  1.71 us
    ppermute x1, starting transfers between devices, inner(): return lax.ppermute(array, ('seq', 'fsdp'), moves)  1.67 us
    pallas_call x1, Pallas kernels, body(): call(functools.partial(lowrank_kernel, send), [((2 * RANK, tok), F32), ((...  1.4 us
    pallas_call x1, Pallas kernels, body(): call(functools.partial(grads_kernel, count, send, blocks, heads), [((RANK...  0.87 us
  transfers between devices with their start and end apart: 16, of which 9 were waited for; matrix products, arithmetic and copies ran while one was open for 1% of the time, Pallas kernels for 3%

profile of v16, /device:TPU:0, one launch (start us, length us, event | category | flops | bytes accessed | tf_op | source)
XLA Modules:
  0.0 38.2 jit_solution(14525243568909465412)
XLA Ops:
  0.6 1.4 %shard_map.112 = (f32[32,128]{1,0:T(8,128)S(1)}, bf16[128,128]{1,0:T(8,128)(2,1)S(1)}, bf16[128,128]{1,0:T(8,128)(2,1)S(1)}, bf16[128,128]{1,0:T(8,128)(2,1)S(1)}, bf16[16,1024]{1,0:T(8,128)(2,1)S(1)}) custom-call(bf16[128,2048]{1,0:T(8,128)(2,1)} %x_ref.1, bf16[32,2048]{1,0:T(8,128)(2,1)} %bitcast.8, bf16[128,128]{1,0:T(8,128)(2,1)} %refs_2_.1, ...), custom_call_target="tpu_custom_call" | custom-call | flops 1 | bytes 1 | tf_op jit(solution)/shard_map/pallas_call | solution.py:273
  2.1 0.5 %collective-permute-start = (f32[32,128]{1,0:T(8,128)S(1)}, f32[32,128]{1,0:T(8,128)S(1)}, u32[]{:S(2)}, u32[]{:S(2)}) collective-permute-start(f32[32,128]{1,0:T(8,128)S(1)} %get-tuple-element.33), channel_id=1, source_target_pairs={{0,1},{1,0},{2,3},{3,2},{4,5},{5,4},{6,7},{7,6},{8,9},{9,8},{10,11... | collective-permute-start | bytes 49160 | tf_op jit(solution)/shard_map/ppermute | solution.py:252
  2.6 2.6 %collective-permute-start.1 = (f32[32,128]{1,0:T(8,128)S(1)}, f32[32,128]{1,0:T(8,128)S(1)}, u32[]{:S(2)}, u32[]{:S(2)}) collective-permute-start(f32[32,128]{1,0:T(8,128)S(1)} %get-tuple-element.33), channel_id=1, source_target_pairs={{0,2},{1,3},{2,0},{3,1},{4,6},{5,7},{6,4},{7,5},{8,10},{9,11},{10,... | collective-permute-start | bytes 49160 | tf_op jit(solution)/shard_map/ppermute | solution.py:252
  5.1 0.1 collective-permute-start.2
  5.2 1.9 %collective-permute-start.3 = (bf16[144,128]{1,0:T(8,128)(2,1)S(1)}, bf16[144,128]{1,0:T(8,128)(2,1)S(1)}, u32[]{:S(2)}, u32[]{:S(2)}) collective-permute-start(bf16[144,128]{1,0:T(8,128)(2,1)S(1)} %pad_maximum_fusion), channel_id=1, source_target_pairs={{0,4},{4,8},{8,12},{12,0},{1,5},{5,9},{9,13},{13,1},{2,6},{6,10},{... | collective-permute-start | bytes 110600 | tf_op jit(solution)/shard_map/ppermute | solution.py:256
  7.1 0.4 %multiply_sine_fusion = (f32[192,64]{1,0:T(8,128)S(1)}, f32[192,64]{1,0:T(8,128)S(1)}) fusion(f32[64]{0:T(128)S(1)} %multiply_power_fusion, f32[192]{0:T(256)S(1)} %add_convert_fusion.1), kind=kLoop, calls=%fused_computation | loop fusion | flops 12288 | bytes 99328 | tf_op jit(solution)/shard_map/sin | solution.py:298
  7.5 0.3 copy-done.3
  7.8 0.5 %collective-permute-done.2 = f32[32,128]{1,0:T(8,128)S(1)} collective-permute-done((f32[32,128]{1,0:T(8,128)S(1)}, f32[32,128]{1,0:T(8,128)S(1)}, u32[]{:S(2)}, u32[]{:S(2)}) %collective-permute-start.2) | collective-permute-done | bytes 16416 | tf_op jit(solution)/shard_map/ppermute | solution.py:252
  8.4 0.4 %copy-done.2 = bf16[128,1024]{1,0:T(8,128)(2,1)S(1)} copy-done((bf16[128,1024]{1,0:T(8,128)(2,1)S(1)}, bf16[128,1024]{1,0:T(8,128)(2,1)}, u32[]{:S(2)}) %copy-start.2) | copy-done | bytes 262168
  8.8 0.6 %shard_map.113 = (bf16[1024,128]{1,0:T(8,128)(2,1)S(1)}, bf16[128,128]{1,0:T(8,128)(2,1)S(1)}, f32[128,1024]{1,0:T(8,128)S(1)}, f32[64,128]{1,0:T(8,128)S(1)}, f32[64,128]{1,0:T(8,128)S(1)}) custom-call(f32[32,128]{1,0:T(8,128)S(1)} %add_add_fusion.low_ref, bf16[128,1024]{1,0:T(8,128)(2,1)S(1)} %copy-done.2, bf16[128,128]{1,0:T(8,128)(2,1)S(1)} %get-tuple-element.35.k_ref, ...), custom_call_target="tpu_custom_call" | custom-call | flops 3145728 | bytes 3145728 | tf_op jit(solution)/shard_map/pallas_call | solution.py:303
  9.4 1.8 %collective-permute-done.3 = bf16[144,128]{1,0:T(8,128)(2,1)S(1)} collective-permute-done((bf16[144,128]{1,0:T(8,128)(2,1)S(1)}, bf16[144,128]{1,0:T(8,128)(2,1)S(1)}, u32[]{:S(2)}, u32[]{:S(2)}) %collective-permute-start.3) | collective-permute-done | bytes 36896 | tf_op jit(solution)/shard_map/ppermute | solution.py:256
  11.1 0.8 %shard_map.114 = (f32[192,1024]{1,0:T(8,128)S(1)}, bf16[128,64]{1,0:T(8,128)(2,1)S(1)}, f32[192,128]{1,0:T(8,128)S(1)}, f32[48,128]{1,0:T(8,128)S(1)}) custom-call(bf16[1024,128]{1,0:T(8,128)(2,1)S(1)} %get-tuple-element.39.qr_ref, f32[128,1024]{1,0:T(8,128)S(1)} %get-tuple-element.40.s_ref, bf16[128,1024]{1,0:T(8,128)(2,1)S(1)} %copy-done, ...), custom_call_target="tpu_custom_call" | custom-call | flops 5242880 | bytes 5242880 | tf_op jit(solution)/shard_map/pallas_call | solution.py:316
  11.9 1.7 %collective-permute-start.4 = (f32[32,128]{1,0:T(8,128)S(1)}, f32[32,128]{1,0:T(8,128)S(1)}, u32[]{:S(2)}, u32[]{:S(2)}) collective-permute-start(f32[32,128]{1,0:T(8,128)S(1)} %slice.41), channel_id=1, source_target_pairs={{0,2},{1,3},{2,0},{3,1},{4,8},{5,9},{6,10},{7,11},{8,4},{9,5},{10,... | collective-permute-start | bytes 49160 | tf_op jit(solution)/shard_map/ppermute | solution.py:264
  13.5 0.4 shard_map.115.dp_ref
  13.9 1.7 %collective-permute-done.4 = f32[32,128]{1,0:T(8,128)S(1)} collective-permute-done((f32[32,128]{1,0:T(8,128)S(1)}, f32[32,128]{1,0:T(8,128)S(1)}, u32[]{:S(2)}, u32[]{:S(2)}) %collective-permute-start.4) | collective-permute-done | bytes 16416 | tf_op jit(solution)/shard_map/ppermute | solution.py:264
  15.6 1.7 %collective-permute-done.5 = f32[32,128]{1,0:T(8,128)S(1)} collective-permute-done((f32[32,128]{1,0:T(8,128)S(1)}, f32[32,128]{1,0:T(8,128)S(1)}, u32[]{:S(2)}, u32[]{:S(2)}) %collective-permute-start.5) | collective-permute-done | bytes 16416 | tf_op jit(solution)/shard_map/ppermute | solution.py:252
  17.3 0.9 %shard_map.116 = (f32[16,128]{1,0:T(8,128)S(1)}, bf16[16,1152]{1,0:T(8,128)(2,1)S(1)}) custom-call(f32[32,128]{1,0:T(8,128)S(1)} %add_add_fusion.low_ref, bf16[1,16,128]{2,1,0:T(8,128)(2,1)S(1)} %fusion.3.far_ref, bf16[1,144,128]{2,1,0:T(8,128)(2,1)S(1)} %bitcast.7, bf16[128,1024]{1,0:T(8,128)(2,1)S(1)} %copy-done, f32[192,1024]{1,0:T(8,128)S(1)} %get-tuple-element.44.w_ref, ...), custom_call_target="tpu_custom_call" | custom-call | flops 25165824 | bytes 25165824 | tf_op jit(solution)/shard_map/pallas_call | solution.py:342
  18.2 0.1 collective-permute-start.6
  18.3 0.4 %collective-permute-start.7 = (f32[32,128]{1,0:T(8,128)S(1)}, f32[32,128]{1,0:T(8,128)S(1)}, u32[]{:S(2)}, u32[]{:S(2)}) collective-permute-start(f32[32,128]{1,0:T(8,128)S(1)} %pad_maximum_fusion.1), channel_id=1, source_target_pairs={{0,2},{1,3},{2,0},{3,1},{4,6},{5,7},{6,4},{7,5},{8,10},{9,11},{10,... | collective-permute-start | bytes 49160 | tf_op jit(solution)/shard_map/ppermute | solution.py:252
  18.7 1.4 %collective-permute-start.8 = (f32[32,128]{1,0:T(8,128)S(1)}, f32[32,128]{1,0:T(8,128)S(1)}, u32[]{:S(2)}, u32[]{:S(2)}) collective-permute-start(f32[32,128]{1,0:T(8,128)S(1)} %pad_maximum_fusion.1), channel_id=1, source_target_pairs={{0,3},{1,2},{2,1},{3,0},{4,7},{5,6},{6,5},{7,4},{8,11},{9,10},{10,... | collective-permute-start | bytes 49160 | tf_op jit(solution)/shard_map/ppermute | solution.py:252
  20.1 1.9 %collective-permute-done.7 = f32[32,128]{1,0:T(8,128)S(1)} collective-permute-done((f32[32,128]{1,0:T(8,128)S(1)}, f32[32,128]{1,0:T(8,128)S(1)}, u32[]{:S(2)}, u32[]{:S(2)}) %collective-permute-start.7) | collective-permute-done | bytes 16416 | tf_op jit(solution)/shard_map/ppermute | solution.py:252
  22.1 0.2 shard_map.117
  22.3 0.7 %collective-permute-start.12 = (bf16[16,2048]{1,0:T(8,128)(2,1)S(1)}, bf16[16,2048]{1,0:T(8,128)(2,1)S(1)}, u32[]{:S(2)}, u32[]{:S(2)}) collective-permute-start(bf16[16,2048]{1,0:T(8,128)(2,1)S(1)} %get-tuple-element.58), channel_id=1, source_target_pairs={{0,8},{4,12},{8,0},{12,4},{1,9},{5,13},{9,1},{13,5},{2,10},{6,14},... | collective-permute-start | bytes 196616 | tf_op jit(solution)/shard_map/ppermute | solution.py:252
  23.0 2.5 %collective-permute-start.11 = (bf16[16,2048]{1,0:T(8,128)(2,1)S(1)}, bf16[16,2048]{1,0:T(8,128)(2,1)S(1)}, u32[]{:S(2)}, u32[]{:S(2)}) collective-permute-start(bf16[16,2048]{1,0:T(8,128)(2,1)S(1)} %get-tuple-element.55.query_ref), channel_id=1, source_target_pairs={{0,12},{4,8},{8,4},{12,0},{1,13},{5,9},{9,5},{13,1},{2,14},{6,10},... | collective-permute-start | bytes 196616 | tf_op jit(solution)/shard_map/ppermute | solution.py:252
  25.5 0.9 %collective-permute-start.10 = (bf16[16,3200]{1,0:T(8,128)(2,1)S(1)}, bf16[16,3200]{1,0:T(8,128)(2,1)S(1)}, u32[]{:S(2)}, u32[]{:S(2)}) collective-permute-start(bf16[16,3200]{1,0:T(8,128)(2,1)S(1)} %shard_map.118.query_ref), channel_id=1, source_target_pairs={{0,8},{4,12},{8,0},{12,4},{1,9},{5,13},{9,1},{13,5},{2,10},{6,14},... | collective-permute-start | bytes 307208 | tf_op jit(solution)/shard_map/ppermute | solution.py:252
  26.4 1.1 %collective-permute-start.14 = (bf16[16,2048]{1,0:T(8,128)(2,1)S(1)}, bf16[16,2048]{1,0:T(8,128)(2,1)S(1)}, u32[]{:S(2)}, u32[]{:S(2)}) collective-permute-start(bf16[16,2048]{1,0:T(8,128)(2,1)S(1)} %get-tuple-element.64), channel_id=1, source_target_pairs={{0,4},{4,0},{8,12},{12,8},{1,5},{5,1},{9,13},{13,9},{2,6},{6,2},{1... | collective-permute-start | bytes 196616 | tf_op jit(solution)/shard_map/ppermute | solution.py:252
  27.6 0.9 %collective-permute-start.15 = (bf16[16,2048]{1,0:T(8,128)(2,1)S(1)}, bf16[16,2048]{1,0:T(8,128)(2,1)S(1)}, u32[]{:S(2)}, u32[]{:S(2)}) collective-permute-start(bf16[16,2048]{1,0:T(8,128)(2,1)S(1)} %get-tuple-element.63), channel_id=1, source_target_pairs={{0,4},{4,0},{8,12},{12,8},{1,5},{5,1},{9,13},{13,9},{2,6},{6,2},{1... | collective-permute-start | bytes 196616 | tf_op jit(solution)/shard_map/ppermute | solution.py:252
  28.5 4.2 %collective-permute-done.12.value_two_ref = bf16[16,2048]{1,0:T(8,128)(2,1)S(1)} collective-permute-done((bf16[16,2048]{1,0:T(8,128)(2,1)S(1)}, bf16[16,2048]{1,0:T(8,128)(2,1)S(1)}, u32[]{:S(2)}, u32[]{:S(2)}) %collective-permute-start.12) | collective-permute-done | bytes 65568 | tf_op jit(solution)/shard_map/ppermute | solution.py:252
  32.7 0.3 collective-permute-done.15.value_one_ref
  33.0 3.1 %collective-permute-done.10.query_two_ref = bf16[16,3200]{1,0:T(8,128)(2,1)S(1)} collective-permute-done((bf16[16,3200]{1,0:T(8,128)(2,1)S(1)}, bf16[16,3200]{1,0:T(8,128)(2,1)S(1)}, u32[]{:S(2)}, u32[]{:S(2)}) %collective-permute-start.10) | collective-permute-done | bytes 102432 | tf_op jit(solution)/shard_map/ppermute | solution.py:252
  36.1 1.3 %collective-permute-done.13.value_three_ref = bf16[16,2048]{1,0:T(8,128)(2,1)S(1)} collective-permute-done((bf16[16,2048]{1,0:T(8,128)(2,1)S(1)}, bf16[16,2048]{1,0:T(8,128)(2,1)S(1)}, u32[]{:S(2)}, u32[]{:S(2)}) %collective-permute-start.13) | collective-permute-done | bytes 65568 | tf_op jit(solution)/shard_map/ppermute | solution.py:252
  37.4 0.8 %shard_map.119 = (f32[32,2048]{1,0:T(8,128)}, f32[16,1024]{1,0:T(8,128)}, f32[16,128]{1,0:T(8,128)}) custom-call(bf16[32,2048]{1,0:T(8,128)(2,1)S(1)} %get-tuple-element.59.mine_ref, bf16[16,3200]{1,0:T(8,128)(2,1)S(1)} %shard_map.118.query_ref, bf16[16,3200]{1,0:T(8,128)(2,1)S(1)} %collective-permute-done.10.query_two_ref, ...), custom_call_target="tpu_custom_call" | custom-call | flops 1 | bytes 1 | tf_op jit(solution)/shard_map/pallas_call | solution.py:365
  (36 shorter events, 0.2 us)
Async XLA Ops:
  2.0 3.2 %copy-start.4 = (s32[128]{0:T(128)S(1)}, s32[128]{0:T(128)}, u32[]{:S(2)}) copy-start(s32[128]{0:T(128)} %param.14) | copy-start | bytes 1540
  2.1 5.8 %collective-permute-start = (f32[32,128]{1,0:T(8,128)S(1)}, f32[32,128]{1,0:T(8,128)S(1)}, u32[]{:S(2)}, u32[]{:S(2)}) collective-permute-start(f32[32,128]{1,0:T(8,128)S(1)} %get-tuple-element.33), channel_id=1, source_target_pairs={{0,1},{1,0},{2,3},{3,2},{4,5},{5,4},{6,7},{7,6},{8,9},{9,8},{10,11... | collective-permute-start | bytes 49160 | tf_op jit(solution)/shard_map/ppermute | solution.py:252
  2.6 5.2 %collective-permute-start.1 = (f32[32,128]{1,0:T(8,128)S(1)}, f32[32,128]{1,0:T(8,128)S(1)}, u32[]{:S(2)}, u32[]{:S(2)}) collective-permute-start(f32[32,128]{1,0:T(8,128)S(1)} %get-tuple-element.33), channel_id=1, source_target_pairs={{0,2},{1,3},{2,0},{3,1},{4,6},{5,7},{6,4},{7,5},{8,10},{9,11},{10,... | collective-permute-start | bytes 49160 | tf_op jit(solution)/shard_map/ppermute | solution.py:252
  5.1 3.2 %collective-permute-start.2 = (f32[32,128]{1,0:T(8,128)S(1)}, f32[32,128]{1,0:T(8,128)S(1)}, u32[]{:S(2)}, u32[]{:S(2)}) collective-permute-start(f32[32,128]{1,0:T(8,128)S(1)} %get-tuple-element.33), channel_id=1, source_target_pairs={{0,3},{1,2},{2,1},{3,0},{4,7},{5,6},{6,5},{7,4},{8,11},{9,10},{10,... | collective-permute-start | bytes 49160 | tf_op jit(solution)/shard_map/ppermute | solution.py:252
  5.2 5.9 %collective-permute-start.3 = (bf16[144,128]{1,0:T(8,128)(2,1)S(1)}, bf16[144,128]{1,0:T(8,128)(2,1)S(1)}, u32[]{:S(2)}, u32[]{:S(2)}) collective-permute-start(bf16[144,128]{1,0:T(8,128)(2,1)S(1)} %pad_maximum_fusion), channel_id=1, source_target_pairs={{0,4},{4,8},{8,12},{12,0},{1,5},{5,9},{9,13},{13,1},{2,6},{6,10},{... | collective-permute-start | bytes 110600 | tf_op jit(solution)/shard_map/ppermute | solution.py:256
  7.1 0.7 %copy-start.3 = (bf16[16,128]{1,0:T(8,128)(2,1)S(1)}, bf16[16,128]{1,0:T(8,128)(2,1)}, u32[]{:S(2)}) copy-start(bf16[16,128]{1,0:T(8,128)(2,1)} %param.17) | copy-start | bytes 12292
  7.8 0.9 %copy-start.2 = (bf16[128,1024]{1,0:T(8,128)(2,1)S(1)}, bf16[128,1024]{1,0:T(8,128)(2,1)}, u32[]{:S(2)}) copy-start(bf16[128,1024]{1,0:T(8,128)(2,1)} %q_ref.1) | copy-start | bytes 786436
  8.3 2.8 %copy-start = (bf16[128,1024]{1,0:T(8,128)(2,1)S(1)}, bf16[128,1024]{1,0:T(8,128)(2,1)}, u32[]{:S(2)}) copy-start(bf16[128,1024]{1,0:T(8,128)(2,1)} %o_ref.5) | copy-start | bytes 786436
  11.9 3.8 %collective-permute-start.4 = (f32[32,128]{1,0:T(8,128)S(1)}, f32[32,128]{1,0:T(8,128)S(1)}, u32[]{:S(2)}, u32[]{:S(2)}) collective-permute-start(f32[32,128]{1,0:T(8,128)S(1)} %slice.41), channel_id=1, source_target_pairs={{0,2},{1,3},{2,0},{3,1},{4,8},{5,9},{6,10},{7,11},{8,4},{9,5},{10,... | collective-permute-start | bytes 49160 | tf_op jit(solution)/shard_map/ppermute | solution.py:264
  13.5 3.7 %collective-permute-start.5 = (f32[32,128]{1,0:T(8,128)S(1)}, f32[32,128]{1,0:T(8,128)S(1)}, u32[]{:S(2)}, u32[]{:S(2)}) collective-permute-start(f32[32,128]{1,0:T(8,128)S(1)} %slice.41), channel_id=1, source_target_pairs={{0,4},{4,0},{8,12},{12,8},{1,5},{5,1},{9,13},{13,9},{2,6},{6,2},{1... | collective-permute-start | bytes 49160 | tf_op jit(solution)/shard_map/ppermute | solution.py:252
  17.3 4.8 %copy-start.1 = (bf16[128,2048]{1,0:T(8,128)(2,1)S(1)}, bf16[128,2048]{1,0:T(8,128)(2,1)}, u32[]{:S(2)}) copy-start(bf16[128,2048]{1,0:T(8,128)(2,1)} %x_ref.1) | copy-start | bytes 1572868
  18.2 1.9 %collective-permute-start.6 = (f32[32,128]{1,0:T(8,128)S(1)}, f32[32,128]{1,0:T(8,128)S(1)}, u32[]{:S(2)}, u32[]{:S(2)}) collective-permute-start(f32[32,128]{1,0:T(8,128)S(1)} %pad_maximum_fusion.1), channel_id=1, source_target_pairs={{0,1},{1,0},{2,3},{3,2},{4,5},{5,4},{6,7},{7,6},{8,9},{9,8},{10,11... | collective-permute-start | bytes 49160 | tf_op jit(solution)/shard_map/ppermute | solution.py:252
  18.3 3.8 %collective-permute-start.7 = (f32[32,128]{1,0:T(8,128)S(1)}, f32[32,128]{1,0:T(8,128)S(1)}, u32[]{:S(2)}, u32[]{:S(2)}) collective-permute-start(f32[32,128]{1,0:T(8,128)S(1)} %pad_maximum_fusion.1), channel_id=1, source_target_pairs={{0,2},{1,3},{2,0},{3,1},{4,6},{5,7},{6,4},{7,5},{8,10},{9,11},{10,... | collective-permute-start | bytes 49160 | tf_op jit(solution)/shard_map/ppermute | solution.py:252
  18.7 3.4 %collective-permute-start.8 = (f32[32,128]{1,0:T(8,128)S(1)}, f32[32,128]{1,0:T(8,128)S(1)}, u32[]{:S(2)}, u32[]{:S(2)}) collective-permute-start(f32[32,128]{1,0:T(8,128)S(1)} %pad_maximum_fusion.1), channel_id=1, source_target_pairs={{0,3},{1,2},{2,1},{3,0},{4,7},{5,6},{6,5},{7,4},{8,11},{9,10},{10,... | collective-permute-start | bytes 49160 | tf_op jit(solution)/shard_map/ppermute | solution.py:252
  20.1 5.4 %collective-permute-start.9 = (bf16[16,1152]{1,0:T(8,128)(2,1)S(1)}, bf16[16,1152]{1,0:T(8,128)(2,1)S(1)}, u32[]{:S(2)}, u32[]{:S(2)}) collective-permute-start(bf16[16,1152]{1,0:T(8,128)(2,1)S(1)} %get-tuple-element.56.up_ref), channel_id=1, source_target_pairs={{0,4},{4,0},{8,12},{12,8},{1,5},{5,1},{9,13},{13,9},{2,6},{6,2},{1... | collective-permute-start | bytes 110600 | tf_op jit(solution)/shard_map/ppermute | solution.py:252
  22.3 10.4 %collective-permute-start.12 = (bf16[16,2048]{1,0:T(8,128)(2,1)S(1)}, bf16[16,2048]{1,0:T(8,128)(2,1)S(1)}, u32[]{:S(2)}, u32[]{:S(2)}) collective-permute-start(bf16[16,2048]{1,0:T(8,128)(2,1)S(1)} %get-tuple-element.58), channel_id=1, source_target_pairs={{0,8},{4,12},{8,0},{12,4},{1,9},{5,13},{9,1},{13,5},{2,10},{6,14},... | collective-permute-start | bytes 196616 | tf_op jit(solution)/shard_map/ppermute | solution.py:252
  23.0 9.7 %collective-permute-start.11 = (bf16[16,2048]{1,0:T(8,128)(2,1)S(1)}, bf16[16,2048]{1,0:T(8,128)(2,1)S(1)}, u32[]{:S(2)}, u32[]{:S(2)}) collective-permute-start(bf16[16,2048]{1,0:T(8,128)(2,1)S(1)} %get-tuple-element.55.query_ref), channel_id=1, source_target_pairs={{0,12},{4,8},{8,4},{12,0},{1,13},{5,9},{9,5},{13,1},{2,14},{6,10},... | collective-permute-start | bytes 196616 | tf_op jit(solution)/shard_map/ppermute | solution.py:252
  25.5 10.6 %collective-permute-start.10 = (bf16[16,3200]{1,0:T(8,128)(2,1)S(1)}, bf16[16,3200]{1,0:T(8,128)(2,1)S(1)}, u32[]{:S(2)}, u32[]{:S(2)}) collective-permute-start(bf16[16,3200]{1,0:T(8,128)(2,1)S(1)} %shard_map.118.query_ref), channel_id=1, source_target_pairs={{0,8},{4,12},{8,0},{12,4},{1,9},{5,13},{9,1},{13,5},{2,10},{6,14},... | collective-permute-start | bytes 307208 | tf_op jit(solution)/shard_map/ppermute | solution.py:252
  26.4 6.3 %collective-permute-start.14 = (bf16[16,2048]{1,0:T(8,128)(2,1)S(1)}, bf16[16,2048]{1,0:T(8,128)(2,1)S(1)}, u32[]{:S(2)}, u32[]{:S(2)}) collective-permute-start(bf16[16,2048]{1,0:T(8,128)(2,1)S(1)} %get-tuple-element.64), channel_id=1, source_target_pairs={{0,4},{4,0},{8,12},{12,8},{1,5},{5,1},{9,13},{13,9},{2,6},{6,2},{1... | collective-permute-start | bytes 196616 | tf_op jit(solution)/shard_map/ppermute | solution.py:252
  27.6 5.4 %collective-permute-start.15 = (bf16[16,2048]{1,0:T(8,128)(2,1)S(1)}, bf16[16,2048]{1,0:T(8,128)(2,1)S(1)}, u32[]{:S(2)}, u32[]{:S(2)}) collective-permute-start(bf16[16,2048]{1,0:T(8,128)(2,1)S(1)} %get-tuple-element.63), channel_id=1, source_target_pairs={{0,4},{4,0},{8,12},{12,8},{1,5},{5,1},{9,13},{13,9},{2,6},{6,2},{1... | collective-permute-start | bytes 196616 | tf_op jit(solution)/shard_map/ppermute | solution.py:252
  32.7 4.7 %collective-permute-start.13 = (bf16[16,2048]{1,0:T(8,128)(2,1)S(1)}, bf16[16,2048]{1,0:T(8,128)(2,1)S(1)}, u32[]{:S(2)}, u32[]{:S(2)}) collective-permute-start(bf16[16,2048]{1,0:T(8,128)(2,1)S(1)} %collective-permute-done.12.value_two_ref), channel_id=1, source_target_pairs={{0,4},{4,0},{8,12},{12,8},{1,5},{5,1},{9,13},{13,9},{2,6},{6,2},{1... | collective-permute-start | bytes 196616 | tf_op jit(solution)/shard_map/ppermute | solution.py:252

commit v17 on v16

--- a/solution.py
+++ b/solution.py
@@ -357,8 +357,8 @@
         partial_kernel, [((2 * RANK, wide), BF16), ((RANK, wide), BF16), ((RANK, wide), BF16)]
     )(sum_fsdp(codes).astype(BF16), x)
     (send_q,) = call(combine_kernel, [((RANK, wide + up.shape[1]), BF16)])(part_q, up, near_up)
-    send_q, late = lax.optimization_barrier((send_q, both))
     value_two = swap(part_v, "seq", 2)
+    value_two, late = lax.optimization_barrier((value_two, both))
     value_three = swap(value_two, "seq", 1)
     query_two, query_three = swap(send_q, "seq", 2), swap(part_q, "seq", 3)
     ones = [swap(late[i * RANK : (i + 1) * RANK], "seq", 1) for i in range(2)]

time: 38.3 us -> 38.6 us (level)
  starting transfers between devices: 14.8 us -> 19.1 us
  waiting for transfers between devices: 16.4 us -> 12.4 us
    ppermute x14, starting transfers between devices: 11.3 us -> 15.6 us  [swap(): return lax.ppermute(array, axis, [(i, i ^ bit) for i in range(size)])]
    ppermute x14, waiting for transfers between devices: 12.9 us -> 8.89 us  [swap(): return lax.ppermute(array, axis, [(i, i ^ bit) for i in range(size)])]
  transfers between devices with their start and end apart: 16 -> 16, of which waited for: 9 -> 11; matrix products, arithmetic and copies ran while one was open for 1% -> 1% of each run, Pallas kernels for 3% -> 3%
where the time goes in v17:
time: 38.6 us; the launch traced here: 38.4 us
  starting transfers between devices  19.1 us (49%)
  waiting for transfers between devices  12.4 us (32%)
  Pallas kernels  4.97 us (13%)
  between operations  0.79 us (2%)
  local copies, waits for them, and re-layouts  0.71 us (2%)
  other arithmetic  0.48 us (1%)
    ppermute x14, starting transfers between devices, swap(): return lax.ppermute(array, axis, [(i, i ^ bit) for i in range(size)])  15.6 us
    ppermute x14, waiting for transfers between devices, swap(): return lax.ppermute(array, axis, [(i, i ^ bit) for i in range(size)])  8.89 us
    ppermute x1, starting transfers between devices, shift(): return lax.ppermute(array, 'seq', moves)  1.87 us
    ppermute x1, waiting for transfers between devices, shift(): return lax.ppermute(array, 'seq', moves)  1.76 us
    ppermute x1, waiting for transfers between devices, inner(): return lax.ppermute(array, ('seq', 'fsdp'), moves)  1.71 us
    ppermute x1, starting transfers between devices, inner(): return lax.ppermute(array, ('seq', 'fsdp'), moves)  1.67 us
    pallas_call x1, Pallas kernels, body(): call(functools.partial(lowrank_kernel, send), [((2 * RANK, tok), F32), ((...  1.4 us
    pallas_call x1, Pallas kernels, body(): call(functools.partial(grads_kernel, count, send, blocks, heads), [((RANK...  0.87 us
  transfers between devices with their start and end apart: 16, of which 11 were waited for; matrix products, arithmetic and copies ran while one was open for 1% of the time, Pallas kernels for 3%

profile of v17, /device:TPU:0, one launch (start us, length us, event | category | flops | bytes accessed | tf_op | source)
XLA Modules:
  0.0 38.4 jit_solution(7994725751060670660)
XLA Ops:
  0.6 1.4 %shard_map.112 = (f32[32,128]{1,0:T(8,128)S(1)}, bf16[128,128]{1,0:T(8,128)(2,1)S(1)}, bf16[128,128]{1,0:T(8,128)(2,1)S(1)}, bf16[128,128]{1,0:T(8,128)(2,1)S(1)}, bf16[16,1024]{1,0:T(8,128)(2,1)S(1)}) custom-call(bf16[128,2048]{1,0:T(8,128)(2,1)} %x_ref.1, bf16[32,2048]{1,0:T(8,128)(2,1)} %bitcast.8, bf16[128,128]{1,0:T(8,128)(2,1)} %refs_2_.1, ...), custom_call_target="tpu_custom_call" | custom-call | flops 1 | bytes 1 | tf_op jit(solution)/shard_map/pallas_call | solution.py:273
  2.1 0.5 %collective-permute-start = (f32[32,128]{1,0:T(8,128)S(1)}, f32[32,128]{1,0:T(8,128)S(1)}, u32[]{:S(2)}, u32[]{:S(2)}) collective-permute-start(f32[32,128]{1,0:T(8,128)S(1)} %get-tuple-element.33), channel_id=1, source_target_pairs={{0,1},{1,0},{2,3},{3,2},{4,5},{5,4},{6,7},{7,6},{8,9},{9,8},{10,11... | collective-permute-start | bytes 49160 | tf_op jit(solution)/shard_map/ppermute | solution.py:252
  2.6 2.6 %collective-permute-start.1 = (f32[32,128]{1,0:T(8,128)S(1)}, f32[32,128]{1,0:T(8,128)S(1)}, u32[]{:S(2)}, u32[]{:S(2)}) collective-permute-start(f32[32,128]{1,0:T(8,128)S(1)} %get-tuple-element.33), channel_id=1, source_target_pairs={{0,2},{1,3},{2,0},{3,1},{4,6},{5,7},{6,4},{7,5},{8,10},{9,11},{10,... | collective-permute-start | bytes 49160 | tf_op jit(solution)/shard_map/ppermute | solution.py:252
  5.2 1.9 %collective-permute-start.3 = (bf16[144,128]{1,0:T(8,128)(2,1)S(1)}, bf16[144,128]{1,0:T(8,128)(2,1)S(1)}, u32[]{:S(2)}, u32[]{:S(2)}) collective-permute-start(bf16[144,128]{1,0:T(8,128)(2,1)S(1)} %pad_maximum_fusion), channel_id=1, source_target_pairs={{0,4},{4,8},{8,12},{12,0},{1,5},{5,9},{9,13},{13,1},{2,6},{6,10},{... | collective-permute-start | bytes 110600 | tf_op jit(solution)/shard_map/ppermute | solution.py:256
  7.1 0.4 %multiply_sine_fusion = (f32[192,64]{1,0:T(8,128)S(1)}, f32[192,64]{1,0:T(8,128)S(1)}) fusion(f32[64]{0:T(128)S(1)} %multiply_power_fusion, f32[192]{0:T(256)S(1)} %add_convert_fusion.1), kind=kLoop, calls=%fused_computation | loop fusion | flops 12288 | bytes 99328 | tf_op jit(solution)/shard_map/sin | solution.py:298
  7.5 0.3 copy-done.3
  7.8 0.5 %collective-permute-done.2 = f32[32,128]{1,0:T(8,128)S(1)} collective-permute-done((f32[32,128]{1,0:T(8,128)S(1)}, f32[32,128]{1,0:T(8,128)S(1)}, u32[]{:S(2)}, u32[]{:S(2)}) %collective-permute-start.2) | collective-permute-done | bytes 16416 | tf_op jit(solution)/shard_map/ppermute | solution.py:252
  8.4 0.4 %copy-done.2 = bf16[128,1024]{1,0:T(8,128)(2,1)S(1)} copy-done((bf16[128,1024]{1,0:T(8,128)(2,1)S(1)}, bf16[128,1024]{1,0:T(8,128)(2,1)}, u32[]{:S(2)}) %copy-start.2) | copy-done | bytes 262168
  8.8 0.6 %shard_map.113 = (bf16[1024,128]{1,0:T(8,128)(2,1)S(1)}, bf16[128,128]{1,0:T(8,128)(2,1)S(1)}, f32[128,1024]{1,0:T(8,128)S(1)}, f32[64,128]{1,0:T(8,128)S(1)}, f32[64,128]{1,0:T(8,128)S(1)}) custom-call(f32[32,128]{1,0:T(8,128)S(1)} %add_add_fusion.low_ref, bf16[128,1024]{1,0:T(8,128)(2,1)S(1)} %copy-done.2, bf16[128,128]{1,0:T(8,128)(2,1)S(1)} %get-tuple-element.35.k_ref, ...), custom_call_target="tpu_custom_call" | custom-call | flops 3145728 | bytes 3145728 | tf_op jit(solution)/shard_map/pallas_call | solution.py:303
  9.4 1.8 %collective-permute-done.3 = bf16[144,128]{1,0:T(8,128)(2,1)S(1)} collective-permute-done((bf16[144,128]{1,0:T(8,128)(2,1)S(1)}, bf16[144,128]{1,0:T(8,128)(2,1)S(1)}, u32[]{:S(2)}, u32[]{:S(2)}) %collective-permute-start.3) | collective-permute-done | bytes 36896 | tf_op jit(solution)/shard_map/ppermute | solution.py:256
  11.1 0.8 %shard_map.114 = (f32[192,1024]{1,0:T(8,128)S(1)}, bf16[128,64]{1,0:T(8,128)(2,1)S(1)}, f32[192,128]{1,0:T(8,128)S(1)}, f32[48,128]{1,0:T(8,128)S(1)}) custom-call(bf16[1024,128]{1,0:T(8,128)(2,1)S(1)} %get-tuple-element.39.qr_ref, f32[128,1024]{1,0:T(8,128)S(1)} %get-tuple-element.40.s_ref, bf16[128,1024]{1,0:T(8,128)(2,1)S(1)} %copy-done, ...), custom_call_target="tpu_custom_call" | custom-call | flops 5242880 | bytes 5242880 | tf_op jit(solution)/shard_map/pallas_call | solution.py:316
  11.9 1.7 %collective-permute-start.4 = (f32[32,128]{1,0:T(8,128)S(1)}, f32[32,128]{1,0:T(8,128)S(1)}, u32[]{:S(2)}, u32[]{:S(2)}) collective-permute-start(f32[32,128]{1,0:T(8,128)S(1)} %slice.41), channel_id=1, source_target_pairs={{0,2},{1,3},{2,0},{3,1},{4,8},{5,9},{6,10},{7,11},{8,4},{9,5},{10,... | collective-permute-start | bytes 49160 | tf_op jit(solution)/shard_map/ppermute | solution.py:264
  13.5 0.4 shard_map.115.dp_ref
  13.9 1.7 %collective-permute-done.4 = f32[32,128]{1,0:T(8,128)S(1)} collective-permute-done((f32[32,128]{1,0:T(8,128)S(1)}, f32[32,128]{1,0:T(8,128)S(1)}, u32[]{:S(2)}, u32[]{:S(2)}) %collective-permute-start.4) | collective-permute-done | bytes 16416 | tf_op jit(solution)/shard_map/ppermute | solution.py:264
  15.6 1.7 %collective-permute-done.5 = f32[32,128]{1,0:T(8,128)S(1)} collective-permute-done((f32[32,128]{1,0:T(8,128)S(1)}, f32[32,128]{1,0:T(8,128)S(1)}, u32[]{:S(2)}, u32[]{:S(2)}) %collective-permute-start.5) | collective-permute-done | bytes 16416 | tf_op jit(solution)/shard_map/ppermute | solution.py:252
  17.3 0.9 %shard_map.116 = (f32[16,128]{1,0:T(8,128)S(1)}, bf16[16,1152]{1,0:T(8,128)(2,1)S(1)}) custom-call(f32[32,128]{1,0:T(8,128)S(1)} %add_add_fusion.low_ref, bf16[1,16,128]{2,1,0:T(8,128)(2,1)S(1)} %fusion.3.far_ref, bf16[1,144,128]{2,1,0:T(8,128)(2,1)S(1)} %bitcast.7, bf16[128,1024]{1,0:T(8,128)(2,1)S(1)} %copy-done, f32[192,1024]{1,0:T(8,128)S(1)} %get-tuple-element.44.w_ref, ...), custom_call_target="tpu_custom_call" | custom-call | flops 25165824 | bytes 25165824 | tf_op jit(solution)/shard_map/pallas_call | solution.py:342
  18.3 0.4 %collective-permute-start.7 = (f32[32,128]{1,0:T(8,128)S(1)}, f32[32,128]{1,0:T(8,128)S(1)}, u32[]{:S(2)}, u32[]{:S(2)}) collective-permute-start(f32[32,128]{1,0:T(8,128)S(1)} %pad_maximum_fusion.1), channel_id=1, source_target_pairs={{0,2},{1,3},{2,0},{3,1},{4,6},{5,7},{6,4},{7,5},{8,10},{9,11},{10,... | collective-permute-start | bytes 49160 | tf_op jit(solution)/shard_map/ppermute | solution.py:252
  18.7 1.4 %collective-permute-start.8 = (f32[32,128]{1,0:T(8,128)S(1)}, f32[32,128]{1,0:T(8,128)S(1)}, u32[]{:S(2)}, u32[]{:S(2)}) collective-permute-start(f32[32,128]{1,0:T(8,128)S(1)} %pad_maximum_fusion.1), channel_id=1, source_target_pairs={{0,3},{1,2},{2,1},{3,0},{4,7},{5,6},{6,5},{7,4},{8,11},{9,10},{10,... | collective-permute-start | bytes 49160 | tf_op jit(solution)/shard_map/ppermute | solution.py:252
  20.1 1.9 %collective-permute-done.7 = f32[32,128]{1,0:T(8,128)S(1)} collective-permute-done((f32[32,128]{1,0:T(8,128)S(1)}, f32[32,128]{1,0:T(8,128)S(1)}, u32[]{:S(2)}, u32[]{:S(2)}) %collective-permute-start.7) | collective-permute-done | bytes 16416 | tf_op jit(solution)/shard_map/ppermute | solution.py:252
  22.3 0.7 %collective-permute-start.12 = (bf16[16,2048]{1,0:T(8,128)(2,1)S(1)}, bf16[16,2048]{1,0:T(8,128)(2,1)S(1)}, u32[]{:S(2)}, u32[]{:S(2)}) collective-permute-start(bf16[16,2048]{1,0:T(8,128)(2,1)S(1)} %get-tuple-element.57), channel_id=1, source_target_pairs={{0,8},{4,12},{8,0},{12,4},{1,9},{5,13},{9,1},{13,5},{2,10},{6,14},... | collective-permute-start | bytes 196616 | tf_op jit(solution)/shard_map/ppermute | solution.py:252
  23.0 1.8 %collective-permute-start.9 = (bf16[16,1152]{1,0:T(8,128)(2,1)S(1)}, bf16[16,1152]{1,0:T(8,128)(2,1)S(1)}, u32[]{:S(2)}, u32[]{:S(2)}) collective-permute-start(bf16[16,1152]{1,0:T(8,128)(2,1)S(1)} %get-tuple-element.56.up_ref), channel_id=1, source_target_pairs={{0,4},{4,0},{8,12},{12,8},{1,5},{5,1},{9,13},{13,9},{2,6},{6,2},{1... | collective-permute-start | bytes 110600 | tf_op jit(solution)/shard_map/ppermute | solution.py:252
  24.9 1.9 %collective-permute-start.11 = (bf16[16,2048]{1,0:T(8,128)(2,1)S(1)}, bf16[16,2048]{1,0:T(8,128)(2,1)S(1)}, u32[]{:S(2)}, u32[]{:S(2)}) collective-permute-start(bf16[16,2048]{1,0:T(8,128)(2,1)S(1)} %get-tuple-element.55.query_ref), channel_id=1, source_target_pairs={{0,12},{4,8},{8,4},{12,0},{1,13},{5,9},{9,5},{13,1},{2,14},{6,10},... | collective-permute-start | bytes 196616 | tf_op jit(solution)/shard_map/ppermute | solution.py:252
  26.8 0.2 collective-permute-done.9.near_ref
  27.0 2.3 %collective-permute-start.10 = (bf16[16,3200]{1,0:T(8,128)(2,1)S(1)}, bf16[16,3200]{1,0:T(8,128)(2,1)S(1)}, u32[]{:S(2)}, u32[]{:S(2)}) collective-permute-start(bf16[16,3200]{1,0:T(8,128)(2,1)S(1)} %shard_map.118.query_ref), channel_id=1, source_target_pairs={{0,8},{4,12},{8,0},{12,4},{1,9},{5,13},{9,1},{13,5},{2,10},{6,14},... | collective-permute-start | bytes 307208 | tf_op jit(solution)/shard_map/ppermute | solution.py:252
  29.3 0.5 %collective-permute-done.12.value_two_ref = bf16[16,2048]{1,0:T(8,128)(2,1)S(1)} collective-permute-done((bf16[16,2048]{1,0:T(8,128)(2,1)S(1)}, bf16[16,2048]{1,0:T(8,128)(2,1)S(1)}, u32[]{:S(2)}, u32[]{:S(2)}) %collective-permute-start.12) | collective-permute-done | bytes 65568 | tf_op jit(solution)/shard_map/ppermute | solution.py:252
  29.8 1.7 %collective-permute-start.14 = (bf16[16,2048]{1,0:T(8,128)(2,1)S(1)}, bf16[16,2048]{1,0:T(8,128)(2,1)S(1)}, u32[]{:S(2)}, u32[]{:S(2)}) collective-permute-start(bf16[16,2048]{1,0:T(8,128)(2,1)S(1)} %get-tuple-element.64), channel_id=1, source_target_pairs={{0,4},{4,0},{8,12},{12,8},{1,5},{5,1},{9,13},{13,9},{2,6},{6,2},{1... | collective-permute-start | bytes 196616 | tf_op jit(solution)/shard_map/ppermute | solution.py:252
  31.5 0.4 %collective-permute-start.15 = (bf16[16,2048]{1,0:T(8,128)(2,1)S(1)}, bf16[16,2048]{1,0:T(8,128)(2,1)S(1)}, u32[]{:S(2)}, u32[]{:S(2)}) collective-permute-start(bf16[16,2048]{1,0:T(8,128)(2,1)S(1)} %get-tuple-element.63), channel_id=1, source_target_pairs={{0,4},{4,0},{8,12},{12,8},{1,5},{5,1},{9,13},{13,9},{2,6},{6,2},{1... | collective-permute-start | bytes 196616 | tf_op jit(solution)/shard_map/ppermute | solution.py:252
  31.9 1.6 %collective-permute-start.13 = (bf16[16,2048]{1,0:T(8,128)(2,1)S(1)}, bf16[16,2048]{1,0:T(8,128)(2,1)S(1)}, u32[]{:S(2)}, u32[]{:S(2)}) collective-permute-start(bf16[16,2048]{1,0:T(8,128)(2,1)S(1)} %collective-permute-done.12.value_two_ref), channel_id=1, source_target_pairs={{0,4},{4,0},{8,12},{12,8},{1,5},{5,1},{9,13},{13,9},{2,6},{6,2},{1... | collective-permute-start | bytes 196616 | tf_op jit(solution)/shard_map/ppermute | solution.py:252
  33.5 2.5 %collective-permute-done.10.query_two_ref = bf16[16,3200]{1,0:T(8,128)(2,1)S(1)} collective-permute-done((bf16[16,3200]{1,0:T(8,128)(2,1)S(1)}, bf16[16,3200]{1,0:T(8,128)(2,1)S(1)}, u32[]{:S(2)}, u32[]{:S(2)}) %collective-permute-start.10) | collective-permute-done | bytes 102432 | tf_op jit(solution)/shard_map/ppermute | solution.py:252
  36.2 0.7 %collective-permute-done.15.value_one_ref = bf16[16,2048]{1,0:T(8,128)(2,1)S(1)} collective-permute-done((bf16[16,2048]{1,0:T(8,128)(2,1)S(1)}, bf16[16,2048]{1,0:T(8,128)(2,1)S(1)}, u32[]{:S(2)}, u32[]{:S(2)}) %collective-permute-start.15) | collective-permute-done | bytes 65568 | tf_op jit(solution)/shard_map/ppermute | solution.py:252
  36.9 0.7 %collective-permute-done.13.value_three_ref = bf16[16,2048]{1,0:T(8,128)(2,1)S(1)} collective-permute-done((bf16[16,2048]{1,0:T(8,128)(2,1)S(1)}, bf16[16,2048]{1,0:T(8,128)(2,1)S(1)}, u32[]{:S(2)}, u32[]{:S(2)}) %collective-permute-start.13) | collective-permute-done | bytes 65568 | tf_op jit(solution)/shard_map/ppermute | solution.py:252
  37.6 0.8 %shard_map.119 = (f32[32,2048]{1,0:T(8,128)}, f32[16,1024]{1,0:T(8,128)}, f32[16,128]{1,0:T(8,128)}) custom-call(bf16[32,2048]{1,0:T(8,128)(2,1)S(1)} %get-tuple-element.59.mine_ref, bf16[16,3200]{1,0:T(8,128)(2,1)S(1)} %shard_map.118.query_ref, bf16[16,3200]{1,0:T(8,128)(2,1)S(1)} %collective-permute-done.10.query_two_ref, ...), custom_call_target="tpu_custom_call" | custom-call | flops 1 | bytes 1 | tf_op jit(solution)/shard_map/pallas_call | solution.py:365
  (36 shorter events, 0.6 us)
Async XLA Ops:
  2.0 3.2 %copy-start.4 = (s32[128]{0:T(128)S(1)}, s32[128]{0:T(128)}, u32[]{:S(2)}) copy-start(s32[128]{0:T(128)} %param.14) | copy-start | bytes 1540
  2.1 5.8 %collective-permute-start = (f32[32,128]{1,0:T(8,128)S(1)}, f32[32,128]{1,0:T(8,128)S(1)}, u32[]{:S(2)}, u32[]{:S(2)}) collective-permute-start(f32[32,128]{1,0:T(8,128)S(1)} %get-tuple-element.33), channel_id=1, source_target_pairs={{0,1},{1,0},{2,3},{3,2},{4,5},{5,4},{6,7},{7,6},{8,9},{9,8},{10,11... | collective-permute-start | bytes 49160 | tf_op jit(solution)/shard_map/ppermute | solution.py:252
  2.6 5.2 %collective-permute-start.1 = (f32[32,128]{1,0:T(8,128)S(1)}, f32[32,128]{1,0:T(8,128)S(1)}, u32[]{:S(2)}, u32[]{:S(2)}) collective-permute-start(f32[32,128]{1,0:T(8,128)S(1)} %get-tuple-element.33), channel_id=1, source_target_pairs={{0,2},{1,3},{2,0},{3,1},{4,6},{5,7},{6,4},{7,5},{8,10},{9,11},{10,... | collective-permute-start | bytes 49160 | tf_op jit(solution)/shard_map/ppermute | solution.py:252
  5.1 3.2 %collective-permute-start.2 = (f32[32,128]{1,0:T(8,128)S(1)}, f32[32,128]{1,0:T(8,128)S(1)}, u32[]{:S(2)}, u32[]{:S(2)}) collective-permute-start(f32[32,128]{1,0:T(8,128)S(1)} %get-tuple-element.33), channel_id=1, source_target_pairs={{0,3},{1,2},{2,1},{3,0},{4,7},{5,6},{6,5},{7,4},{8,11},{9,10},{10,... | collective-permute-start | bytes 49160 | tf_op jit(solution)/shard_map/ppermute | solution.py:252
  5.2 5.9 %collective-permute-start.3 = (bf16[144,128]{1,0:T(8,128)(2,1)S(1)}, bf16[144,128]{1,0:T(8,128)(2,1)S(1)}, u32[]{:S(2)}, u32[]{:S(2)}) collective-permute-start(bf16[144,128]{1,0:T(8,128)(2,1)S(1)} %pad_maximum_fusion), channel_id=1, source_target_pairs={{0,4},{4,8},{8,12},{12,0},{1,5},{5,9},{9,13},{13,1},{2,6},{6,10},{... | collective-permute-start | bytes 110600 | tf_op jit(solution)/shard_map/ppermute | solution.py:256
  7.1 0.7 %copy-start.3 = (bf16[16,128]{1,0:T(8,128)(2,1)S(1)}, bf16[16,128]{1,0:T(8,128)(2,1)}, u32[]{:S(2)}) copy-start(bf16[16,128]{1,0:T(8,128)(2,1)} %param.17) | copy-start | bytes 12292
  7.8 0.9 %copy-start.2 = (bf16[128,1024]{1,0:T(8,128)(2,1)S(1)}, bf16[128,1024]{1,0:T(8,128)(2,1)}, u32[]{:S(2)}) copy-start(bf16[128,1024]{1,0:T(8,128)(2,1)} %q_ref.1) | copy-start | bytes 786436
  8.3 2.8 %copy-start = (bf16[128,1024]{1,0:T(8,128)(2,1)S(1)}, bf16[128,1024]{1,0:T(8,128)(2,1)}, u32[]{:S(2)}) copy-start(bf16[128,1024]{1,0:T(8,128)(2,1)} %o_ref.5) | copy-start | bytes 786436
  11.9 3.8 %collective-permute-start.4 = (f32[32,128]{1,0:T(8,128)S(1)}, f32[32,128]{1,0:T(8,128)S(1)}, u32[]{:S(2)}, u32[]{:S(2)}) collective-permute-start(f32[32,128]{1,0:T(8,128)S(1)} %slice.41), channel_id=1, source_target_pairs={{0,2},{1,3},{2,0},{3,1},{4,8},{5,9},{6,10},{7,11},{8,4},{9,5},{10,... | collective-permute-start | bytes 49160 | tf_op jit(solution)/shard_map/ppermute | solution.py:264
  13.5 3.7 %collective-permute-start.5 = (f32[32,128]{1,0:T(8,128)S(1)}, f32[32,128]{1,0:T(8,128)S(1)}, u32[]{:S(2)}, u32[]{:S(2)}) collective-permute-start(f32[32,128]{1,0:T(8,128)S(1)} %slice.41), channel_id=1, source_target_pairs={{0,4},{4,0},{8,12},{12,8},{1,5},{5,1},{9,13},{13,9},{2,6},{6,2},{1... | collective-permute-start | bytes 49160 | tf_op jit(solution)/shard_map/ppermute | solution.py:252
  17.3 4.8 %copy-start.1 = (bf16[128,2048]{1,0:T(8,128)(2,1)S(1)}, bf16[128,2048]{1,0:T(8,128)(2,1)}, u32[]{:S(2)}) copy-start(bf16[128,2048]{1,0:T(8,128)(2,1)} %x_ref.1) | copy-start | bytes 1572868
  18.2 1.9 %collective-permute-start.6 = (f32[32,128]{1,0:T(8,128)S(1)}, f32[32,128]{1,0:T(8,128)S(1)}, u32[]{:S(2)}, u32[]{:S(2)}) collective-permute-start(f32[32,128]{1,0:T(8,128)S(1)} %pad_maximum_fusion.1), channel_id=1, source_target_pairs={{0,1},{1,0},{2,3},{3,2},{4,5},{5,4},{6,7},{7,6},{8,9},{9,8},{10,11... | collective-permute-start | bytes 49160 | tf_op jit(solution)/shard_map/ppermute | solution.py:252
  18.3 3.8 %collective-permute-start.7 = (f32[32,128]{1,0:T(8,128)S(1)}, f32[32,128]{1,0:T(8,128)S(1)}, u32[]{:S(2)}, u32[]{:S(2)}) collective-permute-start(f32[32,128]{1,0:T(8,128)S(1)} %pad_maximum_fusion.1), channel_id=1, source_target_pairs={{0,2},{1,3},{2,0},{3,1},{4,6},{5,7},{6,4},{7,5},{8,10},{9,11},{10,... | collective-permute-start | bytes 49160 | tf_op jit(solution)/shard_map/ppermute | solution.py:252
  18.7 3.4 %collective-permute-start.8 = (f32[32,128]{1,0:T(8,128)S(1)}, f32[32,128]{1,0:T(8,128)S(1)}, u32[]{:S(2)}, u32[]{:S(2)}) collective-permute-start(f32[32,128]{1,0:T(8,128)S(1)} %pad_maximum_fusion.1), channel_id=1, source_target_pairs={{0,3},{1,2},{2,1},{3,0},{4,7},{5,6},{6,5},{7,4},{8,11},{9,10},{10,... | collective-permute-start | bytes 49160 | tf_op jit(solution)/shard_map/ppermute | solution.py:252
  22.3 7.5 %collective-permute-start.12 = (bf16[16,2048]{1,0:T(8,128)(2,1)S(1)}, bf16[16,2048]{1,0:T(8,128)(2,1)S(1)}, u32[]{:S(2)}, u32[]{:S(2)}) collective-permute-start(bf16[16,2048]{1,0:T(8,128)(2,1)S(1)} %get-tuple-element.57), channel_id=1, source_target_pairs={{0,8},{4,12},{8,0},{12,4},{1,9},{5,13},{9,1},{13,5},{2,10},{6,14},... | collective-permute-start | bytes 196616 | tf_op jit(solution)/shard_map/ppermute | solution.py:252
  23.0 4.0 %collective-permute-start.9 = (bf16[16,1152]{1,0:T(8,128)(2,1)S(1)}, bf16[16,1152]{1,0:T(8,128)(2,1)S(1)}, u32[]{:S(2)}, u32[]{:S(2)}) collective-permute-start(bf16[16,1152]{1,0:T(8,128)(2,1)S(1)} %get-tuple-element.56.up_ref), channel_id=1, source_target_pairs={{0,4},{4,0},{8,12},{12,8},{1,5},{5,1},{9,13},{13,9},{2,6},{6,2},{1... | collective-permute-start | bytes 110600 | tf_op jit(solution)/shard_map/ppermute | solution.py:252
  24.9 8.7 %collective-permute-start.11 = (bf16[16,2048]{1,0:T(8,128)(2,1)S(1)}, bf16[16,2048]{1,0:T(8,128)(2,1)S(1)}, u32[]{:S(2)}, u32[]{:S(2)}) collective-permute-start(bf16[16,2048]{1,0:T(8,128)(2,1)S(1)} %get-tuple-element.55.query_ref), channel_id=1, source_target_pairs={{0,12},{4,8},{8,4},{12,0},{1,13},{5,9},{9,5},{13,1},{2,14},{6,10},... | collective-permute-start | bytes 196616 | tf_op jit(solution)/shard_map/ppermute | solution.py:252
  27.0 9.1 %collective-permute-start.10 = (bf16[16,3200]{1,0:T(8,128)(2,1)S(1)}, bf16[16,3200]{1,0:T(8,128)(2,1)S(1)}, u32[]{:S(2)}, u32[]{:S(2)}) collective-permute-start(bf16[16,3200]{1,0:T(8,128)(2,1)S(1)} %shard_map.118.query_ref), channel_id=1, source_target_pairs={{0,8},{4,12},{8,0},{12,4},{1,9},{5,13},{9,1},{13,5},{2,10},{6,14},... | collective-permute-start | bytes 307208 | tf_op jit(solution)/shard_map/ppermute | solution.py:252
  29.8 6.4 %collective-permute-start.14 = (bf16[16,2048]{1,0:T(8,128)(2,1)S(1)}, bf16[16,2048]{1,0:T(8,128)(2,1)S(1)}, u32[]{:S(2)}, u32[]{:S(2)}) collective-permute-start(bf16[16,2048]{1,0:T(8,128)(2,1)S(1)} %get-tuple-element.64), channel_id=1, source_target_pairs={{0,4},{4,0},{8,12},{12,8},{1,5},{5,1},{9,13},{13,9},{2,6},{6,2},{1... | collective-permute-start | bytes 196616 | tf_op jit(solution)/shard_map/ppermute | solution.py:252
  31.5 5.4 %collective-permute-start.15 = (bf16[16,2048]{1,0:T(8,128)(2,1)S(1)}, bf16[16,2048]{1,0:T(8,128)(2,1)S(1)}, u32[]{:S(2)}, u32[]{:S(2)}) collective-permute-start(bf16[16,2048]{1,0:T(8,128)(2,1)S(1)} %get-tuple-element.63), channel_id=1, source_target_pairs={{0,4},{4,0},{8,12},{12,8},{1,5},{5,1},{9,13},{13,9},{2,6},{6,2},{1... | collective-permute-start | bytes 196616 | tf_op jit(solution)/shard_map/ppermute | solution.py:252
  31.9 5.7 %collective-permute-start.13 = (bf16[16,2048]{1,0:T(8,128)(2,1)S(1)}, bf16[16,2048]{1,0:T(8,128)(2,1)S(1)}, u32[]{:S(2)}, u32[]{:S(2)}) collective-permute-start(bf16[16,2048]{1,0:T(8,128)(2,1)S(1)} %collective-permute-done.12.value_two_ref), channel_id=1, source_target_pairs={{0,4},{4,0},{8,12},{12,8},{1,5},{5,1},{9,13},{13,9},{2,6},{6,2},{1... | collective-permute-start | bytes 196616 | tf_op jit(solution)/shard_map/ppermute | solution.py:252
